TPU v7x, 32 devices: a whole 2x2x4 slice. The times are simulated.
32 devices in a mesh: pts: 8 (over y, x, core), top: 4 (over z).
Axes of the slice: x: 2, y: 2, z: 4, core: 2. Of those that a mesh axis runs over, the one named last changes fastest.
Arguments:
- local_pos: float32 [3, 32768], P(None, ('pts', 'top')), may hold values from -1 to 1
- densities: float32 [8, 32768], P(None, ('pts', 'top')), may hold values from -6 to 6
- morton_slot: int32 [32768], P(('pts', 'top')), may hold values from 0 to 32767, as said below
- slot_leaf: int32 [32768], P(('pts', 'top')), may hold values from 0 to 4095, as said below
- uc2e: float32 [152, 152], replicated, may hold values from -0.5 to 0.5
- m2m: float32 [184832], replicated, may hold values from -0.15625 to 0.15625
- m2l_ops: bfloat16 [7300864], replicated, may hold values from -0.02734375 to 0.02734375
- dc2e: float32 [152, 152], replicated, may hold values from -0.5 to 0.5
- lattice: float32 [152, 152], replicated, may hold values from -0.5 to 0.5
- l2l: float32 [184832], replicated, may hold values from -0.5 to 0.5
Outputs:
- potentials: float32 [8, 32768], P(None, ('pts', 'top'))
Inputs may be any that keep to these rules, and one draw needn't show every extreme that they name: `morton_slot`: every slot 0 to 32767 appears once. The points of one device go to at most 64 slots of any one device of the Morton layout (slot // 1024). `slot_leaf`: Non-decreasing. The leaves of the 4096 slots of one owner (slot // 4096) lie in at most 128 consecutive boxes of level 3 (leaf // 8).
All inputs are finite; a program needn't handle non-finite values.
Results may differ from a plain program's by a relative error of at most 0.003.
Values may be sent and summed in bfloat16 or wider, within the bound.
No kernel may reach another device: no remote copies, remote signals or barrier semaphores. Data moves between devices by JAX's collectives and lax.ppermute only.
A program may use at most 192 MiB of HBM per device.

v0:
```python
import math

import jax
import jax.numpy as jnp
import numpy as np
from jax import lax
from jax.sharding import PartitionSpec as P

LEVEL = 3
EDGE = 6
DENS = 8
BOXES4 = 512


def surface_table():
    grid_vals = np.linspace(-1.0, 1.0, EDGE)
    points_list = []
    for index_a in range(EDGE):
        for index_b in range(EDGE):
            for index_c in range(EDGE):
                if (
                    min(index_a, index_b, index_c) == 0
                    or max(index_a, index_b, index_c) == EDGE - 1
                ):
                    points_list.append([grid_vals[index_a], grid_vals[index_b], grid_vals[index_c]])
    return np.array(points_list, dtype=np.float32).T


def offset_table():
    points_list = []
    for shift_x in range(-3, 4):
        for shift_y in range(-3, 4):
            for shift_z in range(-3, 4):
                if max(abs(shift_x), abs(shift_y), abs(shift_z)) >= 2:
                    points_list.append([shift_x, shift_y, shift_z])
    return np.array(points_list, dtype=np.int32)


def morton_decode(number, bit_count):
    coord_x = jnp.zeros_like(number)
    coord_y = jnp.zeros_like(number)
    coord_z = jnp.zeros_like(number)
    for level_idx in range(bit_count):
        digit_val = number // 8**level_idx % 8
        coord_x = coord_x + digit_val // 4 * 2**level_idx
        coord_y = coord_y + digit_val // 2 % 2 * 2**level_idx
        coord_z = coord_z + digit_val % 2 * 2**level_idx
    return (coord_x, coord_y, coord_z)


def morton_encode(coord_x, coord_y, coord_z, bit_count):
    number = jnp.zeros_like(coord_x)
    for level_idx in range(bit_count):
        digit_val = (
            coord_x // 2**level_idx % 2 * 4
            + coord_y // 2**level_idx % 2 * 2
            + coord_z // 2**level_idx % 2
        )
        number = number + digit_val * 8**level_idx
    return number


def source_boxes(targets):
    side_len = 2**LEVEL
    coord_x, coord_y, coord_z = morton_decode(targets, LEVEL)
    shift_table = jnp.asarray(offset_table())
    return morton_encode(
        (coord_x[None, :] + shift_table[:, 0:1]) % side_len,
        (coord_y[None, :] + shift_table[:, 1:2]) % side_len,
        (coord_z[None, :] + shift_table[:, 2:3]) % side_len,
        LEVEL,
    ).astype(jnp.int32)


def kernel_tile(local_pos):
    surface = surface_table()
    squared = jnp.zeros((local_pos.shape[1], surface.shape[1]), jnp.float32)
    for dim_index in range(3):
        spacing = 1.25 * jnp.asarray(surface[dim_index])[None, :] - local_pos[dim_index][:, None]
        squared = squared + spacing * spacing
    return 1.0 / (4.0 * math.pi * jnp.sqrt(squared))


def upward(level_mult, m2m):
    current = level_mult
    for level_idx in range(LEVEL):
        parents = current.shape[2] // 8
        current = jnp.einsum(
            "oce,ekpo->ckp",
            m2m,
            current.reshape(current.shape[0], current.shape[1], parents, 8),
            precision=lax.Precision.HIGHEST,
        )
    return current


def downward(root_local, l2l, levels):
    current = root_local
    for level_idx in range(levels):
        current = jnp.einsum("oce,ekp->ckpo", l2l, current, precision=lax.Precision.HIGHEST)
        current = current.reshape(current.shape[0], current.shape[1], -1)
    return current


def leaf_window(kernel, dens_vals, leaf_local, uc2e, m2m, box_cap):
    coef_len = kernel.shape[1]
    dens_len = dens_vals.shape[0]
    contrib = (dens_vals.T[:, :, None] * kernel[:, None, :]).reshape(
        kernel.shape[0], dens_len * coef_len
    )
    checks = jax.ops.segment_sum(
        contrib, leaf_local, num_segments=8 * box_cap, indices_are_sorted=True
    )
    checks = checks.reshape(box_cap, 8, dens_len, coef_len)
    leaf_mult = jnp.einsum("ef,bokf->boke", uc2e, checks, precision=lax.Precision.HIGHEST)
    return jnp.einsum("oce,boke->ckb", m2m, leaf_mult, precision=lax.Precision.HIGHEST)


def box_locals(targets, level4_low, m2l_ops, dc2e, coarse, l2l):
    coef_len = m2l_ops.shape[0]
    dens_len = level4_low.shape[1]
    count = targets.shape[0]
    block_len = math.gcd(count, 128)
    sources = source_boxes(targets)

    def one_block(block_idx):
        gathered = level4_low[:, :, sources]
        return jnp.einsum("cds,skdt->ckt", m2l_ops, gathered, preferred_element_type=jnp.float32)

    checks = lax.map(one_block, jnp.arange(count // block_len, dtype=jnp.int32))
    checks = checks.transpose(1, 2, 0, 3).reshape(coef_len, dens_len, count)
    from_checks = jnp.einsum("cd,dkt->ckt", dc2e, checks, precision=lax.Precision.HIGHEST)
    parents = coarse[:, :, targets // 8]
    children = jnp.einsum("oce,ekt->ockt", l2l, parents, precision=lax.Precision.HIGHEST)
    octant_mask = (targets % 8)[None, :] == jnp.arange(8, dtype=jnp.int32)[:, None]
    lattice_part = jnp.sum(jnp.where(octant_mask[:, None, None, :], children, 0.0), axis=0)
    return from_checks + lattice_part


def per_device(
    local_pos, densities, morton_slot, slot_leaf, uc2e, m2m, m2l_ops, dc2e, lattice, l2l
):
    devices = lax.axis_size(("pts", "top"))
    n_pts = lax.axis_size("pts")
    n_top = lax.axis_size("top")
    points_dev = local_pos.shape[1]
    send_cap = 2 * points_dev // devices
    box_cap = 2 * BOXES4 // n_pts
    dens_dev = DENS // n_top
    coef_len = uc2e.shape[0]
    m2m = m2m.reshape(8, coef_len, coef_len)
    l2l = l2l.reshape(8, coef_len, coef_len)
    m2l_ops = m2l_ops.reshape(coef_len, -1, coef_len)
    dest_dev = morton_slot // points_dev
    slot_local = morton_slot % points_dev
    dest_order = jnp.argsort(dest_dev, stable=True)
    sorted_dest = dest_dev[dest_order]
    first_pos = jnp.searchsorted(sorted_dest, jnp.arange(devices, dtype=jnp.int32), side="left")
    rank_sorted = jnp.arange(points_dev, dtype=jnp.int32) - first_pos[sorted_dest]
    rank_vals = jnp.zeros((points_dev,), jnp.int32).at[dest_order].set(rank_sorted)
    position = dest_dev * send_cap + rank_vals
    payload = jnp.concatenate([local_pos, densities], axis=0)
    outgoing = jnp.zeros((3 + DENS, devices * send_cap), jnp.float32).at[:, position].set(payload)
    labels = (
        jnp.full((1, devices * send_cap), points_dev, jnp.int32).at[0, position].set(slot_local)
    )
    incoming, arrivals = (
        lax.all_to_all(outgoing, ("pts", "top"), split_axis=1, concat_axis=1, tiled=True),
        lax.all_to_all(labels, ("pts", "top"), split_axis=1, concat_axis=1, tiled=True),
    )
    slot_vals = (
        jnp.zeros((3 + DENS, points_dev), jnp.float32).at[:, arrivals[0]].set(incoming, mode="drop")
    )
    my_pos = slot_vals[:3]
    my_dens = slot_vals[3:]
    first_box = lax.pmin(slot_leaf[0] // 8, "top")
    leaf_local = slot_leaf - 8 * first_box
    kernel = kernel_tile(my_pos)
    partial_value = leaf_window(kernel, my_dens, leaf_local, uc2e, m2m, box_cap)
    owner_part = lax.psum_scatter(partial_value, "top", scatter_dimension=1, tiled=True)
    rounded = owner_part.astype(jnp.bfloat16)
    box_ids = (first_box + jnp.arange(box_cap, dtype=jnp.int32)).reshape(1, 1, box_cap)
    values = lax.all_gather(rounded, "pts", axis=2, tiled=True)
    id_vals = lax.all_gather(box_ids, "pts", axis=2, tiled=True)
    level4 = (
        jnp.zeros((coef_len, dens_dev, BOXES4), jnp.float32)
        .at[:, :, id_vals[0, 0]]
        .add(values.astype(jnp.float32), mode="drop")
    )
    level4_low = level4.astype(jnp.bfloat16)
    root_mult = upward(level4, m2m)
    root_local = jnp.einsum("ce,ekp->ckp", lattice, root_mult, precision=lax.Precision.HIGHEST)
    coarse = downward(root_local, l2l, LEVEL - 1)
    per_dev = BOXES4 // n_pts
    targets = lax.axis_index("pts") * per_dev + jnp.arange(per_dev, dtype=jnp.int32)
    computed = box_locals(targets, level4_low, m2l_ops, dc2e, coarse, l2l)
    piece_vals = lax.all_gather(computed, "pts", axis=2, tiled=True)
    window_pos = jnp.arange(piece_vals.shape[2], dtype=jnp.int32) - first_box
    window_pos = jnp.where((window_pos >= 0) & (window_pos < box_cap), window_pos, box_cap)
    locals4 = (
        jnp.zeros((coef_len, dens_dev, box_cap), jnp.float32)
        .at[:, :, window_pos]
        .add(piece_vals, mode="drop")
    )
    full_locals = lax.all_gather(locals4, "top", axis=1, tiled=True)
    leaf_locals = jnp.einsum("oce,ekb->ckbo", l2l, full_locals, precision=lax.Precision.HIGHEST)
    leaf_locals = leaf_locals.reshape(coef_len, DENS, 8 * box_cap)
    at_slots = leaf_locals[:, :, leaf_local]
    potential = jnp.einsum("sc,cks->ks", kernel, at_slots, precision=lax.Precision.HIGHEST)
    reply_index = jnp.minimum(arrivals[0], points_dev - 1)
    reply_vals = potential[:, reply_index]
    returned = lax.all_to_all(reply_vals, ("pts", "top"), split_axis=1, concat_axis=1, tiled=True)
    return returned[:, position]


def solution(mesh):
    placed = (
        P(None, ("pts", "top")),
        P(None, ("pts", "top")),
        P(("pts", "top")),
        P(("pts", "top")),
        P(),
        P(),
        P(),
        P(),
        P(),
        P(),
    )
    return jax.shard_map(
        per_device, mesh=mesh, in_specs=placed, out_specs=P(None, ("pts", "top")), check_vma=False
    )
```

profile of v0, /device:TPU:0, one launch (start us, length us, event | category | flops | bytes accessed | tf_op | source)
XLA Modules:
  0.0 621.2 jit_solution(9720386205740874232)
XLA Ops:
  7.4 4.4 sort.17
  11.8 4.5 gather_fusion.1
  16.3 8.0 %while.28 = (s32[]{:T(128)}, u32[32]{0:T(128)S(1)}, u32[32]{0:T(128)S(1)}, s32[1024]{0:T(1024)S(1)}, s32[]{:T(128)}, /*index=5*/s32[]{:T(128)}, s32[]{}) while((s32[]{:T(128)}, u32[32]{0:T(128)S(1)}, u32[32]{0:T(128)S(1)}, s32[1024]{0:T(1024)S(1)}, s32[]{:T(128)}, /*index=5*/s32[]{:T(128)}, s32[]{}) %tuple.100), condition=%wide.region_3.4_spmd.clone, body=%wide.region_2.3_spmd.clone.sunk | while | flops 1444 | bytes 5740 | solution.py:158
  25.8 4.4 compare_select_fusion.5
  30.5 15.7 %select_subtract_fusion = s32[1024]{0:T(1024)S(1)} fusion(pred[1024]{0:T(1024)(128)(4,1)S(1)} %get-tuple-element.132, pred[1024]{0:T(1024)(128)(4,1)S(1)} %get-tuple-element.131, pred[1024]{0:T(1024)(128)(4,1)S(1)} %get-tuple-element.130, pred[1024]{0:T(1024)(128)(4,1)S(1)} %get-tuple-element.129, pred[1024]{0:T(1024)(128)(4,1)S(1)} %get-tuple-element.128, ...), kind=kLoop, calls=%fused_computation.214 | loop fusion | flops 26624 | bytes 33892 | tf_op jit(solution)/shard_map/sub | solution.py:159
  50.8 4.3 scatter_custom_fusion.6
  55.8 7.3 %all-to-all-start = ((s32[1,32,64]{2,0,1:T(1,128)}), s32[1,32,64]{2,0,1:T(1,128)S(1)}, u32[]{:S(2)}, u32[]{:S(2)}) async-start(s32[1,32,64]{2,0,1:T(1,128)} %all_to_all.22), calls=%async_computation | async-start | bytes 32768 | tf_op jit(solution)/shard_map/all_to_all | solution.py:169
  66.5 9.1 %pmin.7 = s32[]{:T(128)} all-reduce(s32[]{:T(128)S(6)} %select_n.510), channel_id=1, replica_groups=mesh['pts'=8,'top'=4] {'top'}, use_global_device_ids=true, to_apply=%region_0.1 | all-reduce | flops 1 | bytes 8 | tf_op jit(solution)/shard_map/pmin | solution.py:176
  91.2 6.6 %all-to-all-done.1 = f32[32,1,704]{2,1,0:T(1,128)S(1)} async-done(((f32[32,1,704]{2,1,0:T(1,128)}), f32[32,1,704]{2,1,0:T(1,128)S(1)}, u32[]{:S(2)}, u32[]{:S(2)}) %all-to-all-start.1) | async-done | bytes 90144 | tf_op jit(solution)/shard_map/all_to_all | solution.py:168
  99.8 5.9 scatter_custom_fusion.2
  111.0 5.9 copy.78
  116.9 13.9 %scatter_custom_fusion.3 = f32[1024,1216]{1,0:T(8,128)} fusion(s32[1024]{0:T(1024)S(1)} %get-tuple-element.144, f32[1024,1216]{1,0:T(8,128)} %copy.78, f32[]{:T(128)} %constant.379.clone.1), kind=kCustom, calls=%fused_computation.29 | custom fusion | flops 1245184 | bytes 4981248 | tf_op jit(solution)/shard_map/scatter-add | solution.py:111
  130.7 9.5 %reshape.1348 = f32[128,8,8,152]{3,2,1,0:T(8,128)} reshape(f32[1024,1216]{1,0:T(8,128)} %scatter_custom_fusion.3) | data formatting | bytes 9961472 | tf_op jit(solution)/shard_map/reshape | solution.py:114
  140.2 17.5 %fusion.9 = f32[128,8,8,152]{0,3,1,2:T(8,128)S(1)} fusion(f32[128,8,8,152]{3,2,1,0:T(8,128)} %reshape.1348, f32[152,152]{1,0:T(8,128)S(1)} %copy-done), kind=kOutput, calls=%fused_computation.27 | convolution fusion | flops 2271215616 | bytes 10053888 | tf_op jit(solution)/shard_map/ef,bokf->boke/dot_general | solution.py:115
  157.7 4.6 convolution_bitcast_fusion.2
  170.5 71.6 %reshape.1350 = bf16[152,316,152]{2,1,0:T(8,128)(2,1)} reshape(bf16[7300864]{0:T(1024)(128)(2,1)} %param.22) | data formatting | bytes 29203456 | tf_op jit(solution)/shard_map/reshape | solution.py:153
  242.1 34.7 %copy.82 = bf16[152,316,152]{1,0,2:T(8,128)(2,1)} copy(bf16[152,316,152]{2,1,0:T(8,128)(2,1)} %reshape.1350) | data formatting | bytes 29203456 | tf_op jit(solution)/shard_map/reshape | solution.py:153
  276.9 8.0 %all_gather.12 = s32[1,1,1024]{2,1,0:T(1,128)S(1)} all-gather(s32[1,1,128]{2,1,0:T(1,128)S(1)} %iota_add_fusion.1), channel_id=1, replica_groups=mesh['pts'=8,'top'=4] {'pts'}, dimensions={2}, use_global_device_ids=true | all-gather | bytes 4608 | tf_op jit(solution)/shard_map/all_gather | solution.py:184
  288.5 10.0 %all_gather.13 = bf16[152,2,1024]{2,0,1:T(8,128)(2,1)S(1)} all-gather(bf16[152,2,128]{2,0,1:T(8,128)(2,1)S(1)} %convert_element_type.20), channel_id=1, replica_groups=mesh['pts'=8,'top'=4] {'pts'}, dimensions={2}, use_global_device_ids=true | all-gather | bytes 700416 | tf_op jit(solution)/shard_map/all_gather | solution.py:183
  301.2 70.8 %scatter_fusion = f32[152,2,512]{0,1,2:T(2,128)S(1)} fusion(f32[152,2,512]{0,1,2:T(2,128)S(1)} %broadcast_in_dim.90, s32[1024]{0:T(1024)S(1)} %bitcast.190, f32[1024,152,2]{1,2,0:T(2,128)} %copy.80), kind=kCustom, calls=%fused_computation.11 | custom fusion | flops 311296 | bytes 3739648 | tf_op jit(solution)/shard_map/scatter-add | solution.py:188
  379.0 71.7 %gather_fusion.2 = bf16[20224,152,2]{1,2,0:T(2,128)(2,1)} fusion(bf16[152,2,512]{0,1,2:T(2,128)(2,1)S(1)} %convert_element_type.22, s32[20480]{0:T(1024)S(1)} %pad_clamp_fusion.1), kind=kCustom, calls=%fused_computation.2 | custom fusion | bytes 24673280 | tf_op jit(solution)/shard_map/while/body/eval_jaxpr/gather | solution.py:127
  450.6 42.0 %copy.81 = bf16[316,64,152,2]{0,1,2,3:T(8,128)(2,1)} copy(bf16[316,64,152,2]{2,3,1,0:T(2,128)(2,1)} %bitcast.169) | data formatting | bytes 24592384 | tf_op jit(solution)/shard_map/while/body/eval_jaxpr/gather | solution.py:127
  494.6 12.4 %fusion.16 = f32[152,2,64]{0,2,1:T(8,128)S(1)} fusion(bf16[152,316,152]{1,0,2:T(8,128)(2,1)} %copy.82, bf16[316,64,152,2]{0,1,2,3:T(8,128)(2,1)} %copy.81), kind=kOutput, calls=%fused_computation.42 | convolution fusion | flops 1869021184 | bytes 26975744 | tf_op jit(solution)/shard_map/while/body/eval_jaxpr/cds,skdt->ckt/dot_general | solution.py:128
  507.3 10.7 %all_gather.14 = f32[152,2,512]{0,2,1:T(8,128)S(1)} all-gather(f32[152,2,64]{0,2,1:T(8,128)S(1)} %fusion.15), channel_id=1, replica_groups=mesh['pts'=8,'top'=4] {'pts'}, dimensions={2}, use_global_device_ids=true | all-gather | bytes 700416 | tf_op jit(solution)/shard_map/all_gather | solution.py:197
  518.9 18.7 %scatter_fusion.1 = f32[152,2,128]{0,1,2:T(2,128)S(1)} fusion(f32[152,2,128]{0,1,2:T(2,128)S(1)} %broadcast_in_dim.89, s32[512]{0:T(512)S(1)} %bitcast.192, f32[512,152,2]{1,2,0:T(2,128)S(1)} %copy.90), kind=kCustom, calls=%fused_computation.12 | custom fusion | flops 155648 | bytes 1869824 | tf_op jit(solution)/shard_map/scatter-add | solution.py:203
  537.8 16.8 %all_gather.15 = f32[152,8,128]{2,0,1:T(8,128)S(1)} all-gather(f32[152,2,128]{2,0,1:T(8,128)S(1)} %copy.91), channel_id=1, replica_groups=mesh['pts'=8,'top'=4] {'top'}, dimensions={1}, use_global_device_ids=true | all-gather | bytes 778240 | tf_op jit(solution)/shard_map/all_gather | solution.py:205
  554.6 5.8 convolution_bitcast_fusion
  560.4 9.0 %copy.110 = f32[152,8,128,8]{0,1,3,2:T(8,128)} copy(f32[152,8,128,8]{2,0,3,1:T(8,128)} %convolution_bitcast_fusion) | data formatting | bytes 9961472 | tf_op jit(solution)/shard_map/reshape | solution.py:207
  569.4 13.1 %gather_fusion.4 = f32[1024,152,8]{1,2,0:T(8,128)} fusion(f32[152,8,1024]{0,1,2:T(8,128)} %bitcast.171, s32[1024]{0:T(1024)S(1)} %get-tuple-element.143), kind=kCustom, calls=%fused_computation.4 | custom fusion | bytes 9965568 | tf_op jit(solution)/shard_map/gather | solution.py:208
  582.5 10.9 %fusion.7 = f32[1024,1,8]{2,1,0:T(1,128)S(1)} fusion(f32[1024,152,1]{1,2,0:T(1,128)S(1)} %copy-done.6, f32[1024,152,8]{1,2,0:T(8,128)} %gather_fusion.4), kind=kOutput, calls=%fused_computation.25 | convolution fusion | flops 14942208 | bytes 5636096 | tf_op jit(solution)/shard_map/sc,cks->ks/dot_general | solution.py:209
  593.4 5.5 gather_fusion.5
  599.4 9.9 %all_to_all.33 = f32[32,1,512]{2,1,0:T(1,128)S(1)} all-to-all(f32[32,1,512]{2,1,0:T(1,128)S(1)} %reshape.1666), channel_id=1, replica_groups=mesh['pts'=8,'top'=4] {'pts','top'}, dimensions={0} | all-to-all | bytes 131072 | tf_op jit(solution)/shard_map/all_to_all | solution.py:212
  (177 shorter events, 68.0 us)
Async XLA Ops:
  6.5 133.7 %copy-start = (f32[152,152]{1,0:T(8,128)S(1)}, f32[152,152]{1,0:T(8,128)}, u32[]{:S(2)}) copy-start(f32[152,152]{1,0:T(8,128)} %param.20) | copy-start | bytes 277252
  6.5 44.0 %copy-start.23 = (s32[2]{0:T(128)S(1)}, s32[2]{0:T(128)}, u32[]{:S(2)}) copy-start(s32[2]{0:T(128)} %constant.414) | copy-start | bytes 28
  6.5 44.1 %copy-start.22 = (s32[2]{0:T(128)S(1)}, s32[2]{0:T(128)}, u32[]{:S(2)}) copy-start(s32[2]{0:T(128)} %constant.411) | copy-start | bytes 28
  6.5 69.9 %copy-start.16 = (s32[316]{0:T(512)S(1)}, s32[316]{0:T(512)}, u32[]{:S(2)}) copy-start(s32[316]{0:T(512)} %constant.427) | copy-start | bytes 3796
  6.5 69.9 %copy-start.17 = (s32[316]{0:T(512)S(1)}, s32[316]{0:T(512)}, u32[]{:S(2)}) copy-start(s32[316]{0:T(512)} %constant.425) | copy-start | bytes 3796
  6.6 69.9 %copy-start.18 = (s32[316]{0:T(512)S(1)}, s32[316]{0:T(512)}, u32[]{:S(2)}) copy-start(s32[316]{0:T(512)} %constant.423) | copy-start | bytes 3796
  6.6 44.0 %copy-start.14 = (s32[1024]{0:T(1024)S(1)}, s32[1024]{0:T(1024)}, u32[]{:S(2)}) copy-start(s32[1024]{0:T(1024)} %param.18) | copy-start | bytes 12292
  6.6 56.5 %copy-start.15 = (s32[1024]{0:T(1024)S(1)}, s32[1024]{0:T(1024)}, u32[]{:S(2)}) copy-start(s32[1024]{0:T(1024)} %param.19) | copy-start | bytes 12292
  6.6 69.8 %copy-start.12 = (f32[8,1024]{1,0:T(8,128)S(1)}, f32[8,1024]{1,0:T(8,128)}, u32[]{:S(2)}) copy-start(f32[8,1024]{1,0:T(8,128)} %param.17) | copy-start | bytes 98308
  6.6 69.8 %copy-start.13 = (f32[3,1024]{1,0:T(4,128)S(1)}, f32[3,1024]{1,0:T(4,128)}, u32[]{:S(2)}) copy-start(f32[3,1024]{1,0:T(4,128)} %param.16) | copy-start | bytes 36868
  55.8 30.3 %all-to-all-start = ((s32[1,32,64]{2,0,1:T(1,128)}), s32[1,32,64]{2,0,1:T(1,128)S(1)}, u32[]{:S(2)}, u32[]{:S(2)}) async-start(s32[1,32,64]{2,0,1:T(1,128)} %all_to_all.22), calls=%async_computation | async-start | bytes 32768 | tf_op jit(solution)/shard_map/all_to_all | solution.py:169
  82.1 24.8 %copy-start.19 = (f32[152]{0:T(256)S(1)}, f32[152]{0:T(256)}, u32[]{:S(2)}) copy-start(f32[152]{0:T(256)} %constant.421) | copy-start | bytes 1828
  82.1 24.8 %copy-start.20 = (f32[152]{0:T(256)S(1)}, f32[152]{0:T(256)}, u32[]{:S(2)}) copy-start(f32[152]{0:T(256)} %constant.420) | copy-start | bytes 1828
  82.1 24.7 %copy-start.21 = (f32[152]{0:T(256)S(1)}, f32[152]{0:T(256)}, u32[]{:S(2)}) copy-start(f32[152]{0:T(256)} %constant.419) | copy-start | bytes 1828
  86.1 11.7 %all-to-all-start.1 = ((f32[32,1,704]{2,1,0:T(1,128)}), f32[32,1,704]{2,1,0:T(1,128)S(1)}, u32[]{:S(2)}, u32[]{:S(2)}) async-start(f32[32,1,704]{2,1,0:T(1,128)} %reshape.1664), calls=%async_computation.1 | async-start | bytes 196608 | tf_op jit(solution)/shard_map/all_to_all | solution.py:168
  89.8 197.7 %reduce-scatter.2.cloned.1.call-start = ((), (), s32[]{:S(2)}) async-start(), calls=%async_computation.4 | async-start | bytes 778240 | tf_op jit(solution)/shard_map/reduce_scatter | solution.py:180
  157.7 4.6 copy-start.7
  157.7 7.3 %copy-start.8 = (f32[184832]{0:T(1024)S(1)}, f32[184832]{0:T(1024)}, u32[]{:S(2)}) copy-start(f32[184832]{0:T(1024)} %param.25) | copy-start | bytes 2217988
  242.1 43.6 %copy-start.9 = (f32[1024,152,1]{0,1,2:T(8,128)S(1)}, f32[1024,152,1]{0,1,2:T(8,128)}, u32[]{:S(2)}) copy-start(f32[1024,152,1]{0,1,2:T(8,128)} %get-tuple-element.150) | copy-start | bytes 1867780
  301.2 75.1 %copy-start.10 = (f32[152,152]{1,0:T(8,128)S(1)}, f32[152,152]{1,0:T(8,128)}, u32[]{:S(2)}) copy-start(f32[152,152]{1,0:T(8,128)} %param.24) | copy-start | bytes 277252
  372.0 3.2 copy-start.5
  372.0 4.4 copy-start.4
  372.1 5.6 copy-start.2
  450.6 42.7 %copy-start.3 = (f32[8,152,152,1]{2,1,0,3:T(8,128)S(1)}, f32[8,152,152,1]{2,1,0,3:T(8,128)}, u32[]{:S(2)}) copy-start(f32[8,152,152,1]{2,1,0,3:T(8,128)} %reshape.1610) | copy-start | bytes 2217988
  494.6 12.4 %copy-start.11 = (f32[152,152]{1,0:T(8,128)S(1)}, f32[152,152]{1,0:T(8,128)}, u32[]{:S(2)}) copy-start(f32[152,152]{1,0:T(8,128)} %param.23) | copy-start | bytes 277252
  569.4 13.1 %copy-start.6 = (f32[1024,152,1]{1,2,0:T(1,128)S(1)}, f32[1024,152,1]{1,2,0:T(1,128)}, u32[]{:S(2)}) copy-start(f32[1024,152,1]{1,2,0:T(1,128)} %copy.104) | copy-start | bytes 1867780
  569.4 44.8 %copy-start.1 = (f32[152,152]{1,0:T(8,128)S(1)}, f32[152,152]{1,0:T(8,128)}, u32[]{:S(2)}) copy-start(f32[152,152]{1,0:T(8,128)} %param.20) | copy-start | bytes 277252
Sparse Core Ops, SparseCore 0:
  162.4 19.0 reduce-scatter.1
where the time goes:
time: 632 us; the launch traced here: 621 us
  local copies, waits for them, and re-layouts  322 us (51%)
  other arithmetic  140 us (22%)
  blocking collectives  64.6 us (10%)
  matrix products  58.9 us (9%)
  between operations  17.8 us (3%)
  starting transfers between devices  11.1 us (2%)
  waiting for transfers between devices  6.6 us (1%)
    gather x2, local copies, waits for them, and re-layouts, one_block(): gathered = level4_low[:, :, sources]  114 us
    reshape x2, local copies, waits for them, and re-layouts, per_device(): m2l_ops = m2l_ops.reshape(coef_len, -1, coef_len)  106 us
    scatter-add x1, other arithmetic, per_device(): level4 = jnp.zeros((coef_len, dens_dev, BOXES4), jnp.float32).at[:, :, id...  70.8 us
    scatter-add x1, other arithmetic, per_device(): locals4 = jnp.zeros((coef_len, dens_dev, box_cap), jnp.float32).at[:, :,...  18.7 us
    dot_general x1, matrix products, leaf_window(): jnp.einsum('ef,bokf->boke', uc2e, checks, precision=lax.Precision.HIGHEST)  17.5 us
    all_gather x1, blocking collectives, per_device(): full_locals = lax.all_gather(locals4, 'top', axis=1, tiled=True)  16.8 us
    sub x1, other arithmetic, per_device(): jnp.arange(points_dev, dtype=jnp.int32) - first_pos[sorted_dest]  15.7 us
    scatter-add x1, other arithmetic, leaf_window(): jax.ops.segment_sum(contrib, leaf_local, num_segments=8 * box_cap, indice...  13.9 us
  transfers between devices with their start and end apart: 3, of which 1 were waited for; matrix products, arithmetic and copies ran while one was open for 21% of the time, Pallas kernels for 0%

commit v1 on v0

v1 whole, which is shorter than its diff:
```python
import functools
import math

import jax
import jax.numpy as jnp
import numpy as np
from jax import lax
from jax.experimental import pallas as pl
from jax.experimental.pallas import tpu as pltpu
from jax.sharding import PartitionSpec as P

LEVEL = 3
EDGE = 6
DENS = 8
SIDE = 2**LEVEL
BOXES4 = SIDE**3
PLANE = SIDE * SIDE
LANE = 128
REACH = 3
SHIFTS = list(range(-REACH, REACH + 1))
OUTER = [s for s in SHIFTS if abs(s) >= 2]
INNER = [s for s in SHIFTS if abs(s) < 2]
bf16 = jnp.bfloat16
f32 = jnp.float32
NN = (((1,), (0,)), ((), ()))
NT = (((1,), (1,)), ((), ()))


def up(value, multiple):
    return -(-value // multiple) * multiple


def surface_table():
    grid_vals = np.linspace(-1.0, 1.0, EDGE)
    points_list = []
    for a in range(EDGE):
        for b in range(EDGE):
            for c in range(EDGE):
                if min(a, b, c) == 0 or max(a, b, c) == EDGE - 1:
                    points_list.append([grid_vals[a], grid_vals[b], grid_vals[c]])
    return np.array(points_list, dtype=np.float32).T


COEF = surface_table().shape[1]
OFFSETS = (2 * REACH + 1) ** 3 - 27
CPAD = up(COEF, 32)


def blocks():
    out, position = [], 0
    for dx in SHIFTS:
        for dy in SHIFTS:
            count = sum(max(abs(dx), abs(dy), abs(dz)) >= 2 for dz in SHIFTS)
            out.append((dx, dy, position, count))
            position += count
    return out


def dot(a, b, dims=NN):
    return lax.dot_general(a, b, dims, preferred_element_type=f32)


def split(value):
    high = value.astype(bf16)
    return high, (value - high.astype(f32)).astype(bf16)


def dot3(a, b, dims=NN):
    return dot(a[0], b[0], dims) + dot(a[1], b[0], dims) + dot(a[0], b[1], dims)


def call(kernel, out_shape, mib, flops, bytes_accessed=1 << 20, **kw):
    return pl.pallas_call(
        kernel,
        out_shape=out_shape,
        compiler_params=pltpu.CompilerParams(vmem_limit_bytes=mib << 20),
        cost_estimate=pl.CostEstimate(
            flops=flops, bytes_accessed=bytes_accessed, transcendentals=0
        ),
        **kw,
    )


VMEM = pl.BlockSpec(memory_space=pltpu.VMEM)
SMEM = pl.BlockSpec(memory_space=pltpu.SMEM)
ANY = pl.BlockSpec(memory_space=pl.ANY)


HG = 4 * OFFSETS * COEF // LANE
KT = up(up(OFFSETS * COEF, LANE) // LANE, 8)
WFULL = up(7 * COEF, LANE)
WIN = up(4 * COEF, LANE)
NG = COEF // 8
STEPS = -(-NG // 4)
ROWS = 16 * STEPS
CHUNK = up(HG + 15, 16)
TAIL = 32
STRIDE = 17


def relayout_kernel(nrows, half_ref, f_hbm, tail_hbm, oa, ob, oc, inb, fbuf, tbuf, tb16, sem):
    step = pl.program_id(0)
    half = half_ref[0]
    end16 = nrows // 16 * 16

    def start_row(st, g):
        return jnp.minimum(4 * st + g, NG - 1) * (2 * HG) + half * HG

    def start(st, slot):
        for g in range(4):
            row = pl.multiple_of(start_row(st, g) // 16 * 16, 16)
            pltpu.make_async_copy(
                f_hbm.at[pl.ds(row, CHUNK - TAIL)],
                inb.at[slot, g, pl.ds(0, CHUNK - TAIL)],
                sem.at[slot, g, 0],
            ).start()
            last = row + CHUNK > end16

            @pl.when(jnp.logical_not(last))
            def _():
                pltpu.make_async_copy(
                    f_hbm.at[pl.ds(pl.multiple_of(row + CHUNK - TAIL, 16), TAIL)],
                    inb.at[slot, g, pl.ds(CHUNK - TAIL, TAIL)],
                    sem.at[slot, g, 1],
                ).start()

            @pl.when(last)
            def _():
                pltpu.make_async_copy(
                    tail_hbm, inb.at[slot, g, pl.ds(CHUNK - TAIL, TAIL)], sem.at[slot, g, 1]
                ).start()

    def wait(slot):
        for g in range(4):
            pltpu.make_async_copy(
                f_hbm.at[pl.ds(0, CHUNK - TAIL)],
                inb.at[slot, g, pl.ds(0, CHUNK - TAIL)],
                sem.at[slot, g, 0],
            ).wait()
            pltpu.make_async_copy(
                tail_hbm, inb.at[slot, g, pl.ds(CHUNK - TAIL, TAIL)], sem.at[slot, g, 1]
            ).wait()

    slot = lax.rem(step, 2)

    @pl.when(step == 0)
    def _():
        fbuf[...] = jnp.zeros_like(fbuf)
        start(0, 0)

    @pl.when(step + 1 < STEPS)
    def _():
        start(step + 1, 1 - slot)

    wait(slot)
    lane = lax.broadcasted_iota(jnp.int32, (8, LANE), 1)
    for g in range(4):
        fbuf[g, 0:CHUNK] = inb[slot, g].astype(f32)
    for g in range(4):
        row = start_row(step, g)
        off = row - row // 16 * 16
        for e in range(4):
            first = OFFSETS * COEF * e
            phase = first % LANE

            @pl.loop(0, KT // 8, unroll=KT // 8)
            def _(n):
                base = off + first // LANE + 8 * n
                value = fbuf[g, pl.ds(base, 8), :]
                if phase:
                    after = fbuf[g, pl.ds(base + 1, 8), :]
                    value = pltpu.roll(jnp.where(lane >= phase, value, after), LANE - phase, 1)
                tbuf[pl.ds(8 * n * STRIDE + 4 * g + e, 8, stride=STRIDE), :] = value

    @pl.loop(0, KT, unroll=8)
    def _(k):
        tb16[k] = tbuf[pl.ds(k * STRIDE, 16), :].astype(bf16)

    for dx, dy, d0, count in blocks():
        tile0, phase = divmod(d0 * COEF, LANE)
        if dy in OUTER:
            ref = oa.at[dx + REACH, OUTER.index(dy)]
        elif dx in OUTER:
            ref = ob.at[OUTER.index(dx), INNER.index(dy)]
        else:
            ref = oc.at[INNER.index(dx), INNER.index(dy)]
        for t in range(up(count * COEF, LANE) // LANE):
            value = tb16[tile0 + t]
            if phase:
                after = tb16[min(tile0 + t + 1, KT - 1)]
                value = jnp.concatenate([value[:, phase:], after[:, :phase]], axis=1)
            ref[:, t * LANE : (t + 1) * LANE] = value


def relayout(flat, half):
    nrows = flat.shape[0] // LANE
    rows = flat.reshape(nrows, LANE)
    tail = rows[nrows // 16 * 16 :]
    tail = jnp.pad(tail, ((0, TAIL - tail.shape[0]), (0, 0)))
    shapes = ((7, 4, ROWS, WFULL), (4, 3, ROWS, WFULL), (3, 3, ROWS, WIN))
    return call(
        functools.partial(relayout_kernel, nrows),
        tuple(jax.ShapeDtypeStruct(s, bf16) for s in shapes),
        58,
        1 << 20,
        16 << 20,
        grid_spec=pltpu.PrefetchScalarGridSpec(
            num_scalar_prefetch=1,
            grid=(STEPS,),
            in_specs=[ANY, ANY],
            out_specs=tuple(
                pl.BlockSpec((s[0], s[1], 16, s[3]), lambda i, h: (0, 0, i, 0)) for s in shapes
            ),
            scratch_shapes=[
                pltpu.VMEM((2, 4, CHUNK, LANE), bf16),
                pltpu.VMEM((4, CHUNK + 16, LANE), f32),
                pltpu.VMEM((KT * STRIDE, LANE), f32),
                pltpu.VMEM((KT, 16, LANE), bf16),
                pltpu.SemaphoreType.DMA((2, 4, 2)),
            ],
        ),
    )(half, rows, tail)


def route_kernel(own, cap, n_top, pos, dens, slot, out):
    points = pos.shape[1]
    owners = out.shape[0]
    slots = slot[...]
    owner = slots // own
    inside = slots - owner * own
    hit = owner == lax.broadcasted_iota(jnp.int32, (owners, points), 0)
    hit = jnp.where(hit, 1.0, 0.0)
    hit16 = hit.astype(bf16)
    row = lax.broadcasted_iota(jnp.int32, (LANE, LANE), 0)
    col = lax.broadcasted_iota(jnp.int32, (LANE, LANE), 1)
    before = jnp.where(row < col, 1.0, 0.0).astype(bf16)
    every = jnp.ones((LANE, LANE), bf16)
    total = jnp.zeros((owners, LANE), f32)
    ranks = []
    for t in range(points // LANE):
        part = hit16[:, t * LANE : (t + 1) * LANE]
        ranks.append(total + dot(part, before))
        total = total + dot(part, every)
    rank = jnp.sum(hit * jnp.concatenate(ranks, axis=1), axis=0, keepdims=True)
    entry = owner * cap + rank.astype(jnp.int32)
    inside_hi = inside // 64
    value = jnp.concatenate([pos[...], dens[...]], axis=0)
    width = value.shape[0]
    high, low = split(value)
    ones = jnp.ones((1, points), f32)
    high = jnp.concatenate(
        [high.astype(f32), inside_hi.astype(f32), (inside - 64 * inside_hi).astype(f32), ones]
        + [jnp.zeros((16 - width - 3, points), f32)],
        axis=0,
    )
    low = jnp.concatenate([low.astype(f32), jnp.zeros((16 - width, points), f32)], axis=0)
    payload = jnp.concatenate([high, low], axis=0).astype(bf16)
    block = max(cap, LANE)
    for o in range(owners * cap // block):
        there = entry == o * block + lax.broadcasted_iota(jnp.int32, (block, points), 0)
        there = jnp.where(there, 1.0, 0.0).astype(bf16)
        got = dot(payload, there, NT)
        value = got[0:width] + got[16 : 16 + width]
        where = got[width : width + 1] * 64.0 + got[width + 1 : width + 2]
        valid = got[width + 2 : width + 3]
        per = DENS // n_top
        for q in range(n_top):
            rows = [value[0:3], where, valid, value[3 + per * q : 3 + per * (q + 1)]]
            rows.append(jnp.zeros((8 - 5 - per, block), f32))
            packed = jnp.concatenate([r for r in rows if r.shape[0]], axis=0)
            for i in range(block // cap):
                out[o * (block // cap) + i, q] = packed[:, i * cap : (i + 1) * cap]


def octant_product(pos, octant, surf, oper_hi, oper_lo):
    squared = None
    for d in range(3):
        spacing = surf[d] - pos[d : d + 1]
        squared = spacing * spacing if squared is None else squared + spacing * spacing
    value = lax.rsqrt(squared)
    value = jnp.concatenate([value, jnp.zeros((CPAD - COEF, value.shape[1]), f32)], axis=0)
    high, low = split(value)
    low = low.astype(f32)
    high = high.astype(f32)
    his = [jnp.where(octant == o, high, 0.0).astype(bf16) for o in range(8)]
    los = [jnp.where(octant == o, low, 0.0).astype(bf16) for o in range(8)]
    return dot3(
        (oper_hi, oper_lo), (jnp.concatenate(his, axis=0), jnp.concatenate(los, axis=0))
    )


def look_up(index, table):
    rows = table.shape[1]
    width = index.shape[1]
    at_row = index // LANE
    at_lane = index - at_row * LANE
    there = at_row == lax.broadcasted_iota(jnp.int32, (rows, width), 0)
    got = dot(table, jnp.where(there, 1.0, 0.0).astype(bf16))
    mine = at_lane == lax.broadcasted_iota(jnp.int32, (LANE, width), 0)
    first = jnp.sum(jnp.where(mine, got[0:LANE], 0.0), axis=0, keepdims=True)
    second = jnp.sum(jnp.where(mine, got[LANE : 2 * LANE], 0.0), axis=0, keepdims=True)
    return first, second


PB = 256


def upward_kernel(own, box_cap, flip_ref, got, table, surf, w_hi, w_lo, out, buf):
    sources, _, cap = got.shape
    wide = up(cap, LANE)
    flip = flip_ref[0]
    buf[...] = jnp.zeros_like(buf)

    def place(s, offset):
        value = got[s]
        count = jnp.sum(value[4:5]).astype(jnp.int32)
        value = jnp.concatenate([value, jnp.zeros((8, wide + LANE - cap), f32)], axis=1)
        tile = offset // LANE
        value = pltpu.roll(value, offset - tile * LANE, 1)
        place_at = pl.ds(pl.multiple_of(tile * LANE, LANE), wide + LANE)
        buf[:, place_at] = buf[:, place_at] + value
        return offset + count

    lax.fori_loop(0, sources, place, jnp.int32(0), unroll=4)
    out_rows = out.shape[1]

    def block(j, total):
        value = buf[:, pl.ds(pl.multiple_of(j * PB, PB), PB)]
        index = value[3:4].astype(jnp.int32) ^ flip
        box, octant = look_up(index, table[...])
        field = split(octant_product(value[0:3], octant, surf, w_hi[...], w_lo[...]))
        rows = []
        at = lax.broadcasted_iota(jnp.int32, (box_cap, PB), 0).astype(f32)
        for k in range(out_rows // box_cap):
            rows.append(jnp.where(box == at, value[5 + k : 6 + k], 0.0))
        return total + dot3(field, split(jnp.concatenate(rows, axis=0)), NT)

    total = lax.fori_loop(0, own // PB, block, jnp.zeros((COEF, out_rows), f32))
    out[...] = total.astype(bf16)


def morton_place(box):
    place = jnp.zeros_like(box)
    for b in range(LEVEL):
        digit = box >> (3 * b)
        place = place + ((((digit >> 2) & 1) << (2 * LEVEL + b)))
        place = place + ((((digit >> 1) & 1) << (LEVEL + b)) + ((digit & 1) << b))
    return place


def target_kernel(flip_ref, pos, slot, table, surf, w_hi, w_lo, field, place):
    flip = flip_ref[0]
    count = pos.shape[1]

    @pl.loop(0, count // PB)
    def _(j):
        at = pl.ds(pl.multiple_of(j * PB, PB), PB)
        index = slot[:, at].astype(jnp.int32) ^ flip
        high, low = look_up(index, table[...])
        leaf = (high * 64.0 + low).astype(jnp.int32)
        octant = leaf & 7
        field[:, at] = octant_product(
            pos[:, at], octant, surf, w_hi[...], w_lo[...]
        )
        place[:, at] = morton_place(leaf >> 3)


def translate_kernel(slabs, x0_ref, ids, part, oa, ob, oc, out, xs, xin, acc, ma, mb, mc, sem):
    copies = []
    for i, (src, dst) in enumerate(((oa, ma), (ob, mb), (oc, mc))):
        for j in range(src.shape[0]):
            copies.append(pltpu.make_async_copy(src.at[j], dst.at[j], sem.at[i, j]))
            copies[-1].start()
    x0 = x0_ref[0]
    dens = part.shape[0]
    place = morton_place(ids[...])
    place = (((place >> 6) - x0 + REACH) & 7) * 64 + (place & 63)
    place = jnp.where((ids[...] >= 0) & (ids[...] < BOXES4), place, -1)
    at = lax.broadcasted_iota(jnp.int32, (BOXES4, ids.shape[1]), 0)
    there = jnp.where(at == place, 1.0, 0.0).astype(bf16)
    columns = dens * PLANE
    for k in range(dens):
        low = dot(there, part[k], NT)
        low = low.astype(bf16).astype(f32)
        for s in range(7 + slabs - 1):
            slab = low[s * PLANE : (s + 1) * PLANE].reshape(SIDE, SIDE, COEF)
            shifted = {}
            for dz in SHIFTS:
                if dz == 0:
                    moved = slab
                else:
                    cut = dz % SIDE
                    moved = jnp.concatenate([slab[:, cut:], slab[:, :cut]], axis=1)
                shifted[dz] = moved.reshape(PLANE, COEF)
            rows = pl.ds(s * columns + k * PLANE, PLANE)
            pad = [jnp.zeros((PLANE, WFULL - 7 * COEF), f32)]
            xs[rows, :] = jnp.concatenate([shifted[z] for z in SHIFTS] + pad, axis=1).astype(bf16)
            pad = [jnp.zeros((PLANE, WIN - 4 * COEF), f32)]
            xin[rows, :] = jnp.concatenate([shifted[z] for z in OUTER] + pad, axis=1).astype(bf16)
    for c in copies:
        c.wait()
    n_out = len(OUTER) * ROWS
    n_in = len(INNER) * ROWS
    for i, dx in enumerate(SHIFTS):
        rows = pl.ds(i * columns, slabs * columns)
        source = xs[rows, :]
        outer = dot(ma[i].reshape(n_out, WFULL), source, NT)
        if dx in OUTER:
            inner = dot(mb[OUTER.index(dx)].reshape(n_in, WFULL), source, NT)
        else:
            inner = dot(mc[INNER.index(dx)].reshape(n_in, WIN), xin[rows, :], NT)
        if i == 0:
            acc[0:n_out] = outer
            acc[n_out : n_out + n_in] = inner
        else:
            acc[0:n_out] += outer
            acc[n_out : n_out + n_in] += inner
    lane = lax.broadcasted_iota(jnp.int32, (ROWS, LANE), 1)
    for t in range(slabs * columns // LANE):
        total = jnp.zeros((ROWS, LANE), f32)
        for i, dy in enumerate(OUTER + INNER):
            value = acc[i * ROWS : (i + 1) * ROWS, t * LANE : (t + 1) * LANE]
            by = SIDE * (dy % SIDE)
            if by:
                near = pltpu.roll(value, LANE - by, 1)
                far = pltpu.roll(value, PLANE - by, 1)
                value = jnp.where((lane & (PLANE - 1)) < PLANE - by, near, far)
            total = total + value
        out[:, t * LANE : (t + 1) * LANE] = total.astype(out.dtype)


def coarse_kernel(ids, part, m2m_hi, m2m_lo, lat_hi, lat_lo, l2l_hi, l2l_lo, out):
    dens = part.shape[0]
    box = ids[...]
    place = ((box & 7) << 6) + (box & 56) + (box >> 6)
    place = jnp.where((box >= 0) & (box < BOXES4), place, -1)
    at = lax.broadcasted_iota(jnp.int32, (BOXES4, ids.shape[1]), 0)
    there = jnp.where(at == place, 1.0, 0.0).astype(bf16)
    level = [dot(there, part[k], NT) for k in range(dens)]

    def oper(hi, lo, o):
        return hi[o], lo[o]

    for _ in range(LEVEL):
        count = level[0].shape[0] // 8
        total = None
        for o in range(8):
            rows = jnp.concatenate([v[o * count : (o + 1) * count] for v in level], axis=0)
            term = dot3(split(rows), oper(m2m_hi, m2m_lo, o), NT)
            total = term if total is None else total + term
        level = [total[k * count : (k + 1) * count] for k in range(dens)]
    rows = jnp.concatenate(level, axis=0)
    rows = dot3(split(rows), (lat_hi[...], lat_lo[...]), NT)
    level = [rows[k : k + 1] for k in range(dens)]
    for _ in range(LEVEL):
        count = level[0].shape[0]
        rows = split(jnp.concatenate(level, axis=0))
        children = [dot3(rows, oper(l2l_hi, l2l_lo, o), NT) for o in range(8)]
        level = [
            jnp.concatenate([c[k * count : (k + 1) * count] for c in children], axis=0)
            for k in range(dens)
        ]
    at = lax.broadcasted_iota(jnp.int32, (BOXES4, BOXES4), 1)
    row = lax.broadcasted_iota(jnp.int32, (BOXES4, BOXES4), 0)
    number = ((row & 7) << 6) + (row & 56) + (row >> 6)
    move = jnp.where(at == morton_place(number), 1.0, 0.0).astype(bf16)
    for k in range(dens):
        high, low = split(level[k])
        turned = (((0,), (0,)), ((), ()))
        out[k] = dot(high, move, turned) + dot(low, move, turned)


def evaluate_kernel(slabs, me_ref, *refs):
    n = SIDE // slabs
    checks = refs[: 2 * n]
    d_hi, d_lo, lattice, field, place, out, stack = refs[2 * n :]
    core = me_ref[0]
    group = me_ref[1]
    dens = lattice.shape[0]
    lane = lax.broadcasted_iota(jnp.int32, (COEF, LANE), 1)
    mine = jnp.concatenate([d_hi[core], d_lo[core]], axis=0)
    other = jnp.concatenate([d_hi[1 - core], d_lo[1 - core]], axis=0)
    for m in range(n):
        value = dot(mine, checks[2 * m][...]) + dot(other, checks[2 * m + 1][...])
        value = value[0:COEF] + value[COEF : 2 * COEF]
        if slabs == 2:
            a, b = value[:, 0:LANE], value[:, LANE : 2 * LANE]
            half = LANE // 2
            pieces = [
                jnp.where(lane < half, a, pltpu.roll(b, half, 1)),
                jnp.where(lane < half, pltpu.roll(a, half, 1), b),
            ]
        else:
            pieces = [value[:, k * PLANE : (k + 1) * PLANE] for k in range(dens)]
        width = slabs * PLANE
        for k in range(dens):
            at = m ^ group
            if width % LANE == 0:
                base = lattice[k, :, pl.ds(pl.multiple_of(at * width, width), width)]
            else:
                pair = lattice[k, :, pl.ds(pl.multiple_of(at // 2 * LANE, LANE), LANE)]
                base = jnp.where(at % 2 == 0, pair[:, :width], pair[:, width:])
            high, low = split(pieces[k] + base)
            rows = pl.ds(k * CPAD, COEF)
            stack[rows, m * width : (m + 1) * width] = high.astype(f32)
            rows = pl.ds((dens + k) * CPAD, COEF)
            stack[rows, m * width : (m + 1) * width] = low.astype(f32)
    local = stack[...].astype(bf16)

    @pl.loop(0, place.shape[1] // PB)
    def _(j):
        at = pl.ds(pl.multiple_of(j * PB, PB), PB)
        want = place[:, at] ^ (group * (slabs * PLANE))
        there = want == lax.broadcasted_iota(jnp.int32, (BOXES4, PB), 0)
        got = dot(local, jnp.where(there, 1.0, 0.0).astype(bf16))
        mine = field[:, at]
        rows = []
        for k in range(dens):
            value = got[k * CPAD : k * CPAD + COEF]
            value = value + got[(dens + k) * CPAD : (dens + k) * CPAD + COEF]
            rows.append(jnp.sum(value * mine, axis=0, keepdims=True))
        out[:, at] = jnp.concatenate(rows, axis=0)


def shifts_of(axis, value, distances):
    size = lax.axis_size(axis)
    return [
        value if m == 0 else lax.ppermute(value, axis, [(i, i ^ m) for i in range(size)])
        for m in distances
    ]


def split_oper(value):
    high = lax.reduce_precision(value, 8, 7)
    return high.astype(bf16), (value - high).astype(bf16)


def per_device(
    local_pos, densities, morton_slot, slot_leaf, uc2e, m2m, m2l_ops, dc2e, lattice, l2l
):
    n_pts = lax.axis_size("pts")
    n_top = lax.axis_size("top")
    me = lax.axis_index("pts")
    top = lax.axis_index("top")
    points = local_pos.shape[1]
    own = points * n_top
    cap = 2 * points // n_pts
    box_cap = 2 * BOXES4 // n_pts
    dens = DENS // n_top
    slabs = max(1, 2 * SIDE // n_pts)
    coef = uc2e.shape[0]
    scalar = lambda *v: jnp.stack([jnp.asarray(x, jnp.int32) for x in v])

    slot_row = morton_slot.reshape(1, points)
    outgoing = call(
        functools.partial(route_kernel, own, cap, n_top),
        jax.ShapeDtypeStruct((n_pts, n_top, 8, cap), f32),
        32,
        1 << 27,
        in_specs=[VMEM] * 3,
        out_specs=VMEM,
    )(local_pos, densities, slot_row)
    outgoing = outgoing.reshape(n_pts * n_top, 8, cap)
    incoming = lax.all_to_all(outgoing, ("pts", "top"), split_axis=0, concat_axis=0, tiled=True)

    shared = jnp.concatenate(
        [
            local_pos,
            morton_slot.astype(f32).reshape(1, points),
            slot_leaf.astype(f32).reshape(1, points),
        ],
        axis=0,
    )
    shared = shifts_of("top", shared, range(n_top))
    leaves = jnp.stack([s[4] for s in shared])
    row_pos = jnp.concatenate([s[0:3] for s in shared], axis=1)
    row_slot = jnp.concatenate([s[3:4] for s in shared], axis=1)
    all_leaves = jnp.stack(shifts_of("pts", leaves, range(n_pts)))
    firsts = (jnp.min(all_leaves, axis=(1, 2)).astype(jnp.int32)) // 8
    box_ids = (firsts[:, None] + jnp.arange(box_cap, dtype=jnp.int32)[None, :]).reshape(1, -1)

    oa, ob, oc = relayout(m2l_ops, scalar(me & 1))
    m2m = m2m.reshape(8, coef, coef)
    l2l = l2l.reshape(8, coef, coef)
    scale = 1.0 / (4.0 * math.pi)
    high = lax.Precision.HIGHEST
    w_up = jnp.einsum("ocf,fe->coe", m2m, uc2e * scale, precision=high)
    pad = ((0, 0), (0, 0), (0, CPAD - coef))
    w_up = split_oper(jnp.pad(w_up, pad).reshape(coef, 8 * CPAD))
    w_down = jnp.transpose(l2l * scale, (2, 0, 1))
    w_down = split_oper(jnp.pad(w_down, pad).reshape(coef, 8 * CPAD))
    surf = jnp.asarray(np.repeat((np.float32(1.25) * surface_table())[:, :, None], PB, axis=2))

    table = leaves.reshape(own // LANE, LANE).T.astype(jnp.int32)
    table = jnp.concatenate([table // 8 - firsts[0], table % 8], axis=0).astype(bf16)
    partial = call(
        functools.partial(upward_kernel, own, box_cap),
        jax.ShapeDtypeStruct((coef, dens * box_cap), bf16),
        32,
        8 << 30,
        in_specs=[SMEM] + [VMEM] * 5,
        out_specs=VMEM,
        scratch_shapes=[pltpu.VMEM((8, up(own + up(cap, LANE) + LANE, PB)), f32)],
    )(scalar(top * points), incoming, table, surf, *w_up)
    parts = shifts_of("pts", partial, range(n_pts))
    part = jnp.stack(
        [
            jnp.concatenate([v[:, k * box_cap : (k + 1) * box_cap] for v in parts], axis=1)
            for k in range(dens)
        ]
    )

    table = all_leaves.reshape(-1, LANE).T.astype(jnp.int32)
    table = jnp.concatenate([table // 64, table % 64], axis=0).astype(bf16)
    field, place = call(
        target_kernel,
        (
            jax.ShapeDtypeStruct((coef, own), f32),
            jax.ShapeDtypeStruct((1, own), jnp.int32),
        ),
        32,
        6 << 30,
        in_specs=[SMEM] + [VMEM] * 6,
        out_specs=(VMEM, VMEM),
    )(scalar(me * own + top * points), row_pos, row_slot, table, surf, *w_down)

    columns = dens * PLANE
    x0 = (me // 2 * 2) * SIDE // n_pts
    checks = call(
        functools.partial(translate_kernel, slabs),
        jax.ShapeDtypeStruct((ROWS, slabs * columns), bf16),
        56,
        8 << 30,
        in_specs=[SMEM, VMEM, VMEM, ANY, ANY, ANY],
        out_specs=VMEM,
        scratch_shapes=[
            pltpu.VMEM(((7 + slabs - 1) * columns, WFULL), bf16),
            pltpu.VMEM(((7 + slabs - 1) * columns, WIN), bf16),
            pltpu.VMEM((7 * ROWS, slabs * columns), f32),
            pltpu.VMEM(oa.shape, bf16),
            pltpu.VMEM(ob.shape, bf16),
            pltpu.VMEM(oc.shape, bf16),
            pltpu.SemaphoreType.DMA((3, 7)),
        ],
    )(scalar(x0), box_ids, part, oa, ob, oc)
    step = n_pts // SIDE * slabs
    distances = [step * m + c for m in range(SIDE // slabs) for c in range(2)]
    gathered = shifts_of("pts", checks, distances)

    lattice4 = call(
        coarse_kernel,
        jax.ShapeDtypeStruct((dens, coef, BOXES4), f32),
        32,
        4 << 30,
        in_specs=[VMEM] * 8,
        out_specs=VMEM,
    )(box_ids, part, *split_oper(m2m), *split_oper(lattice), *split_oper(l2l))

    halves = dc2e.reshape(coef, NG, 2, 4).transpose(2, 0, 1, 3).reshape(2, coef, 4 * NG)
    halves = split_oper(jnp.pad(halves, ((0, 0), (0, 0), (0, ROWS - 4 * NG))))
    reply = call(
        functools.partial(evaluate_kernel, slabs),
        jax.ShapeDtypeStruct((dens, own), f32),
        32,
        4 << 30,
        in_specs=[SMEM] + [VMEM] * (len(gathered) + 5),
        out_specs=VMEM,
        scratch_shapes=[pltpu.VMEM((2 * dens * CPAD, BOXES4), f32)],
    )(scalar(me & 1, me // step), *gathered, *halves, lattice4, field, place)
    reply = reply.reshape(dens, n_top, points)
    answers = []
    for m in range(n_top):
        value = reply[:, m]
        if m:
            value = lax.ppermute(value, "top", [(i, i ^ m) for i in range(n_top)])
        answers.append(value)
    answers = jnp.stack(answers)
    order = jnp.arange(n_top, dtype=jnp.int32) ^ top
    picked = sum(
        jnp.where(order[:, None, None, None] == m, answers[m][None], 0.0) for m in range(n_top)
    )
    return picked.reshape(DENS, points)


def solution(mesh):
    split_all = P(None, ("pts", "top"))
    placed = (split_all, split_all, P(("pts", "top")), P(("pts", "top"))) + (P(),) * 6
    return jax.shard_map(
        per_device, mesh=mesh, in_specs=placed, out_specs=split_all, check_vma=False
    )
```

time: 632 us -> 173 us (0.27); the launches traced: 621 us -> 171 us
  local copies, waits for them, and re-layouts: 322 us -> 36.6 us
  other arithmetic: 140 us -> 18.1 us
  Pallas kernels: 0 us -> 71 us
  blocking collectives: 64.6 us -> 0 us
  matrix products: 58.9 us -> 1.14 us
  starting transfers between devices: 11.1 us -> 35.6 us
  between operations: 17.8 us -> 0.61 us
    gather x21 -> x0, local copies, waits for them, and re-layouts: 150 us -> none  [the longest x2 114 us: one_block(): gathered = level4_low[:, :, sources]]
    reshape x9 -> x7, local copies, waits for them, and re-layouts: 136 us -> 7.71 us  [the longest x1 2.7 us: per_device(): l2l = l2l.reshape(8, coef, coef)]
    scatter-add x3 -> x0, other arithmetic: 103 us -> none  [the longest x1 70.8 us: per_device(): level4 = jnp.zeros((coef_len, dens_dev, BOXES4), jnp.float32).at[:, :, id...]
    pallas_call x0 -> x7, Pallas kernels: none -> 71 us  [the longest x1 19 us: per_device(): call(functools.partial(upward_kernel, own, box_cap), jax.ShapeDtypeStruct...]
    dot_general x13 -> x1, matrix products: 58.9 us -> 1.14 us  [per_device(): w_up = jnp.einsum('ocf,fe->coe', m2m, uc2e * scale, precision=high)]
    all_gather x4 -> x0, blocking collectives: 45.5 us -> none  [the longest x1 16.8 us: per_device(): full_locals = lax.all_gather(locals4, 'top', axis=1, tiled=True)]
    ppermute x0 -> x27, starting transfers between devices: none -> 29.5 us  [the longest x24 25.1 us: shifts_of(): lax.ppermute(value, axis, [(i, i ^ m) for i in range(size)])]
    sub x1 -> x0, other arithmetic: 15.7 us -> none  [per_device(): jnp.arange(points_dev, dtype=jnp.int32) - first_pos[sorted_dest]]
  transfers between devices with their start and end apart: 3 -> 28, of which waited for: 1 -> 6; matrix products, arithmetic and copies ran while one was open for 21% -> 26% of each run, Pallas kernels for 0% -> 21%
where the time goes in v1:
time: 173 us; the launch traced here: 171 us
  Pallas kernels  71 us (41%)
  local copies, waits for them, and re-layouts  36.6 us (21%)
  starting transfers between devices  35.6 us (21%)
  other arithmetic  18.1 us (10%)
  waiting for transfers between devices  8.18 us (5%)
    ppermute x24, starting transfers between devices, shifts_of(): lax.ppermute(value, axis, [(i, i ^ m) for i in range(size)])  25.1 us
    pallas_call x1, Pallas kernels, per_device(): call(functools.partial(upward_kernel, own, box_cap), jax.ShapeDtypeStruct...  19 us
    pallas_call x1, Pallas kernels, relayout(): call(functools.partial(relayout_kernel, nrows), tuple((jax.ShapeDtypeStru...  14 us
    unnamed x75, local copies, waits for them, and re-layouts  13.9 us
    pallas_call x1, Pallas kernels, per_device(): call(target_kernel, (jax.ShapeDtypeStruct((coef, own), f32), jax.ShapeDty...  12.4 us
    pallas_call x1, Pallas kernels, per_device(): call(functools.partial(translate_kernel, slabs), jax.ShapeDtypeStruct((RO...  9.5 us
    pallas_call x1, Pallas kernels, per_device(): call(coarse_kernel, jax.ShapeDtypeStruct((dens, coef, BOXES4), f32), 32,...  7.09 us
    pallas_call x1, Pallas kernels, per_device(): call(functools.partial(evaluate_kernel, slabs), jax.ShapeDtypeStruct((den...  6.65 us
  transfers between devices with their start and end apart: 28, of which 6 were waited for; matrix products, arithmetic and copies ran while one was open for 26% of the time, Pallas kernels for 21%

profile of v1, /device:TPU:0, one launch (start us, length us, event | category | flops | bytes accessed | tf_op | source)
XLA Modules:
  0.0 171.2 jit_solution(9533127060106849982)
XLA Ops:
  1.4 1.3 pad_maximum_fusion.3
  2.7 5.0 %collective-permute-start.2 = (f32[5,1024]{1,0:T(8,128)}, f32[5,1024]{1,0:T(8,128)}, u32[]{:S(2)}, u32[]{:S(2)}) collective-permute-start(f32[5,1024]{1,0:T(8,128)} %pad_maximum_fusion.3), channel_id=1, source_target_pairs={{0,3},{1,2},{2,1},{3,0},{4,7},{5,6},{6,5},{7,4},{8,11},{9,10},{10,... | collective-permute-start | bytes 61448 | tf_op jit(solution)/shard_map/ppermute | solution.py:528
  10.5 2.4 %shard_map.109 = f32[8,4,8,256]{3,2,1,0:T(8,128)} custom-call(f32[3,1024]{1,0:T(4,128)S(1)} %copy-done.10, f32[8,1024]{1,0:T(8,128)S(1)} %copy-done.15, s32[1,1024]{1,0:T(1,128)S(1)} %bitcast.128), custom_call_target="tpu_custom_call" | custom-call | flops 134217728 | bytes 1048576 | tf_op jit(solution)/shard_map/pallas_call | solution.py:555
  12.9 6.1 %all-to-all-start = ((f32[32,8,256]{2,1,0:T(8,128)}), f32[32,8,256]{2,1,0:T(8,128)S(1)}, u32[]{:S(2)}, u32[]{:S(2)}) async-start(f32[32,8,256]{2,1,0:T(8,128)} %bitcast.16), calls=%async_computation | async-start | bytes 524288 | tf_op jit(solution)/shard_map/all_to_all | solution.py:564
  19.0 1.6 reshape.138
  25.6 2.7 %reshape.143 = f32[8,152,152]{2,1,0:T(8,128)} reshape(f32[184832]{0:T(1024)S(1)} %copy-done.20) | data formatting | bytes 1478656 | tf_op jit(solution)/shard_map/reshape | solution.py:584
  28.3 2.1 %fusion = (bf16[8,152,152]{2,1,0:T(8,128)(2,1)S(1)}, bf16[8,152,152]{2,1,0:T(8,128)(2,1)S(1)}, bf16[8,152,152]{2,1,0:T(8,128)(2,1)S(1)}, bf16[8,152,152]{2,1,0:T(8,128)(2,1)S(1)}, f32[152,8,152]{0,2,1:T(8,128)S(1)}) fusion(f32[8,152,152]{2,1,0:T(8,128)} %copy-done.18, f32[8,152,152]{2,1,0:T(8,128)} %reshape.143), kind=kLoop, calls=%fused_computation.5 | loop fusion | flops 1663488 | bytes 3696640 | tf_op jit(solution)/shard_map/convert_element_type | solution.py:535
  32.4 2.6 %copy.30 = f32[152,1280]{1,0:T(8,128)} copy(f32[152,1280]{0,1:T(8,128)} %bitcast.130) | data formatting | bytes 1556480 | tf_op jit(solution)/shard_map/reshape | solution.py:591
  37.5 14.0 %shard_map.111 = (bf16[7,4,80,1152]{3,2,1,0:T(8,128)(2,1)}, bf16[4,3,80,1152]{3,2,1,0:T(8,128)(2,1)}, bf16[3,3,80,640]{3,2,1,0:T(8,128)(2,1)}) custom-call(s32[1]{0:T(128)} %bitcast.half_ref, bf16[57038,128]{1,0:T(8,128)(2,1)} %bitcast.129, bf16[32,128]{1,0:T(8,128)(2,1)} %pad.16.tail_hbm), custom_call_target="tpu_custom_call" | custom-call | flops 1048576 | bytes 16777216 | tf_op jit(solution)/shard_map/pallas_call | solution.py:201
  54.9 1.7 collective-permute-start.4
  60.2 1.7 collective-permute-start.6
  62.0 1.3 convert_element_type.80
  63.3 2.6 %collective-permute-start.8 = (f32[4,1024]{1,0:T(4,128)}, f32[4,1024]{1,0:T(4,128)S(1)}, u32[]{:S(2)}, u32[]{:S(2)}) collective-permute-start(f32[4,1024]{1,0:T(4,128)} %get-tuple-element.61), channel_id=1, source_target_pairs={{0,24},{4,28},{8,16},{12,20},{16,8},{20,12},{24,0},{28,4},{1,25},{... | collective-permute-start | bytes 49160 | tf_op jit(solution)/shard_map/ppermute | solution.py:528
  68.5 1.3 constant_dynamic-update-slice_fusion.4
  69.9 1.3 constant_dynamic-update-slice_fusion.3
  71.2 1.3 constant_dynamic-update-slice_fusion.2
  73.7 1.7 fusion.26
  76.8 1.4 copy.24.table
  78.2 1.6 convert_element_type.93
  79.9 1.7 copy.28
  87.7 19.0 %shard_map.110 = bf16[152,256]{1,0:T(8,128)(2,1)S(1)} custom-call(s32[1]{0:T(128)} %bitcast.14.flip_ref, f32[32,8,256]{2,1,0:T(8,128)S(1)} %all-to-all-done.got, bf16[256,32]{1,0:T(8,128)(2,1)S(1)} %copy-done.8, f32[3,152,256]{2,1,0:T(8,128)S(1)} %copy-done.16, bf16[152,1280]{1,0:T(8,128)(2,1)S(1)} %copy-done.2, bf16[152,1280]{1,0:T(8,128)(2,1)S(1)} %copy-done.1), custom_call_target="tpu_custom_call" | custom-call | flops 8589934592 | bytes 1048576 | tf_op jit(solution)/shard_map/pallas_call | solution.py:596
  107.3 1.7 %collective-permute-start.11 = (bf16[152,256]{1,0:T(8,128)(2,1)S(1)}, bf16[152,256]{1,0:T(8,128)(2,1)S(1)}, u32[]{:S(2)}, u32[]{:S(2)}) collective-permute-start(bf16[152,256]{1,0:T(8,128)(2,1)S(1)} %shard_map.110), channel_id=1, source_target_pairs={{0,8},{4,12},{8,0},{12,4},{16,24},{20,28},{24,16},{28,20},{1,9},{5... | collective-permute-start | bytes 233480 | tf_op jit(solution)/shard_map/ppermute | solution.py:528
  109.1 1.5 collective-permute-start.13
  110.9 2.6 %collective-permute-start.15 = (bf16[152,256]{1,0:T(8,128)(2,1)S(1)}, bf16[152,256]{1,0:T(8,128)(2,1)S(1)}, u32[]{:S(2)}, u32[]{:S(2)}) collective-permute-start(bf16[152,256]{1,0:T(8,128)(2,1)S(1)} %shard_map.110), channel_id=1, source_target_pairs={{0,24},{4,28},{8,16},{12,20},{16,8},{20,12},{24,0},{28,4},{1,25},{... | collective-permute-start | bytes 233480 | tf_op jit(solution)/shard_map/ppermute | solution.py:528
  114.1 3.9 %collective-permute-done.14 = bf16[152,256]{1,0:T(8,128)(2,1)S(1)} collective-permute-done((bf16[152,256]{1,0:T(8,128)(2,1)S(1)}, bf16[152,256]{1,0:T(8,128)(2,1)S(1)}, u32[]{:S(2)}, u32[]{:S(2)}) %collective-permute-start.14) | collective-permute-done | bytes 77856 | tf_op jit(solution)/shard_map/ppermute | solution.py:528
  120.0 9.5 %shard_map.112.refs_0_ = bf16[80,256]{1,0:T(8,128)(2,1)} custom-call(s32[1]{0:T(128)} %bitcast.2.x0_ref, s32[1,1024]{1,0:T(1,128)} %bitcast.126, bf16[2,152,1024]{2,1,0:T(8,128)(2,1)} %pad_maximum_fusion.part, bf16[7,4,80,1152]{3,2,1,0:T(8,128)(2,1)} %get-tuple-element.10.oa, bf16[4,3,80,1152]{3,2,1,0:T(8,128)(2,1)} %get-tuple-element.11.ob, ...), custom_call_target="tpu_custom_call" | custom-call | flops 8589934592 | bytes 1048576 | tf_op jit(solution)/shard_map/pallas_call | solution.py:629
  131.0 12.4 %shard_map.114 = (f32[152,4096]{1,0:T(8,128)S(1)}, s32[1,4096]{1,0:T(1,128)S(1)}) custom-call(s32[1]{0:T(128)} %bitcast.27.flip_ref, f32[3,4096]{1,0:T(4,128)S(1)} %copy-done.9, f32[1,4096]{1,0:T(1,128)S(1)} %pad_maximum_fusion.6.slot, bf16[256,256]{1,0:T(8,128)(2,1)S(1)} %copy-done.3, f32[3,152,256]{2,1,0:T(8,128)S(1)} %copy-done.17, ...), custom_call_target="tpu_custom_call" | custom-call | flops 6442450944 | bytes 1048576 | tf_op jit(solution)/shard_map/pallas_call | solution.py:615
  145.7 2.2 %collective-permute-start.22 = (bf16[80,256]{1,0:T(8,128)(2,1)S(1)}, bf16[80,256]{1,0:T(8,128)(2,1)S(1)}, u32[]{:S(2)}, u32[]{:S(2)}) collective-permute-start(bf16[80,256]{1,0:T(8,128)(2,1)S(1)} %copy-done.14), channel_id=1, source_target_pairs={{0,24},{4,28},{8,16},{12,20},{16,8},{20,12},{24,0},{28,4},{1,25},{... | collective-permute-start | bytes 122888 | tf_op jit(solution)/shard_map/ppermute | solution.py:528
  148.5 7.1 %shard_map.113.refs_10_ = f32[2,152,512]{2,1,0:T(8,128)S(1)} custom-call(s32[1,1024]{1,0:T(1,128)S(1)} %bitcast.127, bf16[2,152,1024]{2,1,0:T(8,128)(2,1)S(1)} %copy-done, bf16[8,152,152]{2,1,0:T(8,128)(2,1)S(1)} %get-tuple-element.19.m2m_hi, bf16[8,152,152]{2,1,0:T(8,128)(2,1)S(1)} %get-tuple-element.18.m2m_lo, bf16[152,152]{1,0:T(8,128)(2,1)S(1)} %copy-done.7, ...), custom_call_target="tpu_custom_call" | custom-call | flops 4294967296 | bytes 1048576 | tf_op jit(solution)/shard_map/pallas_call | solution.py:650
  155.7 6.7 %shard_map.115 = f32[2,4096]{1,0:T(2,128)S(1)} custom-call(s32[2]{0:T(128)S(1)} %pad_add_fusion.me_ref, bf16[80,256]{1,0:T(8,128)(2,1)S(1)} %copy-done.14, bf16[80,256]{1,0:T(8,128)(2,1)S(1)} %collective-permute-done.17.refs_1_, bf16[80,256]{1,0:T(8,128)(2,1)S(1)} %collective-permute-done.18.refs_2_, bf16[80,256]{1,0:T(8,128)(2,1)S(1)} %collective-permute-done.19.refs_3_, ...), custom_call_target="tpu_custom_call" | custom-call | flops 4294967296 | bytes 1048576 | tf_op jit(solution)/shard_map/pallas_call | solution.py:661
  162.4 3.4 %collective-permute-start.26 = (f32[2,1024]{1,0:T(2,128)S(1)}, f32[2,1024]{1,0:T(2,128)S(1)}, u32[]{:S(2)}, u32[]{:S(2)}) collective-permute-start(f32[2,1024]{1,0:T(2,128)S(1)} %bitcast.143), channel_id=1, source_target_pairs={{0,3},{1,2},{2,1},{3,0},{4,7},{5,6},{6,5},{7,4},{8,11},{9,10},{10,... | collective-permute-start | bytes 24584 | tf_op jit(solution)/shard_map/ppermute | solution.py:675
  168.0 2.4 %collective-permute-done.25 = f32[2,1024]{1,0:T(2,128)S(1)} collective-permute-done((f32[2,1024]{1,0:T(2,128)S(1)}, f32[2,1024]{1,0:T(2,128)S(1)}, u32[]{:S(2)}, u32[]{:S(2)}) %collective-permute-start.25) | collective-permute-done | bytes 8224 | tf_op jit(solution)/shard_map/ppermute | solution.py:675
  (172 shorter events, 42.7 us)
Async XLA Ops:
  2.7 48.7 %collective-permute-start.2 = (f32[5,1024]{1,0:T(8,128)}, f32[5,1024]{1,0:T(8,128)}, u32[]{:S(2)}, u32[]{:S(2)}) collective-permute-start(f32[5,1024]{1,0:T(8,128)} %pad_maximum_fusion.3), channel_id=1, source_target_pairs={{0,3},{1,2},{2,1},{3,0},{4,7},{5,6},{6,5},{7,4},{8,11},{9,10},{10,... | collective-permute-start | bytes 61448 | tf_op jit(solution)/shard_map/ppermute | solution.py:528
  7.8 44.5 %collective-permute-start.1 = (f32[5,1024]{1,0:T(8,128)}, f32[5,1024]{1,0:T(8,128)}, u32[]{:S(2)}, u32[]{:S(2)}) collective-permute-start(f32[5,1024]{1,0:T(8,128)} %pad_maximum_fusion.3), channel_id=1, source_target_pairs={{0,2},{1,3},{2,0},{3,1},{4,6},{5,7},{6,4},{7,5},{8,10},{9,11},{10,... | collective-permute-start | bytes 61448 | tf_op jit(solution)/shard_map/ppermute | solution.py:528
  7.8 45.4 %collective-permute-start = (f32[5,1024]{1,0:T(8,128)}, f32[5,1024]{1,0:T(8,128)}, u32[]{:S(2)}, u32[]{:S(2)}) collective-permute-start(f32[5,1024]{1,0:T(8,128)} %pad_maximum_fusion.3), channel_id=1, source_target_pairs={{0,1},{1,0},{2,3},{3,2},{4,5},{5,4},{6,7},{7,6},{8,9},{9,8},{10,11... | collective-permute-start | bytes 61448 | tf_op jit(solution)/shard_map/ppermute | solution.py:528
  12.9 71.0 %all-to-all-start = ((f32[32,8,256]{2,1,0:T(8,128)}), f32[32,8,256]{2,1,0:T(8,128)S(1)}, u32[]{:S(2)}, u32[]{:S(2)}) async-start(f32[32,8,256]{2,1,0:T(8,128)} %bitcast.16), calls=%async_computation | async-start | bytes 524288 | tf_op jit(solution)/shard_map/all_to_all | solution.py:564
  37.5 21.4 %copy-start.11 = (f32[3,1024]{1,0:T(4,128)S(1)}, f32[3,1024]{1,0:T(4,128)}, u32[]{:S(2)}) copy-start(f32[3,1024]{1,0:T(4,128)} %pos.1) | copy-start | bytes 36868
  37.5 22.0 %copy-start.25 = (f32[1024]{0:T(1024)S(1)}, f32[1024]{0:T(1024)}, u32[]{:S(2)}) copy-start(f32[1024]{0:T(1024)} %copy-done.24) | copy-start | bytes 12292
  54.7 8.6 %collective-permute-start.3 = (f32[4,1024]{1,0:T(4,128)}, f32[4,1024]{1,0:T(4,128)}, u32[]{:S(2)}, u32[]{:S(2)}) collective-permute-start(f32[4,1024]{1,0:T(4,128)} %get-tuple-element.61), channel_id=1, source_target_pairs={{0,4},{4,0},{8,12},{12,8},{16,20},{20,16},{24,28},{28,24},{1,5},{5... | collective-permute-start | bytes 49160 | tf_op jit(solution)/shard_map/ppermute | solution.py:528
  54.9 12.3 %collective-permute-start.4 = (f32[4,1024]{1,0:T(4,128)}, f32[4,1024]{1,0:T(4,128)}, u32[]{:S(2)}, u32[]{:S(2)}) collective-permute-start(f32[4,1024]{1,0:T(4,128)} %get-tuple-element.61), channel_id=1, source_target_pairs={{0,8},{4,12},{8,0},{12,4},{16,24},{20,28},{24,16},{28,20},{1,9},{5... | collective-permute-start | bytes 49160 | tf_op jit(solution)/shard_map/ppermute | solution.py:528
  60.2 8.4 %collective-permute-start.5 = (f32[4,1024]{1,0:T(4,128)}, f32[4,1024]{1,0:T(4,128)}, u32[]{:S(2)}, u32[]{:S(2)}) collective-permute-start(f32[4,1024]{1,0:T(4,128)} %get-tuple-element.61), channel_id=1, source_target_pairs={{0,12},{4,8},{8,4},{12,0},{16,28},{20,24},{24,20},{28,16},{1,13},{... | collective-permute-start | bytes 49160 | tf_op jit(solution)/shard_map/ppermute | solution.py:528
  60.2 9.7 %collective-permute-start.6 = (f32[4,1024]{1,0:T(4,128)}, f32[4,1024]{1,0:T(4,128)}, u32[]{:S(2)}, u32[]{:S(2)}) collective-permute-start(f32[4,1024]{1,0:T(4,128)} %get-tuple-element.61), channel_id=1, source_target_pairs={{0,16},{4,20},{8,24},{12,28},{16,0},{20,4},{24,8},{28,12},{1,17},{... | collective-permute-start | bytes 49160 | tf_op jit(solution)/shard_map/ppermute | solution.py:528
  61.9 9.3 %collective-permute-start.7 = (f32[4,1024]{1,0:T(4,128)}, f32[4,1024]{1,0:T(4,128)}, u32[]{:S(2)}, u32[]{:S(2)}) collective-permute-start(f32[4,1024]{1,0:T(4,128)} %get-tuple-element.61), channel_id=1, source_target_pairs={{0,20},{4,16},{8,28},{12,24},{16,4},{20,0},{24,12},{28,8},{1,21},{... | collective-permute-start | bytes 49160 | tf_op jit(solution)/shard_map/ppermute | solution.py:528
  63.3 9.2 %collective-permute-start.8 = (f32[4,1024]{1,0:T(4,128)}, f32[4,1024]{1,0:T(4,128)S(1)}, u32[]{:S(2)}, u32[]{:S(2)}) collective-permute-start(f32[4,1024]{1,0:T(4,128)} %get-tuple-element.61), channel_id=1, source_target_pairs={{0,24},{4,28},{8,16},{12,20},{16,8},{20,12},{24,0},{28,4},{1,25},{... | collective-permute-start | bytes 49160 | tf_op jit(solution)/shard_map/ppermute | solution.py:528
  67.2 5.9 %collective-permute-start.9 = (f32[4,1024]{1,0:T(4,128)}, f32[4,1024]{1,0:T(4,128)S(1)}, u32[]{:S(2)}, u32[]{:S(2)}) collective-permute-start(f32[4,1024]{1,0:T(4,128)} %get-tuple-element.61), channel_id=1, source_target_pairs={{0,28},{4,24},{8,20},{12,16},{16,12},{20,8},{24,4},{28,0},{1,29},{... | collective-permute-start | bytes 49160 | tf_op jit(solution)/shard_map/ppermute | solution.py:528
  106.8 4.1 %collective-permute-start.10 = (bf16[152,256]{1,0:T(8,128)(2,1)S(1)}, bf16[152,256]{1,0:T(8,128)(2,1)S(1)}, u32[]{:S(2)}, u32[]{:S(2)}) collective-permute-start(bf16[152,256]{1,0:T(8,128)(2,1)S(1)} %shard_map.110), channel_id=1, source_target_pairs={{0,4},{4,0},{8,12},{12,8},{16,20},{20,16},{24,28},{28,24},{1,5},{5... | collective-permute-start | bytes 233480 | tf_op jit(solution)/shard_map/ppermute | solution.py:528
  107.3 6.2 %collective-permute-start.11 = (bf16[152,256]{1,0:T(8,128)(2,1)S(1)}, bf16[152,256]{1,0:T(8,128)(2,1)S(1)}, u32[]{:S(2)}, u32[]{:S(2)}) collective-permute-start(bf16[152,256]{1,0:T(8,128)(2,1)S(1)} %shard_map.110), channel_id=1, source_target_pairs={{0,8},{4,12},{8,0},{12,4},{16,24},{20,28},{24,16},{28,20},{1,9},{5... | collective-permute-start | bytes 233480 | tf_op jit(solution)/shard_map/ppermute | solution.py:528
  109.1 4.6 %collective-permute-start.12 = (bf16[152,256]{1,0:T(8,128)(2,1)S(1)}, bf16[152,256]{1,0:T(8,128)(2,1)S(1)}, u32[]{:S(2)}, u32[]{:S(2)}) collective-permute-start(bf16[152,256]{1,0:T(8,128)(2,1)S(1)} %shard_map.110), channel_id=1, source_target_pairs={{0,12},{4,8},{8,4},{12,0},{16,28},{20,24},{24,20},{28,16},{1,13},{... | collective-permute-start | bytes 233480 | tf_op jit(solution)/shard_map/ppermute | solution.py:528
  109.1 5.0 %collective-permute-start.13 = (bf16[152,256]{1,0:T(8,128)(2,1)S(1)}, bf16[152,256]{1,0:T(8,128)(2,1)S(1)}, u32[]{:S(2)}, u32[]{:S(2)}) collective-permute-start(bf16[152,256]{1,0:T(8,128)(2,1)S(1)} %shard_map.110), channel_id=1, source_target_pairs={{0,16},{4,20},{8,24},{12,28},{16,0},{20,4},{24,8},{28,12},{1,17},{... | collective-permute-start | bytes 233480 | tf_op jit(solution)/shard_map/ppermute | solution.py:528
  110.6 7.4 %collective-permute-start.14 = (bf16[152,256]{1,0:T(8,128)(2,1)S(1)}, bf16[152,256]{1,0:T(8,128)(2,1)S(1)}, u32[]{:S(2)}, u32[]{:S(2)}) collective-permute-start(bf16[152,256]{1,0:T(8,128)(2,1)S(1)} %shard_map.110), channel_id=1, source_target_pairs={{0,20},{4,16},{8,28},{12,24},{16,4},{20,0},{24,12},{28,8},{1,21},{... | collective-permute-start | bytes 233480 | tf_op jit(solution)/shard_map/ppermute | solution.py:528
  110.9 7.1 %collective-permute-start.15 = (bf16[152,256]{1,0:T(8,128)(2,1)S(1)}, bf16[152,256]{1,0:T(8,128)(2,1)S(1)}, u32[]{:S(2)}, u32[]{:S(2)}) collective-permute-start(bf16[152,256]{1,0:T(8,128)(2,1)S(1)} %shard_map.110), channel_id=1, source_target_pairs={{0,24},{4,28},{8,16},{12,20},{16,8},{20,12},{24,0},{28,4},{1,25},{... | collective-permute-start | bytes 233480 | tf_op jit(solution)/shard_map/ppermute | solution.py:528
  113.5 5.6 %collective-permute-start.16 = (bf16[152,256]{1,0:T(8,128)(2,1)S(1)}, bf16[152,256]{1,0:T(8,128)(2,1)S(1)}, u32[]{:S(2)}, u32[]{:S(2)}) collective-permute-start(bf16[152,256]{1,0:T(8,128)(2,1)S(1)} %shard_map.110), channel_id=1, source_target_pairs={{0,28},{4,24},{8,20},{12,16},{16,12},{20,8},{24,4},{28,0},{1,29},{... | collective-permute-start | bytes 233480 | tf_op jit(solution)/shard_map/ppermute | solution.py:528
  129.5 16.2 %collective-permute-start.17 = (bf16[80,256]{1,0:T(8,128)(2,1)}, bf16[80,256]{1,0:T(8,128)(2,1)S(1)}, u32[]{:S(2)}, u32[]{:S(2)}) collective-permute-start(bf16[80,256]{1,0:T(8,128)(2,1)} %shard_map.112.refs_0_), channel_id=1, source_target_pairs={{0,4},{4,0},{8,12},{12,8},{16,20},{20,16},{24,28},{28,24},{1,5},{5... | collective-permute-start | bytes 122888 | tf_op jit(solution)/shard_map/ppermute | solution.py:528
  129.7 18.3 %collective-permute-start.18 = (bf16[80,256]{1,0:T(8,128)(2,1)}, bf16[80,256]{1,0:T(8,128)(2,1)S(1)}, u32[]{:S(2)}, u32[]{:S(2)}) collective-permute-start(bf16[80,256]{1,0:T(8,128)(2,1)} %shard_map.112.refs_0_), channel_id=1, source_target_pairs={{0,8},{4,12},{8,0},{12,4},{16,24},{20,28},{24,16},{28,20},{1,9},{5... | collective-permute-start | bytes 122888 | tf_op jit(solution)/shard_map/ppermute | solution.py:528
  130.9 17.5 %copy-start = (bf16[2,152,1024]{2,1,0:T(8,128)(2,1)S(1)}, bf16[2,152,1024]{2,1,0:T(8,128)(2,1)}, u32[]{:S(2)}) copy-start(bf16[2,152,1024]{2,1,0:T(8,128)(2,1)} %pad_maximum_fusion.part) | copy-start | bytes 1867780
  131.0 17.5 %copy-start.6 = (bf16[152,152]{1,0:T(8,128)(2,1)S(1)}, bf16[152,152]{1,0:T(8,128)(2,1)}, u32[]{:S(2)}) copy-start(bf16[152,152]{1,0:T(8,128)(2,1)} %get-tuple-element.24.lat_lo) | copy-start | bytes 138628
  143.4 12.2 %collective-permute-start.19 = (bf16[80,256]{1,0:T(8,128)(2,1)S(1)}, bf16[80,256]{1,0:T(8,128)(2,1)S(1)}, u32[]{:S(2)}, u32[]{:S(2)}) collective-permute-start(bf16[80,256]{1,0:T(8,128)(2,1)S(1)} %copy-done.14), channel_id=1, source_target_pairs={{0,12},{4,8},{8,4},{12,0},{16,28},{20,24},{24,20},{28,16},{1,13},{... | collective-permute-start | bytes 122888 | tf_op jit(solution)/shard_map/ppermute | solution.py:528
  144.0 11.5 %collective-permute-start.20 = (bf16[80,256]{1,0:T(8,128)(2,1)S(1)}, bf16[80,256]{1,0:T(8,128)(2,1)S(1)}, u32[]{:S(2)}, u32[]{:S(2)}) collective-permute-start(bf16[80,256]{1,0:T(8,128)(2,1)S(1)} %copy-done.14), channel_id=1, source_target_pairs={{0,16},{4,20},{8,24},{12,28},{16,0},{20,4},{24,8},{28,12},{1,17},{... | collective-permute-start | bytes 122888 | tf_op jit(solution)/shard_map/ppermute | solution.py:528
  145.2 10.4 %collective-permute-start.21 = (bf16[80,256]{1,0:T(8,128)(2,1)S(1)}, bf16[80,256]{1,0:T(8,128)(2,1)S(1)}, u32[]{:S(2)}, u32[]{:S(2)}) collective-permute-start(bf16[80,256]{1,0:T(8,128)(2,1)S(1)} %copy-done.14), channel_id=1, source_target_pairs={{0,20},{4,16},{8,28},{12,24},{16,4},{20,0},{24,12},{28,8},{1,21},{... | collective-permute-start | bytes 122888 | tf_op jit(solution)/shard_map/ppermute | solution.py:528
  145.7 9.9 %collective-permute-start.22 = (bf16[80,256]{1,0:T(8,128)(2,1)S(1)}, bf16[80,256]{1,0:T(8,128)(2,1)S(1)}, u32[]{:S(2)}, u32[]{:S(2)}) collective-permute-start(bf16[80,256]{1,0:T(8,128)(2,1)S(1)} %copy-done.14), channel_id=1, source_target_pairs={{0,24},{4,28},{8,16},{12,20},{16,8},{20,12},{24,0},{28,4},{1,25},{... | collective-permute-start | bytes 122888 | tf_op jit(solution)/shard_map/ppermute | solution.py:528
  148.0 7.7 %collective-permute-start.23 = (bf16[80,256]{1,0:T(8,128)(2,1)S(1)}, bf16[80,256]{1,0:T(8,128)(2,1)S(1)}, u32[]{:S(2)}, u32[]{:S(2)}) collective-permute-start(bf16[80,256]{1,0:T(8,128)(2,1)S(1)} %copy-done.14), channel_id=1, source_target_pairs={{0,28},{4,24},{8,20},{12,16},{16,12},{20,8},{24,4},{28,0},{1,29},{... | collective-permute-start | bytes 122888 | tf_op jit(solution)/shard_map/ppermute | solution.py:528
  162.4 5.5 %collective-permute-start.26 = (f32[2,1024]{1,0:T(2,128)S(1)}, f32[2,1024]{1,0:T(2,128)S(1)}, u32[]{:S(2)}, u32[]{:S(2)}) collective-permute-start(f32[2,1024]{1,0:T(2,128)S(1)} %bitcast.143), channel_id=1, source_target_pairs={{0,3},{1,2},{2,1},{3,0},{4,7},{5,6},{6,5},{7,4},{8,11},{9,10},{10,... | collective-permute-start | bytes 24584 | tf_op jit(solution)/shard_map/ppermute | solution.py:675
  165.9 4.5 %collective-permute-start.25 = (f32[2,1024]{1,0:T(2,128)S(1)}, f32[2,1024]{1,0:T(2,128)S(1)}, u32[]{:S(2)}, u32[]{:S(2)}) collective-permute-start(f32[2,1024]{1,0:T(2,128)S(1)} %bitcast.142), channel_id=1, source_target_pairs={{0,2},{1,3},{2,0},{3,1},{4,6},{5,7},{6,4},{7,5},{8,10},{9,11},{10,... | collective-permute-start | bytes 24584 | tf_op jit(solution)/shard_map/ppermute | solution.py:675
  165.9 4.6 %collective-permute-start.24 = (f32[2,1024]{1,0:T(2,128)S(1)}, f32[2,1024]{1,0:T(2,128)S(1)}, u32[]{:S(2)}, u32[]{:S(2)}) collective-permute-start(f32[2,1024]{1,0:T(2,128)S(1)} %bitcast.141), channel_id=1, source_target_pairs={{0,1},{1,0},{2,3},{3,2},{4,5},{5,4},{6,7},{7,6},{8,9},{9,8},{10,11... | collective-permute-start | bytes 24584 | tf_op jit(solution)/shard_map/ppermute | solution.py:675
  (24 other events, 154.1 us)

commit v2 on v1

--- a/solution.py
+++ b/solution.py
@@ -69,6 +69,13 @@
     return dot(a[0], b[0], dims) + dot(a[1], b[0], dims) + dot(a[0], b[1], dims)
 
 
+def dot3_rows(a, b, dims=NN):
+    rows = a[0].shape[0]
+    both = jnp.concatenate([x.astype(f32) for x in a], axis=0).astype(bf16)
+    both = dot(both, b[0], dims)
+    return both[0:rows] + both[rows : 2 * rows] + dot(a[0], b[1], dims)
+
+
 def call(kernel, out_shape, mib, flops, bytes_accessed=1 << 20, **kw):
     return pl.pallas_call(
         kernel,
@@ -98,9 +105,9 @@
 STRIDE = 17
 
 
-def relayout_kernel(nrows, half_ref, f_hbm, tail_hbm, oa, ob, oc, inb, fbuf, tbuf, tb16, sem):
+def relayout_kernel(nrows, me_ref, f_hbm, tail_ref, oa, ob, oc, inb, fbuf, tbuf, tb16, sem):
     step = pl.program_id(0)
-    half = half_ref[0]
+    half = me_ref[0] & 1
     end16 = nrows // 16 * 16
 
     def start_row(st, g):
@@ -124,22 +131,30 @@
                     sem.at[slot, g, 1],
                 ).start()
 
-            @pl.when(last)
-            def _():
-                pltpu.make_async_copy(
-                    tail_hbm, inb.at[slot, g, pl.ds(CHUNK - TAIL, TAIL)], sem.at[slot, g, 1]
-                ).start()
-
-    def wait(slot):
+
+    def wait(st, slot):
         for g in range(4):
+            row = pl.multiple_of(start_row(st, g) // 16 * 16, 16)
             pltpu.make_async_copy(
-                f_hbm.at[pl.ds(0, CHUNK - TAIL)],
+                f_hbm.at[pl.ds(row, CHUNK - TAIL)],
                 inb.at[slot, g, pl.ds(0, CHUNK - TAIL)],
                 sem.at[slot, g, 0],
             ).wait()
-            pltpu.make_async_copy(
-                tail_hbm, inb.at[slot, g, pl.ds(CHUNK - TAIL, TAIL)], sem.at[slot, g, 1]
-            ).wait()
+            last = row + CHUNK > end16
+
+            @pl.when(jnp.logical_not(last))
+            def _():
+                pltpu.make_async_copy(
+                    f_hbm.at[pl.ds(pl.multiple_of(row + CHUNK - TAIL, 16), TAIL)],
+                    inb.at[slot, g, pl.ds(CHUNK - TAIL, TAIL)],
+                    sem.at[slot, g, 1],
+                ).wait()
+
+            @pl.when(last)
+            def _():
+                row16 = lax.broadcasted_iota(jnp.int32, (16, LANE), 0)
+                tail = jnp.where(row16 < nrows - end16, tail_ref[...].astype(f32), 0.0)
+                inb[slot, g, CHUNK - TAIL : CHUNK - TAIL + 16] = tail.astype(bf16)
 
     slot = lax.rem(step, 2)
 
@@ -152,7 +167,7 @@
     def _():
         start(step + 1, 1 - slot)
 
-    wait(slot)
+    wait(step, slot)
     lane = lax.broadcasted_iota(jnp.int32, (8, LANE), 1)
     for g in range(4):
         fbuf[g, 0:CHUNK] = inb[slot, g].astype(f32)
@@ -192,11 +207,9 @@
             ref[:, t * LANE : (t + 1) * LANE] = value
 
 
-def relayout(flat, half):
+def relayout(flat, me):
     nrows = flat.shape[0] // LANE
     rows = flat.reshape(nrows, LANE)
-    tail = rows[nrows // 16 * 16 :]
-    tail = jnp.pad(tail, ((0, TAIL - tail.shape[0]), (0, 0)))
     shapes = ((7, 4, ROWS, WFULL), (4, 3, ROWS, WFULL), (3, 3, ROWS, WIN))
     return call(
         functools.partial(relayout_kernel, nrows),
@@ -207,7 +220,7 @@
         grid_spec=pltpu.PrefetchScalarGridSpec(
             num_scalar_prefetch=1,
             grid=(STEPS,),
-            in_specs=[ANY, ANY],
+            in_specs=[ANY, pl.BlockSpec((16, LANE), lambda i, h: (nrows // 16, 0))],
             out_specs=tuple(
                 pl.BlockSpec((s[0], s[1], 16, s[3]), lambda i, h: (0, 0, i, 0)) for s in shapes
             ),
@@ -219,13 +232,79 @@
                 pltpu.SemaphoreType.DMA((2, 4, 2)),
             ],
         ),
-    )(half, rows, tail)
-
-
-def route_kernel(own, cap, n_top, pos, dens, slot, out):
+    )(me, rows, rows)
+
+
+GROUP = 16
+
+
+def square(flat, out):
+    per = GROUP * COEF // LANE
+    groups = flat.shape[0] // per
+    lane = lax.broadcasted_iota(jnp.int32, (groups, LANE), 1)
+    for r in range(GROUP):
+        first, phase = divmod(r * COEF, LANE)
+        got = []
+        for t in range(3):
+            row = min(first + t, per - 1)
+            got.append(flat[pl.ds(row, groups, stride=per), :])
+        for t in range(2):
+            value = got[t]
+            if phase:
+                value = jnp.where(lane >= phase, got[t], got[t + 1])
+                value = pltpu.roll(value, LANE - phase, 1)
+            out[t, pl.ds(r, groups, stride=GROUP), :] = value
+
+
+def operators_kernel(
+    m2m, l2l, uc2e, dc2e, lattice, w_up, w_down, m2m_hi, m2m_lo, l2l_hi, l2l_lo, lat_hi, lat_lo,
+    d_hi, d_lo, rows
+):
+    scale = 1.0 / (4.0 * math.pi)
+    lat_hi[...], lat_lo[...] = split(lattice[...])
+    first = split(uc2e[...] * scale)
+
+    def stack(pieces, out):
+        blank = jnp.zeros((COEF, CPAD - COEF), f32)
+        wide = jnp.concatenate([x for p in pieces for x in (p, blank)], axis=1)
+        high, low = split(wide)
+        out[0:COEF] = high
+        out[COEF : 2 * COEF] = low
+
+    def matrix(o):
+        at = slice(o * COEF, (o + 1) * COEF)
+        return jnp.concatenate([rows[0, at], rows[1, at, 0 : COEF - LANE]], axis=1)
+
+    square(m2m, rows)
+    pieces = []
+    for o in range(8):
+        high, low = split(matrix(o))
+        m2m_hi[o], m2m_lo[o] = high, low
+        pieces.append(dot3((high, low), first))
+    stack(pieces, w_up)
+    square(l2l, rows)
+    pieces = []
+    for o in range(8):
+        value = matrix(o)
+        l2l_hi[o], l2l_lo[o] = split(value)
+        pieces.append(jnp.transpose(value) * scale)
+    stack(pieces, w_down)
+    high, low = split(dc2e[...])
+    i = lax.broadcasted_iota(jnp.int32, (COEF, ROWS), 0)
+    r = lax.broadcasted_iota(jnp.int32, (COEF, ROWS), 1)
+    for h in range(2):
+        here = (i == (r >> 2) * 8 + 4 * h + (r & 3)) & (r < 4 * NG)
+        here = jnp.where(here, 1.0, 0.0).astype(bf16)
+        d_hi[h] = dot(high, here).astype(bf16)
+        d_lo[h] = dot(low, here).astype(bf16)
+
+
+def route_kernel(own, cap, n_top, pos, dens, slot, leaf, out, shared):
     points = pos.shape[1]
     owners = out.shape[0]
     slots = slot[...]
+    shared[0:3] = pos[...]
+    shared[3:4] = slots.astype(f32)
     owner = slots // own
     inside = slots - owner * own
     hit = owner == lax.broadcasted_iota(jnp.int32, (owners, points), 0)
@@ -256,6 +335,12 @@
     low = jnp.concatenate([low.astype(f32), jnp.zeros((16 - width, points), f32)], axis=0)
     payload = jnp.concatenate([high, low], axis=0).astype(bf16)
     block = max(cap, LANE)
+    per = DENS // n_top
+    leaves = leaf[...].astype(f32)
+    if leaves.shape[1] < cap:
+        leaves = jnp.concatenate(
+            [leaves, jnp.zeros((leaves.shape[0], cap - leaves.shape[1]), f32)], axis=1
+        )
     for o in range(owners * cap // block):
         there = entry == o * block + lax.broadcasted_iota(jnp.int32, (block, points), 0)
         there = jnp.where(there, 1.0, 0.0).astype(bf16)
@@ -263,16 +348,17 @@
         value = got[0:width] + got[16 : 16 + width]
         where = got[width : width + 1] * 64.0 + got[width + 1 : width + 2]
         valid = got[width + 2 : width + 3]
-        per = DENS // n_top
         for q in range(n_top):
             rows = [value[0:3], where, valid, value[3 + per * q : 3 + per * (q + 1)]]
             rows.append(jnp.zeros((8 - 5 - per, block), f32))
             packed = jnp.concatenate([r for r in rows if r.shape[0]], axis=0)
             for i in range(block // cap):
-                out[o * (block // cap) + i, q] = packed[:, i * cap : (i + 1) * cap]
-
-
-def octant_product(pos, octant, surf, oper_hi, oper_lo):
+                at = o * (block // cap) + i
+                out[at, q, 0:8] = packed[:, i * cap : (i + 1) * cap]
+                out[at, q, 8:] = leaves
+
+
+def octant_product(pos, octant, surf, oper):
     squared = None
     for d in range(3):
         spacing = surf[d] - pos[d : d + 1]
@@ -280,39 +366,48 @@
     value = lax.rsqrt(squared)
     value = jnp.concatenate([value, jnp.zeros((CPAD - COEF, value.shape[1]), f32)], axis=0)
     high, low = split(value)
-    low = low.astype(f32)
-    high = high.astype(f32)
-    his = [jnp.where(octant == o, high, 0.0).astype(bf16) for o in range(8)]
-    los = [jnp.where(octant == o, low, 0.0).astype(bf16) for o in range(8)]
-    return dot3(
-        (oper_hi, oper_lo), (jnp.concatenate(his, axis=0), jnp.concatenate(los, axis=0))
-    )
-
-
-def look_up(index, table):
-    rows = table.shape[1]
+    masks = [jnp.where(octant == o, 1.0, 0.0).astype(bf16) for o in range(8)]
+    got = dot(oper[...], jnp.concatenate([high * m for m in masks], axis=0))
+    got = got[0:COEF] + got[COEF : 2 * COEF]
+    return got + dot(oper[0:COEF], jnp.concatenate([low * m for m in masks], axis=0))
+
+
+TURNED = (((0,), (0,)), ((), ()))
+
+
+def look_up(index, first, second):
+    rows, lanes = first.shape
     width = index.shape[1]
-    at_row = index // LANE
-    at_lane = index - at_row * LANE
+    at_row = index // lanes
+    at_lane = index - at_row * lanes
     there = at_row == lax.broadcasted_iota(jnp.int32, (rows, width), 0)
-    got = dot(table, jnp.where(there, 1.0, 0.0).astype(bf16))
-    mine = at_lane == lax.broadcasted_iota(jnp.int32, (LANE, width), 0)
-    first = jnp.sum(jnp.where(mine, got[0:LANE], 0.0), axis=0, keepdims=True)
-    second = jnp.sum(jnp.where(mine, got[LANE : 2 * LANE], 0.0), axis=0, keepdims=True)
-    return first, second
+    there = jnp.where(there, 1.0, 0.0).astype(bf16)
+    mine = at_lane == lax.broadcasted_iota(jnp.int32, (lanes, width), 0)
+    out = []
+    for table in (first, second):
+        got = dot(table, there, TURNED)
+        out.append(jnp.sum(jnp.where(mine, got, 0.0), axis=0, keepdims=True))
+    return out
 
 
 PB = 256
 
 
-def upward_kernel(own, box_cap, flip_ref, got, table, surf, w_hi, w_lo, out, buf):
+def fill_surface(surf, column):
+    for d in range(3):
+        surf[d] = jnp.broadcast_to(column[:, d : d + 1], surf.shape[1:])
+
+
+def upward_kernel(n_top, own, box_cap, me_ref, got, column, oper, out, ids, buf, surf):
     sources, _, cap = got.shape
+    lanes = min(cap, LANE)
     wide = up(cap, LANE)
-    flip = flip_ref[0]
+    me = me_ref[0]
     buf[...] = jnp.zeros_like(buf)
+    fill_surface(surf, column)
 
     def place(s, offset):
-        value = got[s]
+        value = got[s, 0:8]
         count = jnp.sum(value[4:5]).astype(jnp.int32)
         value = jnp.concatenate([value, jnp.zeros((8, wide + LANE - cap), f32)], axis=1)
         tile = offset // LANE
@@ -323,17 +418,29 @@
 
     lax.fori_loop(0, sources, place, jnp.int32(0), unroll=4)
     out_rows = out.shape[1]
+    firsts = []
+    at = lax.broadcasted_iota(jnp.int32, (1, box_cap), 1)
+    for m in range(sources // n_top):
+        leaf = got[(me ^ m) * n_top, 8:9, 0:1].astype(jnp.int32)
+        firsts.append((leaf >> 3) + at)
+    ids[...] = jnp.concatenate(firsts, axis=1)
+    leaf = got[pl.ds(me * n_top, n_top), 8:, 0:lanes].reshape(own // lanes, lanes)
+    leaf = leaf.astype(jnp.int32)
+    first = got[me * n_top, 8:9, 0:1].astype(jnp.int32) >> 3
+    boxes = ((leaf >> 3) - first).astype(f32).astype(bf16)
+    octants = (leaf & 7).astype(f32).astype(bf16)
 
     def block(j, total):
         value = buf[:, pl.ds(pl.multiple_of(j * PB, PB), PB)]
-        index = value[3:4].astype(jnp.int32) ^ flip
-        box, octant = look_up(index, table[...])
-        field = split(octant_product(value[0:3], octant, surf, w_hi[...], w_lo[...]))
+        box, octant = look_up(value[3:4].astype(jnp.int32), boxes, octants)
+        high, low = split(octant_product(value[0:3], octant, surf, oper))
         rows = []
         at = lax.broadcasted_iota(jnp.int32, (box_cap, PB), 0).astype(f32)
         for k in range(out_rows // box_cap):
             rows.append(jnp.where(box == at, value[5 + k : 6 + k], 0.0))
-        return total + dot3(field, split(jnp.concatenate(rows, axis=0)), NT)
+        a_high, a_low = split(jnp.concatenate(rows, axis=0))
+        both = dot(jnp.concatenate([high, low], axis=0), a_high, NT)
+        return total + both[0:COEF] + both[COEF : 2 * COEF] + dot(high, a_low, NT)
 
     total = lax.fori_loop(0, own // PB, block, jnp.zeros((COEF, out_rows), f32))
     out[...] = total.astype(bf16)
@@ -348,31 +455,43 @@
     return place
 
 
-def target_kernel(flip_ref, pos, slot, table, surf, w_hi, w_lo, field, place):
-    flip = flip_ref[0]
-    count = pos.shape[1]
-
-    @pl.loop(0, count // PB)
-    def _(j):
-        at = pl.ds(pl.multiple_of(j * PB, PB), PB)
-        index = slot[:, at].astype(jnp.int32) ^ flip
-        high, low = look_up(index, table[...])
-        leaf = (high * 64.0 + low).astype(jnp.int32)
-        octant = leaf & 7
-        field[:, at] = octant_product(
-            pos[:, at], octant, surf, w_hi[...], w_lo[...]
-        )
-        place[:, at] = morton_place(leaf >> 3)
-
-
-def translate_kernel(slabs, x0_ref, ids, part, oa, ob, oc, out, xs, xin, acc, ma, mb, mc, sem):
+def target_kernel(n_top, got, *refs):
+    shared = refs[:n_top]
+    column, oper, field, place, surf = refs[n_top:]
+    fill_surface(surf, column)
+    lanes = min(got.shape[2], LANE)
+    leaf = got[:, 8:, 0:lanes].reshape(-1, lanes).astype(jnp.int32)
+    boxes = (leaf >> 6).astype(f32).astype(bf16)
+    rest = (leaf & 63).astype(f32).astype(bf16)
+    points = shared[0].shape[1]
+    for m in range(n_top):
+        source = shared[m]
+
+        @pl.loop(0, points // PB)
+        def _(j):
+            at = pl.ds(pl.multiple_of(j * PB, PB), PB)
+            value = source[:, at]
+            high, low = look_up(value[3:4].astype(jnp.int32), boxes, rest)
+            leaf = (high * 64.0 + low).astype(jnp.int32)
+            to = pl.ds(pl.multiple_of(m * points + j * PB, PB), PB)
+            field[:, to] = octant_product(value[0:3], leaf & 7, surf, oper)
+            place[:, to] = morton_place(leaf >> 3)
+
+
+def all_parts(parts, k, dens):
+    width = parts[0].shape[1] // dens
+    return jnp.concatenate([p[:, k * width : (k + 1) * width] for p in parts], axis=1)
+
+
+def translate_kernel(slabs, dens, me_ref, ids, *refs):
+    parts = refs[:-11]
+    oa, ob, oc, out, xs, xin, acc, ma, mb, mc, sem = refs[-11:]
     copies = []
     for i, (src, dst) in enumerate(((oa, ma), (ob, mb), (oc, mc))):
         for j in range(src.shape[0]):
             copies.append(pltpu.make_async_copy(src.at[j], dst.at[j], sem.at[i, j]))
             copies[-1].start()
-    x0 = x0_ref[0]
-    dens = part.shape[0]
+    x0 = (me_ref[0] // 2 * 2) * SIDE // len(parts)
     place = morton_place(ids[...])
     place = (((place >> 6) - x0 + REACH) & 7) * 64 + (place & 63)
     place = jnp.where((ids[...] >= 0) & (ids[...] < BOXES4), place, -1)
@@ -380,7 +499,7 @@
     there = jnp.where(at == place, 1.0, 0.0).astype(bf16)
     columns = dens * PLANE
     for k in range(dens):
-        low = dot(there, part[k], NT)
+        low = dot(there, all_parts(parts, k, dens), NT)
         low = low.astype(bf16).astype(f32)
         for s in range(7 + slabs - 1):
             slab = low[s * PLANE : (s + 1) * PLANE].reshape(SIDE, SIDE, COEF)
@@ -429,14 +548,16 @@
         out[:, t * LANE : (t + 1) * LANE] = total.astype(out.dtype)
 
 
-def coarse_kernel(ids, part, m2m_hi, m2m_lo, lat_hi, lat_lo, l2l_hi, l2l_lo, out):
-    dens = part.shape[0]
+def coarse_kernel(ids, *refs):
+    parts = refs[:-7]
+    m2m_hi, m2m_lo, lat_hi, lat_lo, l2l_hi, l2l_lo, out = refs[-7:]
+    dens = out.shape[0]
     box = ids[...]
     place = ((box & 7) << 6) + (box & 56) + (box >> 6)
     place = jnp.where((box >= 0) & (box < BOXES4), place, -1)
     at = lax.broadcasted_iota(jnp.int32, (BOXES4, ids.shape[1]), 0)
     there = jnp.where(at == place, 1.0, 0.0).astype(bf16)
-    level = [dot(there, part[k], NT) for k in range(dens)]
+    level = [dot(there, all_parts(parts, k, dens), NT) for k in range(dens)]
 
     def oper(hi, lo, o):
         return hi[o], lo[o]
@@ -446,7 +567,7 @@
         total = None
         for o in range(8):
             rows = jnp.concatenate([v[o * count : (o + 1) * count] for v in level], axis=0)
-            term = dot3(split(rows), oper(m2m_hi, m2m_lo, o), NT)
+            term = dot3_rows(split(rows), oper(m2m_hi, m2m_lo, o), NT)
             total = term if total is None else total + term
         level = [total[k * count : (k + 1) * count] for k in range(dens)]
     rows = jnp.concatenate(level, axis=0)
@@ -455,7 +576,7 @@
     for _ in range(LEVEL):
         count = level[0].shape[0]
         rows = split(jnp.concatenate(level, axis=0))
-        children = [dot3(rows, oper(l2l_hi, l2l_lo, o), NT) for o in range(8)]
+        children = [dot3_rows(rows, oper(l2l_hi, l2l_lo, o), NT) for o in range(8)]
         level = [
             jnp.concatenate([c[k * count : (k + 1) * count] for c in children], axis=0)
             for k in range(dens)
@@ -466,17 +587,17 @@
     move = jnp.where(at == morton_place(number), 1.0, 0.0).astype(bf16)
     for k in range(dens):
         high, low = split(level[k])
-        turned = (((0,), (0,)), ((), ()))
-        out[k] = dot(high, move, turned) + dot(low, move, turned)
-
-
-def evaluate_kernel(slabs, me_ref, *refs):
+        out[k] = dot(high, move, TURNED) + dot(low, move, TURNED)
+
+
+def evaluate_kernel(slabs, step, me_ref, *refs):
     n = SIDE // slabs
     checks = refs[: 2 * n]
     d_hi, d_lo, lattice, field, place, out, stack = refs[2 * n :]
-    core = me_ref[0]
-    group = me_ref[1]
+    core = me_ref[0] & 1
+    group = me_ref[0] // step
     dens = lattice.shape[0]
+    points = out.shape[2]
     lane = lax.broadcasted_iota(jnp.int32, (COEF, LANE), 1)
     mine = jnp.concatenate([d_hi[core], d_lo[core]], axis=0)
     other = jnp.concatenate([d_hi[1 - core], d_lo[1 - core]], axis=0)
@@ -510,6 +631,8 @@
     @pl.loop(0, place.shape[1] // PB)
     def _(j):
         at = pl.ds(pl.multiple_of(j * PB, PB), PB)
+        m = j // (points // PB)
+        to = pl.ds(pl.multiple_of((j - m * (points // PB)) * PB, PB), PB)
         want = place[:, at] ^ (group * (slabs * PLANE))
         there = want == lax.broadcasted_iota(jnp.int32, (BOXES4, PB), 0)
         got = dot(local, jnp.where(there, 1.0, 0.0).astype(bf16))
@@ -519,20 +642,18 @@
             value = got[k * CPAD : k * CPAD + COEF]
             value = value + got[(dens + k) * CPAD : (dens + k) * CPAD + COEF]
             rows.append(jnp.sum(value * mine, axis=0, keepdims=True))
-        out[:, at] = jnp.concatenate(rows, axis=0)
-
-
-def shifts_of(axis, value, distances):
+        out[m, :, to] = jnp.concatenate(rows, axis=0)
+
+
+def shift_by(axis, value, distance):
     size = lax.axis_size(axis)
-    return [
-        value if m == 0 else lax.ppermute(value, axis, [(i, i ^ m) for i in range(size)])
-        for m in distances
-    ]
-
-
-def split_oper(value):
-    high = lax.reduce_precision(value, 8, 7)
-    return high.astype(bf16), (value - high).astype(bf16)
+    return lax.ppermute(value, axis, [(i, i ^ distance) for i in range(size)])
+
+
+def gather_by(value, distances):
+    got = {m: shift_by("pts", value, m) if m else value for m in distances if m % 2 == 0}
+    got.update({m + 1: shift_by("pts", got[m], 1) for m in list(got) if m + 1 in distances})
+    return [got[m] for m in distances]
 
 
 def per_device(
@@ -540,98 +661,89 @@
 ):
     n_pts = lax.axis_size("pts")
     n_top = lax.axis_size("top")
-    me = lax.axis_index("pts")
     top = lax.axis_index("top")
+    me = lax.axis_index("pts").astype(jnp.int32).reshape(1)
     points = local_pos.shape[1]
     own = points * n_top
     cap = 2 * points // n_pts
+    lanes = min(cap, LANE)
     box_cap = 2 * BOXES4 // n_pts
     dens = DENS // n_top
     slabs = max(1, 2 * SIDE // n_pts)
     coef = uc2e.shape[0]
-    scalar = lambda *v: jnp.stack([jnp.asarray(x, jnp.int32) for x in v])
-
-    slot_row = morton_slot.reshape(1, points)
-    outgoing = call(
+
+    def shape(*dims, dtype=bf16):
+        return jax.ShapeDtypeStruct(dims, dtype)
+
+    rows = 8 + points // lanes
+    outgoing, shared = call(
         functools.partial(route_kernel, own, cap, n_top),
-        jax.ShapeDtypeStruct((n_pts, n_top, 8, cap), f32),
+        (shape(n_pts, n_top, rows, cap, dtype=f32), shape(4, points, dtype=f32)),
         32,
         1 << 27,
-        in_specs=[VMEM] * 3,
-        out_specs=VMEM,
-    )(local_pos, densities, slot_row)
-    outgoing = outgoing.reshape(n_pts * n_top, 8, cap)
+        in_specs=[VMEM] * 4,
+        out_specs=(VMEM, VMEM),
+    )(
+        local_pos,
+        densities,
+        morton_slot.reshape(1, points),
+        slot_leaf.reshape(points // lanes, lanes),
+    )
+    outgoing = outgoing.reshape(n_pts * n_top, rows, cap)
     incoming = lax.all_to_all(outgoing, ("pts", "top"), split_axis=0, concat_axis=0, tiled=True)
 
-    shared = jnp.concatenate(
-        [
-            local_pos,
-            morton_slot.astype(f32).reshape(1, points),
-            slot_leaf.astype(f32).reshape(1, points),
-        ],
-        axis=0,
+    shared = [shift_by("top", shared, m) if m else shared for m in range(n_top)]
+    flat = (-1, LANE)
+    two = 2 * coef
+    square_shape = shape(8, coef, coef)
+    w_up, w_down, *coarse_ops = call(
+        operators_kernel,
+        (shape(two, 8 * CPAD), shape(two, 8 * CPAD))
+        + (square_shape,) * 4
+        + (shape(coef, coef),) * 2
+        + (shape(2, coef, ROWS),) * 2,
+        32,
+        1 << 30,
+        in_specs=[VMEM] * 5,
+        out_specs=(VMEM,) * 10,
+        scratch_shapes=[pltpu.VMEM((2, 8 * coef, LANE), f32)],
+    )(m2m.reshape(flat), l2l.reshape(flat), uc2e, dc2e, lattice)
+    coarse_ops, halves = coarse_ops[:6], coarse_ops[6:]
+    m2m_hi, m2m_lo, l2l_hi, l2l_lo, lat_hi, lat_lo = coarse_ops
+    oa, ob, oc = relayout(m2l_ops, me)
+    column = jnp.asarray(
+        np.pad((np.float32(1.25) * surface_table()).T, ((0, 0), (0, LANE - 3)))
     )
-    shared = shifts_of("top", shared, range(n_top))
-    leaves = jnp.stack([s[4] for s in shared])
-    row_pos = jnp.concatenate([s[0:3] for s in shared], axis=1)
-    row_slot = jnp.concatenate([s[3:4] for s in shared], axis=1)
-    all_leaves = jnp.stack(shifts_of("pts", leaves, range(n_pts)))
-    firsts = (jnp.min(all_leaves, axis=(1, 2)).astype(jnp.int32)) // 8
-    box_ids = (firsts[:, None] + jnp.arange(box_cap, dtype=jnp.int32)[None, :]).reshape(1, -1)
-
-    oa, ob, oc = relayout(m2l_ops, scalar(me & 1))
-    m2m = m2m.reshape(8, coef, coef)
-    l2l = l2l.reshape(8, coef, coef)
-    scale = 1.0 / (4.0 * math.pi)
-    high = lax.Precision.HIGHEST
-    w_up = jnp.einsum("ocf,fe->coe", m2m, uc2e * scale, precision=high)
-    pad = ((0, 0), (0, 0), (0, CPAD - coef))
-    w_up = split_oper(jnp.pad(w_up, pad).reshape(coef, 8 * CPAD))
-    w_down = jnp.transpose(l2l * scale, (2, 0, 1))
-    w_down = split_oper(jnp.pad(w_down, pad).reshape(coef, 8 * CPAD))
-    surf = jnp.asarray(np.repeat((np.float32(1.25) * surface_table())[:, :, None], PB, axis=2))
-
-    table = leaves.reshape(own // LANE, LANE).T.astype(jnp.int32)
-    table = jnp.concatenate([table // 8 - firsts[0], table % 8], axis=0).astype(bf16)
-    partial = call(
-        functools.partial(upward_kernel, own, box_cap),
-        jax.ShapeDtypeStruct((coef, dens * box_cap), bf16),
+
+    surf = pltpu.VMEM((3, coef, PB), f32)
+    partial, ids = call(
+        functools.partial(upward_kernel, n_top, own, box_cap),
+        (shape(coef, dens * box_cap), shape(1, n_pts * box_cap, dtype=jnp.int32)),
         32,
         8 << 30,
-        in_specs=[SMEM] + [VMEM] * 5,
-        out_specs=VMEM,
-        scratch_shapes=[pltpu.VMEM((8, up(own + up(cap, LANE) + LANE, PB)), f32)],
-    )(scalar(top * points), incoming, table, surf, *w_up)
-    parts = shifts_of("pts", partial, range(n_pts))
-    part = jnp.stack(
-        [
-            jnp.concatenate([v[:, k * box_cap : (k + 1) * box_cap] for v in parts], axis=1)
-            for k in range(dens)
-        ]
-    )
-
-    table = all_leaves.reshape(-1, LANE).T.astype(jnp.int32)
-    table = jnp.concatenate([table // 64, table % 64], axis=0).astype(bf16)
+        in_specs=[SMEM] + [VMEM] * 3,
+        out_specs=(VMEM, VMEM),
+        scratch_shapes=[pltpu.VMEM((8, up(own + up(cap, LANE) + LANE, PB)), f32), surf],
+    )(me, incoming, column, w_up)
+    parts = gather_by(partial, range(n_pts))
+
     field, place = call(
-        target_kernel,
-        (
-            jax.ShapeDtypeStruct((coef, own), f32),
-            jax.ShapeDtypeStruct((1, own), jnp.int32),
-        ),
+        functools.partial(target_kernel, n_top),
+        (shape(coef, own, dtype=f32), shape(1, own, dtype=jnp.int32)),
         32,
         6 << 30,
-        in_specs=[SMEM] + [VMEM] * 6,
+        in_specs=[VMEM] * (n_top + 3),
         out_specs=(VMEM, VMEM),
-    )(scalar(me * own + top * points), row_pos, row_slot, table, surf, *w_down)
+        scratch_shapes=[surf],
+    )(incoming, *shared, column, w_down)
 
     columns = dens * PLANE
-    x0 = (me // 2 * 2) * SIDE // n_pts
     checks = call(
-        functools.partial(translate_kernel, slabs),
-        jax.ShapeDtypeStruct((ROWS, slabs * columns), bf16),
+        functools.partial(translate_kernel, slabs, dens),
+        shape(ROWS, slabs * columns),
         56,
         8 << 30,
-        in_specs=[SMEM, VMEM, VMEM, ANY, ANY, ANY],
+        in_specs=[SMEM] + [VMEM] * (1 + n_pts) + [ANY] * 3,
         out_specs=VMEM,
         scratch_shapes=[
             pltpu.VMEM(((7 + slabs - 1) * columns, WFULL), bf16),
@@ -642,42 +754,32 @@
             pltpu.VMEM(oc.shape, bf16),
             pltpu.SemaphoreType.DMA((3, 7)),
         ],
-    )(scalar(x0), box_ids, part, oa, ob, oc)
+    )(me, ids, *parts, oa, ob, oc)
     step = n_pts // SIDE * slabs
-    distances = [step * m + c for m in range(SIDE // slabs) for c in range(2)]
-    gathered = shifts_of("pts", checks, distances)
+    gathered = gather_by(checks, [step * m + c for m in range(SIDE // slabs) for c in range(2)])
 
     lattice4 = call(
         coarse_kernel,
-        jax.ShapeDtypeStruct((dens, coef, BOXES4), f32),
+        shape(dens, coef, BOXES4, dtype=f32),
         32,
         4 << 30,
-        in_specs=[VMEM] * 8,
+        in_specs=[VMEM] * (n_pts + 7),
         out_specs=VMEM,
-    )(box_ids, part, *split_oper(m2m), *split_oper(lattice), *split_oper(l2l))
-
-    halves = dc2e.reshape(coef, NG, 2, 4).transpose(2, 0, 1, 3).reshape(2, coef, 4 * NG)
-    halves = split_oper(jnp.pad(halves, ((0, 0), (0, 0), (0, ROWS - 4 * NG))))
+    )(ids, *parts, m2m_hi, m2m_lo, lat_hi, lat_lo, l2l_hi, l2l_lo)
+
     reply = call(
-        functools.partial(evaluate_kernel, slabs),
-        jax.ShapeDtypeStruct((dens, own), f32),
+        functools.partial(evaluate_kernel, slabs, step),
+        shape(n_top, dens, points, dtype=f32),
         32,
         4 << 30,
         in_specs=[SMEM] + [VMEM] * (len(gathered) + 5),
         out_specs=VMEM,
         scratch_shapes=[pltpu.VMEM((2 * dens * CPAD, BOXES4), f32)],
-    )(scalar(me & 1, me // step), *gathered, *halves, lattice4, field, place)
-    reply = reply.reshape(dens, n_top, points)
-    answers = []
-    for m in range(n_top):
-        value = reply[:, m]
-        if m:
-            value = lax.ppermute(value, "top", [(i, i ^ m) for i in range(n_top)])
-        answers.append(value)
-    answers = jnp.stack(answers)
+    )(me, *gathered, *halves, lattice4, field, place)
+    answers = [shift_by("top", reply[m], m) if m else reply[m] for m in range(n_top)]
     order = jnp.arange(n_top, dtype=jnp.int32) ^ top
     picked = sum(
-        jnp.where(order[:, None, None, None] == m, answers[m][None], 0.0) for m in range(n_top)
+        jnp.where(order[:, None, None] == m, answers[m][None], 0.0) for m in range(n_top)
     )
     return picked.reshape(DENS, points)
 

time: 173 us -> 118 us (0.68)
  local copies, waits for them, and re-layouts: 36.6 us -> 12.3 us
  other arithmetic: 18.1 us -> 0.71 us
  starting transfers between devices: 35.6 us -> 24.9 us
    ppermute x27 -> x20, starting transfers between devices: 29.5 us -> 17.6 us  [shift_by(): return lax.ppermute(value, axis, [(i, i ^ distance) for i in range(size)])]
    convert_element_type x9 -> x0, other arithmetic: 9.4 us -> none  [the longest x5 5.71 us: split_oper(): return (high.astype(bf16), (value - high).astype(bf16))]
    reshape x7 -> x0, local copies, waits for them, and re-layouts: 7.71 us -> none  [the longest x1 2.7 us: per_device(): l2l = l2l.reshape(8, coef, coef)]
    slice x8 -> x0, local copies, waits for them, and re-layouts: 5.53 us -> none  [the longest x3 2.54 us: per_device(): row_slot = jnp.concatenate([s[3:4] for s in shared], axis=1)]
    ppermute x27 -> x20, waiting for transfers between devices: 8.18 us -> 3.09 us  [shift_by(): return lax.ppermute(value, axis, [(i, i ^ distance) for i in range(size)])]
    convert_element_type x3 -> x0, local copies, waits for them, and re-layouts: 4.6 us -> none  [the longest x2 3.28 us: per_device(): table = all_leaves.reshape(-1, LANE).T.astype(jnp.int32)]
    all_to_all x1, waiting for transfers between devices: 0.01 us -> 4.05 us  [per_device(): lax.all_to_all(outgoing, ('pts', 'top'), split_axis=0, concat_axis=0, til...]
    concatenate x5 -> x0, other arithmetic: 3.29 us -> none  [the longest x1 1.35 us: per_device(): jnp.concatenate([local_pos, morton_slot.astype(f32).reshape(1, points), s...]
  transfers between devices with their start and end apart: 28 -> 21, of which waited for: 6 -> 5; matrix products, arithmetic and copies ran while one was open for 26% -> 1% of each run, Pallas kernels for 21% -> 38%
where the time goes in v2:
time: 118 us; the launch traced here: 117 us
  Pallas kernels  71.6 us (61%)
  starting transfers between devices  24.9 us (21%)
  local copies, waits for them, and re-layouts  12.3 us (10%)
  waiting for transfers between devices  7.14 us (6%)
    pallas_call x1, Pallas kernels, per_device(): call(functools.partial(upward_kernel, n_top, own, box_cap), (shape(coef,...  18.8 us
    ppermute x20, starting transfers between devices, shift_by(): return lax.ppermute(value, axis, [(i, i ^ distance) for i in range(size)])  17.6 us
    pallas_call x1, Pallas kernels, relayout(): call(functools.partial(relayout_kernel, nrows), tuple((jax.ShapeDtypeStru...  14.7 us
    pallas_call x1, Pallas kernels, per_device(): call(functools.partial(target_kernel, n_top), (shape(coef, own, dtype=f32...  12.4 us
    unnamed x70, local copies, waits for them, and re-layouts  11.6 us
    pallas_call x1, Pallas kernels, per_device(): call(functools.partial(translate_kernel, slabs, dens), shape(ROWS, slabs...  9.01 us
    all_to_all x1, starting transfers between devices, per_device(): lax.all_to_all(outgoing, ('pts', 'top'), split_axis=0, concat_axis=0, til...  7.29 us
    pallas_call x1, Pallas kernels, per_device(): call(functools.partial(evaluate_kernel, slabs, step), shape(n_top, dens,...  6.11 us
  transfers between devices with their start and end apart: 21, of which 5 were waited for; matrix products, arithmetic and copies ran while one was open for 1% of the time, Pallas kernels for 38%

profile of v2, /device:TPU:0, one launch (start us, length us, event | category | flops | bytes accessed | tf_op | source)
XLA Modules:
  0.0 117.2 jit_solution(3550582386302080002)
XLA Ops:
  0.0 0.8 copy-done.22
  0.8 0.7 copy-done.23
  2.9 2.5 %shard_map.109 = (f32[8,4,16,256]{3,2,1,0:T(8,128)}, f32[4,1024]{1,0:T(4,128)S(1)}) custom-call(f32[3,1024]{1,0:T(4,128)S(1)} %copy-done.23, f32[8,1024]{1,0:T(8,128)S(1)} %copy-done.22, s32[1,1024]{1,0:T(1,128)S(1)} %bitcast.17, s32[8,128]{1,0:T(8,128)S(1)} %bitcast.18), custom_call_target="tpu_custom_call" | custom-call | flops 134217728 | bytes 1048576 | tf_op jit(solution)/shard_map/pallas_call | solution.py:679
  5.3 7.3 %all-to-all-start = ((f32[32,16,256]{2,1,0:T(8,128)}), f32[32,16,256]{2,1,0:T(8,128)S(1)}, u32[]{:S(2)}, u32[]{:S(2)}) async-start(f32[32,16,256]{2,1,0:T(8,128)} %bitcast.3), calls=%async_computation | async-start | bytes 1048576 | tf_op jit(solution)/shard_map/all_to_all | solution.py:693
  12.6 1.1 copy-done
  13.7 1.1 copy-done.1
  14.9 0.9 copy-done.2
  15.8 0.9 copy-done.3
  16.7 0.9 copy-done.4
  17.6 2.8 %shard_map.110 = (bf16[304,1280]{1,0:T(8,128)(2,1)S(1)}, bf16[304,1280]{1,0:T(8,128)(2,1)S(1)}, bf16[8,152,152]{2,1,0:T(8,128)(2,1)S(1)}, bf16[8,152,152]{2,1,0:...) custom-call(f32[1444,128]{1,0:T(8,128)S(1)} %bitcast.15, ...), custom_call_target="tpu_custom_call" | custom-call | flops 1073741824 | bytes 1048576 | tf_op jit(solution)/shard_map/pallas_call | solution.py:699
  20.5 0.8 copy-done.27
  21.3 0.8 copy-done.29
  22.1 0.8 copy-done.31
  22.9 4.1 %all-to-all-done.got = f32[32,16,256]{2,1,0:T(8,128)S(1)} async-done(((f32[32,16,256]{2,1,0:T(8,128)}), f32[32,16,256]{2,1,0:T(8,128)S(1)}, u32[]{:S(2)}, u32[]{:S(2)}) %all-to-all-start) | async-done | bytes 524320 | tf_op jit(solution)/shard_map/all_to_all | solution.py:693
  27.0 18.8 %shard_map.111 = (bf16[152,256]{1,0:T(8,128)(2,1)S(1)}, s32[1,1024]{1,0:T(1,128)S(1)}) custom-call(s32[1]{0:T(128)} %bitcast.me_ref, f32[32,16,256]{2,1,0:T(8,128)S(1)} %all-to-all-done.got, f32[152,128]{1,0:T(8,128)S(1)} %copy-done.26, bf16[304,1280]{1,0:T(8,128)(2,1)S(1)} %get-tuple-element.25.oper), custom_call_target="tpu_custom_call" | custom-call | flops 8589934592 | bytes 1048576 | tf_op jit(solution)/shard_map/pallas_call | solution.py:719
  46.4 1.5 %collective-permute-start.1 = (bf16[152,256]{1,0:T(8,128)(2,1)S(1)}, bf16[152,256]{1,0:T(8,128)(2,1)S(1)}, u32[]{:S(2)}, u32[]{:S(2)}) collective-permute-start(bf16[152,256]{1,0:T(8,128)(2,1)S(1)} %get-tuple-element.27.refs_0_), channel_id=1, source_target_pairs={{0,8},{4,12},{8,0},{12,4},{16,24},{20,28},{24,16},{28,20},{1,9},{5... | collective-permute-start | bytes 233480 | tf_op jit(solution)/shard_map/ppermute | solution.py:650
  47.8 1.3 %collective-permute-start.3 = (bf16[152,256]{1,0:T(8,128)(2,1)S(1)}, bf16[152,256]{1,0:T(8,128)(2,1)S(1)}, u32[]{:S(2)}, u32[]{:S(2)}) collective-permute-start(bf16[152,256]{1,0:T(8,128)(2,1)S(1)} %get-tuple-element.27.refs_0_), channel_id=1, source_target_pairs={{0,16},{4,20},{8,24},{12,28},{16,0},{20,4},{24,8},{28,12},{1,17},{... | collective-permute-start | bytes 233480 | tf_op jit(solution)/shard_map/ppermute | solution.py:650
  49.1 0.7 collective-permute-start.5
  49.8 2.5 %collective-permute-start.14 = (f32[4,1024]{1,0:T(4,128)S(1)}, f32[4,1024]{1,0:T(4,128)S(1)}, u32[]{:S(2)}, u32[]{:S(2)}) collective-permute-start(f32[4,1024]{1,0:T(4,128)S(1)} %get-tuple-element.39.refs_0_), channel_id=1, source_target_pairs={{0,1},{1,0},{2,3},{3,2},{4,5},{5,4},{6,7},{7,6},{8,9},{9,8},{10,11... | collective-permute-start | bytes 49160 | tf_op jit(solution)/shard_map/ppermute | solution.py:650
  52.4 14.7 %shard_map.112 = (bf16[7,4,80,1152]{3,2,1,0:T(8,128)(2,1)}, bf16[4,3,80,1152]{3,2,1,0:T(8,128)(2,1)}, bf16[3,3,80,640]{3,2,1,0:T(8,128)(2,1)}) custom-call(s32[1]{0:T(128)} %bitcast.me_ref, bf16[57038,128]{1,0:T(8,128)(2,1)} %bitcast.19, bf16[57038,128]{1,0:T(8,128)(2,1)} %bitcast.20), custom_call_target="tpu_custom_call" | custom-call | flops 1048576 | bytes 16777216 | tf_op jit(solution)/shard_map/pallas_call | solution.py:214
  68.4 0.8 collective-permute-start.15
  69.2 1.5 %collective-permute-start.16 = (f32[4,1024]{1,0:T(4,128)S(1)}, f32[4,1024]{1,0:T(4,128)S(1)}, u32[]{:S(2)}, u32[]{:S(2)}) collective-permute-start(f32[4,1024]{1,0:T(4,128)S(1)} %get-tuple-element.39.refs_0_), channel_id=1, source_target_pairs={{0,3},{1,2},{2,1},{3,0},{4,7},{5,6},{6,5},{7,4},{8,11},{9,10},{10,... | collective-permute-start | bytes 49160 | tf_op jit(solution)/shard_map/ppermute | solution.py:650
  71.4 9.0 %shard_map.113.refs_0_ = bf16[80,256]{1,0:T(8,128)(2,1)} custom-call(s32[1]{0:T(128)} %bitcast.me_ref, s32[1,1024]{1,0:T(1,128)} %copy-done.33, bf16[152,256]{1,0:T(8,128)(2,1)} %copy-done.5, bf16[152,256]{1,0:T(8,128)(2,1)} %copy-done.13, bf16[152,256]{1,0:T(8,128)(2,1)} %copy-done.7, bf16[152,256]{1,0:T(8,128)(2,1)} %copy-done.15, ...), custom_call_target="tpu_custom_call" | custom-call | flops 8589934592 | bytes 1048576 | tf_op jit(solution)/shard_map/pallas_call | solution.py:741
  80.4 1.0 collective-permute-start.10
  81.5 1.5 %collective-permute-start.12 = (bf16[80,256]{1,0:T(8,128)(2,1)}, bf16[80,256]{1,0:T(8,128)(2,1)S(1)}, u32[]{:S(2)}, u32[]{:S(2)}) collective-permute-start(bf16[80,256]{1,0:T(8,128)(2,1)} %shard_map.113.refs_0_), channel_id=1, source_target_pairs={{0,24},{4,28},{8,16},{12,20},{16,8},{20,12},{24,0},{28,4},{1,25},{... | collective-permute-start | bytes 122888 | tf_op jit(solution)/shard_map/ppermute | solution.py:650
  82.9 1.1 collective-permute-start.8
  84.1 12.4 %shard_map.115 = (f32[152,4096]{1,0:T(8,128)S(1)}, s32[1,4096]{1,0:T(1,128)S(1)}) custom-call(f32[32,16,256]{2,1,0:T(8,128)S(1)} %all-to-all-done.got, f32[4,1024]{1,0:T(4,128)S(1)} %get-tuple-element.39.refs_0_, f32[4,1024]{1,0:T(4,128)S(1)} %collective-permute-done.14.refs_1_, f32[4,1024]{1,0:T(4,128)S(1)} %collective-permute-done.15.refs_2_, ...), custom_call_target="tpu_custom_call" | custom-call | flops 6442450944 | bytes 1048576 | tf_op jit(solution)/shard_map/pallas_call | solution.py:730
  97.7 5.4 %shard_map.114.refs_10_ = f32[2,152,512]{2,1,0:T(8,128)S(1)} custom-call(s32[1,1024]{1,0:T(1,128)S(1)} %copy-done.34, bf16[152,256]{1,0:T(8,128)(2,1)S(1)} %copy-done.6, bf16[152,256]{1,0:T(8,128)(2,1)S(1)} %copy-done.14, bf16[152,256]{1,0:T(8,128)(2,1)S(1)} %copy-done.8, bf16[152,256]{1,0:T(8,128)(2,1)S(1)} %copy-done.16, bf16[152,256]{1,0:T(8,128)(2,1)S(1)} %copy-done.10, ...), custom_call_target="tpu_custom_call" | custom-call | flops 4294967296 | bytes 1048576 | tf_op jit(solution)/shard_map/pallas_call | solution.py:761
  103.2 6.1 %shard_map.116 = f32[4,2,1024]{2,1,0:T(2,128)S(1)} custom-call(s32[1]{0:T(128)} %bitcast.me_ref, bf16[80,256]{1,0:T(8,128)(2,1)S(1)} %copy-done.21, bf16[80,256]{1,0:T(8,128)(2,1)S(1)} %collective-permute-done.7.refs_1_, bf16[80,256]{1,0:T(8,128)(2,1)S(1)} %collective-permute-done.8.refs_2_, bf16[80,256]{1,0:T(8,128)(2,1)S(1)} %collective-permute-done.9.refs_3_, ...), custom_call_target="tpu_custom_call" | custom-call | flops 4294967296 | bytes 1048576 | tf_op jit(solution)/shard_map/pallas_call | solution.py:770
  109.9 2.9 %collective-permute-start.19 = (f32[2,1024]{1,0:T(2,128)S(1)}, f32[2,1024]{1,0:T(2,128)S(1)}, u32[]{:S(2)}, u32[]{:S(2)}) collective-permute-start(f32[2,1024]{1,0:T(2,128)S(1)} %get-tuple-element.44), channel_id=1, source_target_pairs={{0,3},{1,2},{2,1},{3,0},{4,7},{5,6},{6,5},{7,4},{8,11},{9,10},{10,... | collective-permute-start | bytes 24584 | tf_op jit(solution)/shard_map/ppermute | solution.py:650
  113.9 1.4 %collective-permute-done.19 = f32[2,1024]{1,0:T(2,128)S(1)} collective-permute-done((f32[2,1024]{1,0:T(2,128)S(1)}, f32[2,1024]{1,0:T(2,128)S(1)}, u32[]{:S(2)}, u32[]{:S(2)}) %collective-permute-start.19) | collective-permute-done | bytes 8224 | tf_op jit(solution)/shard_map/ppermute | solution.py:650
  115.4 1.0 collective-permute-done.17
  (108 shorter events, 7.6 us)
Async XLA Ops:
  2.9 24.1 %copy-start.26 = (f32[152,128]{1,0:T(8,128)S(1)}, f32[152,128]{1,0:T(8,128)}, u32[]{:S(2)}) copy-start(f32[152,128]{1,0:T(8,128)} %constant.21.clone.column.refs_4_) | copy-start | bytes 233476
  5.3 21.7 %all-to-all-start = ((f32[32,16,256]{2,1,0:T(8,128)}), f32[32,16,256]{2,1,0:T(8,128)S(1)}, u32[]{:S(2)}, u32[]{:S(2)}) async-start(f32[32,16,256]{2,1,0:T(8,128)} %bitcast.3), calls=%async_computation | async-start | bytes 1048576 | tf_op jit(solution)/shard_map/all_to_all | solution.py:693
  46.4 20.7 %copy-start.5 = (bf16[152,256]{1,0:T(8,128)(2,1)}, bf16[152,256]{1,0:T(8,128)(2,1)S(1)}, u32[]{:S(2)}) copy-start(bf16[152,256]{1,0:T(8,128)(2,1)S(1)} %get-tuple-element.27.refs_0_) | copy-start | bytes 233476
  46.4 20.8 %collective-permute-start.1 = (bf16[152,256]{1,0:T(8,128)(2,1)S(1)}, bf16[152,256]{1,0:T(8,128)(2,1)S(1)}, u32[]{:S(2)}, u32[]{:S(2)}) collective-permute-start(bf16[152,256]{1,0:T(8,128)(2,1)S(1)} %get-tuple-element.27.refs_0_), channel_id=1, source_target_pairs={{0,8},{4,12},{8,0},{12,4},{16,24},{20,28},{24,16},{28,20},{1,9},{5... | collective-permute-start | bytes 233480 | tf_op jit(solution)/shard_map/ppermute | solution.py:650
  47.8 19.8 %collective-permute-start.3 = (bf16[152,256]{1,0:T(8,128)(2,1)S(1)}, bf16[152,256]{1,0:T(8,128)(2,1)S(1)}, u32[]{:S(2)}, u32[]{:S(2)}) collective-permute-start(bf16[152,256]{1,0:T(8,128)(2,1)S(1)} %get-tuple-element.27.refs_0_), channel_id=1, source_target_pairs={{0,16},{4,20},{8,24},{12,28},{16,0},{20,4},{24,8},{28,12},{1,17},{... | collective-permute-start | bytes 233480 | tf_op jit(solution)/shard_map/ppermute | solution.py:650
  49.1 18.6 %collective-permute-start.5 = (bf16[152,256]{1,0:T(8,128)(2,1)S(1)}, bf16[152,256]{1,0:T(8,128)(2,1)S(1)}, u32[]{:S(2)}, u32[]{:S(2)}) collective-permute-start(bf16[152,256]{1,0:T(8,128)(2,1)S(1)} %get-tuple-element.27.refs_0_), channel_id=1, source_target_pairs={{0,24},{4,28},{8,16},{12,20},{16,8},{20,12},{24,0},{28,4},{1,25},{... | collective-permute-start | bytes 233480 | tf_op jit(solution)/shard_map/ppermute | solution.py:650
  49.8 33.1 %collective-permute-start.14 = (f32[4,1024]{1,0:T(4,128)S(1)}, f32[4,1024]{1,0:T(4,128)S(1)}, u32[]{:S(2)}, u32[]{:S(2)}) collective-permute-start(f32[4,1024]{1,0:T(4,128)S(1)} %get-tuple-element.39.refs_0_), channel_id=1, source_target_pairs={{0,1},{1,0},{2,3},{3,2},{4,5},{5,4},{6,7},{7,6},{8,9},{9,8},{10,11... | collective-permute-start | bytes 49160 | tf_op jit(solution)/shard_map/ppermute | solution.py:650
  67.1 1.3 %collective-permute-start = (bf16[152,256]{1,0:T(8,128)(2,1)S(1)}, bf16[152,256]{1,0:T(8,128)(2,1)S(1)}, u32[]{:S(2)}, u32[]{:S(2)}) collective-permute-start(bf16[152,256]{1,0:T(8,128)(2,1)S(1)} %get-tuple-element.27.refs_0_), channel_id=1, source_target_pairs={{0,4},{4,0},{8,12},{12,8},{16,20},{20,16},{24,28},{28,24},{1,5},{5... | collective-permute-start | bytes 233480 | tf_op jit(solution)/shard_map/ppermute | solution.py:650
  67.2 2.1 %collective-permute-start.2 = (bf16[152,256]{1,0:T(8,128)(2,1)S(1)}, bf16[152,256]{1,0:T(8,128)(2,1)S(1)}, u32[]{:S(2)}, u32[]{:S(2)}) collective-permute-start(bf16[152,256]{1,0:T(8,128)(2,1)S(1)} %collective-permute-done.1.refs_2_), channel_id=1, source_target_pairs={{0,4},{4,0},{8,12},{12,8},{16,20},{20,16},{24,28},{28,24},{1,5},{5... | collective-permute-start | bytes 233480 | tf_op jit(solution)/shard_map/ppermute | solution.py:650
  67.6 3.1 %collective-permute-start.4 = (bf16[152,256]{1,0:T(8,128)(2,1)S(1)}, bf16[152,256]{1,0:T(8,128)(2,1)S(1)}, u32[]{:S(2)}, u32[]{:S(2)}) collective-permute-start(bf16[152,256]{1,0:T(8,128)(2,1)S(1)} %collective-permute-done.3.refs_4_), channel_id=1, source_target_pairs={{0,4},{4,0},{8,12},{12,8},{16,20},{20,16},{24,28},{28,24},{1,5},{5... | collective-permute-start | bytes 233480 | tf_op jit(solution)/shard_map/ppermute | solution.py:650
  67.7 3.0 %collective-permute-start.6 = (bf16[152,256]{1,0:T(8,128)(2,1)S(1)}, bf16[152,256]{1,0:T(8,128)(2,1)S(1)}, u32[]{:S(2)}, u32[]{:S(2)}) collective-permute-start(bf16[152,256]{1,0:T(8,128)(2,1)S(1)} %collective-permute-done.5.refs_6_), channel_id=1, source_target_pairs={{0,4},{4,0},{8,12},{12,8},{16,20},{20,16},{24,28},{28,24},{1,5},{5... | collective-permute-start | bytes 233480 | tf_op jit(solution)/shard_map/ppermute | solution.py:650
  68.4 15.6 %collective-permute-start.15 = (f32[4,1024]{1,0:T(4,128)S(1)}, f32[4,1024]{1,0:T(4,128)S(1)}, u32[]{:S(2)}, u32[]{:S(2)}) collective-permute-start(f32[4,1024]{1,0:T(4,128)S(1)} %get-tuple-element.39.refs_0_), channel_id=1, source_target_pairs={{0,2},{1,3},{2,0},{3,1},{4,6},{5,7},{6,4},{7,5},{8,10},{9,11},{10,... | collective-permute-start | bytes 49160 | tf_op jit(solution)/shard_map/ppermute | solution.py:650
  69.2 14.8 %collective-permute-start.16 = (f32[4,1024]{1,0:T(4,128)S(1)}, f32[4,1024]{1,0:T(4,128)S(1)}, u32[]{:S(2)}, u32[]{:S(2)}) collective-permute-start(f32[4,1024]{1,0:T(4,128)S(1)} %get-tuple-element.39.refs_0_), channel_id=1, source_target_pairs={{0,3},{1,2},{2,1},{3,0},{4,7},{5,6},{6,5},{7,4},{8,11},{9,10},{10,... | collective-permute-start | bytes 49160 | tf_op jit(solution)/shard_map/ppermute | solution.py:650
  80.4 16.2 %collective-permute-start.10 = (bf16[80,256]{1,0:T(8,128)(2,1)}, bf16[80,256]{1,0:T(8,128)(2,1)S(1)}, u32[]{:S(2)}, u32[]{:S(2)}) collective-permute-start(bf16[80,256]{1,0:T(8,128)(2,1)} %shard_map.113.refs_0_), channel_id=1, source_target_pairs={{0,16},{4,20},{8,24},{12,28},{16,0},{20,4},{24,8},{28,12},{1,17},{... | collective-permute-start | bytes 122888 | tf_op jit(solution)/shard_map/ppermute | solution.py:650
  81.5 15.6 %collective-permute-start.12 = (bf16[80,256]{1,0:T(8,128)(2,1)}, bf16[80,256]{1,0:T(8,128)(2,1)S(1)}, u32[]{:S(2)}, u32[]{:S(2)}) collective-permute-start(bf16[80,256]{1,0:T(8,128)(2,1)} %shard_map.113.refs_0_), channel_id=1, source_target_pairs={{0,24},{4,28},{8,16},{12,20},{16,8},{20,12},{24,0},{28,4},{1,25},{... | collective-permute-start | bytes 122888 | tf_op jit(solution)/shard_map/ppermute | solution.py:650
  82.9 14.3 %collective-permute-start.8 = (bf16[80,256]{1,0:T(8,128)(2,1)}, bf16[80,256]{1,0:T(8,128)(2,1)S(1)}, u32[]{:S(2)}, u32[]{:S(2)}) collective-permute-start(bf16[80,256]{1,0:T(8,128)(2,1)} %shard_map.113.refs_0_), channel_id=1, source_target_pairs={{0,8},{4,12},{8,0},{12,4},{16,24},{20,28},{24,16},{28,20},{1,9},{5... | collective-permute-start | bytes 122888 | tf_op jit(solution)/shard_map/ppermute | solution.py:650
  84.0 13.6 %copy-start.6 = (bf16[152,256]{1,0:T(8,128)(2,1)S(1)}, bf16[152,256]{1,0:T(8,128)(2,1)}, u32[]{:S(2)}) copy-start(bf16[152,256]{1,0:T(8,128)(2,1)} %copy-done.5) | copy-start | bytes 233476
  84.0 13.6 %copy-start.8 = (bf16[152,256]{1,0:T(8,128)(2,1)S(1)}, bf16[152,256]{1,0:T(8,128)(2,1)}, u32[]{:S(2)}) copy-start(bf16[152,256]{1,0:T(8,128)(2,1)} %copy-done.7) | copy-start | bytes 233476
  84.0 13.6 %copy-start.10 = (bf16[152,256]{1,0:T(8,128)(2,1)S(1)}, bf16[152,256]{1,0:T(8,128)(2,1)}, u32[]{:S(2)}) copy-start(bf16[152,256]{1,0:T(8,128)(2,1)} %copy-done.9) | copy-start | bytes 233476
  84.0 13.6 %copy-start.12 = (bf16[152,256]{1,0:T(8,128)(2,1)S(1)}, bf16[152,256]{1,0:T(8,128)(2,1)}, u32[]{:S(2)}) copy-start(bf16[152,256]{1,0:T(8,128)(2,1)} %copy-done.11) | copy-start | bytes 233476
  84.1 13.6 %copy-start.14 = (bf16[152,256]{1,0:T(8,128)(2,1)S(1)}, bf16[152,256]{1,0:T(8,128)(2,1)}, u32[]{:S(2)}) copy-start(bf16[152,256]{1,0:T(8,128)(2,1)} %copy-done.13) | copy-start | bytes 233476
  84.1 13.6 %copy-start.16 = (bf16[152,256]{1,0:T(8,128)(2,1)S(1)}, bf16[152,256]{1,0:T(8,128)(2,1)}, u32[]{:S(2)}) copy-start(bf16[152,256]{1,0:T(8,128)(2,1)} %copy-done.15) | copy-start | bytes 233476
  84.1 13.6 %copy-start.18 = (bf16[152,256]{1,0:T(8,128)(2,1)S(1)}, bf16[152,256]{1,0:T(8,128)(2,1)}, u32[]{:S(2)}) copy-start(bf16[152,256]{1,0:T(8,128)(2,1)} %copy-done.17) | copy-start | bytes 233476
  84.1 13.6 %copy-start.20 = (bf16[152,256]{1,0:T(8,128)(2,1)S(1)}, bf16[152,256]{1,0:T(8,128)(2,1)}, u32[]{:S(2)}) copy-start(bf16[152,256]{1,0:T(8,128)(2,1)} %copy-done.19) | copy-start | bytes 233476
  84.1 13.6 %copy-start.28 = (bf16[8,152,152]{2,1,0:T(8,128)(2,1)S(1)}, bf16[8,152,152]{2,1,0:T(8,128)(2,1)}, u32[]{:S(2)}) copy-start(bf16[8,152,152]{2,1,0:T(8,128)(2,1)} %copy-done.27) | copy-start | bytes 1108996
  96.5 6.6 %collective-permute-start.7 = (bf16[80,256]{1,0:T(8,128)(2,1)S(1)}, bf16[80,256]{1,0:T(8,128)(2,1)S(1)}, u32[]{:S(2)}, u32[]{:S(2)}) collective-permute-start(bf16[80,256]{1,0:T(8,128)(2,1)S(1)} %copy-done.21), channel_id=1, source_target_pairs={{0,4},{4,0},{8,12},{12,8},{16,20},{20,16},{24,28},{28,24},{1,5},{5... | collective-permute-start | bytes 122888 | tf_op jit(solution)/shard_map/ppermute | solution.py:650
  96.6 6.5 %collective-permute-start.11 = (bf16[80,256]{1,0:T(8,128)(2,1)S(1)}, bf16[80,256]{1,0:T(8,128)(2,1)S(1)}, u32[]{:S(2)}, u32[]{:S(2)}) collective-permute-start(bf16[80,256]{1,0:T(8,128)(2,1)S(1)} %collective-permute-done.10.refs_4_), channel_id=1, source_target_pairs={{0,4},{4,0},{8,12},{12,8},{16,20},{20,16},{24,28},{28,24},{1,5},{5... | collective-permute-start | bytes 122888 | tf_op jit(solution)/shard_map/ppermute | solution.py:650
  97.1 6.0 %collective-permute-start.13 = (bf16[80,256]{1,0:T(8,128)(2,1)S(1)}, bf16[80,256]{1,0:T(8,128)(2,1)S(1)}, u32[]{:S(2)}, u32[]{:S(2)}) collective-permute-start(bf16[80,256]{1,0:T(8,128)(2,1)S(1)} %collective-permute-done.12.refs_6_), channel_id=1, source_target_pairs={{0,4},{4,0},{8,12},{12,8},{16,20},{20,16},{24,28},{28,24},{1,5},{5... | collective-permute-start | bytes 122888 | tf_op jit(solution)/shard_map/ppermute | solution.py:650
  97.2 5.9 %collective-permute-start.9 = (bf16[80,256]{1,0:T(8,128)(2,1)S(1)}, bf16[80,256]{1,0:T(8,128)(2,1)S(1)}, u32[]{:S(2)}, u32[]{:S(2)}) collective-permute-start(bf16[80,256]{1,0:T(8,128)(2,1)S(1)} %collective-permute-done.8.refs_2_), channel_id=1, source_target_pairs={{0,4},{4,0},{8,12},{12,8},{16,20},{20,16},{24,28},{28,24},{1,5},{5... | collective-permute-start | bytes 122888 | tf_op jit(solution)/shard_map/ppermute | solution.py:650
  109.3 4.6 %collective-permute-start.18 = (f32[2,1024]{1,0:T(2,128)S(1)}, f32[2,1024]{1,0:T(2,128)S(1)}, u32[]{:S(2)}, u32[]{:S(2)}) collective-permute-start(f32[2,1024]{1,0:T(2,128)S(1)} %get-tuple-element.45), channel_id=1, source_target_pairs={{0,2},{1,3},{2,0},{3,1},{4,6},{5,7},{6,4},{7,5},{8,10},{9,11},{10,... | collective-permute-start | bytes 24584 | tf_op jit(solution)/shard_map/ppermute | solution.py:650
  109.9 5.5 %collective-permute-start.19 = (f32[2,1024]{1,0:T(2,128)S(1)}, f32[2,1024]{1,0:T(2,128)S(1)}, u32[]{:S(2)}, u32[]{:S(2)}) collective-permute-start(f32[2,1024]{1,0:T(2,128)S(1)} %get-tuple-element.44), channel_id=1, source_target_pairs={{0,3},{1,2},{2,1},{3,0},{4,7},{5,6},{6,5},{7,4},{8,11},{9,10},{10,... | collective-permute-start | bytes 24584 | tf_op jit(solution)/shard_map/ppermute | solution.py:650
  112.8 3.7 %collective-permute-start.17 = (f32[2,1024]{1,0:T(2,128)S(1)}, f32[2,1024]{1,0:T(2,128)S(1)}, u32[]{:S(2)}, u32[]{:S(2)}) collective-permute-start(f32[2,1024]{1,0:T(2,128)S(1)} %get-tuple-element.46), channel_id=1, source_target_pairs={{0,1},{1,0},{2,3},{3,2},{4,5},{5,4},{6,7},{7,6},{8,9},{9,8},{10,11... | collective-permute-start | bytes 24584 | tf_op jit(solution)/shard_map/ppermute | solution.py:650
  (24 other events, 79.4 us)

commit v3 on v2

--- a/solution.py
+++ b/solution.py
@@ -43,7 +43,24 @@
 
 COEF = surface_table().shape[1]
 OFFSETS = (2 * REACH + 1) ** 3 - 27
+FEATURES = 4
+PB = 256
+STRIP = 16
+GRANT = 58
 CPAD = up(COEF, 32)
+
+
+def column_table():
+    surface = 1.25 * surface_table().astype(np.float64)
+    grid = np.linspace(-0.9, 0.9, 10)
+    points = np.stack(np.meshgrid(grid, grid, grid, indexing="ij")).reshape(3, -1)
+    values = 1.0 / np.sqrt(((surface[:, :, None] - points[:, None, :]) ** 2).sum(axis=0))
+    scale = (points**2).sum(axis=1)
+    out = np.zeros((surface.shape[1], LANE), np.float32)
+    out[:, 0:3] = (np.float32(1.25) * surface_table()).T
+    out[:, 8] = values.mean(axis=1)
+    out[:, 9:12] = values @ points.T / scale
+    return out
 
 
 def blocks():
@@ -89,6 +106,7 @@
 
 
 VMEM = pl.BlockSpec(memory_space=pltpu.VMEM)
+WHOLE = pl.BlockSpec()
 SMEM = pl.BlockSpec(memory_space=pltpu.SMEM)
 ANY = pl.BlockSpec(memory_space=pl.ANY)
 
@@ -214,7 +232,7 @@
     return call(
         functools.partial(relayout_kernel, nrows),
         tuple(jax.ShapeDtypeStruct(s, bf16) for s in shapes),
-        58,
+        GRANT,
         1 << 20,
         16 << 20,
         grid_spec=pltpu.PrefetchScalarGridSpec(
@@ -257,19 +275,23 @@
 
 
 def operators_kernel(
-    m2m, l2l, uc2e, dc2e, lattice, w_up, w_down, m2m_hi, m2m_lo, l2l_hi, l2l_lo, lat_hi, lat_lo,
+    m2m, l2l, uc2e, dc2e, lattice, column, w_both, m2m_hi, m2m_lo, l2l_hi, l2l_lo, lat_hi, lat_lo,
     d_hi, d_lo, rows
 ):
     scale = 1.0 / (4.0 * math.pi)
     lat_hi[...], lat_lo[...] = split(lattice[...])
     first = split(uc2e[...] * scale)
 
-    def stack(pieces, out):
-        blank = jnp.zeros((COEF, CPAD - COEF), f32)
-        wide = jnp.concatenate([x for p in pieces for x in (p, blank)], axis=1)
-        high, low = split(wide)
-        out[0:COEF] = high
-        out[COEF : 2 * COEF] = low
+    plane = split(column[...])
+
+    def stack(pieces, first):
+        wide = []
+        for piece in pieces:
+            high, low = split(dot3(split(piece), plane)[:, 8 : 8 + FEATURES])
+            wide += [piece, high.astype(f32), low.astype(f32)]
+            wide.append(jnp.zeros((COEF, CPAD - COEF - 2 * FEATURES), f32))
+        wide = jnp.concatenate([w for w in wide if w.shape[1]], axis=1).astype(bf16)
+        w_both[first : first + COEF] = wide
 
     def matrix(o):
         at = slice(o * COEF, (o + 1) * COEF)
@@ -281,14 +303,14 @@
         high, low = split(matrix(o))
         m2m_hi[o], m2m_lo[o] = high, low
         pieces.append(dot3((high, low), first))
-    stack(pieces, w_up)
+    stack(pieces, 0)
     square(l2l, rows)
     pieces = []
     for o in range(8):
         value = matrix(o)
         l2l_hi[o], l2l_lo[o] = split(value)
         pieces.append(jnp.transpose(value) * scale)
-    stack(pieces, w_down)
+    stack(pieces, COEF)
     high, low = split(dc2e[...])
     i = lax.broadcasted_iota(jnp.int32, (COEF, ROWS), 0)
     r = lax.broadcasted_iota(jnp.int32, (COEF, ROWS), 1)
@@ -299,12 +321,10 @@
         d_lo[h] = dot(low, here).astype(bf16)
 
 
-def route_kernel(own, cap, n_top, pos, dens, slot, leaf, out, shared):
+def route_kernel(own, cap, n_top, pos, dens, slot, out, entries):
     points = pos.shape[1]
     owners = out.shape[0]
     slots = slot[...]
-    shared[0:3] = pos[...]
-    shared[3:4] = slots.astype(f32)
     owner = slots // own
     inside = slots - owner * own
     hit = owner == lax.broadcasted_iota(jnp.int32, (owners, points), 0)
@@ -322,6 +342,7 @@
         total = total + dot(part, every)
     rank = jnp.sum(hit * jnp.concatenate(ranks, axis=1), axis=0, keepdims=True)
     entry = owner * cap + rank.astype(jnp.int32)
+    entries[...] = entry
     inside_hi = inside // 64
     value = jnp.concatenate([pos[...], dens[...]], axis=0)
     width = value.shape[0]
@@ -336,11 +357,6 @@
     payload = jnp.concatenate([high, low], axis=0).astype(bf16)
     block = max(cap, LANE)
     per = DENS // n_top
-    leaves = leaf[...].astype(f32)
-    if leaves.shape[1] < cap:
-        leaves = jnp.concatenate(
-            [leaves, jnp.zeros((leaves.shape[0], cap - leaves.shape[1]), f32)], axis=1
-        )
     for o in range(owners * cap // block):
         there = entry == o * block + lax.broadcasted_iota(jnp.int32, (block, points), 0)
         there = jnp.where(there, 1.0, 0.0).astype(bf16)
@@ -354,8 +370,26 @@
             packed = jnp.concatenate([r for r in rows if r.shape[0]], axis=0)
             for i in range(block // cap):
                 at = o * (block // cap) + i
-                out[at, q, 0:8] = packed[:, i * cap : (i + 1) * cap]
-                out[at, q, 8:] = leaves
+                out[at, q] = packed[:, i * cap : (i + 1) * cap]
+
+
+def restore_kernel(got, entries, out):
+    devices, per, cap = got.shape
+    n_top = out.shape[0] // per
+    points = out.shape[1]
+    block = max(cap, PB)
+    total = jnp.zeros((2 * out.shape[0], points), f32)
+    for o in range(devices // n_top * cap // block):
+        count = block // cap
+        value = []
+        for q in range(n_top):
+            pieces = [got[(o * count + i) * n_top + q] for i in range(count)]
+            value.append(jnp.concatenate(pieces, axis=1))
+        high, low = split(jnp.concatenate(value, axis=0))
+        both = jnp.concatenate([high.astype(f32), low.astype(f32)], axis=0).astype(bf16)
+        at = o * block + lax.broadcasted_iota(jnp.int32, (block, points), 0)
+        total = total + dot(both, jnp.where(entries[...] == at, 1.0, 0.0).astype(bf16))
+    out[...] = total[0 : out.shape[0]] + total[out.shape[0] :]
 
 
 def octant_product(pos, octant, surf, oper):
@@ -364,76 +398,86 @@
         spacing = surf[d] - pos[d : d + 1]
         squared = spacing * spacing if squared is None else squared + spacing * spacing
     value = lax.rsqrt(squared)
-    value = jnp.concatenate([value, jnp.zeros((CPAD - COEF, value.shape[1]), f32)], axis=0)
-    high, low = split(value)
+    round_pos = pos.astype(bf16).astype(f32)
+    value = value - surf[3]
+    for d in range(3):
+        value = value - surf[4 + d] * round_pos[d : d + 1]
+    features = [jnp.ones_like(round_pos[0:1]), round_pos]
+    blank = jnp.zeros((CPAD - COEF - 2 * FEATURES, value.shape[1]), f32)
+    value = [value] + features + features + [blank]
+    value = jnp.concatenate([v for v in value if v.shape[0]], axis=0).astype(bf16)
     masks = [jnp.where(octant == o, 1.0, 0.0).astype(bf16) for o in range(8)]
-    got = dot(oper[...], jnp.concatenate([high * m for m in masks], axis=0))
-    got = got[0:COEF] + got[COEF : 2 * COEF]
-    return got + dot(oper[0:COEF], jnp.concatenate([low * m for m in masks], axis=0))
+    return dot(oper[...], jnp.concatenate([value * m for m in masks], axis=0))
 
 
 TURNED = (((0,), (0,)), ((), ()))
 
 
-def look_up(index, first, second):
-    rows, lanes = first.shape
+def look_up(index, table):
+    lanes, rows = table.shape[0] // 2, table.shape[1]
     width = index.shape[1]
     at_row = index // lanes
     at_lane = index - at_row * lanes
     there = at_row == lax.broadcasted_iota(jnp.int32, (rows, width), 0)
-    there = jnp.where(there, 1.0, 0.0).astype(bf16)
+    got = dot(table, jnp.where(there, 1.0, 0.0).astype(bf16))
     mine = at_lane == lax.broadcasted_iota(jnp.int32, (lanes, width), 0)
-    out = []
-    for table in (first, second):
-        got = dot(table, there, TURNED)
-        out.append(jnp.sum(jnp.where(mine, got, 0.0), axis=0, keepdims=True))
-    return out
-
-
-PB = 256
+    first = jnp.sum(jnp.where(mine, got[0:lanes], 0.0), axis=0, keepdims=True)
+    return first, jnp.sum(jnp.where(mine, got[lanes:], 0.0), axis=0, keepdims=True)
 
 
 def fill_surface(surf, column):
-    for d in range(3):
-        surf[d] = jnp.broadcast_to(column[:, d : d + 1], surf.shape[1:])
-
-
-def upward_kernel(n_top, own, box_cap, me_ref, got, column, oper, out, ids, buf, surf):
+    for i, lane in enumerate((0, 1, 2, 8, 9, 10, 11)):
+        surf[i] = jnp.broadcast_to(column[:, lane : lane + 1], surf.shape[1:])
+
+
+def morton_place(box):
+    place = jnp.zeros_like(box)
+    for b in range(LEVEL):
+        digit = box >> (3 * b)
+        place = place + ((((digit >> 2) & 1) << (2 * LEVEL + b)))
+        place = place + ((((digit >> 1) & 1) << (LEVEL + b)) + ((digit & 1) << b))
+    return place
+
+
+def points_kernel(n_top, box_cap, me_ref, got, *refs):
+    leaves = refs[:n_top]
+    column, oper, out, field, place, offsets, buf, surf = refs[n_top:]
     sources, _, cap = got.shape
-    lanes = min(cap, LANE)
+    own = field.shape[1]
     wide = up(cap, LANE)
-    me = me_ref[0]
+    flip = me_ref[1] * (own // n_top)
     buf[...] = jnp.zeros_like(buf)
     fill_surface(surf, column)
 
-    def place(s, offset):
-        value = got[s, 0:8]
-        count = jnp.sum(value[4:5]).astype(jnp.int32)
-        value = jnp.concatenate([value, jnp.zeros((8, wide + LANE - cap), f32)], axis=1)
-        tile = offset // LANE
-        value = pltpu.roll(value, offset - tile * LANE, 1)
-        place_at = pl.ds(pl.multiple_of(tile * LANE, LANE), wide + LANE)
-        buf[:, place_at] = buf[:, place_at] + value
-        return offset + count
-
-    lax.fori_loop(0, sources, place, jnp.int32(0), unroll=4)
+    def put(i, offset):
+        values = [got[i * STRIP + s] for s in range(STRIP)]
+        counts = [jnp.sum(v[4:5]).astype(jnp.int32) for v in values]
+        for s, (value, count) in enumerate(zip(values, counts)):
+            offsets[i * STRIP + s] = offset
+            value = jnp.concatenate([value, jnp.zeros((8, wide + LANE - cap), f32)], axis=1)
+            tile = offset // LANE
+            value = pltpu.roll(value, offset - tile * LANE, 1)
+            at = pl.ds(pl.multiple_of(tile * LANE, LANE), wide + LANE)
+            buf[:, at] = buf[:, at] + value
+            offset = offset + count
+        return offset
+
+    lax.fori_loop(0, sources // STRIP, put, jnp.int32(0))
+    leaf = jnp.concatenate([v[...] for v in leaves], axis=0)
+    low = jnp.min(jnp.min(leaf.astype(f32), axis=1, keepdims=True), axis=0, keepdims=True)
+    first = low.astype(jnp.int32) >> 3
+    table = jnp.concatenate([(leaf >> 3) - first, leaf & 7], axis=1).astype(f32)
+    table = jnp.transpose(table).astype(bf16)
     out_rows = out.shape[1]
-    firsts = []
-    at = lax.broadcasted_iota(jnp.int32, (1, box_cap), 1)
-    for m in range(sources // n_top):
-        leaf = got[(me ^ m) * n_top, 8:9, 0:1].astype(jnp.int32)
-        firsts.append((leaf >> 3) + at)
-    ids[...] = jnp.concatenate(firsts, axis=1)
-    leaf = got[pl.ds(me * n_top, n_top), 8:, 0:lanes].reshape(own // lanes, lanes)
-    leaf = leaf.astype(jnp.int32)
-    first = got[me * n_top, 8:9, 0:1].astype(jnp.int32) >> 3
-    boxes = ((leaf >> 3) - first).astype(f32).astype(bf16)
-    octants = (leaf & 7).astype(f32).astype(bf16)
 
     def block(j, total):
-        value = buf[:, pl.ds(pl.multiple_of(j * PB, PB), PB)]
-        box, octant = look_up(value[3:4].astype(jnp.int32), boxes, octants)
-        high, low = split(octant_product(value[0:3], octant, surf, oper))
+        to = pl.ds(pl.multiple_of(j * PB, PB), PB)
+        value = buf[:, to]
+        box, octant = look_up(value[3:4].astype(jnp.int32) ^ flip, table)
+        place[:, to] = morton_place(first + box.astype(jnp.int32))
+        both = octant_product(value[0:3], octant, surf, oper)
+        field[:, to] = both[COEF : 2 * COEF]
+        high, low = split(both[0:COEF])
         rows = []
         at = lax.broadcasted_iota(jnp.int32, (box_cap, PB), 0).astype(f32)
         for k in range(out_rows // box_cap):
@@ -442,48 +486,29 @@
         both = dot(jnp.concatenate([high, low], axis=0), a_high, NT)
         return total + both[0:COEF] + both[COEF : 2 * COEF] + dot(high, a_low, NT)
 
-    total = lax.fori_loop(0, own // PB, block, jnp.zeros((COEF, out_rows), f32))
-    out[...] = total.astype(bf16)
-
-
-def morton_place(box):
-    place = jnp.zeros_like(box)
-    for b in range(LEVEL):
-        digit = box >> (3 * b)
-        place = place + ((((digit >> 2) & 1) << (2 * LEVEL + b)))
-        place = place + ((((digit >> 1) & 1) << (LEVEL + b)) + ((digit & 1) << b))
-    return place
-
-
-def target_kernel(n_top, got, *refs):
-    shared = refs[:n_top]
-    column, oper, field, place, surf = refs[n_top:]
-    fill_surface(surf, column)
-    lanes = min(got.shape[2], LANE)
-    leaf = got[:, 8:, 0:lanes].reshape(-1, lanes).astype(jnp.int32)
-    boxes = (leaf >> 6).astype(f32).astype(bf16)
-    rest = (leaf & 63).astype(f32).astype(bf16)
-    points = shared[0].shape[1]
-    for m in range(n_top):
-        source = shared[m]
-
-        @pl.loop(0, points // PB)
-        def _(j):
-            at = pl.ds(pl.multiple_of(j * PB, PB), PB)
-            value = source[:, at]
-            high, low = look_up(value[3:4].astype(jnp.int32), boxes, rest)
-            leaf = (high * 64.0 + low).astype(jnp.int32)
-            to = pl.ds(pl.multiple_of(m * points + j * PB, PB), PB)
-            field[:, to] = octant_product(value[0:3], leaf & 7, surf, oper)
-            place[:, to] = morton_place(leaf >> 3)
+    total = lax.fori_loop(0, own // PB, block, jnp.zeros((COEF, out_rows), f32), unroll=2)
+    digits = jnp.concatenate([first >> 3, first & 7], axis=0).astype(f32)
+    digits = jnp.broadcast_to(digits, (2, out_rows))
+    blank = jnp.zeros((out.shape[0] - COEF - 2, out_rows), f32)
+    out[...] = jnp.concatenate([total, digits, blank], axis=0).astype(bf16)
+
+
+def box_ids(parts, dens):
+    ids = []
+    for part in parts:
+        digits = part[COEF : COEF + 8, 0:1].astype(f32).astype(jnp.int32)
+        first = digits[0:1] * 8 + digits[1:2]
+        at = lax.broadcasted_iota(jnp.int32, (1, part.shape[1] // dens), 1)
+        ids.append(first + at)
+    return jnp.concatenate(ids, axis=1)
 
 
 def all_parts(parts, k, dens):
     width = parts[0].shape[1] // dens
-    return jnp.concatenate([p[:, k * width : (k + 1) * width] for p in parts], axis=1)
-
-
-def translate_kernel(slabs, dens, me_ref, ids, *refs):
+    return jnp.concatenate([p[0:COEF, k * width : (k + 1) * width] for p in parts], axis=1)
+
+
+def translate_kernel(slabs, dens, me_ref, *refs):
     parts = refs[:-11]
     oa, ob, oc, out, xs, xin, acc, ma, mb, mc, sem = refs[-11:]
     copies = []
@@ -492,9 +517,10 @@
             copies.append(pltpu.make_async_copy(src.at[j], dst.at[j], sem.at[i, j]))
             copies[-1].start()
     x0 = (me_ref[0] // 2 * 2) * SIDE // len(parts)
-    place = morton_place(ids[...])
+    ids = box_ids(parts, dens)
+    place = morton_place(ids)
     place = (((place >> 6) - x0 + REACH) & 7) * 64 + (place & 63)
-    place = jnp.where((ids[...] >= 0) & (ids[...] < BOXES4), place, -1)
+    place = jnp.where(ids < BOXES4, place, -1)
     at = lax.broadcasted_iota(jnp.int32, (BOXES4, ids.shape[1]), 0)
     there = jnp.where(at == place, 1.0, 0.0).astype(bf16)
     columns = dens * PLANE
@@ -548,13 +574,13 @@
         out[:, t * LANE : (t + 1) * LANE] = total.astype(out.dtype)
 
 
-def coarse_kernel(ids, *refs):
+def coarse_kernel(*refs):
     parts = refs[:-7]
     m2m_hi, m2m_lo, lat_hi, lat_lo, l2l_hi, l2l_lo, out = refs[-7:]
     dens = out.shape[0]
-    box = ids[...]
+    box = ids = box_ids(parts, dens)
     place = ((box & 7) << 6) + (box & 56) + (box >> 6)
-    place = jnp.where((box >= 0) & (box < BOXES4), place, -1)
+    place = jnp.where(box < BOXES4, place, -1)
     at = lax.broadcasted_iota(jnp.int32, (BOXES4, ids.shape[1]), 0)
     there = jnp.where(at == place, 1.0, 0.0).astype(bf16)
     level = [dot(there, all_parts(parts, k, dens), NT) for k in range(dens)]
@@ -593,11 +619,10 @@
 def evaluate_kernel(slabs, step, me_ref, *refs):
     n = SIDE // slabs
     checks = refs[: 2 * n]
-    d_hi, d_lo, lattice, field, place, out, stack = refs[2 * n :]
+    d_hi, d_lo, lattice, field, place, offsets, out, stack, found = refs[2 * n :]
     core = me_ref[0] & 1
     group = me_ref[0] // step
     dens = lattice.shape[0]
-    points = out.shape[2]
     lane = lax.broadcasted_iota(jnp.int32, (COEF, LANE), 1)
     mine = jnp.concatenate([d_hi[core], d_lo[core]], axis=0)
     other = jnp.concatenate([d_hi[1 - core], d_lo[1 - core]], axis=0)
@@ -626,13 +651,12 @@
             stack[rows, m * width : (m + 1) * width] = high.astype(f32)
             rows = pl.ds((dens + k) * CPAD, COEF)
             stack[rows, m * width : (m + 1) * width] = low.astype(f32)
+    found[:, place.shape[1] :] = jnp.zeros((8, found.shape[1] - place.shape[1]), f32)
     local = stack[...].astype(bf16)
 
     @pl.loop(0, place.shape[1] // PB)
     def _(j):
         at = pl.ds(pl.multiple_of(j * PB, PB), PB)
-        m = j // (points // PB)
-        to = pl.ds(pl.multiple_of((j - m * (points // PB)) * PB, PB), PB)
         want = place[:, at] ^ (group * (slabs * PLANE))
         there = want == lax.broadcasted_iota(jnp.int32, (BOXES4, PB), 0)
         got = dot(local, jnp.where(there, 1.0, 0.0).astype(bf16))
@@ -642,7 +666,20 @@
             value = got[k * CPAD : k * CPAD + COEF]
             value = value + got[(dens + k) * CPAD : (dens + k) * CPAD + COEF]
             rows.append(jnp.sum(value * mine, axis=0, keepdims=True))
-        out[m, :, to] = jnp.concatenate(rows, axis=0)
+        rows.append(jnp.zeros((8 - dens, PB), f32))
+        found[:, at] = jnp.concatenate(rows, axis=0)
+
+    sources, _, cap = out.shape
+    wide = up(cap, LANE) + LANE
+
+    @pl.loop(0, sources // STRIP)
+    def _(i):
+        for s in range(STRIP):
+            offset = offsets[i * STRIP + s]
+            tile = offset // LANE
+            value = found[:, pl.ds(pl.multiple_of(tile * LANE, LANE), wide)]
+            value = pltpu.roll(value, wide - (offset - tile * LANE), 1)
+            out[i * STRIP + s] = value[0:dens, 0:cap]
 
 
 def shift_by(axis, value, distance):
@@ -661,90 +698,79 @@
 ):
     n_pts = lax.axis_size("pts")
     n_top = lax.axis_size("top")
-    top = lax.axis_index("top")
-    me = lax.axis_index("pts").astype(jnp.int32).reshape(1)
+    me = jnp.stack([lax.axis_index("pts"), lax.axis_index("top")]).astype(jnp.int32)
     points = local_pos.shape[1]
     own = points * n_top
     cap = 2 * points // n_pts
-    lanes = min(cap, LANE)
     box_cap = 2 * BOXES4 // n_pts
     dens = DENS // n_top
     slabs = max(1, 2 * SIDE // n_pts)
     coef = uc2e.shape[0]
+    sources = n_pts * n_top
 
     def shape(*dims, dtype=bf16):
         return jax.ShapeDtypeStruct(dims, dtype)
 
-    rows = 8 + points // lanes
-    outgoing, shared = call(
+    outgoing, entries = call(
         functools.partial(route_kernel, own, cap, n_top),
-        (shape(n_pts, n_top, rows, cap, dtype=f32), shape(4, points, dtype=f32)),
-        32,
+        (shape(n_pts, n_top, 8, cap, dtype=f32), shape(1, points, dtype=jnp.int32)),
+        GRANT,
         1 << 27,
-        in_specs=[VMEM] * 4,
-        out_specs=(VMEM, VMEM),
-    )(
-        local_pos,
-        densities,
-        morton_slot.reshape(1, points),
-        slot_leaf.reshape(points // lanes, lanes),
-    )
-    outgoing = outgoing.reshape(n_pts * n_top, rows, cap)
+        in_specs=[WHOLE] * 3,
+        out_specs=(WHOLE, WHOLE),
+    )(local_pos, densities, morton_slot.reshape(1, points))
+    outgoing = outgoing.reshape(sources, 8, cap)
     incoming = lax.all_to_all(outgoing, ("pts", "top"), split_axis=0, concat_axis=0, tiled=True)
 
-    shared = [shift_by("top", shared, m) if m else shared for m in range(n_top)]
+    leaf = slot_leaf.reshape(points // LANE, LANE)
+    leaves = [shift_by("top", leaf, m) if m else leaf for m in range(n_top)]
     flat = (-1, LANE)
-    two = 2 * coef
+    column = jnp.asarray(column_table())
     square_shape = shape(8, coef, coef)
-    w_up, w_down, *coarse_ops = call(
+    w_both, *coarse_ops = call(
         operators_kernel,
-        (shape(two, 8 * CPAD), shape(two, 8 * CPAD))
+        (shape(2 * coef, 8 * CPAD),)
         + (square_shape,) * 4
         + (shape(coef, coef),) * 2
         + (shape(2, coef, ROWS),) * 2,
-        32,
+        GRANT,
         1 << 30,
-        in_specs=[VMEM] * 5,
-        out_specs=(VMEM,) * 10,
+        in_specs=[WHOLE] * 6,
+        out_specs=(WHOLE,) * 9,
         scratch_shapes=[pltpu.VMEM((2, 8 * coef, LANE), f32)],
-    )(m2m.reshape(flat), l2l.reshape(flat), uc2e, dc2e, lattice)
+    )(m2m.reshape(flat), l2l.reshape(flat), uc2e, dc2e, lattice, column)
     coarse_ops, halves = coarse_ops[:6], coarse_ops[6:]
     m2m_hi, m2m_lo, l2l_hi, l2l_lo, lat_hi, lat_lo = coarse_ops
     oa, ob, oc = relayout(m2l_ops, me)
-    column = jnp.asarray(
-        np.pad((np.float32(1.25) * surface_table()).T, ((0, 0), (0, LANE - 3)))
-    )
-
-    surf = pltpu.VMEM((3, coef, PB), f32)
-    partial, ids = call(
-        functools.partial(upward_kernel, n_top, own, box_cap),
-        (shape(coef, dens * box_cap), shape(1, n_pts * box_cap, dtype=jnp.int32)),
-        32,
+    incoming, oa, ob, oc = lax.optimization_barrier((incoming, oa, ob, oc))
+
+    partial, field, place, offsets = call(
+        functools.partial(points_kernel, n_top, box_cap),
+        (
+            shape(up(coef + 2, 16), dens * box_cap),
+            shape(coef, own, dtype=f32),
+            shape(1, own, dtype=jnp.int32),
+            shape(sources, dtype=jnp.int32),
+        ),
+        GRANT,
         8 << 30,
-        in_specs=[SMEM] + [VMEM] * 3,
-        out_specs=(VMEM, VMEM),
-        scratch_shapes=[pltpu.VMEM((8, up(own + up(cap, LANE) + LANE, PB)), f32), surf],
-    )(me, incoming, column, w_up)
+        in_specs=[SMEM] + [WHOLE] * (n_top + 3),
+        out_specs=(WHOLE, WHOLE, WHOLE, SMEM),
+        scratch_shapes=[
+            pltpu.VMEM((8, up(own + up(cap, LANE) + LANE, PB)), f32),
+            pltpu.VMEM((3 + FEATURES, coef, PB), f32),
+        ],
+    )(me, incoming, *leaves, column, w_both)
     parts = gather_by(partial, range(n_pts))
-
-    field, place = call(
-        functools.partial(target_kernel, n_top),
-        (shape(coef, own, dtype=f32), shape(1, own, dtype=jnp.int32)),
-        32,
-        6 << 30,
-        in_specs=[VMEM] * (n_top + 3),
-        out_specs=(VMEM, VMEM),
-        scratch_shapes=[surf],
-    )(incoming, *shared, column, w_down)
 
     columns = dens * PLANE
     checks = call(
         functools.partial(translate_kernel, slabs, dens),
         shape(ROWS, slabs * columns),
-        56,
+        GRANT,
         8 << 30,
-        in_specs=[SMEM] + [VMEM] * (1 + n_pts) + [ANY] * 3,
-        out_specs=VMEM,
+        in_specs=[SMEM] + [WHOLE] * n_pts + [ANY] * 3,
+        out_specs=WHOLE,
         scratch_shapes=[
             pltpu.VMEM(((7 + slabs - 1) * columns, WFULL), bf16),
             pltpu.VMEM(((7 + slabs - 1) * columns, WIN), bf16),
@@ -754,34 +780,40 @@
             pltpu.VMEM(oc.shape, bf16),
             pltpu.SemaphoreType.DMA((3, 7)),
         ],
-    )(me, ids, *parts, oa, ob, oc)
+    )(me, *parts, oa, ob, oc)
     step = n_pts // SIDE * slabs
     gathered = gather_by(checks, [step * m + c for m in range(SIDE // slabs) for c in range(2)])
 
     lattice4 = call(
         coarse_kernel,
         shape(dens, coef, BOXES4, dtype=f32),
-        32,
+        GRANT,
         4 << 30,
-        in_specs=[VMEM] * (n_pts + 7),
-        out_specs=VMEM,
-    )(ids, *parts, m2m_hi, m2m_lo, lat_hi, lat_lo, l2l_hi, l2l_lo)
+        in_specs=[WHOLE] * (n_pts + 6),
+        out_specs=WHOLE,
+    )(*parts, m2m_hi, m2m_lo, lat_hi, lat_lo, l2l_hi, l2l_lo)
 
     reply = call(
         functools.partial(evaluate_kernel, slabs, step),
-        shape(n_top, dens, points, dtype=f32),
-        32,
+        shape(sources, dens, cap, dtype=f32),
+        GRANT,
         4 << 30,
-        in_specs=[SMEM] + [VMEM] * (len(gathered) + 5),
-        out_specs=VMEM,
-        scratch_shapes=[pltpu.VMEM((2 * dens * CPAD, BOXES4), f32)],
-    )(me, *gathered, *halves, lattice4, field, place)
-    answers = [shift_by("top", reply[m], m) if m else reply[m] for m in range(n_top)]
-    order = jnp.arange(n_top, dtype=jnp.int32) ^ top
-    picked = sum(
-        jnp.where(order[:, None, None] == m, answers[m][None], 0.0) for m in range(n_top)
-    )
-    return picked.reshape(DENS, points)
+        in_specs=[SMEM] + [WHOLE] * (len(gathered) + 5) + [SMEM],
+        out_specs=WHOLE,
+        scratch_shapes=[
+            pltpu.VMEM((2 * dens * CPAD, BOXES4), f32),
+            pltpu.VMEM((8, own + up(cap, LANE) + LANE), f32),
+        ],
+    )(me, *gathered, *halves, lattice4, field, place, offsets)
+    returned = lax.all_to_all(reply, ("pts", "top"), split_axis=0, concat_axis=0, tiled=True)
+    return call(
+        restore_kernel,
+        shape(DENS, points, dtype=f32),
+        GRANT,
+        1 << 28,
+        in_specs=[WHOLE] * 2,
+        out_specs=WHOLE,
+    )(returned, entries)
 
 
 def solution(mesh):

time: 118 us -> 109 us (0.924)
  blocking collectives: 0 us -> 12.6 us
  local copies, waits for them, and re-layouts: 12.3 us -> 2 us
  starting transfers between devices: 24.9 us -> 18.9 us
  Pallas kernels: 71.6 us -> 65.7 us
  waiting for transfers between devices: 7.14 us -> 8.93 us
    all_to_all x0 -> x1, blocking collectives: none -> 12.6 us  [per_device(): lax.all_to_all(reply, ('pts', 'top'), split_axis=0, concat_axis=0, tiled=...]
    unnamed x70 -> x36, local copies, waits for them, and re-layouts: 11.6 us -> 2 us
    pallas_call x5, Pallas kernels: 45.5 us -> 38.2 us  [the longest x1 12.4 us: per_device(): call(functools.partial(points_kernel, n_top, box_cap), (shape(up(coef + 2...]
    ppermute x20 -> x17, starting transfers between devices: 17.6 us -> 11.6 us  [shift_by(): return lax.ppermute(value, axis, [(i, i ^ distance) for i in range(size)])]
    ppermute x20 -> x17, waiting for transfers between devices: 3.09 us -> 8.93 us  [shift_by(): return lax.ppermute(value, axis, [(i, i ^ distance) for i in range(size)])]
    all_to_all x1, waiting for transfers between devices: 4.05 us -> 0.01 us  [per_device(): lax.all_to_all(outgoing, ('pts', 'top'), split_axis=0, concat_axis=0, til...]
  transfers between devices with their start and end apart: 21 -> 18, of which waited for: 5 -> 8; matrix products, arithmetic and copies ran while one was open for 1% -> 1% of each run, Pallas kernels for 38% -> 27%
where the time goes in v3:
time: 109 us
  Pallas kernels  65.7 us (60%)
  starting transfers between devices  18.9 us (17%)
  blocking collectives  12.6 us (12%)
  waiting for transfers between devices  8.93 us (8%)
  local copies, waits for them, and re-layouts  2 us (2%)
    pallas_call x1, Pallas kernels, relayout(): call(functools.partial(relayout_kernel, nrows), tuple((jax.ShapeDtypeStru...  15.3 us
    all_to_all x1, blocking collectives, per_device(): lax.all_to_all(reply, ('pts', 'top'), split_axis=0, concat_axis=0, tiled=...  12.6 us
    pallas_call x1, Pallas kernels, per_device(): call(functools.partial(points_kernel, n_top, box_cap), (shape(up(coef + 2...  12.4 us
    ppermute x17, starting transfers between devices, shift_by(): return lax.ppermute(value, axis, [(i, i ^ distance) for i in range(size)])  11.6 us
    pallas_call x1, Pallas kernels, per_device(): call(functools.partial(evaluate_kernel, slabs, step), shape(sources, dens...  9.15 us
    pallas_call x1, Pallas kernels, per_device(): call(functools.partial(translate_kernel, slabs, dens), shape(ROWS, slabs...  9.07 us
    ppermute x17, waiting for transfers between devices, shift_by(): return lax.ppermute(value, axis, [(i, i ^ distance) for i in range(size)])  8.93 us
    pallas_call x1, Pallas kernels, per_device(): call(coarse_kernel, shape(dens, coef, BOXES4, dtype=f32), GRANT, 4 << 30,...  8.29 us
  transfers between devices with their start and end apart: 18, of which 8 were waited for; matrix products, arithmetic and copies ran while one was open for 1% of the time, Pallas kernels for 27%

profile of v3, /device:TPU:0, one launch (start us, length us, event | category | flops | bytes accessed | tf_op | source)
XLA Modules:
  0.0 108.9 jit_solution(15862377677720577527)
XLA Ops:
  0.0 3.1 %shard_map.109 = (f32[8,4,8,256]{3,2,1,0:T(8,128)}, s32[1,1024]{1,0:T(1,128)}) custom-call(f32[3,1024]{1,0:T(4,128)} %pos.1, f32[8,1024]{1,0:T(8,128)} %dens.1, s32[1,1024]{1,0:T(1,128)} %bitcast.13), custom_call_target="tpu_custom_call" | custom-call | flops 134217728 | bytes 1048576 | tf_op jit(solution)/shard_map/pallas_call | solution.py:714
  3.1 7.3 %all-to-all-start = ((f32[32,8,256]{2,1,0:T(8,128)}), f32[32,8,256]{2,1,0:T(8,128)S(1)}, u32[]{:S(2)}, u32[]{:S(2)}) async-start(f32[32,8,256]{2,1,0:T(8,128)} %bitcast.10), calls=%async_computation | async-start | bytes 524288 | tf_op jit(solution)/shard_map/all_to_all | solution.py:723
  10.4 3.7 %collective-permute-start.2 = (s32[8,128]{1,0:T(8,128)}, s32[8,128]{1,0:T(8,128)S(1)}, u32[]{:S(2)}, u32[]{:S(2)}) collective-permute-start(s32[8,128]{1,0:T(8,128)} %bitcast.14), channel_id=1, source_target_pairs={{0,3},{1,2},{2,1},{3,0},{4,7},{5,6},{6,5},{7,4},{8,11},{9,10},{10,... | collective-permute-start | bytes 12296 | tf_op jit(solution)/shard_map/ppermute | solution.py:687
  14.1 0.8 collective-permute-start
  14.9 0.6 pad_add_fusion.me_ref
  15.5 6.2 %shard_map.111 = (bf16[304,1280]{1,0:T(8,128)(2,1)}, bf16[8,152,152]{2,1,0:T(8,128)(2,1)}, bf16[8,152,152]{2,1,0:T(8,128)(2,1)}, bf16[8,152,152]{2,1,0:T(8,128)(...) custom-call(f32[1444,128]{1,0:T(8,128)} %bitcast.11, ...), custom_call_target="tpu_custom_call" | custom-call | flops 1073741824 | bytes 1048576 | tf_op jit(solution)/shard_map/pallas_call | solution.py:730
  21.6 15.3 %shard_map.110 = (bf16[7,4,80,1152]{3,2,1,0:T(8,128)(2,1)}, bf16[4,3,80,1152]{3,2,1,0:T(8,128)(2,1)}, bf16[3,3,80,640]{3,2,1,0:T(8,128)(2,1)}) custom-call(s32[2]{0:T(128)} %pad_add_fusion.me_ref, bf16[57038,128]{1,0:T(8,128)(2,1)} %bitcast.8, bf16[57038,128]{1,0:T(8,128)(2,1)} %bitcast.9), custom_call_target="tpu_custom_call" | custom-call | flops 1048576 | bytes 16777216 | tf_op jit(solution)/shard_map/pallas_call | solution.py:232
  37.0 0.6 copy-done
  37.7 12.4 %shard_map.112 = (bf16[160,256]{1,0:T(8,128)(2,1)}, f32[152,4096]{1,0:T(8,128)}, s32[1,4096]{1,0:T(1,128)}, s32[32]{0:T(128)}) custom-call(s32[2]{0:T(128)} %pad_add_fusion.me_ref, f32[32,8,256]{2,1,0:T(8,128)} %copy-done, s32[8,128]{1,0:T(8,128)} %bitcast.17, s32[8,128]{1,0:T(8,128)} %copy-done.17, s32[8,128]{1,0:T(8,128)} %copy-done.16, ...), custom_call_target="tpu_custom_call" | custom-call | flops 8589934592 | bytes 1048576 | tf_op jit(solution)/shard_map/pallas_call | solution.py:747
  50.1 2.7 %collective-permute-start.8 = (bf16[160,256]{1,0:T(8,128)(2,1)}, bf16[160,256]{1,0:T(8,128)(2,1)S(1)}, u32[]{:S(2)}, u32[]{:S(2)}) collective-permute-start(bf16[160,256]{1,0:T(8,128)(2,1)} %get-tuple-element.33.refs_0_), channel_id=1, source_target_pairs={{0,24},{4,28},{8,16},{12,20},{16,8},{20,12},{24,0},{28,4},{1,25},{... | collective-permute-start | bytes 245768 | tf_op jit(solution)/shard_map/ppermute | solution.py:687
  52.9 0.6 collective-permute-start.6
  53.4 0.3 collective-permute-start.4
  53.7 2.2 %collective-permute-done.8.refs_6_ = bf16[160,256]{1,0:T(8,128)(2,1)S(1)} collective-permute-done((bf16[160,256]{1,0:T(8,128)(2,1)}, bf16[160,256]{1,0:T(8,128)(2,1)S(1)}, u32[]{:S(2)}, u32[]{:S(2)}) %collective-permute-start.8) | collective-permute-done | bytes 81952 | tf_op jit(solution)/shard_map/ppermute | solution.py:687
  55.9 1.7 %collective-permute-done.6.refs_4_ = bf16[160,256]{1,0:T(8,128)(2,1)S(1)} collective-permute-done((bf16[160,256]{1,0:T(8,128)(2,1)}, bf16[160,256]{1,0:T(8,128)(2,1)S(1)}, u32[]{:S(2)}, u32[]{:S(2)}) %collective-permute-start.6) | collective-permute-done | bytes 81952 | tf_op jit(solution)/shard_map/ppermute | solution.py:687
  57.5 0.6 collective-permute-done.4.refs_2_
  58.1 0.7 collective-permute-done.7.refs_5_
  58.8 0.6 collective-permute-done.5.refs_3_
  59.4 0.0 copy-done.6
  59.4 0.6 copy-done.7
  60.1 9.1 %shard_map.113.refs_0_ = bf16[80,256]{1,0:T(8,128)(2,1)} custom-call(s32[2]{0:T(128)} %pad_add_fusion.me_ref, bf16[160,256]{1,0:T(8,128)(2,1)} %get-tuple-element.33.refs_0_, bf16[160,256]{1,0:T(8,128)(2,1)} %copy-done.4, bf16[160,256]{1,0:T(8,128)(2,1)} %copy-done.3, bf16[160,256]{1,0:T(8,128)(2,1)} %copy-done.7, bf16[160,256]{1,0:T(8,128)(2,1)} %copy-done.2, ...), custom_call_target="tpu_custom_call" | custom-call | flops 8589934592 | bytes 1048576 | tf_op jit(solution)/shard_map/pallas_call | solution.py:767
  69.2 1.5 %collective-permute-start.15 = (bf16[80,256]{1,0:T(8,128)(2,1)}, bf16[80,256]{1,0:T(8,128)(2,1)S(1)}, u32[]{:S(2)}, u32[]{:S(2)}) collective-permute-start(bf16[80,256]{1,0:T(8,128)(2,1)} %shard_map.113.refs_0_), channel_id=1, source_target_pairs={{0,24},{4,28},{8,16},{12,20},{16,8},{20,12},{24,0},{28,4},{1,25},{... | collective-permute-start | bytes 122888 | tf_op jit(solution)/shard_map/ppermute | solution.py:687
  70.7 1.2 %collective-permute-start.13 = (bf16[80,256]{1,0:T(8,128)(2,1)}, bf16[80,256]{1,0:T(8,128)(2,1)S(1)}, u32[]{:S(2)}, u32[]{:S(2)}) collective-permute-start(bf16[80,256]{1,0:T(8,128)(2,1)} %shard_map.113.refs_0_), channel_id=1, source_target_pairs={{0,16},{4,20},{8,24},{12,28},{16,0},{20,4},{24,8},{28,12},{1,17},{... | collective-permute-start | bytes 122888 | tf_op jit(solution)/shard_map/ppermute | solution.py:687
  71.8 0.9 collective-permute-start.11
  72.7 1.7 %collective-permute-done.15.refs_6_ = bf16[80,256]{1,0:T(8,128)(2,1)S(1)} collective-permute-done((bf16[80,256]{1,0:T(8,128)(2,1)}, bf16[80,256]{1,0:T(8,128)(2,1)S(1)}, u32[]{:S(2)}, u32[]{:S(2)}) %collective-permute-start.15) | collective-permute-done | bytes 40992 | tf_op jit(solution)/shard_map/ppermute | solution.py:687
  74.4 0.5 collective-permute-done.13.refs_4_
  74.9 1.1 %collective-permute-done.11.refs_2_ = bf16[80,256]{1,0:T(8,128)(2,1)S(1)} collective-permute-done((bf16[80,256]{1,0:T(8,128)(2,1)}, bf16[80,256]{1,0:T(8,128)(2,1)S(1)}, u32[]{:S(2)}, u32[]{:S(2)}) %collective-permute-start.11) | collective-permute-done | bytes 40992 | tf_op jit(solution)/shard_map/ppermute | solution.py:687
  76.1 8.3 %shard_map.114.refs_10_ = f32[2,152,512]{2,1,0:T(8,128)} custom-call(bf16[160,256]{1,0:T(8,128)(2,1)} %get-tuple-element.33.refs_0_, bf16[160,256]{1,0:T(8,128)(2,1)} %copy-done.4, bf16[160,256]{1,0:T(8,128)(2,1)} %copy-done.3, bf16[160,256]{1,0:T(8,128)(2,1)} %copy-done.7, bf16[160,256]{1,0:T(8,128)(2,1)} %copy-done.2, bf16[160,256]{1,0:T(8,128)(2,1)} %copy-done.6, ...), custom_call_target="tpu_custom_call" | custom-call | flops 4294967296 | bytes 1048576 | tf_op jit(solution)/shard_map/pallas_call | solution.py:787
  84.5 0.5 copy-done.11
  85.0 0.0 copy-done.12
  85.1 9.2 %shard_map.115 = f32[32,2,256]{2,1,0:T(2,128)} custom-call(s32[2]{0:T(128)} %pad_add_fusion.me_ref, bf16[80,256]{1,0:T(8,128)(2,1)} %shard_map.113.refs_0_, bf16[80,256]{1,0:T(8,128)(2,1)} %copy-done.11, bf16[80,256]{1,0:T(8,128)(2,1)} %copy-done.10, bf16[80,256]{1,0:T(8,128)(2,1)} %copy-done.14, bf16[80,256]{1,0:T(8,128)(2,1)} %copy-done.9, ...), custom_call_target="tpu_custom_call" | custom-call | flops 4294967296 | bytes 1048576 | tf_op jit(solution)/shard_map/pallas_call | solution.py:796
  94.2 12.6 %all_to_all.10.got = f32[32,2,256]{2,1,0:T(2,128)} all-to-all(f32[32,2,256]{2,1,0:T(2,128)} %shard_map.115), channel_id=1, replica_groups=mesh['pts'=8,'top'=4] {'pts','top'}, dimensions={0} | all-to-all | bytes 131072 | tf_op jit(solution)/shard_map/all_to_all | solution.py:808
  106.8 2.1 %shard_map.116 = f32[8,1024]{1,0:T(8,128)} custom-call(f32[32,2,256]{2,1,0:T(2,128)} %all_to_all.10.got, s32[1,1024]{1,0:T(1,128)} %get-tuple-element.48.entries), custom_call_target="tpu_custom_call" | custom-call | flops 268435456 | bytes 1048576 | tf_op jit(solution)/shard_map/pallas_call | solution.py:809
  (50 shorter events, 0.2 us)
Async XLA Ops:
  3.1 33.9 %all-to-all-start = ((f32[32,8,256]{2,1,0:T(8,128)}), f32[32,8,256]{2,1,0:T(8,128)S(1)}, u32[]{:S(2)}, u32[]{:S(2)}) async-start(f32[32,8,256]{2,1,0:T(8,128)} %bitcast.10), calls=%async_computation | async-start | bytes 524288 | tf_op jit(solution)/shard_map/all_to_all | solution.py:723
  10.4 26.6 %collective-permute-start.2 = (s32[8,128]{1,0:T(8,128)}, s32[8,128]{1,0:T(8,128)S(1)}, u32[]{:S(2)}, u32[]{:S(2)}) collective-permute-start(s32[8,128]{1,0:T(8,128)} %bitcast.14), channel_id=1, source_target_pairs={{0,3},{1,2},{2,1},{3,0},{4,7},{5,6},{6,5},{7,4},{8,11},{9,10},{10,... | collective-permute-start | bytes 12296 | tf_op jit(solution)/shard_map/ppermute | solution.py:687
  14.1 22.9 %collective-permute-start.1 = (s32[8,128]{1,0:T(8,128)}, s32[8,128]{1,0:T(8,128)S(1)}, u32[]{:S(2)}, u32[]{:S(2)}) collective-permute-start(s32[8,128]{1,0:T(8,128)} %bitcast.15), channel_id=1, source_target_pairs={{0,2},{1,3},{2,0},{3,1},{4,6},{5,7},{6,4},{7,5},{8,10},{9,11},{10,... | collective-permute-start | bytes 12296 | tf_op jit(solution)/shard_map/ppermute | solution.py:687
  14.1 22.9 %collective-permute-start = (s32[8,128]{1,0:T(8,128)}, s32[8,128]{1,0:T(8,128)S(1)}, u32[]{:S(2)}, u32[]{:S(2)}) collective-permute-start(s32[8,128]{1,0:T(8,128)} %bitcast.16), channel_id=1, source_target_pairs={{0,1},{1,0},{2,3},{3,2},{4,5},{5,4},{6,7},{7,6},{8,9},{9,8},{10,11... | collective-permute-start | bytes 12296 | tf_op jit(solution)/shard_map/ppermute | solution.py:687
  37.0 0.7 copy-start
  37.0 0.7 copy-start.15
  37.0 0.7 copy-start.16
  37.0 0.7 copy-start.17
  50.1 5.7 %collective-permute-start.8 = (bf16[160,256]{1,0:T(8,128)(2,1)}, bf16[160,256]{1,0:T(8,128)(2,1)S(1)}, u32[]{:S(2)}, u32[]{:S(2)}) collective-permute-start(bf16[160,256]{1,0:T(8,128)(2,1)} %get-tuple-element.33.refs_0_), channel_id=1, source_target_pairs={{0,24},{4,28},{8,16},{12,20},{16,8},{20,12},{24,0},{28,4},{1,25},{... | collective-permute-start | bytes 245768 | tf_op jit(solution)/shard_map/ppermute | solution.py:687
  52.9 4.7 %collective-permute-start.6 = (bf16[160,256]{1,0:T(8,128)(2,1)}, bf16[160,256]{1,0:T(8,128)(2,1)S(1)}, u32[]{:S(2)}, u32[]{:S(2)}) collective-permute-start(bf16[160,256]{1,0:T(8,128)(2,1)} %get-tuple-element.33.refs_0_), channel_id=1, source_target_pairs={{0,16},{4,20},{8,24},{12,28},{16,0},{20,4},{24,8},{28,12},{1,17},{... | collective-permute-start | bytes 245768 | tf_op jit(solution)/shard_map/ppermute | solution.py:687
  53.4 4.7 %collective-permute-start.4 = (bf16[160,256]{1,0:T(8,128)(2,1)}, bf16[160,256]{1,0:T(8,128)(2,1)S(1)}, u32[]{:S(2)}, u32[]{:S(2)}) collective-permute-start(bf16[160,256]{1,0:T(8,128)(2,1)} %get-tuple-element.33.refs_0_), channel_id=1, source_target_pairs={{0,8},{4,12},{8,0},{12,4},{16,24},{20,28},{24,16},{28,20},{1,9},{5... | collective-permute-start | bytes 245768 | tf_op jit(solution)/shard_map/ppermute | solution.py:687
  53.7 4.4 %collective-permute-start.3 = (bf16[160,256]{1,0:T(8,128)(2,1)}, bf16[160,256]{1,0:T(8,128)(2,1)S(1)}, u32[]{:S(2)}, u32[]{:S(2)}) collective-permute-start(bf16[160,256]{1,0:T(8,128)(2,1)} %get-tuple-element.33.refs_0_), channel_id=1, source_target_pairs={{0,4},{4,0},{8,12},{12,8},{16,20},{20,16},{24,28},{28,24},{1,5},{5... | collective-permute-start | bytes 245768 | tf_op jit(solution)/shard_map/ppermute | solution.py:687
  55.9 3.5 %copy-start.1 = (bf16[160,256]{1,0:T(8,128)(2,1)}, bf16[160,256]{1,0:T(8,128)(2,1)S(1)}, u32[]{:S(2)}) copy-start(bf16[160,256]{1,0:T(8,128)(2,1)S(1)} %collective-permute-done.8.refs_6_) | copy-start | bytes 245764
  55.9 2.2 %collective-permute-start.9 = (bf16[160,256]{1,0:T(8,128)(2,1)S(1)}, bf16[160,256]{1,0:T(8,128)(2,1)S(1)}, u32[]{:S(2)}, u32[]{:S(2)}) collective-permute-start(bf16[160,256]{1,0:T(8,128)(2,1)S(1)} %collective-permute-done.8.refs_6_), channel_id=1, source_target_pairs={{0,4},{4,0},{8,12},{12,8},{16,20},{20,16},{24,28},{28,24},{1,5},{5... | collective-permute-start | bytes 245768 | tf_op jit(solution)/shard_map/ppermute | solution.py:687
  57.5 1.8 %copy-start.2 = (bf16[160,256]{1,0:T(8,128)(2,1)}, bf16[160,256]{1,0:T(8,128)(2,1)S(1)}, u32[]{:S(2)}) copy-start(bf16[160,256]{1,0:T(8,128)(2,1)S(1)} %collective-permute-done.6.refs_4_) | copy-start | bytes 245764
  57.5 1.3 %collective-permute-start.7 = (bf16[160,256]{1,0:T(8,128)(2,1)S(1)}, bf16[160,256]{1,0:T(8,128)(2,1)S(1)}, u32[]{:S(2)}, u32[]{:S(2)}) collective-permute-start(bf16[160,256]{1,0:T(8,128)(2,1)S(1)} %collective-permute-done.6.refs_4_), channel_id=1, source_target_pairs={{0,4},{4,0},{8,12},{12,8},{16,20},{20,16},{24,28},{28,24},{1,5},{5... | collective-permute-start | bytes 245768 | tf_op jit(solution)/shard_map/ppermute | solution.py:687
  58.1 1.3 %copy-start.3 = (bf16[160,256]{1,0:T(8,128)(2,1)}, bf16[160,256]{1,0:T(8,128)(2,1)S(1)}, u32[]{:S(2)}) copy-start(bf16[160,256]{1,0:T(8,128)(2,1)S(1)} %collective-permute-done.4.refs_2_) | copy-start | bytes 245764
  58.1 1.3 %collective-permute-start.5 = (bf16[160,256]{1,0:T(8,128)(2,1)S(1)}, bf16[160,256]{1,0:T(8,128)(2,1)S(1)}, u32[]{:S(2)}, u32[]{:S(2)}) collective-permute-start(bf16[160,256]{1,0:T(8,128)(2,1)S(1)} %collective-permute-done.4.refs_2_), channel_id=1, source_target_pairs={{0,4},{4,0},{8,12},{12,8},{16,20},{20,16},{24,28},{28,24},{1,5},{5... | collective-permute-start | bytes 245768 | tf_op jit(solution)/shard_map/ppermute | solution.py:687
  58.1 1.3 %copy-start.4 = (bf16[160,256]{1,0:T(8,128)(2,1)}, bf16[160,256]{1,0:T(8,128)(2,1)S(1)}, u32[]{:S(2)}) copy-start(bf16[160,256]{1,0:T(8,128)(2,1)S(1)} %collective-permute-done.3.refs_1_) | copy-start | bytes 245764
  58.1 1.3 %copy-start.5 = (bf16[160,256]{1,0:T(8,128)(2,1)}, bf16[160,256]{1,0:T(8,128)(2,1)S(1)}, u32[]{:S(2)}) copy-start(bf16[160,256]{1,0:T(8,128)(2,1)S(1)} %collective-permute-done.9.refs_7_) | copy-start | bytes 245764
  58.8 0.6 copy-start.6
  59.4 0.6 copy-start.7
  69.2 5.2 %collective-permute-start.15 = (bf16[80,256]{1,0:T(8,128)(2,1)}, bf16[80,256]{1,0:T(8,128)(2,1)S(1)}, u32[]{:S(2)}, u32[]{:S(2)}) collective-permute-start(bf16[80,256]{1,0:T(8,128)(2,1)} %shard_map.113.refs_0_), channel_id=1, source_target_pairs={{0,24},{4,28},{8,16},{12,20},{16,8},{20,12},{24,0},{28,4},{1,25},{... | collective-permute-start | bytes 122888 | tf_op jit(solution)/shard_map/ppermute | solution.py:687
  70.7 4.2 %collective-permute-start.13 = (bf16[80,256]{1,0:T(8,128)(2,1)}, bf16[80,256]{1,0:T(8,128)(2,1)S(1)}, u32[]{:S(2)}, u32[]{:S(2)}) collective-permute-start(bf16[80,256]{1,0:T(8,128)(2,1)} %shard_map.113.refs_0_), channel_id=1, source_target_pairs={{0,16},{4,20},{8,24},{12,28},{16,0},{20,4},{24,8},{28,12},{1,17},{... | collective-permute-start | bytes 122888 | tf_op jit(solution)/shard_map/ppermute | solution.py:687
  71.8 4.2 %collective-permute-start.11 = (bf16[80,256]{1,0:T(8,128)(2,1)}, bf16[80,256]{1,0:T(8,128)(2,1)S(1)}, u32[]{:S(2)}, u32[]{:S(2)}) collective-permute-start(bf16[80,256]{1,0:T(8,128)(2,1)} %shard_map.113.refs_0_), channel_id=1, source_target_pairs={{0,8},{4,12},{8,0},{12,4},{16,24},{20,28},{24,16},{28,20},{1,9},{5... | collective-permute-start | bytes 122888 | tf_op jit(solution)/shard_map/ppermute | solution.py:687
  72.7 11.7 %collective-permute-start.10 = (bf16[80,256]{1,0:T(8,128)(2,1)}, bf16[80,256]{1,0:T(8,128)(2,1)S(1)}, u32[]{:S(2)}, u32[]{:S(2)}) collective-permute-start(bf16[80,256]{1,0:T(8,128)(2,1)} %shard_map.113.refs_0_), channel_id=1, source_target_pairs={{0,4},{4,0},{8,12},{12,8},{16,20},{20,16},{24,28},{28,24},{1,5},{5... | collective-permute-start | bytes 122888 | tf_op jit(solution)/shard_map/ppermute | solution.py:687
  74.4 10.0 %copy-start.8 = (bf16[80,256]{1,0:T(8,128)(2,1)}, bf16[80,256]{1,0:T(8,128)(2,1)S(1)}, u32[]{:S(2)}) copy-start(bf16[80,256]{1,0:T(8,128)(2,1)S(1)} %collective-permute-done.15.refs_6_) | copy-start | bytes 122884
  74.4 10.0 %collective-permute-start.16 = (bf16[80,256]{1,0:T(8,128)(2,1)S(1)}, bf16[80,256]{1,0:T(8,128)(2,1)S(1)}, u32[]{:S(2)}, u32[]{:S(2)}) collective-permute-start(bf16[80,256]{1,0:T(8,128)(2,1)S(1)} %collective-permute-done.15.refs_6_), channel_id=1, source_target_pairs={{0,4},{4,0},{8,12},{12,8},{16,20},{20,16},{24,28},{28,24},{1,5},{5... | collective-permute-start | bytes 122888 | tf_op jit(solution)/shard_map/ppermute | solution.py:687
  74.9 9.5 %copy-start.9 = (bf16[80,256]{1,0:T(8,128)(2,1)}, bf16[80,256]{1,0:T(8,128)(2,1)S(1)}, u32[]{:S(2)}) copy-start(bf16[80,256]{1,0:T(8,128)(2,1)S(1)} %collective-permute-done.13.refs_4_) | copy-start | bytes 122884
  74.9 9.5 %collective-permute-start.14 = (bf16[80,256]{1,0:T(8,128)(2,1)S(1)}, bf16[80,256]{1,0:T(8,128)(2,1)S(1)}, u32[]{:S(2)}, u32[]{:S(2)}) collective-permute-start(bf16[80,256]{1,0:T(8,128)(2,1)S(1)} %collective-permute-done.13.refs_4_), channel_id=1, source_target_pairs={{0,4},{4,0},{8,12},{12,8},{16,20},{20,16},{24,28},{28,24},{1,5},{5... | collective-permute-start | bytes 122888 | tf_op jit(solution)/shard_map/ppermute | solution.py:687
  76.1 8.3 %copy-start.10 = (bf16[80,256]{1,0:T(8,128)(2,1)}, bf16[80,256]{1,0:T(8,128)(2,1)S(1)}, u32[]{:S(2)}) copy-start(bf16[80,256]{1,0:T(8,128)(2,1)S(1)} %collective-permute-done.11.refs_2_) | copy-start | bytes 122884
  76.1 8.4 %collective-permute-start.12 = (bf16[80,256]{1,0:T(8,128)(2,1)S(1)}, bf16[80,256]{1,0:T(8,128)(2,1)S(1)}, u32[]{:S(2)}, u32[]{:S(2)}) collective-permute-start(bf16[80,256]{1,0:T(8,128)(2,1)S(1)} %collective-permute-done.11.refs_2_), channel_id=1, source_target_pairs={{0,4},{4,0},{8,12},{12,8},{16,20},{20,16},{24,28},{28,24},{1,5},{5... | collective-permute-start | bytes 122888 | tf_op jit(solution)/shard_map/ppermute | solution.py:687
  (4 other events, 2.5 us)

commit v4 on v3

--- a/solution.py
+++ b/solution.py
@@ -120,16 +120,18 @@
 ROWS = 16 * STEPS
 CHUNK = up(HG + 15, 16)
 TAIL = 32
+EARLY = 3
 STRIDE = 17
-
-
-def relayout_kernel(nrows, me_ref, f_hbm, tail_ref, oa, ob, oc, inb, fbuf, tbuf, tb16, sem):
+PIECES = ((4, 7, WFULL), (3, 4, WFULL), (3, 3, WIN))
+
+
+def relayout_kernel(nrows, step0, steps, me_ref, f_hbm, tail_ref, oa, ob, oc, inb, fbuf, tbuf, tb16, sem):
     step = pl.program_id(0)
     half = me_ref[0] & 1
     end16 = nrows // 16 * 16
 
     def start_row(st, g):
-        return jnp.minimum(4 * st + g, NG - 1) * (2 * HG) + half * HG
+        return jnp.minimum(4 * (st + step0) + g, NG - 1) * (2 * HG) + half * HG
 
     def start(st, slot):
         for g in range(4):
@@ -181,7 +183,7 @@
         fbuf[...] = jnp.zeros_like(fbuf)
         start(0, 0)
 
-    @pl.when(step + 1 < STEPS)
+    @pl.when(step + 1 < steps)
     def _():
         start(step + 1, 1 - slot)
 
@@ -211,10 +213,10 @@
 
     for dx, dy, d0, count in blocks():
         tile0, phase = divmod(d0 * COEF, LANE)
-        if dy in OUTER:
-            ref = oa.at[dx + REACH, OUTER.index(dy)]
-        elif dx in OUTER:
-            ref = ob.at[OUTER.index(dx), INNER.index(dy)]
+        if dx in OUTER:
+            ref = oa.at[OUTER.index(dx), (OUTER + INNER).index(dy)]
+        elif dy in OUTER:
+            ref = ob.at[INNER.index(dx), OUTER.index(dy)]
         else:
             ref = oc.at[INNER.index(dx), INNER.index(dy)]
         for t in range(up(count * COEF, LANE) // LANE):
@@ -225,19 +227,19 @@
             ref[:, t * LANE : (t + 1) * LANE] = value
 
 
-def relayout(flat, me):
+def relayout(flat, me, step0, steps):
     nrows = flat.shape[0] // LANE
     rows = flat.reshape(nrows, LANE)
-    shapes = ((7, 4, ROWS, WFULL), (4, 3, ROWS, WFULL), (3, 3, ROWS, WIN))
+    shapes = tuple((a, b, 16 * steps, c) for a, b, c in PIECES)
     return call(
-        functools.partial(relayout_kernel, nrows),
+        functools.partial(relayout_kernel, nrows, step0, steps),
         tuple(jax.ShapeDtypeStruct(s, bf16) for s in shapes),
         GRANT,
         1 << 20,
-        16 << 20,
+        steps << 21,
         grid_spec=pltpu.PrefetchScalarGridSpec(
             num_scalar_prefetch=1,
-            grid=(STEPS,),
+            grid=(steps,),
             in_specs=[ANY, pl.BlockSpec((16, LANE), lambda i, h: (nrows // 16, 0))],
             out_specs=tuple(
                 pl.BlockSpec((s[0], s[1], 16, s[3]), lambda i, h: (0, 0, i, 0)) for s in shapes
@@ -321,7 +323,7 @@
         d_lo[h] = dot(low, here).astype(bf16)
 
 
-def route_kernel(own, cap, n_top, pos, dens, slot, out, entries):
+def route_kernel(own, cap, n_top, pos, dens, slot, leaf, out, entries):
     points = pos.shape[1]
     owners = out.shape[0]
     slots = slot[...]
@@ -357,6 +359,10 @@
     payload = jnp.concatenate([high, low], axis=0).astype(bf16)
     block = max(cap, LANE)
     per = DENS // n_top
+    leaves = leaf[...].astype(f32)
+    if leaves.shape[1] < cap:
+        blank = jnp.zeros((leaves.shape[0], cap - leaves.shape[1]), f32)
+        leaves = jnp.concatenate([leaves, blank], axis=1)
     for o in range(owners * cap // block):
         there = entry == o * block + lax.broadcasted_iota(jnp.int32, (block, points), 0)
         there = jnp.where(there, 1.0, 0.0).astype(bf16)
@@ -370,12 +376,14 @@
             packed = jnp.concatenate([r for r in rows if r.shape[0]], axis=0)
             for i in range(block // cap):
                 at = o * (block // cap) + i
-                out[at, q] = packed[:, i * cap : (i + 1) * cap]
-
-
-def restore_kernel(got, entries, out):
-    devices, per, cap = got.shape
-    n_top = out.shape[0] // per
+                out[at, q, 0:8] = packed[:, i * cap : (i + 1) * cap]
+                out[at, q, 8:] = leaves
+
+
+def restore_kernel(n_top, got, entries, out):
+    devices = got.shape[0]
+    per = out.shape[0] // n_top
+    cap = got.shape[2] // per
     points = out.shape[1]
     block = max(cap, PB)
     total = jnp.zeros((2 * out.shape[0], points), f32)
@@ -383,8 +391,12 @@
         count = block // cap
         value = []
         for q in range(n_top):
-            pieces = [got[(o * count + i) * n_top + q] for i in range(count)]
-            value.append(jnp.concatenate(pieces, axis=1))
+            for k in range(per):
+                pieces = []
+                for i in range(count):
+                    row = (o * count + i) * n_top + q
+                    pieces.append(got[row, :, k * cap : (k + 1) * cap])
+                value.append(jnp.concatenate(pieces, axis=1))
         high, low = split(jnp.concatenate(value, axis=0))
         both = jnp.concatenate([high.astype(f32), low.astype(f32)], axis=0).astype(bf16)
         at = o * block + lax.broadcasted_iota(jnp.int32, (block, points), 0)
@@ -440,17 +452,19 @@
 
 
 def points_kernel(n_top, box_cap, me_ref, got, *refs):
-    leaves = refs[:n_top]
-    column, oper, out, field, place, offsets, buf, surf = refs[n_top:]
+    column, oper_hbm, out, field, place, offsets, buf, surf, oper, sem = refs
+    fetch = pltpu.make_async_copy(oper_hbm, oper, sem)
+    fetch.start()
     sources, _, cap = got.shape
+    lanes = min(cap, LANE)
     own = field.shape[1]
     wide = up(cap, LANE)
-    flip = me_ref[1] * (own // n_top)
+    me = me_ref[0]
     buf[...] = jnp.zeros_like(buf)
     fill_surface(surf, column)
 
     def put(i, offset):
-        values = [got[i * STRIP + s] for s in range(STRIP)]
+        values = [got[i * STRIP + s, 0:8] for s in range(STRIP)]
         counts = [jnp.sum(v[4:5]).astype(jnp.int32) for v in values]
         for s, (value, count) in enumerate(zip(values, counts)):
             offsets[i * STRIP + s] = offset
@@ -463,9 +477,11 @@
         return offset
 
     lax.fori_loop(0, sources // STRIP, put, jnp.int32(0))
-    leaf = jnp.concatenate([v[...] for v in leaves], axis=0)
-    low = jnp.min(jnp.min(leaf.astype(f32), axis=1, keepdims=True), axis=0, keepdims=True)
-    first = low.astype(jnp.int32) >> 3
+    leaf = got[pl.ds(me * n_top, n_top), 8:, 0:lanes].reshape(own // lanes, lanes)
+    leaf = leaf.astype(jnp.int32)
+    first = got[me * n_top, 8:9, 0:1].astype(jnp.int32) >> 3
+    offsets[sources] = jnp.sum(got[me * n_top, 8:9, 0:1]).astype(jnp.int32) >> 3
+    fetch.wait()
     table = jnp.concatenate([(leaf >> 3) - first, leaf & 7], axis=1).astype(f32)
     table = jnp.transpose(table).astype(bf16)
     out_rows = out.shape[1]
@@ -473,8 +489,8 @@
     def block(j, total):
         to = pl.ds(pl.multiple_of(j * PB, PB), PB)
         value = buf[:, to]
-        box, octant = look_up(value[3:4].astype(jnp.int32) ^ flip, table)
-        place[:, to] = morton_place(first + box.astype(jnp.int32))
+        box, octant = look_up(value[3:4].astype(jnp.int32), table)
+        place[:, to] = box.astype(jnp.int32)
         both = octant_product(value[0:3], octant, surf, oper)
         field[:, to] = both[COEF : 2 * COEF]
         high, low = split(both[0:COEF])
@@ -509,13 +525,21 @@
 
 
 def translate_kernel(slabs, dens, me_ref, *refs):
-    parts = refs[:-11]
-    oa, ob, oc, out, xs, xin, acc, ma, mb, mc, sem = refs[-11:]
+    parts = refs[:-14]
+    pieces = refs[-14:-8]
+    out, xs, xin, acc, ma, mb, mc, sem = refs[-8:]
     copies = []
-    for i, (src, dst) in enumerate(((oa, ma), (ob, mb), (oc, mc))):
-        for j in range(src.shape[0]):
-            copies.append(pltpu.make_async_copy(src.at[j], dst.at[j], sem.at[i, j]))
-            copies[-1].start()
+    for j in range(4):
+        row = 0
+        for h in range(2):
+            for i, dst in enumerate((ma, mb, mc)):
+                src = pieces[3 * h + i]
+                if j < src.shape[0]:
+                    rows = pl.ds(row, src.shape[2])
+                    copy = pltpu.make_async_copy(src.at[j], dst.at[j, :, rows], sem.at[h, i, j])
+                    copy.start()
+                    copies.append(copy)
+            row += pieces[3 * h].shape[2]
     x0 = (me_ref[0] // 2 * 2) * SIDE // len(parts)
     ids = box_ids(parts, dens)
     place = morton_place(ids)
@@ -545,21 +569,20 @@
     for c in copies:
         c.wait()
     n_out = len(OUTER) * ROWS
-    n_in = len(INNER) * ROWS
-    for i, dx in enumerate(SHIFTS):
-        rows = pl.ds(i * columns, slabs * columns)
+    n_all = len(SHIFTS) * ROWS
+    for i, dx in enumerate(OUTER + INNER):
+        rows = pl.ds((dx + REACH) * columns, slabs * columns)
         source = xs[rows, :]
-        outer = dot(ma[i].reshape(n_out, WFULL), source, NT)
         if dx in OUTER:
-            inner = dot(mb[OUTER.index(dx)].reshape(n_in, WFULL), source, NT)
+            term = dot(ma[OUTER.index(dx)].reshape(n_all, WFULL), source, NT)
+            if i == 0:
+                acc[...] = term
+            else:
+                acc[...] += term
         else:
-            inner = dot(mc[INNER.index(dx)].reshape(n_in, WIN), xin[rows, :], NT)
-        if i == 0:
-            acc[0:n_out] = outer
-            acc[n_out : n_out + n_in] = inner
-        else:
-            acc[0:n_out] += outer
-            acc[n_out : n_out + n_in] += inner
+            acc[0:n_out] += dot(mb[INNER.index(dx)].reshape(n_out, WFULL), source, NT)
+            inner = mc[INNER.index(dx)].reshape(n_all - n_out, WIN)
+            acc[n_out:n_all] += dot(inner, xin[rows, :], NT)
     lane = lax.broadcasted_iota(jnp.int32, (ROWS, LANE), 1)
     for t in range(slabs * columns // LANE):
         total = jnp.zeros((ROWS, LANE), f32)
@@ -575,8 +598,13 @@
 
 
 def coarse_kernel(*refs):
-    parts = refs[:-7]
-    m2m_hi, m2m_lo, lat_hi, lat_lo, l2l_hi, l2l_lo, out = refs[-7:]
+    parts = refs[:-14]
+    out = refs[-8]
+    m2m_hi, m2m_lo, lat_hi, lat_lo, l2l_hi, l2l_lo, sem = refs[-7:]
+    copies = []
+    for i in range(6):
+        copies.append(pltpu.make_async_copy(refs[-14 + i], refs[-7 + i], sem.at[i]))
+        copies[-1].start()
     dens = out.shape[0]
     box = ids = box_ids(parts, dens)
     place = ((box & 7) << 6) + (box & 56) + (box >> 6)
@@ -584,6 +612,9 @@
     at = lax.broadcasted_iota(jnp.int32, (BOXES4, ids.shape[1]), 0)
     there = jnp.where(at == place, 1.0, 0.0).astype(bf16)
     level = [dot(there, all_parts(parts, k, dens), NT) for k in range(dens)]
+
+    for copy in copies:
+        copy.wait()
 
     def oper(hi, lo, o):
         return hi[o], lo[o]
@@ -616,13 +647,16 @@
         out[k] = dot(high, move, TURNED) + dot(low, move, TURNED)
 
 
-def evaluate_kernel(slabs, step, me_ref, *refs):
+def evaluate_kernel(slabs, step, window, me_ref, *refs):
     n = SIDE // slabs
     checks = refs[: 2 * n]
-    d_hi, d_lo, lattice, field, place, offsets, out, stack, found = refs[2 * n :]
+    d_hi, d_lo, lattice, field_hbm, place, offsets, out, stack, found, field, sem = refs[2 * n :]
+    fetch = pltpu.make_async_copy(field_hbm, field, sem)
+    fetch.start()
     core = me_ref[0] & 1
     group = me_ref[0] // step
     dens = lattice.shape[0]
+    sources, cap = out.shape[0], out.shape[2] // dens
     lane = lax.broadcasted_iota(jnp.int32, (COEF, LANE), 1)
     mine = jnp.concatenate([d_hi[core], d_lo[core]], axis=0)
     other = jnp.concatenate([d_hi[1 - core], d_lo[1 - core]], axis=0)
@@ -651,25 +685,35 @@
             stack[rows, m * width : (m + 1) * width] = high.astype(f32)
             rows = pl.ds((dens + k) * CPAD, COEF)
             stack[rows, m * width : (m + 1) * width] = low.astype(f32)
+    box = offsets[sources] + lax.broadcasted_iota(jnp.int32, (1, window), 1)
+    want = morton_place(box) ^ (group * (slabs * PLANE))
+    want = jnp.where(box < BOXES4, want, -1)
+    pick = want == lax.broadcasted_iota(jnp.int32, (BOXES4, window), 0)
+    pick = jnp.where(pick, 1.0, 0.0).astype(bf16)
+    half = dens * CPAD
+    local = jnp.concatenate(
+        [dot(stack[h * half : (h + 1) * half].astype(bf16), pick) for h in range(2)], axis=1
+    ).astype(bf16)
     found[:, place.shape[1] :] = jnp.zeros((8, found.shape[1] - place.shape[1]), f32)
-    local = stack[...].astype(bf16)
-
-    @pl.loop(0, place.shape[1] // PB)
-    def _(j):
+    fetch.wait()
+
+    def block(j, carry):
         at = pl.ds(pl.multiple_of(j * PB, PB), PB)
-        want = place[:, at] ^ (group * (slabs * PLANE))
-        there = want == lax.broadcasted_iota(jnp.int32, (BOXES4, PB), 0)
-        got = dot(local, jnp.where(there, 1.0, 0.0).astype(bf16))
+        there = place[:, at] == lax.broadcasted_iota(jnp.int32, (window, PB), 0)
+        there = jnp.where(there, 1.0, 0.0)
+        there = jnp.concatenate([there, there], axis=0).astype(bf16)
+        got = dot(local, there)
         mine = field[:, at]
         rows = []
         for k in range(dens):
             value = got[k * CPAD : k * CPAD + COEF]
-            value = value + got[(dens + k) * CPAD : (dens + k) * CPAD + COEF]
             rows.append(jnp.sum(value * mine, axis=0, keepdims=True))
         rows.append(jnp.zeros((8 - dens, PB), f32))
         found[:, at] = jnp.concatenate(rows, axis=0)
-
-    sources, _, cap = out.shape
+        return carry
+
+    lax.fori_loop(0, place.shape[1] // PB, block, 0, unroll=2)
+
     wide = up(cap, LANE) + LANE
 
     @pl.loop(0, sources // STRIP)
@@ -679,7 +723,8 @@
             tile = offset // LANE
             value = found[:, pl.ds(pl.multiple_of(tile * LANE, LANE), wide)]
             value = pltpu.roll(value, wide - (offset - tile * LANE), 1)
-            out[i * STRIP + s] = value[0:dens, 0:cap]
+            for k in range(dens):
+                out[i * STRIP + s, :, k * cap : (k + 1) * cap] = value[k : k + 1, 0:cap]
 
 
 def shift_by(axis, value, distance):
@@ -687,10 +732,11 @@
     return lax.ppermute(value, axis, [(i, i ^ distance) for i in range(size)])
 
 
-def gather_by(value, distances):
+def gather_by(value, distances, beside):
     got = {m: shift_by("pts", value, m) if m else value for m in distances if m % 2 == 0}
+    got, beside = lax.optimization_barrier((got, beside))
     got.update({m + 1: shift_by("pts", got[m], 1) for m in list(got) if m + 1 in distances})
-    return [got[m] for m in distances]
+    return [got[m] for m in distances], beside
 
 
 def per_device(
@@ -707,23 +753,28 @@
     slabs = max(1, 2 * SIDE // n_pts)
     coef = uc2e.shape[0]
     sources = n_pts * n_top
+    lanes = min(cap, LANE)
+    rows = 8 + points // lanes
 
     def shape(*dims, dtype=bf16):
         return jax.ShapeDtypeStruct(dims, dtype)
 
     outgoing, entries = call(
         functools.partial(route_kernel, own, cap, n_top),
-        (shape(n_pts, n_top, 8, cap, dtype=f32), shape(1, points, dtype=jnp.int32)),
+        (shape(n_pts, n_top, rows, cap, dtype=f32), shape(1, points, dtype=jnp.int32)),
         GRANT,
         1 << 27,
-        in_specs=[WHOLE] * 3,
+        in_specs=[WHOLE] * 4,
         out_specs=(WHOLE, WHOLE),
-    )(local_pos, densities, morton_slot.reshape(1, points))
-    outgoing = outgoing.reshape(sources, 8, cap)
+    )(
+        local_pos,
+        densities,
+        morton_slot.reshape(1, points),
+        slot_leaf.reshape(points // lanes, lanes),
+    )
+    outgoing = outgoing.reshape(sources, rows, cap)
     incoming = lax.all_to_all(outgoing, ("pts", "top"), split_axis=0, concat_axis=0, tiled=True)
 
-    leaf = slot_leaf.reshape(points // LANE, LANE)
-    leaves = [shift_by("top", leaf, m) if m else leaf for m in range(n_top)]
     flat = (-1, LANE)
     column = jnp.asarray(column_table())
     square_shape = shape(8, coef, coef)
@@ -741,8 +792,9 @@
     )(m2m.reshape(flat), l2l.reshape(flat), uc2e, dc2e, lattice, column)
     coarse_ops, halves = coarse_ops[:6], coarse_ops[6:]
     m2m_hi, m2m_lo, l2l_hi, l2l_lo, lat_hi, lat_lo = coarse_ops
-    oa, ob, oc = relayout(m2l_ops, me)
-    incoming, oa, ob, oc = lax.optimization_barrier((incoming, oa, ob, oc))
+    coarse_ops = (m2m_hi, m2m_lo, lat_hi, lat_lo, l2l_hi, l2l_lo)
+    first = relayout(m2l_ops, me, 0, EARLY)
+    incoming, first = lax.optimization_barrier((incoming, first))
 
     partial, field, place, offsets = call(
         functools.partial(points_kernel, n_top, box_cap),
@@ -750,18 +802,22 @@
             shape(up(coef + 2, 16), dens * box_cap),
             shape(coef, own, dtype=f32),
             shape(1, own, dtype=jnp.int32),
-            shape(sources, dtype=jnp.int32),
+            shape(sources + 1, dtype=jnp.int32),
         ),
         GRANT,
         8 << 30,
-        in_specs=[SMEM] + [WHOLE] * (n_top + 3),
+        in_specs=[SMEM] + [WHOLE] * 2 + [ANY],
         out_specs=(WHOLE, WHOLE, WHOLE, SMEM),
         scratch_shapes=[
             pltpu.VMEM((8, up(own + up(cap, LANE) + LANE, PB)), f32),
             pltpu.VMEM((3 + FEATURES, coef, PB), f32),
+            pltpu.VMEM(w_both.shape, bf16),
+            pltpu.SemaphoreType.DMA,
         ],
-    )(me, incoming, *leaves, column, w_both)
-    parts = gather_by(partial, range(n_pts))
+    )(me, incoming, column, w_both)
+    later, flat_ops = lax.optimization_barrier((partial, m2l_ops))
+    rest = relayout(flat_ops, me, EARLY, STEPS - EARLY)
+    parts, rest = gather_by(later, range(n_pts), rest)
 
     columns = dens * PLANE
     checks = call(
@@ -769,45 +825,48 @@
         shape(ROWS, slabs * columns),
         GRANT,
         8 << 30,
-        in_specs=[SMEM] + [WHOLE] * n_pts + [ANY] * 3,
+        in_specs=[SMEM] + [WHOLE] * n_pts + [ANY] * 6,
         out_specs=WHOLE,
         scratch_shapes=[
             pltpu.VMEM(((7 + slabs - 1) * columns, WFULL), bf16),
             pltpu.VMEM(((7 + slabs - 1) * columns, WIN), bf16),
             pltpu.VMEM((7 * ROWS, slabs * columns), f32),
-            pltpu.VMEM(oa.shape, bf16),
-            pltpu.VMEM(ob.shape, bf16),
-            pltpu.VMEM(oc.shape, bf16),
-            pltpu.SemaphoreType.DMA((3, 7)),
+            *[pltpu.VMEM((a, b, ROWS, c), bf16) for a, b, c in PIECES],
+            pltpu.SemaphoreType.DMA((2, 3, 4)),
         ],
-    )(me, *parts, oa, ob, oc)
-    step = n_pts // SIDE * slabs
-    gathered = gather_by(checks, [step * m + c for m in range(SIDE // slabs) for c in range(2)])
-
+    )(me, *parts, *first, *rest)
     lattice4 = call(
         coarse_kernel,
         shape(dens, coef, BOXES4, dtype=f32),
         GRANT,
         4 << 30,
-        in_specs=[WHOLE] * (n_pts + 6),
+        in_specs=[WHOLE] * n_pts + [ANY] * 6,
         out_specs=WHOLE,
-    )(*parts, m2m_hi, m2m_lo, lat_hi, lat_lo, l2l_hi, l2l_lo)
+        scratch_shapes=[pltpu.VMEM(v.shape, bf16) for v in coarse_ops]
+        + [pltpu.SemaphoreType.DMA((6,))],
+    )(*parts, *coarse_ops)
+
+    step = n_pts // SIDE * slabs
+    distances = [step * m + c for m in range(SIDE // slabs) for c in range(2)]
+    gathered, lattice4 = gather_by(checks, distances, lattice4)
 
     reply = call(
-        functools.partial(evaluate_kernel, slabs, step),
-        shape(sources, dens, cap, dtype=f32),
+        functools.partial(evaluate_kernel, slabs, step, box_cap),
+        shape(sources, 1, dens * cap, dtype=f32),
         GRANT,
         4 << 30,
-        in_specs=[SMEM] + [WHOLE] * (len(gathered) + 5) + [SMEM],
+        in_specs=[SMEM] + [WHOLE] * (len(gathered) + 3) + [ANY, WHOLE, SMEM],
         out_specs=WHOLE,
         scratch_shapes=[
             pltpu.VMEM((2 * dens * CPAD, BOXES4), f32),
             pltpu.VMEM((8, own + up(cap, LANE) + LANE), f32),
+            pltpu.VMEM(field.shape, f32),
+            pltpu.SemaphoreType.DMA,
         ],
     )(me, *gathered, *halves, lattice4, field, place, offsets)
     returned = lax.all_to_all(reply, ("pts", "top"), split_axis=0, concat_axis=0, tiled=True)
     return call(
-        restore_kernel,
+        functools.partial(restore_kernel, n_top),
         shape(DENS, points, dtype=f32),
         GRANT,
         1 << 28,

time: 109 us -> 103 us (0.945)
  waiting for transfers between devices: 8.93 us -> 1.8 us
  starting transfers between devices: 18.9 us -> 16.6 us
    ppermute x17 -> x14, waiting for transfers between devices: 8.93 us -> 1.79 us  [shift_by(): return lax.ppermute(value, axis, [(i, i ^ distance) for i in range(size)])]
    ppermute x17 -> x14, starting transfers between devices: 11.6 us -> 9.26 us  [shift_by(): return lax.ppermute(value, axis, [(i, i ^ distance) for i in range(size)])]
    pallas_call x3 -> x4, Pallas kernels: 26.6 us -> 27.7 us  [the longest x2 19.4 us: relayout(): call(functools.partial(relayout_kernel, nrows, step0, steps), tuple((jax....]
    unnamed x36 -> x34, local copies, waits for them, and re-layouts: 2 us -> 2.53 us
  transfers between devices with their start and end apart: 18 -> 15, of which waited for: 8 -> 8; matrix products, arithmetic and copies ran while one was open for 1% -> 1% of each run, Pallas kernels for 27% -> 33%
where the time goes in v4:
time: 103 us; the launch traced here: 102 us
  Pallas kernels  66.7 us (65%)
  starting transfers between devices  16.6 us (16%)
  blocking collectives  13.5 us (13%)
  local copies, waits for them, and re-layouts  2.53 us (2%)
  waiting for transfers between devices  1.8 us (2%)
    pallas_call x2, Pallas kernels, relayout(): call(functools.partial(relayout_kernel, nrows, step0, steps), tuple((jax....  19.4 us
    all_to_all x1, blocking collectives, per_device(): lax.all_to_all(reply, ('pts', 'top'), split_axis=0, concat_axis=0, tiled=...  13.5 us
    pallas_call x1, Pallas kernels, per_device(): call(functools.partial(points_kernel, n_top, box_cap), (shape(up(coef + 2...  12.3 us
    ppermute x14, starting transfers between devices, shift_by(): return lax.ppermute(value, axis, [(i, i ^ distance) for i in range(size)])  9.26 us
    pallas_call x1, Pallas kernels, per_device(): call(functools.partial(translate_kernel, slabs, dens), shape(ROWS, slabs...  8.77 us
    pallas_call x1, Pallas kernels, per_device(): call(coarse_kernel, shape(dens, coef, BOXES4, dtype=f32), GRANT, 4 << 30,...  8.59 us
    all_to_all x1, starting transfers between devices, per_device(): lax.all_to_all(outgoing, ('pts', 'top'), split_axis=0, concat_axis=0, til...  7.3 us
    pallas_call x1, Pallas kernels, per_device(): call(functools.partial(evaluate_kernel, slabs, step, box_cap), shape(sour...  6.24 us
  transfers between devices with their start and end apart: 15, of which 8 were waited for; matrix products, arithmetic and copies ran while one was open for 1% of the time, Pallas kernels for 33%

profile of v4, /device:TPU:0, one launch (start us, length us, event | category | flops | bytes accessed | tf_op | source)
XLA Modules:
  0.0 101.9 jit_solution(1022849690610843596)
XLA Ops:
  0.0 3.2 %shard_map.109 = (f32[8,4,16,256]{3,2,1,0:T(8,128)}, s32[1,1024]{1,0:T(1,128)}) custom-call(f32[3,1024]{1,0:T(4,128)} %pos.1, f32[8,1024]{1,0:T(8,128)} %dens.1, s32[1,1024]{1,0:T(1,128)} %bitcast.16, s32[8,128]{1,0:T(8,128)} %bitcast.17), custom_call_target="tpu_custom_call" | custom-call | flops 134217728 | bytes 1048576 | tf_op jit(solution)/shard_map/pallas_call | solution.py:762
  3.2 7.3 %all-to-all-start = ((f32[32,16,256]{2,1,0:T(8,128)}), f32[32,16,256]{2,1,0:T(8,128)S(1)}, u32[]{:S(2)}, u32[]{:S(2)}) async-start(f32[32,16,256]{2,1,0:T(8,128)} %bitcast.13), calls=%async_computation | async-start | bytes 1048576 | tf_op jit(solution)/shard_map/all_to_all | solution.py:776
  10.5 0.6 pad_add_fusion.me_ref
  11.1 10.8 %shard_map.110 = (bf16[4,7,48,1152]{3,2,1,0:T(8,128)(2,1)}, bf16[3,4,48,1152]{3,2,1,0:T(8,128)(2,1)}, bf16[3,3,48,640]{3,2,1,0:T(8,128)(2,1)}) custom-call(s32[2]{0:T(128)} %pad_add_fusion.me_ref, bf16[57038,128]{1,0:T(8,128)(2,1)} %bitcast.9, bf16[57038,128]{1,0:T(8,128)(2,1)} %bitcast.10), custom_call_target="tpu_custom_call" | custom-call | flops 1048576 | bytes 6291456 | tf_op jit(solution)/shard_map/pallas_call | solution.py:234
  21.9 6.2 %shard_map.111 = (bf16[304,1280]{1,0:T(8,128)(2,1)}, bf16[8,152,152]{2,1,0:T(8,128)(2,1)}, bf16[8,152,152]{2,1,0:T(8,128)(2,1)}, bf16[8,152,152]{2,1,0:T(8,128)(...) custom-call(f32[1444,128]{1,0:T(8,128)} %bitcast.14, ...), custom_call_target="tpu_custom_call" | custom-call | flops 1073741824 | bytes 1048576 | tf_op jit(solution)/shard_map/pallas_call | solution.py:781
  28.1 0.8 copy-done
  28.8 12.3 %shard_map.112 = (bf16[160,256]{1,0:T(8,128)(2,1)}, f32[152,4096]{1,0:T(8,128)}, s32[1,4096]{1,0:T(1,128)}, s32[33]{0:T(128)}) custom-call(s32[2]{0:T(128)} %pad_add_fusion.me_ref, f32[32,16,256]{2,1,0:T(8,128)} %copy-done, f32[152,128]{1,0:T(8,128)} %constant.11.clone.column.refs_0_, bf16[304,1280]{1,0:T(8,128)(2,1)} %get-tuple-element.49.refs_1_), custom_call_target="tpu_custom_call" | custom-call | flops 8589934592 | bytes 1048576 | tf_op jit(solution)/shard_map/pallas_call | solution.py:799
  41.1 2.7 %collective-permute-start.2 = (bf16[160,256]{1,0:T(8,128)(2,1)}, bf16[160,256]{1,0:T(8,128)(2,1)S(1)}, u32[]{:S(2)}, u32[]{:S(2)}) collective-permute-start(bf16[160,256]{1,0:T(8,128)(2,1)} %get-tuple-element.56.refs_0_), channel_id=1, source_target_pairs={{0,24},{4,28},{8,16},{12,20},{16,8},{20,12},{24,0},{28,4},{1,25},{... | collective-permute-start | bytes 245768 | tf_op jit(solution)/shard_map/ppermute | solution.py:732
  43.8 0.6 collective-permute-start.1
  44.4 0.3 collective-permute-start
  44.7 8.6 %shard_map.113 = (bf16[4,7,32,1152]{3,2,1,0:T(8,128)(2,1)}, bf16[3,4,32,1152]{3,2,1,0:T(8,128)(2,1)}, bf16[3,3,32,640]{3,2,1,0:T(8,128)(2,1)}) custom-call(s32[2]{0:T(128)} %pad_add_fusion.me_ref, bf16[57038,128]{1,0:T(8,128)(2,1)} %bitcast.11, bf16[57038,128]{1,0:T(8,128)(2,1)} %bitcast.12), custom_call_target="tpu_custom_call" | custom-call | flops 1048576 | bytes 4194304 | tf_op jit(solution)/shard_map/pallas_call | solution.py:234
  53.4 0.5 collective-permute-start.4
  54.0 0.4 collective-permute-start.6
  54.4 0.3 collective-permute-done.3.refs_1_
  54.8 0.4 collective-permute-done.5.refs_5_
  55.5 0.4 copy-done.7
  55.8 0.6 copy-done.8
  56.5 8.8 %shard_map.114.refs_0_ = bf16[80,256]{1,0:T(8,128)(2,1)} custom-call(s32[2]{0:T(128)} %pad_add_fusion.me_ref, bf16[160,256]{1,0:T(8,128)(2,1)} %get-tuple-element.56.refs_0_, bf16[160,256]{1,0:T(8,128)(2,1)} %copy-done.5, bf16[160,256]{1,0:T(8,128)(2,1)} %copy-done.4, bf16[160,256]{1,0:T(8,128)(2,1)} %copy-done.6, bf16[160,256]{1,0:T(8,128)(2,1)} %copy-done.3, ...), custom_call_target="tpu_custom_call" | custom-call | flops 8589934592 | bytes 1048576 | tf_op jit(solution)/shard_map/pallas_call | solution.py:823
  65.2 2.7 %collective-permute-start.9 = (bf16[80,256]{1,0:T(8,128)(2,1)}, bf16[80,256]{1,0:T(8,128)(2,1)S(1)}, u32[]{:S(2)}, u32[]{:S(2)}) collective-permute-start(bf16[80,256]{1,0:T(8,128)(2,1)} %shard_map.114.refs_0_), channel_id=1, source_target_pairs={{0,24},{4,28},{8,16},{12,20},{16,8},{20,12},{24,0},{28,4},{1,25},{... | collective-permute-start | bytes 122888 | tf_op jit(solution)/shard_map/ppermute | solution.py:732
  68.0 0.6 collective-permute-start.8
  68.5 0.3 collective-permute-start.7
  68.8 8.6 %shard_map.115.refs_10_ = f32[2,152,512]{2,1,0:T(8,128)} custom-call(bf16[160,256]{1,0:T(8,128)(2,1)} %get-tuple-element.56.refs_0_, bf16[160,256]{1,0:T(8,128)(2,1)} %copy-done.5, bf16[160,256]{1,0:T(8,128)(2,1)} %copy-done.4, bf16[160,256]{1,0:T(8,128)(2,1)} %copy-done.6, bf16[160,256]{1,0:T(8,128)(2,1)} %copy-done.3, bf16[160,256]{1,0:T(8,128)(2,1)} %copy-done.7, ...), custom_call_target="tpu_custom_call" | custom-call | flops 4294967296 | bytes 1048576 | tf_op jit(solution)/shard_map/pallas_call | solution.py:838
  77.6 0.5 collective-permute-start.11
  78.1 0.4 collective-permute-start.13
  78.6 0.2 collective-permute-done.10.refs_1_
  78.8 0.2 collective-permute-done.11.refs_3_
  78.9 0.3 collective-permute-done.12.refs_5_
  79.3 0.2 collective-permute-done.13.refs_7_
  79.5 0.4 copy-done.15
  80.0 6.2 %shard_map.116 = f32[32,1,512]{2,1,0:T(1,128)} custom-call(s32[2]{0:T(128)} %pad_add_fusion.me_ref, bf16[80,256]{1,0:T(8,128)(2,1)} %shard_map.114.refs_0_, bf16[80,256]{1,0:T(8,128)(2,1)} %copy-done.13, bf16[80,256]{1,0:T(8,128)(2,1)} %copy-done.12, bf16[80,256]{1,0:T(8,128)(2,1)} %copy-done.14, bf16[80,256]{1,0:T(8,128)(2,1)} %copy-done.11, ...), custom_call_target="tpu_custom_call" | custom-call | flops 4294967296 | bytes 1048576 | tf_op jit(solution)/shard_map/pallas_call | solution.py:853
  86.3 13.5 %all_to_all.10.got = f32[32,1,512]{2,1,0:T(1,128)} all-to-all(f32[32,1,512]{2,1,0:T(1,128)} %shard_map.116), channel_id=1, replica_groups=mesh['pts'=8,'top'=4] {'pts','top'}, dimensions={0} | all-to-all | bytes 131072 | tf_op jit(solution)/shard_map/all_to_all | solution.py:867
  99.7 2.1 %shard_map.117 = f32[8,1024]{1,0:T(8,128)} custom-call(f32[32,1,512]{2,1,0:T(1,128)} %all_to_all.10.got, s32[1,1024]{1,0:T(1,128)} %get-tuple-element.82.entries), custom_call_target="tpu_custom_call" | custom-call | flops 268435456 | bytes 1048576 | tf_op jit(solution)/shard_map/pallas_call | solution.py:868
  (43 shorter events, 1.0 us)
Async XLA Ops:
  3.2 24.8 %all-to-all-start = ((f32[32,16,256]{2,1,0:T(8,128)}), f32[32,16,256]{2,1,0:T(8,128)S(1)}, u32[]{:S(2)}, u32[]{:S(2)}) async-start(f32[32,16,256]{2,1,0:T(8,128)} %bitcast.13), calls=%async_computation | async-start | bytes 1048576 | tf_op jit(solution)/shard_map/all_to_all | solution.py:776
  28.0 0.8 copy-start
  41.1 12.2 %collective-permute-start.2 = (bf16[160,256]{1,0:T(8,128)(2,1)}, bf16[160,256]{1,0:T(8,128)(2,1)S(1)}, u32[]{:S(2)}, u32[]{:S(2)}) collective-permute-start(bf16[160,256]{1,0:T(8,128)(2,1)} %get-tuple-element.56.refs_0_), channel_id=1, source_target_pairs={{0,24},{4,28},{8,16},{12,20},{16,8},{20,12},{24,0},{28,4},{1,25},{... | collective-permute-start | bytes 245768 | tf_op jit(solution)/shard_map/ppermute | solution.py:732
  43.8 9.5 %collective-permute-start.1 = (bf16[160,256]{1,0:T(8,128)(2,1)}, bf16[160,256]{1,0:T(8,128)(2,1)S(1)}, u32[]{:S(2)}, u32[]{:S(2)}) collective-permute-start(bf16[160,256]{1,0:T(8,128)(2,1)} %get-tuple-element.56.refs_0_), channel_id=1, source_target_pairs={{0,16},{4,20},{8,24},{12,28},{16,0},{20,4},{24,8},{28,12},{1,17},{... | collective-permute-start | bytes 245768 | tf_op jit(solution)/shard_map/ppermute | solution.py:732
  44.4 8.9 %collective-permute-start = (bf16[160,256]{1,0:T(8,128)(2,1)}, bf16[160,256]{1,0:T(8,128)(2,1)S(1)}, u32[]{:S(2)}, u32[]{:S(2)}) collective-permute-start(bf16[160,256]{1,0:T(8,128)(2,1)} %get-tuple-element.56.refs_0_), channel_id=1, source_target_pairs={{0,8},{4,12},{8,0},{12,4},{16,24},{20,28},{24,16},{28,20},{1,9},{5... | collective-permute-start | bytes 245768 | tf_op jit(solution)/shard_map/ppermute | solution.py:732
  44.7 8.7 %copy-start.1 = (bf16[160,256]{1,0:T(8,128)(2,1)S(1)}, bf16[160,256]{1,0:T(8,128)(2,1)}, u32[]{:S(2)}) copy-start(bf16[160,256]{1,0:T(8,128)(2,1)} %get-tuple-element.56.refs_0_) | copy-start | bytes 245764
  53.3 2.1 %copy-start.2 = (bf16[160,256]{1,0:T(8,128)(2,1)}, bf16[160,256]{1,0:T(8,128)(2,1)S(1)}, u32[]{:S(2)}) copy-start(bf16[160,256]{1,0:T(8,128)(2,1)S(1)} %collective-permute-done.2.refs_6_) | copy-start | bytes 245764
  53.3 2.1 %copy-start.3 = (bf16[160,256]{1,0:T(8,128)(2,1)}, bf16[160,256]{1,0:T(8,128)(2,1)S(1)}, u32[]{:S(2)}) copy-start(bf16[160,256]{1,0:T(8,128)(2,1)S(1)} %collective-permute-done.1.refs_4_) | copy-start | bytes 245764
  53.3 2.0 %copy-start.4 = (bf16[160,256]{1,0:T(8,128)(2,1)}, bf16[160,256]{1,0:T(8,128)(2,1)S(1)}, u32[]{:S(2)}) copy-start(bf16[160,256]{1,0:T(8,128)(2,1)S(1)} %collective-permute-done.refs_2_) | copy-start | bytes 245764
  53.3 1.3 %collective-permute-start.3 = (bf16[160,256]{1,0:T(8,128)(2,1)S(1)}, bf16[160,256]{1,0:T(8,128)(2,1)S(1)}, u32[]{:S(2)}, u32[]{:S(2)}) collective-permute-start(bf16[160,256]{1,0:T(8,128)(2,1)S(1)} %copy-done.1), channel_id=1, source_target_pairs={{0,4},{4,0},{8,12},{12,8},{16,20},{20,16},{24,28},{28,24},{1,5},{5... | collective-permute-start | bytes 245768 | tf_op jit(solution)/shard_map/ppermute | solution.py:732
  53.4 1.4 %collective-permute-start.4 = (bf16[160,256]{1,0:T(8,128)(2,1)S(1)}, bf16[160,256]{1,0:T(8,128)(2,1)S(1)}, u32[]{:S(2)}, u32[]{:S(2)}) collective-permute-start(bf16[160,256]{1,0:T(8,128)(2,1)S(1)} %collective-permute-done.refs_2_), channel_id=1, source_target_pairs={{0,4},{4,0},{8,12},{12,8},{16,20},{20,16},{24,28},{28,24},{1,5},{5... | collective-permute-start | bytes 245768 | tf_op jit(solution)/shard_map/ppermute | solution.py:732
  53.9 1.3 %collective-permute-start.5 = (bf16[160,256]{1,0:T(8,128)(2,1)S(1)}, bf16[160,256]{1,0:T(8,128)(2,1)S(1)}, u32[]{:S(2)}, u32[]{:S(2)}) collective-permute-start(bf16[160,256]{1,0:T(8,128)(2,1)S(1)} %collective-permute-done.1.refs_4_), channel_id=1, source_target_pairs={{0,4},{4,0},{8,12},{12,8},{16,20},{20,16},{24,28},{28,24},{1,5},{5... | collective-permute-start | bytes 245768 | tf_op jit(solution)/shard_map/ppermute | solution.py:732
  54.0 1.4 %collective-permute-start.6 = (bf16[160,256]{1,0:T(8,128)(2,1)S(1)}, bf16[160,256]{1,0:T(8,128)(2,1)S(1)}, u32[]{:S(2)}, u32[]{:S(2)}) collective-permute-start(bf16[160,256]{1,0:T(8,128)(2,1)S(1)} %collective-permute-done.2.refs_6_), channel_id=1, source_target_pairs={{0,4},{4,0},{8,12},{12,8},{16,20},{20,16},{24,28},{28,24},{1,5},{5... | collective-permute-start | bytes 245768 | tf_op jit(solution)/shard_map/ppermute | solution.py:732
  54.7 0.7 copy-start.5
  54.8 0.6 copy-start.6
  55.2 0.6 copy-start.7
  55.8 0.6 copy-start.8
  65.2 12.2 %collective-permute-start.9 = (bf16[80,256]{1,0:T(8,128)(2,1)}, bf16[80,256]{1,0:T(8,128)(2,1)S(1)}, u32[]{:S(2)}, u32[]{:S(2)}) collective-permute-start(bf16[80,256]{1,0:T(8,128)(2,1)} %shard_map.114.refs_0_), channel_id=1, source_target_pairs={{0,24},{4,28},{8,16},{12,20},{16,8},{20,12},{24,0},{28,4},{1,25},{... | collective-permute-start | bytes 122888 | tf_op jit(solution)/shard_map/ppermute | solution.py:732
  68.0 9.4 %collective-permute-start.8 = (bf16[80,256]{1,0:T(8,128)(2,1)}, bf16[80,256]{1,0:T(8,128)(2,1)S(1)}, u32[]{:S(2)}, u32[]{:S(2)}) collective-permute-start(bf16[80,256]{1,0:T(8,128)(2,1)} %shard_map.114.refs_0_), channel_id=1, source_target_pairs={{0,16},{4,20},{8,24},{12,28},{16,0},{20,4},{24,8},{28,12},{1,17},{... | collective-permute-start | bytes 122888 | tf_op jit(solution)/shard_map/ppermute | solution.py:732
  68.5 8.9 %collective-permute-start.7 = (bf16[80,256]{1,0:T(8,128)(2,1)}, bf16[80,256]{1,0:T(8,128)(2,1)S(1)}, u32[]{:S(2)}, u32[]{:S(2)}) collective-permute-start(bf16[80,256]{1,0:T(8,128)(2,1)} %shard_map.114.refs_0_), channel_id=1, source_target_pairs={{0,8},{4,12},{8,0},{12,4},{16,24},{20,28},{24,16},{28,20},{1,9},{5... | collective-permute-start | bytes 122888 | tf_op jit(solution)/shard_map/ppermute | solution.py:732
  68.8 8.7 %copy-start.9 = (bf16[80,256]{1,0:T(8,128)(2,1)S(1)}, bf16[80,256]{1,0:T(8,128)(2,1)}, u32[]{:S(2)}) copy-start(bf16[80,256]{1,0:T(8,128)(2,1)} %shard_map.114.refs_0_) | copy-start | bytes 122884
  77.4 2.0 %copy-start.10 = (bf16[80,256]{1,0:T(8,128)(2,1)}, bf16[80,256]{1,0:T(8,128)(2,1)S(1)}, u32[]{:S(2)}) copy-start(bf16[80,256]{1,0:T(8,128)(2,1)S(1)} %collective-permute-done.9.refs_6_) | copy-start | bytes 122884
  77.4 2.0 %copy-start.11 = (bf16[80,256]{1,0:T(8,128)(2,1)}, bf16[80,256]{1,0:T(8,128)(2,1)S(1)}, u32[]{:S(2)}) copy-start(bf16[80,256]{1,0:T(8,128)(2,1)S(1)} %collective-permute-done.8.refs_4_) | copy-start | bytes 122884
  77.5 2.0 %copy-start.12 = (bf16[80,256]{1,0:T(8,128)(2,1)}, bf16[80,256]{1,0:T(8,128)(2,1)S(1)}, u32[]{:S(2)}) copy-start(bf16[80,256]{1,0:T(8,128)(2,1)S(1)} %collective-permute-done.7.refs_2_) | copy-start | bytes 122884
  77.5 1.3 %collective-permute-start.10 = (bf16[80,256]{1,0:T(8,128)(2,1)S(1)}, bf16[80,256]{1,0:T(8,128)(2,1)S(1)}, u32[]{:S(2)}, u32[]{:S(2)}) collective-permute-start(bf16[80,256]{1,0:T(8,128)(2,1)S(1)} %copy-done.9), channel_id=1, source_target_pairs={{0,4},{4,0},{8,12},{12,8},{16,20},{20,16},{24,28},{28,24},{1,5},{5... | collective-permute-start | bytes 122888 | tf_op jit(solution)/shard_map/ppermute | solution.py:732
  77.6 1.4 %collective-permute-start.11 = (bf16[80,256]{1,0:T(8,128)(2,1)S(1)}, bf16[80,256]{1,0:T(8,128)(2,1)S(1)}, u32[]{:S(2)}, u32[]{:S(2)}) collective-permute-start(bf16[80,256]{1,0:T(8,128)(2,1)S(1)} %collective-permute-done.7.refs_2_), channel_id=1, source_target_pairs={{0,4},{4,0},{8,12},{12,8},{16,20},{20,16},{24,28},{28,24},{1,5},{5... | collective-permute-start | bytes 122888 | tf_op jit(solution)/shard_map/ppermute | solution.py:732
  78.0 1.2 %collective-permute-start.12 = (bf16[80,256]{1,0:T(8,128)(2,1)S(1)}, bf16[80,256]{1,0:T(8,128)(2,1)S(1)}, u32[]{:S(2)}, u32[]{:S(2)}) collective-permute-start(bf16[80,256]{1,0:T(8,128)(2,1)S(1)} %collective-permute-done.8.refs_4_), channel_id=1, source_target_pairs={{0,4},{4,0},{8,12},{12,8},{16,20},{20,16},{24,28},{28,24},{1,5},{5... | collective-permute-start | bytes 122888 | tf_op jit(solution)/shard_map/ppermute | solution.py:732
  78.1 1.3 %collective-permute-start.13 = (bf16[80,256]{1,0:T(8,128)(2,1)S(1)}, bf16[80,256]{1,0:T(8,128)(2,1)S(1)}, u32[]{:S(2)}, u32[]{:S(2)}) collective-permute-start(bf16[80,256]{1,0:T(8,128)(2,1)S(1)} %collective-permute-done.9.refs_6_), channel_id=1, source_target_pairs={{0,4},{4,0},{8,12},{12,8},{16,20},{20,16},{24,28},{28,24},{1,5},{5... | collective-permute-start | bytes 122888 | tf_op jit(solution)/shard_map/ppermute | solution.py:732
  78.8 0.7 copy-start.13
  78.9 0.6 copy-start.14
  79.3 0.6 copy-start.15
  79.4 0.6 copy-start.16

commit v5 on v4

--- a/solution.py
+++ b/solution.py
@@ -46,7 +46,10 @@
 FEATURES = 4
 PB = 256
 STRIP = 16
-GRANT = 58
+GRANT = 28
+GRANT_FIRST = 60
+GRANT_EARLY = 52
+GRANT_LATER = 49
 CPAD = up(COEF, 32)
 
 
@@ -105,10 +108,67 @@
     )
 
 
+SMEM = pl.BlockSpec(memory_space=pltpu.SMEM)
 VMEM = pl.BlockSpec(memory_space=pltpu.VMEM)
-WHOLE = pl.BlockSpec()
-SMEM = pl.BlockSpec(memory_space=pltpu.SMEM)
-ANY = pl.BlockSpec(memory_space=pl.ANY)
+HBM = pl.BlockSpec(memory_space=pltpu.HBM)
+
+class Buffers:
+    def __init__(self, scalars, ins, outs, moved, sources, targets, sem_in, sem_out):
+        self.scalars, self.ins, self.outs, self.targets = scalars, ins, outs, targets
+        self.sem_out = sem_out
+        self.coming, self.going, self.waited = {}, {}, set()
+        for i in moved:
+            self.coming[i] = pltpu.make_async_copy(sources[i], ins[i], sem_in.at[i])
+            self.coming[i].start()
+
+    def wait(self, *which):
+        for i in which:
+            if i in self.coming and i not in self.waited:
+                self.waited.add(i)
+                self.coming[i].wait()
+
+    def send(self, *which):
+        for i in which:
+            if i not in self.going:
+                copy = pltpu.make_async_copy(self.outs[i], self.targets[i], self.sem_out.at[i])
+                copy.start()
+                self.going[i] = copy
+
+
+def run(kernel, scalars, ins, outs, flops, scratch=(), late=(), here=(), stays=(), numbers=(), grant=GRANT):
+    n_s, n_i, n_o, n_n = len(scalars), len(ins), len(outs), len(numbers)
+    moved_in = [i for i in range(n_i) if i not in here]
+    moved_out = [i for i in range(n_o) if i not in stays]
+
+    def body(*refs):
+        refs = list(refs)
+        take = lambda count: [refs.pop(0) for _ in range(count)]
+        given, sources, targets, counts = take(n_s), take(n_i), take(n_o), take(n_n)
+        in_refs, out_refs = list(sources), list(targets)
+        for i in moved_in:
+            in_refs[i] = refs.pop(0)
+        for i in moved_out:
+            out_refs[i] = refs.pop(0)
+        io = Buffers(given, in_refs, out_refs, moved_in, sources, targets, *take(2))
+        io.wait(*[i for i in moved_in if i not in late])
+        kernel(io, *counts, *refs)
+        io.wait(*moved_in)
+        io.send(*moved_out)
+        for i in moved_out:
+            io.going[i].wait()
+
+    return call(
+        body,
+        tuple(outs) + tuple(numbers),
+        grant,
+        flops,
+        in_specs=[SMEM] * n_s + [VMEM if i in here else HBM for i in range(n_i)],
+        out_specs=tuple(VMEM if i in stays else HBM for i in range(n_o)) + (SMEM,) * n_n,
+        scratch_shapes=[pltpu.VMEM(ins[i].shape, ins[i].dtype) for i in moved_in]
+        + [pltpu.VMEM(outs[i].shape, outs[i].dtype) for i in moved_out]
+        + [pltpu.SemaphoreType.DMA((max(n, 1),)) for n in (n_i, n_o)]
+        + list(scratch),
+    )(*scalars, *ins)
 
 
 HG = 4 * OFFSETS * COEF // LANE
@@ -211,6 +271,7 @@
     def _(k):
         tb16[k] = tbuf[pl.ds(k * STRIDE, 16), :].astype(bf16)
 
+    here = pl.ds(pl.multiple_of(step * 16, 16), 16)
     for dx, dy, d0, count in blocks():
         tile0, phase = divmod(d0 * COEF, LANE)
         if dx in OUTER:
@@ -224,26 +285,24 @@
             if phase:
                 after = tb16[min(tile0 + t + 1, KT - 1)]
                 value = jnp.concatenate([value[:, phase:], after[:, :phase]], axis=1)
-            ref[:, t * LANE : (t + 1) * LANE] = value
-
-
-def relayout(flat, me, step0, steps):
+            ref[here, t * LANE : (t + 1) * LANE] = value
+
+
+def relayout(flat, me, step0, steps, grant):
     nrows = flat.shape[0] // LANE
     rows = flat.reshape(nrows, LANE)
     shapes = tuple((a, b, 16 * steps, c) for a, b, c in PIECES)
     return call(
         functools.partial(relayout_kernel, nrows, step0, steps),
         tuple(jax.ShapeDtypeStruct(s, bf16) for s in shapes),
-        GRANT,
+        grant,
         1 << 20,
         steps << 21,
         grid_spec=pltpu.PrefetchScalarGridSpec(
             num_scalar_prefetch=1,
             grid=(steps,),
-            in_specs=[ANY, pl.BlockSpec((16, LANE), lambda i, h: (nrows // 16, 0))],
-            out_specs=tuple(
-                pl.BlockSpec((s[0], s[1], 16, s[3]), lambda i, h: (0, 0, i, 0)) for s in shapes
-            ),
+            in_specs=[HBM, pl.BlockSpec((16, LANE), lambda i, h: (nrows // 16, 0))],
+            out_specs=(VMEM,) * len(shapes),
             scratch_shapes=[
                 pltpu.VMEM((2, 4, CHUNK, LANE), bf16),
                 pltpu.VMEM((4, CHUNK + 16, LANE), f32),
@@ -276,12 +335,11 @@
             out[t, pl.ds(r, groups, stride=GROUP), :] = value
 
 
-def operators_kernel(
-    m2m, l2l, uc2e, dc2e, lattice, column, w_both, m2m_hi, m2m_lo, l2l_hi, l2l_lo, lat_hi, lat_lo,
-    d_hi, d_lo, rows
-):
+def operators_kernel(io, rows):
+    m2m, l2l, uc2e, dc2e, lattice, column = io.ins
+    w_both, coarse, d_hi, d_lo = io.outs
     scale = 1.0 / (4.0 * math.pi)
-    lat_hi[...], lat_lo[...] = split(lattice[...])
+    coarse[32], coarse[33] = split(lattice[...])
     first = split(uc2e[...] * scale)
 
     plane = split(column[...])
@@ -299,18 +357,20 @@
         at = slice(o * COEF, (o + 1) * COEF)
         return jnp.concatenate([rows[0, at], rows[1, at, 0 : COEF - LANE]], axis=1)
 
+    io.wait(0)
     square(m2m, rows)
     pieces = []
     for o in range(8):
         high, low = split(matrix(o))
-        m2m_hi[o], m2m_lo[o] = high, low
+        coarse[o], coarse[8 + o] = high, low
         pieces.append(dot3((high, low), first))
     stack(pieces, 0)
+    io.wait(1)
     square(l2l, rows)
     pieces = []
     for o in range(8):
         value = matrix(o)
-        l2l_hi[o], l2l_lo[o] = split(value)
+        coarse[16 + o], coarse[24 + o] = split(value)
         pieces.append(jnp.transpose(value) * scale)
     stack(pieces, COEF)
     high, low = split(dc2e[...])
@@ -323,7 +383,9 @@
         d_lo[h] = dot(low, here).astype(bf16)
 
 
-def route_kernel(own, cap, n_top, pos, dens, slot, leaf, out, entries):
+def route_kernel(own, cap, n_top, io):
+    pos, dens, slot, leaf = io.ins
+    out, entries = io.outs
     points = pos.shape[1]
     owners = out.shape[0]
     slots = slot[...]
@@ -380,7 +442,9 @@
                 out[at, q, 8:] = leaves
 
 
-def restore_kernel(n_top, got, entries, out):
+def restore_kernel(n_top, io):
+    got, entries = io.ins
+    out = io.outs[0]
     devices = got.shape[0]
     per = out.shape[0] // n_top
     cap = got.shape[2] // per
@@ -451,17 +515,17 @@
     return place
 
 
-def points_kernel(n_top, box_cap, me_ref, got, *refs):
-    column, oper_hbm, out, field, place, offsets, buf, surf, oper, sem = refs
-    fetch = pltpu.make_async_copy(oper_hbm, oper, sem)
-    fetch.start()
+def points_kernel(n_top, box_cap, io, offsets, buf, surf):
+    got, column, oper = io.ins
+    out, field, place = io.outs
     sources, _, cap = got.shape
     lanes = min(cap, LANE)
     own = field.shape[1]
     wide = up(cap, LANE)
-    me = me_ref[0]
+    me = io.scalars[0][0]
     buf[...] = jnp.zeros_like(buf)
     fill_surface(surf, column)
+    io.wait(0)
 
     def put(i, offset):
         values = [got[i * STRIP + s, 0:8] for s in range(STRIP)]
@@ -481,7 +545,7 @@
     leaf = leaf.astype(jnp.int32)
     first = got[me * n_top, 8:9, 0:1].astype(jnp.int32) >> 3
     offsets[sources] = jnp.sum(got[me * n_top, 8:9, 0:1]).astype(jnp.int32) >> 3
-    fetch.wait()
+    io.wait(2)
     table = jnp.concatenate([(leaf >> 3) - first, leaf & 7], axis=1).astype(f32)
     table = jnp.transpose(table).astype(bf16)
     out_rows = out.shape[1]
@@ -507,6 +571,7 @@
     digits = jnp.broadcast_to(digits, (2, out_rows))
     blank = jnp.zeros((out.shape[0] - COEF - 2, out_rows), f32)
     out[...] = jnp.concatenate([total, digits, blank], axis=0).astype(bf16)
+    io.send(0)
 
 
 def box_ids(parts, dens):
@@ -524,23 +589,11 @@
     return jnp.concatenate([p[0:COEF, k * width : (k + 1) * width] for p in parts], axis=1)
 
 
-def translate_kernel(slabs, dens, me_ref, *refs):
-    parts = refs[:-14]
-    pieces = refs[-14:-8]
-    out, xs, xin, acc, ma, mb, mc, sem = refs[-8:]
-    copies = []
-    for j in range(4):
-        row = 0
-        for h in range(2):
-            for i, dst in enumerate((ma, mb, mc)):
-                src = pieces[3 * h + i]
-                if j < src.shape[0]:
-                    rows = pl.ds(row, src.shape[2])
-                    copy = pltpu.make_async_copy(src.at[j], dst.at[j, :, rows], sem.at[h, i, j])
-                    copy.start()
-                    copies.append(copy)
-            row += pieces[3 * h].shape[2]
-    x0 = (me_ref[0] // 2 * 2) * SIDE // len(parts)
+def translate_kernel(slabs, dens, io, xs, xin, acc):
+    parts = io.ins[:-6]
+    first, rest = io.ins[-6:-3], io.ins[-3:]
+    out = io.outs[0]
+    x0 = (io.scalars[0][0] // 2 * 2) * SIDE // len(parts)
     ids = box_ids(parts, dens)
     place = morton_place(ids)
     place = (((place >> 6) - x0 + REACH) & 7) * 64 + (place & 63)
@@ -566,23 +619,25 @@
             xs[rows, :] = jnp.concatenate([shifted[z] for z in SHIFTS] + pad, axis=1).astype(bf16)
             pad = [jnp.zeros((PLANE, WIN - 4 * COEF), f32)]
             xin[rows, :] = jnp.concatenate([shifted[z] for z in OUTER] + pad, axis=1).astype(bf16)
-    for c in copies:
-        c.wait()
+
+    def rows_of(i, j):
+        value = jnp.concatenate([first[i][j], rest[i][j]], axis=1)
+        return value.reshape(-1, value.shape[2])
+
     n_out = len(OUTER) * ROWS
     n_all = len(SHIFTS) * ROWS
     for i, dx in enumerate(OUTER + INNER):
         rows = pl.ds((dx + REACH) * columns, slabs * columns)
         source = xs[rows, :]
         if dx in OUTER:
-            term = dot(ma[OUTER.index(dx)].reshape(n_all, WFULL), source, NT)
+            term = dot(rows_of(0, OUTER.index(dx)), source, NT)
             if i == 0:
                 acc[...] = term
             else:
                 acc[...] += term
         else:
-            acc[0:n_out] += dot(mb[INNER.index(dx)].reshape(n_out, WFULL), source, NT)
-            inner = mc[INNER.index(dx)].reshape(n_all - n_out, WIN)
-            acc[n_out:n_all] += dot(inner, xin[rows, :], NT)
+            acc[0:n_out] += dot(rows_of(1, INNER.index(dx)), source, NT)
+            acc[n_out:n_all] += dot(rows_of(2, INNER.index(dx)), xin[rows, :], NT)
     lane = lax.broadcasted_iota(jnp.int32, (ROWS, LANE), 1)
     for t in range(slabs * columns // LANE):
         total = jnp.zeros((ROWS, LANE), f32)
@@ -597,14 +652,10 @@
         out[:, t * LANE : (t + 1) * LANE] = total.astype(out.dtype)
 
 
-def coarse_kernel(*refs):
-    parts = refs[:-14]
-    out = refs[-8]
-    m2m_hi, m2m_lo, lat_hi, lat_lo, l2l_hi, l2l_lo, sem = refs[-7:]
-    copies = []
-    for i in range(6):
-        copies.append(pltpu.make_async_copy(refs[-14 + i], refs[-7 + i], sem.at[i]))
-        copies[-1].start()
+def coarse_kernel(io):
+    out = io.outs[0]
+    parts = io.ins[:-1]
+    opers = io.ins[-1]
     dens = out.shape[0]
     box = ids = box_ids(parts, dens)
     place = ((box & 7) << 6) + (box & 56) + (box >> 6)
@@ -613,48 +664,47 @@
     there = jnp.where(at == place, 1.0, 0.0).astype(bf16)
     level = [dot(there, all_parts(parts, k, dens), NT) for k in range(dens)]
 
-    for copy in copies:
-        copy.wait()
-
-    def oper(hi, lo, o):
-        return hi[o], lo[o]
+    io.wait(*range(len(io.ins)))
 
     for _ in range(LEVEL):
         count = level[0].shape[0] // 8
         total = None
         for o in range(8):
             rows = jnp.concatenate([v[o * count : (o + 1) * count] for v in level], axis=0)
-            term = dot3_rows(split(rows), oper(m2m_hi, m2m_lo, o), NT)
+            term = dot3_rows(split(rows), (opers[o], opers[8 + o]), NT)
             total = term if total is None else total + term
         level = [total[k * count : (k + 1) * count] for k in range(dens)]
     rows = jnp.concatenate(level, axis=0)
-    rows = dot3(split(rows), (lat_hi[...], lat_lo[...]), NT)
+    rows = dot3(split(rows), (opers[32], opers[33]), NT)
     level = [rows[k : k + 1] for k in range(dens)]
     for _ in range(LEVEL):
         count = level[0].shape[0]
         rows = split(jnp.concatenate(level, axis=0))
-        children = [dot3_rows(rows, oper(l2l_hi, l2l_lo, o), NT) for o in range(8)]
+        children = [dot3_rows(rows, (opers[16 + o], opers[24 + o]), NT) for o in range(8)]
         level = [
             jnp.concatenate([c[k * count : (k + 1) * count] for c in children], axis=0)
             for k in range(dens)
         ]
-    at = lax.broadcasted_iota(jnp.int32, (BOXES4, BOXES4), 1)
+    at = lax.broadcasted_iota(jnp.int32, (1, BOXES4), 1)
+    number = jnp.zeros_like(at)
+    for b in range(LEVEL):
+        digit = ((at >> (2 * LEVEL + b)) & 1) * 4 + ((at >> (LEVEL + b)) & 1) * 2 + ((at >> b) & 1)
+        number = number + (digit << (3 * (LEVEL - 1 - b)))
     row = lax.broadcasted_iota(jnp.int32, (BOXES4, BOXES4), 0)
-    number = ((row & 7) << 6) + (row & 56) + (row >> 6)
-    move = jnp.where(at == morton_place(number), 1.0, 0.0).astype(bf16)
+    move = jnp.where(row == number, 1.0, 0.0).astype(bf16)
     for k in range(dens):
         high, low = split(level[k])
         out[k] = dot(high, move, TURNED) + dot(low, move, TURNED)
 
 
-def evaluate_kernel(slabs, step, window, me_ref, *refs):
+def evaluate_kernel(slabs, step, window, io, stack, found):
     n = SIDE // slabs
-    checks = refs[: 2 * n]
-    d_hi, d_lo, lattice, field_hbm, place, offsets, out, stack, found, field, sem = refs[2 * n :]
-    fetch = pltpu.make_async_copy(field_hbm, field, sem)
-    fetch.start()
-    core = me_ref[0] & 1
-    group = me_ref[0] // step
+    checks = io.ins[: 2 * n]
+    d_hi, d_lo, lattice, place, field = io.ins[2 * n :]
+    offsets = io.scalars[1]
+    out = io.outs[0]
+    core = io.scalars[0][0] & 1
+    group = io.scalars[0][0] // step
     dens = lattice.shape[0]
     sources, cap = out.shape[0], out.shape[2] // dens
     lane = lax.broadcasted_iota(jnp.int32, (COEF, LANE), 1)
@@ -695,7 +745,7 @@
         [dot(stack[h * half : (h + 1) * half].astype(bf16), pick) for h in range(2)], axis=1
     ).astype(bf16)
     found[:, place.shape[1] :] = jnp.zeros((8, found.shape[1] - place.shape[1]), f32)
-    fetch.wait()
+    io.wait(*range(len(io.ins)))
 
     def block(j, carry):
         at = pl.ds(pl.multiple_of(j * PB, PB), PB)
@@ -759,120 +809,110 @@
     def shape(*dims, dtype=bf16):
         return jax.ShapeDtypeStruct(dims, dtype)
 
-    outgoing, entries = call(
+    outgoing, entries = run(
         functools.partial(route_kernel, own, cap, n_top),
-        (shape(n_pts, n_top, rows, cap, dtype=f32), shape(1, points, dtype=jnp.int32)),
-        GRANT,
+        [],
+        [
+            local_pos,
+            densities,
+            morton_slot.reshape(1, points),
+            slot_leaf.reshape(points // lanes, lanes),
+        ],
+        [shape(n_pts, n_top, rows, cap, dtype=f32), shape(1, points, dtype=jnp.int32)],
         1 << 27,
-        in_specs=[WHOLE] * 4,
-        out_specs=(WHOLE, WHOLE),
-    )(
-        local_pos,
-        densities,
-        morton_slot.reshape(1, points),
-        slot_leaf.reshape(points // lanes, lanes),
+        stays=(1,),
+        grant=GRANT_FIRST,
     )
     outgoing = outgoing.reshape(sources, rows, cap)
     incoming = lax.all_to_all(outgoing, ("pts", "top"), split_axis=0, concat_axis=0, tiled=True)
 
     flat = (-1, LANE)
     column = jnp.asarray(column_table())
-    square_shape = shape(8, coef, coef)
-    w_both, *coarse_ops = call(
+    w_both, opers, *halves = run(
         operators_kernel,
-        (shape(2 * coef, 8 * CPAD),)
-        + (square_shape,) * 4
-        + (shape(coef, coef),) * 2
-        + (shape(2, coef, ROWS),) * 2,
-        GRANT,
+        [],
+        [m2m.reshape(flat), l2l.reshape(flat), uc2e, dc2e, lattice, column],
+        [shape(2 * coef, 8 * CPAD), shape(34, coef, coef)] + [shape(2, coef, ROWS)] * 2,
         1 << 30,
-        in_specs=[WHOLE] * 6,
-        out_specs=(WHOLE,) * 9,
-        scratch_shapes=[pltpu.VMEM((2, 8 * coef, LANE), f32)],
-    )(m2m.reshape(flat), l2l.reshape(flat), uc2e, dc2e, lattice, column)
-    coarse_ops, halves = coarse_ops[:6], coarse_ops[6:]
-    m2m_hi, m2m_lo, l2l_hi, l2l_lo, lat_hi, lat_lo = coarse_ops
-    coarse_ops = (m2m_hi, m2m_lo, lat_hi, lat_lo, l2l_hi, l2l_lo)
-    first = relayout(m2l_ops, me, 0, EARLY)
+        late=(0, 1),
+        stays=range(4),
+        scratch=[pltpu.VMEM((2, 8 * coef, LANE), f32)],
+    )
+    first = relayout(m2l_ops, me, 0, EARLY, GRANT_EARLY)
     incoming, first = lax.optimization_barrier((incoming, first))
 
-    partial, field, place, offsets = call(
+    partial, field, place, offsets = run(
         functools.partial(points_kernel, n_top, box_cap),
-        (
+        [me],
+        [incoming, column, w_both],
+        [
             shape(up(coef + 2, 16), dens * box_cap),
             shape(coef, own, dtype=f32),
             shape(1, own, dtype=jnp.int32),
-            shape(sources + 1, dtype=jnp.int32),
-        ),
-        GRANT,
+        ],
         8 << 30,
-        in_specs=[SMEM] + [WHOLE] * 2 + [ANY],
-        out_specs=(WHOLE, WHOLE, WHOLE, SMEM),
-        scratch_shapes=[
+        late=(0,),
+        here=(2,),
+        stays=(1, 2),
+        numbers=[shape(sources + 1, dtype=jnp.int32)],
+        scratch=[
             pltpu.VMEM((8, up(own + up(cap, LANE) + LANE, PB)), f32),
             pltpu.VMEM((3 + FEATURES, coef, PB), f32),
-            pltpu.VMEM(w_both.shape, bf16),
-            pltpu.SemaphoreType.DMA,
         ],
-    )(me, incoming, column, w_both)
+    )
     later, flat_ops = lax.optimization_barrier((partial, m2l_ops))
-    rest = relayout(flat_ops, me, EARLY, STEPS - EARLY)
+    rest = relayout(flat_ops, me, EARLY, STEPS - EARLY, GRANT_LATER)
     parts, rest = gather_by(later, range(n_pts), rest)
 
     columns = dens * PLANE
-    checks = call(
+    (checks,) = run(
         functools.partial(translate_kernel, slabs, dens),
-        shape(ROWS, slabs * columns),
-        GRANT,
+        [me],
+        [*parts, *first, *rest],
+        [shape(ROWS, slabs * columns)],
         8 << 30,
-        in_specs=[SMEM] + [WHOLE] * n_pts + [ANY] * 6,
-        out_specs=WHOLE,
-        scratch_shapes=[
+        here=range(n_pts, n_pts + 6),
+        scratch=[
             pltpu.VMEM(((7 + slabs - 1) * columns, WFULL), bf16),
             pltpu.VMEM(((7 + slabs - 1) * columns, WIN), bf16),
             pltpu.VMEM((7 * ROWS, slabs * columns), f32),
-            *[pltpu.VMEM((a, b, ROWS, c), bf16) for a, b, c in PIECES],
-            pltpu.SemaphoreType.DMA((2, 3, 4)),
         ],
-    )(me, *parts, *first, *rest)
-    lattice4 = call(
+    )
+    (lattice4,) = run(
         coarse_kernel,
-        shape(dens, coef, BOXES4, dtype=f32),
-        GRANT,
+        [],
+        [*parts, opers],
+        [shape(dens, coef, BOXES4, dtype=f32)],
         4 << 30,
-        in_specs=[WHOLE] * n_pts + [ANY] * 6,
-        out_specs=WHOLE,
-        scratch_shapes=[pltpu.VMEM(v.shape, bf16) for v in coarse_ops]
-        + [pltpu.SemaphoreType.DMA((6,))],
-    )(*parts, *coarse_ops)
-
+        here=(n_pts,),
+        stays=(0,),
+    )
     step = n_pts // SIDE * slabs
     distances = [step * m + c for m in range(SIDE // slabs) for c in range(2)]
     gathered, lattice4 = gather_by(checks, distances, lattice4)
 
-    reply = call(
+    (reply,) = run(
         functools.partial(evaluate_kernel, slabs, step, box_cap),
-        shape(sources, 1, dens * cap, dtype=f32),
-        GRANT,
+        [me, offsets],
+        [*gathered, *halves, lattice4, place, field],
+        [shape(sources, 1, dens * cap, dtype=f32)],
         4 << 30,
-        in_specs=[SMEM] + [WHOLE] * (len(gathered) + 3) + [ANY, WHOLE, SMEM],
-        out_specs=WHOLE,
-        scratch_shapes=[
+        here=range(len(gathered), len(gathered) + 5),
+        scratch=[
             pltpu.VMEM((2 * dens * CPAD, BOXES4), f32),
             pltpu.VMEM((8, own + up(cap, LANE) + LANE), f32),
-            pltpu.VMEM(field.shape, f32),
-            pltpu.SemaphoreType.DMA,
         ],
-    )(me, *gathered, *halves, lattice4, field, place, offsets)
+    )
     returned = lax.all_to_all(reply, ("pts", "top"), split_axis=0, concat_axis=0, tiled=True)
-    return call(
+    (out,) = run(
         functools.partial(restore_kernel, n_top),
-        shape(DENS, points, dtype=f32),
-        GRANT,
+        [],
+        [returned, entries],
+        [shape(DENS, points, dtype=f32)],
         1 << 28,
-        in_specs=[WHOLE] * 2,
-        out_specs=WHOLE,
-    )(returned, entries)
+        here=(1,),
+    )
+    return out
 
 
 def solution(mesh):

time: 103 us -> 89.9 us (0.87)
  Pallas kernels: 66.7 us -> 55.9 us
    pallas_call x7, Pallas kernels: 47.3 us -> 37.5 us  [run(): call(body, tuple(outs) + tuple(numbers), grant, flops, in_specs=[SMEM] *...]
    unnamed x34 -> x20, local copies, waits for them, and re-layouts: 2.53 us -> 1.54 us
  transfers between devices with their start and end apart: 15 -> 15, of which waited for: 8 -> 8; matrix products, arithmetic and copies ran while one was open for 1% -> 0% of each run, Pallas kernels for 33% -> 33%
where the time goes in v5:
time: 89.9 us; the launch traced here: 89.4 us
  Pallas kernels  55.9 us (62%)
  starting transfers between devices  16.6 us (18%)
  blocking collectives  13.2 us (15%)
  waiting for transfers between devices  1.81 us (2%)
  local copies, waits for them, and re-layouts  1.54 us (2%)
    pallas_call x7, Pallas kernels, run(): call(body, tuple(outs) + tuple(numbers), grant, flops, in_specs=[SMEM] *...  37.5 us
    pallas_call x2, Pallas kernels, relayout(): call(functools.partial(relayout_kernel, nrows, step0, steps), tuple((jax....  18.4 us
    all_to_all x1, blocking collectives, per_device(): lax.all_to_all(reply, ('pts', 'top'), split_axis=0, concat_axis=0, tiled=...  13.2 us
    ppermute x14, starting transfers between devices, shift_by(): return lax.ppermute(value, axis, [(i, i ^ distance) for i in range(size)])  9.28 us
    all_to_all x1, starting transfers between devices, per_device(): lax.all_to_all(outgoing, ('pts', 'top'), split_axis=0, concat_axis=0, til...  7.3 us
    ppermute x14, waiting for transfers between devices, shift_by(): return lax.ppermute(value, axis, [(i, i ^ distance) for i in range(size)])  1.81 us
  transfers between devices with their start and end apart: 15, of which 8 were waited for; matrix products, arithmetic and copies ran while one was open for 0% of the time, Pallas kernels for 33%

profile of v5, /device:TPU:0, one launch (start us, length us, event | category | flops | bytes accessed | tf_op | source)
XLA Modules:
  0.0 89.4 jit_solution(4562121524839092587)
XLA Ops:
  0.0 3.9 %shard_map.109 = (f32[8,4,16,256]{3,2,1,0:T(8,128)}, s32[1,1024]{1,0:T(1,128)}) custom-call(f32[3,1024]{1,0:T(4,128)} %refs_0_.1, f32[8,1024]{1,0:T(8,128)} %refs_1_.1, s32[1,1024]{1,0:T(1,128)} %bitcast.16, s32[8,128]{1,0:T(8,128)} %bitcast.17), custom_call_target="tpu_custom_call" | custom-call | flops 134217728 | bytes 1048576 | tf_op jit(solution)/shard_map/pallas_call | solution.py:160
  3.9 7.3 %all-to-all-start = ((f32[32,16,256]{2,1,0:T(8,128)}), f32[32,16,256]{2,1,0:T(8,128)S(1)}, u32[]{:S(2)}, u32[]{:S(2)}) async-start(f32[32,16,256]{2,1,0:T(8,128)} %bitcast.15), calls=%async_computation | async-start | bytes 1048576 | tf_op jit(solution)/shard_map/all_to_all | solution.py:827
  11.3 11.0 %shard_map.110 = (bf16[4,7,48,1152]{3,2,1,0:T(8,128)(2,1)}, bf16[3,4,48,1152]{3,2,1,0:T(8,128)(2,1)S(1)}, bf16[3,3,48,640]{3,2,1,0:T(8,128)(2,1)S(1)}) custom-call(s32[2]{0:T(128)S(1)} %pad_add_fusion.me_ref.refs_0_, bf16[57038,128]{1,0:T(8,128)(2,1)} %bitcast.11, bf16[57038,128]{1,0:T(8,128)(2,1)} %bitcast.12), custom_call_target="tpu_custom_call" | custom-call | flops 1048576 | bytes 6291456 | tf_op jit(solution)/shard_map/pallas_call | solution.py:295
  22.4 4.9 %shard_map.111 = (bf16[304,1280]{1,0:T(8,128)(2,1)S(1)}, bf16[34,152,152]{2,1,0:T(8,128)(2,1)S(1)}, bf16[2,152,80]{2,1,0:T(8,128)(2,1)S(1)}, bf16[2,152,80]{2,1,0:T(8,128)(2,1)S(1)}) custom-call(f32[1444,128]{1,0:T(8,128)S(1)} %bitcast.9, f32[1444,128]{1,0:T(8,128)S(1)} %bitcast.10, f32[152,152]{1,0:T(8,128)S(1)} %copy-done.3, f32[152,152]{1,0:T(8,128)S(1)} %copy-done.4, ...), custom_call_target="tpu_custom_call" | custom-call | flops 1073741824 | bytes 1048576 | tf_op jit(solution)/shard_map/pallas_call | solution.py:160
  27.3 1.5 %copy-done.7 = bf16[34,152,152]{2,1,0:T(8,128)(2,1)} copy-done((bf16[34,152,152]{2,1,0:T(8,128)(2,1)}, bf16[34,152,152]{2,1,0:T(8,128)(2,1)S(1)}, u32[]{:S(2)}) %copy-start.7) | copy-done | bytes 1571096
  28.8 11.3 %shard_map.112 = (bf16[160,256]{1,0:T(8,128)(2,1)S(1)}, f32[152,4096]{1,0:T(8,128)S(1)}, s32[1,4096]{1,0:T(1,128)S(1)}, s32[33]{0:T(128)S(1)}) custom-call(s32[2]{0:T(128)S(1)} %pad_add_fusion.me_ref.refs_0_, f32[32,16,256]{2,1,0:T(8,128)S(1)} %all-to-all-done.refs_1_, f32[152,128]{1,0:T(8,128)S(1)} %copy-done.6, bf16[304,1280]{1,0:T(8,128)(2,1)S(1)} %get-tuple-element.44.refs_3_), custom_call_target="tpu_custom_call" | custom-call | flops 8589934592 | bytes 1048576 | tf_op jit(solution)/shard_map/pallas_call | solution.py:160
  40.0 2.7 %collective-permute-start.2 = (bf16[160,256]{1,0:T(8,128)(2,1)S(1)}, bf16[160,256]{1,0:T(8,128)(2,1)S(1)}, u32[]{:S(2)}, u32[]{:S(2)}) collective-permute-start(bf16[160,256]{1,0:T(8,128)(2,1)S(1)} %get-tuple-element.52.refs_1_.refs_0_), channel_id=1, source_target_pairs={{0,24},{4,28},{8,16},{12,20},{16,8},{20,12},{24,0},{28,4},{1,25},{... | collective-permute-start | bytes 245768 | tf_op jit(solution)/shard_map/ppermute | solution.py:782
  42.8 0.6 collective-permute-start.1
  43.3 0.3 collective-permute-start
  43.6 7.4 %shard_map.113 = (bf16[4,7,32,1152]{3,2,1,0:T(8,128)(2,1)S(1)}, bf16[3,4,32,1152]{3,2,1,0:T(8,128)(2,1)S(1)}, bf16[3,3,32,640]{3,2,1,0:T(8,128)(2,1)S(1)}) custom-call(s32[2]{0:T(128)S(1)} %pad_add_fusion.me_ref.refs_0_, bf16[57038,128]{1,0:T(8,128)(2,1)} %bitcast.13, bf16[57038,128]{1,0:T(8,128)(2,1)} %bitcast.14), custom_call_target="tpu_custom_call" | custom-call | flops 1048576 | bytes 4194304 | tf_op jit(solution)/shard_map/pallas_call | solution.py:295
  51.1 0.5 collective-permute-start.4
  51.6 0.1 collective-permute-start.5
  51.7 0.4 collective-permute-start.6
  52.1 0.3 collective-permute-done.3.refs_2_.refs_1_
  52.4 0.2 collective-permute-done.4.refs_4_.refs_3_
  52.5 0.4 collective-permute-done.5.refs_6_.refs_5_
  52.9 0.2 collective-permute-done.6.refs_8_.refs_7_
  53.0 5.6 %shard_map.114.refs_2_ = bf16[80,256]{1,0:T(8,128)(2,1)S(1)} custom-call(s32[2]{0:T(128)S(1)} %pad_add_fusion.me_ref.refs_0_, bf16[160,256]{1,0:T(8,128)(2,1)S(1)} %get-tuple-element.52.refs_1_.refs_0_, bf16[160,256]{1,0:T(8,128)(2,1)S(1)} %collective-permute-done.3.refs_2_.refs_1_, bf16[160,256]{1,0:T(8,128)(2,1)S(1)} %collective-permute-done.refs_3_.refs_2_, ...), custom_call_target="tpu_custom_call" | custom-call | flops 8589934592 | bytes 1048576 | tf_op jit(solution)/shard_map/pallas_call | solution.py:160
  58.6 2.7 %collective-permute-start.9 = (bf16[80,256]{1,0:T(8,128)(2,1)S(1)}, bf16[80,256]{1,0:T(8,128)(2,1)S(1)}, u32[]{:S(2)}, u32[]{:S(2)}) collective-permute-start(bf16[80,256]{1,0:T(8,128)(2,1)S(1)} %shard_map.114.refs_2_), channel_id=1, source_target_pairs={{0,24},{4,28},{8,16},{12,20},{16,8},{20,12},{24,0},{28,4},{1,25},{... | collective-permute-start | bytes 122888 | tf_op jit(solution)/shard_map/ppermute | solution.py:782
  61.4 0.6 collective-permute-start.8
  61.9 0.3 collective-permute-start.7
  62.2 6.1 %shard_map.115.refs_12_ = f32[2,152,512]{2,1,0:T(8,128)S(1)} custom-call(bf16[160,256]{1,0:T(8,128)(2,1)S(1)} %get-tuple-element.52.refs_1_.refs_0_, bf16[160,256]{1,0:T(8,128)(2,1)S(1)} %collective-permute-done.3.refs_2_.refs_1_, bf16[160,256]{1,0:T(8,128)(2,1)S(1)} %collective-permute-done.refs_3_.refs_2_, ...), custom_call_target="tpu_custom_call" | custom-call | flops 4294967296 | bytes 1048576 | tf_op jit(solution)/shard_map/pallas_call | solution.py:160
  68.4 0.5 collective-permute-start.11
  68.9 0.1 collective-permute-start.12
  69.0 0.4 collective-permute-start.13
  69.4 0.2 collective-permute-done.10.refs_3_
  69.6 0.2 collective-permute-done.11.refs_5_
  69.8 0.3 collective-permute-done.12.refs_7_
  70.1 0.2 collective-permute-done.13.refs_9_
  70.3 4.5 %shard_map.116 = f32[32,1,512]{2,1,0:T(1,128)S(1)} custom-call(s32[2]{0:T(128)S(1)} %pad_add_fusion.me_ref.refs_0_, s32[33]{0:T(128)S(1)} %get-tuple-element.45.refs_1_, bf16[80,256]{1,0:T(8,128)(2,1)S(1)} %shard_map.114.refs_2_, bf16[80,256]{1,0:T(8,128)(2,1)S(1)} %collective-permute-done.10.refs_3_, bf16[80,256]{1,0:T(8,128)(2,1)S(1)} %collective-permute-done.7.refs_4_, ...), custom_call_target="tpu_custom_call" | custom-call | flops 4294967296 | bytes 1048576 | tf_op jit(solution)/shard_map/pallas_call | solution.py:160
  74.8 13.2 %all_to_all.10.refs_0_ = f32[32,1,512]{2,1,0:T(1,128)S(1)} all-to-all(f32[32,1,512]{2,1,0:T(1,128)S(1)} %shard_map.116), channel_id=1, replica_groups=mesh['pts'=8,'top'=4] {'pts','top'}, dimensions={0} | all-to-all | bytes 131072 | tf_op jit(solution)/shard_map/all_to_all | solution.py:906
  87.9 1.4 %shard_map.117 = f32[8,1024]{1,0:T(8,128)} custom-call(f32[32,1,512]{2,1,0:T(1,128)S(1)} %all_to_all.10.refs_0_, s32[1,1024]{1,0:T(1,128)S(1)} %copy-done.9), custom_call_target="tpu_custom_call" | custom-call | flops 268435456 | bytes 1048576 | tf_op jit(solution)/shard_map/pallas_call | solution.py:160
  (29 shorter events, 0.3 us)
Async XLA Ops:
  3.9 24.9 %all-to-all-start = ((f32[32,16,256]{2,1,0:T(8,128)}), f32[32,16,256]{2,1,0:T(8,128)S(1)}, u32[]{:S(2)}, u32[]{:S(2)}) async-start(f32[32,16,256]{2,1,0:T(8,128)} %bitcast.15), calls=%async_computation | async-start | bytes 1048576 | tf_op jit(solution)/shard_map/all_to_all | solution.py:827
  11.3 11.0 %copy-start.1 = (f32[184832]{0:T(1024)S(1)}, f32[184832]{0:T(1024)}, u32[]{:S(2)}) copy-start(f32[184832]{0:T(1024)} %param.16) | copy-start | bytes 2217988
  11.3 11.0 %copy-start.2 = (f32[184832]{0:T(1024)S(1)}, f32[184832]{0:T(1024)}, u32[]{:S(2)}) copy-start(f32[184832]{0:T(1024)} %param.20) | copy-start | bytes 2217988
  11.3 11.0 %copy-start.3 = (f32[152,152]{1,0:T(8,128)S(1)}, f32[152,152]{1,0:T(8,128)}, u32[]{:S(2)}) copy-start(f32[152,152]{1,0:T(8,128)} %refs_2_.2) | copy-start | bytes 277252
  11.3 11.1 %copy-start.4 = (f32[152,152]{1,0:T(8,128)S(1)}, f32[152,152]{1,0:T(8,128)}, u32[]{:S(2)}) copy-start(f32[152,152]{1,0:T(8,128)} %refs_3_.1) | copy-start | bytes 277252
  11.3 11.1 %copy-start.5 = (f32[152,152]{1,0:T(8,128)S(1)}, f32[152,152]{1,0:T(8,128)}, u32[]{:S(2)}) copy-start(f32[152,152]{1,0:T(8,128)} %refs_4_.1) | copy-start | bytes 277252
  11.3 11.1 %copy-start.6 = (f32[152,128]{1,0:T(8,128)S(1)}, f32[152,128]{1,0:T(8,128)}, u32[]{:S(2)}) copy-start(f32[152,128]{1,0:T(8,128)} %constant.11.clone.refs_5_.refs_2_) | copy-start | bytes 233476
  27.2 1.5 %copy-start.7 = (bf16[34,152,152]{2,1,0:T(8,128)(2,1)}, bf16[34,152,152]{2,1,0:T(8,128)(2,1)S(1)}, u32[]{:S(2)}) copy-start(bf16[34,152,152]{2,1,0:T(8,128)(2,1)S(1)} %get-tuple-element.62.refs_8_) | copy-start | bytes 4713220
  40.0 11.0 %collective-permute-start.2 = (bf16[160,256]{1,0:T(8,128)(2,1)S(1)}, bf16[160,256]{1,0:T(8,128)(2,1)S(1)}, u32[]{:S(2)}, u32[]{:S(2)}) collective-permute-start(bf16[160,256]{1,0:T(8,128)(2,1)S(1)} %get-tuple-element.52.refs_1_.refs_0_), channel_id=1, source_target_pairs={{0,24},{4,28},{8,16},{12,20},{16,8},{20,12},{24,0},{28,4},{1,25},{... | collective-permute-start | bytes 245768 | tf_op jit(solution)/shard_map/ppermute | solution.py:782
  42.8 8.2 %collective-permute-start.1 = (bf16[160,256]{1,0:T(8,128)(2,1)S(1)}, bf16[160,256]{1,0:T(8,128)(2,1)S(1)}, u32[]{:S(2)}, u32[]{:S(2)}) collective-permute-start(bf16[160,256]{1,0:T(8,128)(2,1)S(1)} %get-tuple-element.52.refs_1_.refs_0_), channel_id=1, source_target_pairs={{0,16},{4,20},{8,24},{12,28},{16,0},{20,4},{24,8},{28,12},{1,17},{... | collective-permute-start | bytes 245768 | tf_op jit(solution)/shard_map/ppermute | solution.py:782
  43.3 7.7 %collective-permute-start = (bf16[160,256]{1,0:T(8,128)(2,1)S(1)}, bf16[160,256]{1,0:T(8,128)(2,1)S(1)}, u32[]{:S(2)}, u32[]{:S(2)}) collective-permute-start(bf16[160,256]{1,0:T(8,128)(2,1)S(1)} %get-tuple-element.52.refs_1_.refs_0_), channel_id=1, source_target_pairs={{0,8},{4,12},{8,0},{12,4},{16,24},{20,28},{24,16},{28,20},{1,9},{5... | collective-permute-start | bytes 245768 | tf_op jit(solution)/shard_map/ppermute | solution.py:782
  43.6 9.4 %copy-start = (bf16[4,7,48,1152]{3,2,1,0:T(8,128)(2,1)S(1)}, bf16[4,7,48,1152]{3,2,1,0:T(8,128)(2,1)}, u32[]{:S(2)}) copy-start(bf16[4,7,48,1152]{3,2,1,0:T(8,128)(2,1)} %get-tuple-element.56.refs_9_) | copy-start | bytes 9289732
  51.0 11.2 %copy-start.8 = (bf16[34,152,152]{2,1,0:T(8,128)(2,1)S(1)}, bf16[34,152,152]{2,1,0:T(8,128)(2,1)}, u32[]{:S(2)}) copy-start(bf16[34,152,152]{2,1,0:T(8,128)(2,1)} %copy-done.7) | copy-start | bytes 4713220
  51.0 1.3 %collective-permute-start.3 = (bf16[160,256]{1,0:T(8,128)(2,1)S(1)}, bf16[160,256]{1,0:T(8,128)(2,1)S(1)}, u32[]{:S(2)}, u32[]{:S(2)}) collective-permute-start(bf16[160,256]{1,0:T(8,128)(2,1)S(1)} %get-tuple-element.52.refs_1_.refs_0_), channel_id=1, source_target_pairs={{0,4},{4,0},{8,12},{12,8},{16,20},{20,16},{24,28},{28,24},{1,5},{5... | collective-permute-start | bytes 245768 | tf_op jit(solution)/shard_map/ppermute | solution.py:782
  51.1 1.4 %collective-permute-start.4 = (bf16[160,256]{1,0:T(8,128)(2,1)S(1)}, bf16[160,256]{1,0:T(8,128)(2,1)S(1)}, u32[]{:S(2)}, u32[]{:S(2)}) collective-permute-start(bf16[160,256]{1,0:T(8,128)(2,1)S(1)} %collective-permute-done.refs_3_.refs_2_), channel_id=1, source_target_pairs={{0,4},{4,0},{8,12},{12,8},{16,20},{20,16},{24,28},{28,24},{1,5},{5... | collective-permute-start | bytes 245768 | tf_op jit(solution)/shard_map/ppermute | solution.py:782
  51.6 1.3 %collective-permute-start.5 = (bf16[160,256]{1,0:T(8,128)(2,1)S(1)}, bf16[160,256]{1,0:T(8,128)(2,1)S(1)}, u32[]{:S(2)}, u32[]{:S(2)}) collective-permute-start(bf16[160,256]{1,0:T(8,128)(2,1)S(1)} %collective-permute-done.1.refs_5_.refs_4_), channel_id=1, source_target_pairs={{0,4},{4,0},{8,12},{12,8},{16,20},{20,16},{24,28},{28,24},{1,5},{5... | collective-permute-start | bytes 245768 | tf_op jit(solution)/shard_map/ppermute | solution.py:782
  51.7 1.4 %collective-permute-start.6 = (bf16[160,256]{1,0:T(8,128)(2,1)S(1)}, bf16[160,256]{1,0:T(8,128)(2,1)S(1)}, u32[]{:S(2)}, u32[]{:S(2)}) collective-permute-start(bf16[160,256]{1,0:T(8,128)(2,1)S(1)} %collective-permute-done.2.refs_7_.refs_6_), channel_id=1, source_target_pairs={{0,4},{4,0},{8,12},{12,8},{16,20},{20,16},{24,28},{28,24},{1,5},{5... | collective-permute-start | bytes 245768 | tf_op jit(solution)/shard_map/ppermute | solution.py:782
  58.6 9.7 %collective-permute-start.9 = (bf16[80,256]{1,0:T(8,128)(2,1)S(1)}, bf16[80,256]{1,0:T(8,128)(2,1)S(1)}, u32[]{:S(2)}, u32[]{:S(2)}) collective-permute-start(bf16[80,256]{1,0:T(8,128)(2,1)S(1)} %shard_map.114.refs_2_), channel_id=1, source_target_pairs={{0,24},{4,28},{8,16},{12,20},{16,8},{20,12},{24,0},{28,4},{1,25},{... | collective-permute-start | bytes 122888 | tf_op jit(solution)/shard_map/ppermute | solution.py:782
  61.4 6.9 %collective-permute-start.8 = (bf16[80,256]{1,0:T(8,128)(2,1)S(1)}, bf16[80,256]{1,0:T(8,128)(2,1)S(1)}, u32[]{:S(2)}, u32[]{:S(2)}) collective-permute-start(bf16[80,256]{1,0:T(8,128)(2,1)S(1)} %shard_map.114.refs_2_), channel_id=1, source_target_pairs={{0,16},{4,20},{8,24},{12,28},{16,0},{20,4},{24,8},{28,12},{1,17},{... | collective-permute-start | bytes 122888 | tf_op jit(solution)/shard_map/ppermute | solution.py:782
  61.9 6.4 %collective-permute-start.7 = (bf16[80,256]{1,0:T(8,128)(2,1)S(1)}, bf16[80,256]{1,0:T(8,128)(2,1)S(1)}, u32[]{:S(2)}, u32[]{:S(2)}) collective-permute-start(bf16[80,256]{1,0:T(8,128)(2,1)S(1)} %shard_map.114.refs_2_), channel_id=1, source_target_pairs={{0,8},{4,12},{8,0},{12,4},{16,24},{20,28},{24,16},{28,20},{1,9},{5... | collective-permute-start | bytes 122888 | tf_op jit(solution)/shard_map/ppermute | solution.py:782
  68.3 1.3 %collective-permute-start.10 = (bf16[80,256]{1,0:T(8,128)(2,1)S(1)}, bf16[80,256]{1,0:T(8,128)(2,1)S(1)}, u32[]{:S(2)}, u32[]{:S(2)}) collective-permute-start(bf16[80,256]{1,0:T(8,128)(2,1)S(1)} %shard_map.114.refs_2_), channel_id=1, source_target_pairs={{0,4},{4,0},{8,12},{12,8},{16,20},{20,16},{24,28},{28,24},{1,5},{5... | collective-permute-start | bytes 122888 | tf_op jit(solution)/shard_map/ppermute | solution.py:782
  68.4 1.4 %collective-permute-start.11 = (bf16[80,256]{1,0:T(8,128)(2,1)S(1)}, bf16[80,256]{1,0:T(8,128)(2,1)S(1)}, u32[]{:S(2)}, u32[]{:S(2)}) collective-permute-start(bf16[80,256]{1,0:T(8,128)(2,1)S(1)} %collective-permute-done.7.refs_4_), channel_id=1, source_target_pairs={{0,4},{4,0},{8,12},{12,8},{16,20},{20,16},{24,28},{28,24},{1,5},{5... | collective-permute-start | bytes 122888 | tf_op jit(solution)/shard_map/ppermute | solution.py:782
  68.9 1.2 %collective-permute-start.12 = (bf16[80,256]{1,0:T(8,128)(2,1)S(1)}, bf16[80,256]{1,0:T(8,128)(2,1)S(1)}, u32[]{:S(2)}, u32[]{:S(2)}) collective-permute-start(bf16[80,256]{1,0:T(8,128)(2,1)S(1)} %collective-permute-done.8.refs_6_), channel_id=1, source_target_pairs={{0,4},{4,0},{8,12},{12,8},{16,20},{20,16},{24,28},{28,24},{1,5},{5... | collective-permute-start | bytes 122888 | tf_op jit(solution)/shard_map/ppermute | solution.py:782
  69.0 1.3 %collective-permute-start.13 = (bf16[80,256]{1,0:T(8,128)(2,1)S(1)}, bf16[80,256]{1,0:T(8,128)(2,1)S(1)}, u32[]{:S(2)}, u32[]{:S(2)}) collective-permute-start(bf16[80,256]{1,0:T(8,128)(2,1)S(1)} %collective-permute-done.9.refs_8_), channel_id=1, source_target_pairs={{0,4},{4,0},{8,12},{12,8},{16,20},{20,16},{24,28},{28,24},{1,5},{5... | collective-permute-start | bytes 122888 | tf_op jit(solution)/shard_map/ppermute | solution.py:782
  70.3 17.6 %copy-start.9 = (s32[1,1024]{1,0:T(1,128)S(1)}, s32[1,1024]{1,0:T(1,128)}, u32[]{:S(2)}) copy-start(s32[1,1024]{1,0:T(1,128)} %get-tuple-element.72.refs_1_) | copy-start | bytes 12292

commit v6 on v5

--- a/solution.py
+++ b/solution.py
@@ -185,7 +185,7 @@
 PIECES = ((4, 7, WFULL), (3, 4, WFULL), (3, 3, WIN))
 
 
-def relayout_kernel(nrows, step0, steps, me_ref, f_hbm, tail_ref, oa, ob, oc, inb, fbuf, tbuf, tb16, sem):
+def relayout_kernel(nrows, step0, steps, me_ref, f_hbm, tail_ref, oa, ob, oc, inb, fbuf, tbuf, sem):
     step = pl.program_id(0)
     half = me_ref[0] & 1
     end16 = nrows // 16 * 16
@@ -236,16 +236,14 @@
                 tail = jnp.where(row16 < nrows - end16, tail_ref[...].astype(f32), 0.0)
                 inb[slot, g, CHUNK - TAIL : CHUNK - TAIL + 16] = tail.astype(bf16)
 
-    slot = lax.rem(step, 2)
+    slot = step
 
     @pl.when(step == 0)
     def _():
         fbuf[...] = jnp.zeros_like(fbuf)
-        start(0, 0)
-
-    @pl.when(step + 1 < steps)
-    def _():
-        start(step + 1, 1 - slot)
+        inb[:, :, CHUNK - 16 :] = jnp.zeros_like(inb[:, :, CHUNK - 16 :])
+        for st in range(steps):
+            start(st, st)
 
     wait(step, slot)
     lane = lax.broadcasted_iota(jnp.int32, (8, LANE), 1)
@@ -267,10 +265,14 @@
                     value = pltpu.roll(jnp.where(lane >= phase, value, after), LANE - phase, 1)
                 tbuf[pl.ds(8 * n * STRIDE + 4 * g + e, 8, stride=STRIDE), :] = value
 
-    @pl.loop(0, KT, unroll=8)
-    def _(k):
-        tb16[k] = tbuf[pl.ds(k * STRIDE, 16), :].astype(bf16)
-
+    packed = {}
+
+    def tile(k):
+        if k not in packed:
+            packed[k] = tbuf[k * STRIDE : k * STRIDE + 16, :].astype(bf16)
+        return packed[k]
+
+    lane16 = lax.broadcasted_iota(jnp.int32, (16, LANE), 1)
     here = pl.ds(pl.multiple_of(step * 16, 16), 16)
     for dx, dy, d0, count in blocks():
         tile0, phase = divmod(d0 * COEF, LANE)
@@ -281,10 +283,10 @@
         else:
             ref = oc.at[INNER.index(dx), INNER.index(dy)]
         for t in range(up(count * COEF, LANE) // LANE):
-            value = tb16[tile0 + t]
+            value = tile(tile0 + t)
             if phase:
-                after = tb16[min(tile0 + t + 1, KT - 1)]
-                value = jnp.concatenate([value[:, phase:], after[:, :phase]], axis=1)
+                after = tile(min(tile0 + t + 1, KT - 1))
+                value = pltpu.roll(jnp.where(lane16 >= phase, value, after), LANE - phase, 1)
             ref[here, t * LANE : (t + 1) * LANE] = value
 
 
@@ -304,11 +306,10 @@
             in_specs=[HBM, pl.BlockSpec((16, LANE), lambda i, h: (nrows // 16, 0))],
             out_specs=(VMEM,) * len(shapes),
             scratch_shapes=[
-                pltpu.VMEM((2, 4, CHUNK, LANE), bf16),
+                pltpu.VMEM((steps, 4, CHUNK, LANE), bf16),
                 pltpu.VMEM((4, CHUNK + 16, LANE), f32),
                 pltpu.VMEM((KT * STRIDE, LANE), f32),
-                pltpu.VMEM((KT, 16, LANE), bf16),
-                pltpu.SemaphoreType.DMA((2, 4, 2)),
+                pltpu.SemaphoreType.DMA((steps, 4, 2)),
             ],
         ),
     )(me, rows, rows)

time: 89.9 us -> 85.9 us (0.956)
  Pallas kernels: 55.9 us -> 51.9 us
    pallas_call x2, Pallas kernels: 18.4 us -> 14.4 us  [relayout(): call(functools.partial(relayout_kernel, nrows, step0, steps), tuple((jax....]
  transfers between devices with their start and end apart: 15 -> 15, of which waited for: 8 -> 8; matrix products, arithmetic and copies ran while one was open for 0% -> 0% of each run, Pallas kernels for 33% -> 30%
where the time goes in v6:
time: 85.9 us; the launch traced here: 85.5 us
  Pallas kernels  51.9 us (60%)
  starting transfers between devices  16.6 us (19%)
  blocking collectives  13.2 us (15%)
  waiting for transfers between devices  1.81 us (2%)
  local copies, waits for them, and re-layouts  1.54 us (2%)
    pallas_call x7, Pallas kernels, run(): call(body, tuple(outs) + tuple(numbers), grant, flops, in_specs=[SMEM] *...  37.5 us
    pallas_call x2, Pallas kernels, relayout(): call(functools.partial(relayout_kernel, nrows, step0, steps), tuple((jax....  14.4 us
    all_to_all x1, blocking collectives, per_device(): lax.all_to_all(reply, ('pts', 'top'), split_axis=0, concat_axis=0, tiled=...  13.2 us
    ppermute x14, starting transfers between devices, shift_by(): return lax.ppermute(value, axis, [(i, i ^ distance) for i in range(size)])  9.26 us
    all_to_all x1, starting transfers between devices, per_device(): lax.all_to_all(outgoing, ('pts', 'top'), split_axis=0, concat_axis=0, til...  7.3 us
    ppermute x14, waiting for transfers between devices, shift_by(): return lax.ppermute(value, axis, [(i, i ^ distance) for i in range(size)])  1.81 us
  transfers between devices with their start and end apart: 15, of which 8 were waited for; matrix products, arithmetic and copies ran while one was open for 0% of the time, Pallas kernels for 30%

profile of v6, /device:TPU:0, one launch (start us, length us, event | category | flops | bytes accessed | tf_op | source)
XLA Modules:
  0.0 85.5 jit_solution(18131389761805096646)
XLA Ops:
  0.0 3.9 %shard_map.109 = (f32[8,4,16,256]{3,2,1,0:T(8,128)}, s32[1,1024]{1,0:T(1,128)}) custom-call(f32[3,1024]{1,0:T(4,128)} %refs_0_.1, f32[8,1024]{1,0:T(8,128)} %refs_1_.1, s32[1,1024]{1,0:T(1,128)} %bitcast.16, s32[8,128]{1,0:T(8,128)} %bitcast.17), custom_call_target="tpu_custom_call" | custom-call | flops 134217728 | bytes 1048576 | tf_op jit(solution)/shard_map/pallas_call | solution.py:160
  3.9 7.3 %all-to-all-start = ((f32[32,16,256]{2,1,0:T(8,128)}), f32[32,16,256]{2,1,0:T(8,128)S(1)}, u32[]{:S(2)}, u32[]{:S(2)}) async-start(f32[32,16,256]{2,1,0:T(8,128)} %bitcast.15), calls=%async_computation | async-start | bytes 1048576 | tf_op jit(solution)/shard_map/all_to_all | solution.py:828
  11.3 8.6 %shard_map.110 = (bf16[4,7,48,1152]{3,2,1,0:T(8,128)(2,1)}, bf16[3,4,48,1152]{3,2,1,0:T(8,128)(2,1)S(1)}, bf16[3,3,48,640]{3,2,1,0:T(8,128)(2,1)S(1)}) custom-call(s32[2]{0:T(128)S(1)} %pad_add_fusion.me_ref.refs_0_, bf16[57038,128]{1,0:T(8,128)(2,1)} %bitcast.11, bf16[57038,128]{1,0:T(8,128)(2,1)} %bitcast.12), custom_call_target="tpu_custom_call" | custom-call | flops 1048576 | bytes 6291456 | tf_op jit(solution)/shard_map/pallas_call | solution.py:297
  20.0 4.9 %shard_map.111 = (bf16[304,1280]{1,0:T(8,128)(2,1)S(1)}, bf16[34,152,152]{2,1,0:T(8,128)(2,1)S(1)}, bf16[2,152,80]{2,1,0:T(8,128)(2,1)S(1)}, bf16[2,152,80]{2,1,0:T(8,128)(2,1)S(1)}) custom-call(f32[1444,128]{1,0:T(8,128)S(1)} %bitcast.9, f32[1444,128]{1,0:T(8,128)S(1)} %bitcast.10, f32[152,152]{1,0:T(8,128)S(1)} %copy-done.3, f32[152,152]{1,0:T(8,128)S(1)} %copy-done.4, ...), custom_call_target="tpu_custom_call" | custom-call | flops 1073741824 | bytes 1048576 | tf_op jit(solution)/shard_map/pallas_call | solution.py:160
  24.9 1.5 %copy-done.7 = bf16[34,152,152]{2,1,0:T(8,128)(2,1)} copy-done((bf16[34,152,152]{2,1,0:T(8,128)(2,1)}, bf16[34,152,152]{2,1,0:T(8,128)(2,1)S(1)}, u32[]{:S(2)}) %copy-start.7) | copy-done | bytes 1571096
  26.4 11.3 %shard_map.112 = (bf16[160,256]{1,0:T(8,128)(2,1)S(1)}, f32[152,4096]{1,0:T(8,128)S(1)}, s32[1,4096]{1,0:T(1,128)S(1)}, s32[33]{0:T(128)S(1)}) custom-call(s32[2]{0:T(128)S(1)} %pad_add_fusion.me_ref.refs_0_, f32[32,16,256]{2,1,0:T(8,128)S(1)} %all-to-all-done.refs_1_, f32[152,128]{1,0:T(8,128)S(1)} %copy-done.6, bf16[304,1280]{1,0:T(8,128)(2,1)S(1)} %get-tuple-element.44.refs_3_), custom_call_target="tpu_custom_call" | custom-call | flops 8589934592 | bytes 1048576 | tf_op jit(solution)/shard_map/pallas_call | solution.py:160
  37.7 2.7 %collective-permute-start.2 = (bf16[160,256]{1,0:T(8,128)(2,1)S(1)}, bf16[160,256]{1,0:T(8,128)(2,1)S(1)}, u32[]{:S(2)}, u32[]{:S(2)}) collective-permute-start(bf16[160,256]{1,0:T(8,128)(2,1)S(1)} %get-tuple-element.52.refs_1_.refs_0_), channel_id=1, source_target_pairs={{0,24},{4,28},{8,16},{12,20},{16,8},{20,12},{24,0},{28,4},{1,25},{... | collective-permute-start | bytes 245768 | tf_op jit(solution)/shard_map/ppermute | solution.py:783
  40.4 0.6 collective-permute-start.1
  41.0 0.3 collective-permute-start
  41.2 5.8 %shard_map.113 = (bf16[4,7,32,1152]{3,2,1,0:T(8,128)(2,1)S(1)}, bf16[3,4,32,1152]{3,2,1,0:T(8,128)(2,1)S(1)}, bf16[3,3,32,640]{3,2,1,0:T(8,128)(2,1)S(1)}) custom-call(s32[2]{0:T(128)S(1)} %pad_add_fusion.me_ref.refs_0_, bf16[57038,128]{1,0:T(8,128)(2,1)} %bitcast.13, bf16[57038,128]{1,0:T(8,128)(2,1)} %bitcast.14), custom_call_target="tpu_custom_call" | custom-call | flops 1048576 | bytes 4194304 | tf_op jit(solution)/shard_map/pallas_call | solution.py:297
  47.2 0.5 collective-permute-start.4
  47.7 0.1 collective-permute-start.5
  47.7 0.4 collective-permute-start.6
  48.2 0.3 collective-permute-done.3.refs_2_.refs_1_
  48.4 0.2 collective-permute-done.4.refs_4_.refs_3_
  48.6 0.4 collective-permute-done.5.refs_6_.refs_5_
  48.9 0.2 collective-permute-done.6.refs_8_.refs_7_
  49.1 5.4 %shard_map.114.refs_2_ = bf16[80,256]{1,0:T(8,128)(2,1)S(1)} custom-call(s32[2]{0:T(128)S(1)} %pad_add_fusion.me_ref.refs_0_, bf16[160,256]{1,0:T(8,128)(2,1)S(1)} %get-tuple-element.52.refs_1_.refs_0_, bf16[160,256]{1,0:T(8,128)(2,1)S(1)} %collective-permute-done.3.refs_2_.refs_1_, bf16[160,256]{1,0:T(8,128)(2,1)S(1)} %collective-permute-done.refs_3_.refs_2_, ...), custom_call_target="tpu_custom_call" | custom-call | flops 8589934592 | bytes 1048576 | tf_op jit(solution)/shard_map/pallas_call | solution.py:160
  54.5 2.7 %collective-permute-start.9 = (bf16[80,256]{1,0:T(8,128)(2,1)S(1)}, bf16[80,256]{1,0:T(8,128)(2,1)S(1)}, u32[]{:S(2)}, u32[]{:S(2)}) collective-permute-start(bf16[80,256]{1,0:T(8,128)(2,1)S(1)} %shard_map.114.refs_2_), channel_id=1, source_target_pairs={{0,24},{4,28},{8,16},{12,20},{16,8},{20,12},{24,0},{28,4},{1,25},{... | collective-permute-start | bytes 122888 | tf_op jit(solution)/shard_map/ppermute | solution.py:783
  57.2 0.6 collective-permute-start.8
  57.8 0.3 collective-permute-start.7
  58.1 6.3 %shard_map.115.refs_12_ = f32[2,152,512]{2,1,0:T(8,128)S(1)} custom-call(bf16[160,256]{1,0:T(8,128)(2,1)S(1)} %get-tuple-element.52.refs_1_.refs_0_, bf16[160,256]{1,0:T(8,128)(2,1)S(1)} %collective-permute-done.3.refs_2_.refs_1_, bf16[160,256]{1,0:T(8,128)(2,1)S(1)} %collective-permute-done.refs_3_.refs_2_, ...), custom_call_target="tpu_custom_call" | custom-call | flops 4294967296 | bytes 1048576 | tf_op jit(solution)/shard_map/pallas_call | solution.py:160
  64.4 0.5 collective-permute-start.11
  64.9 0.1 collective-permute-start.12
  65.0 0.4 collective-permute-start.13
  65.4 0.2 collective-permute-done.10.refs_3_
  65.6 0.2 collective-permute-done.11.refs_5_
  65.8 0.3 collective-permute-done.12.refs_7_
  66.1 0.2 collective-permute-done.13.refs_9_
  66.3 4.5 %shard_map.116 = f32[32,1,512]{2,1,0:T(1,128)S(1)} custom-call(s32[2]{0:T(128)S(1)} %pad_add_fusion.me_ref.refs_0_, s32[33]{0:T(128)S(1)} %get-tuple-element.45.refs_1_, bf16[80,256]{1,0:T(8,128)(2,1)S(1)} %shard_map.114.refs_2_, bf16[80,256]{1,0:T(8,128)(2,1)S(1)} %collective-permute-done.10.refs_3_, bf16[80,256]{1,0:T(8,128)(2,1)S(1)} %collective-permute-done.7.refs_4_, ...), custom_call_target="tpu_custom_call" | custom-call | flops 4294967296 | bytes 1048576 | tf_op jit(solution)/shard_map/pallas_call | solution.py:160
  70.8 13.2 %all_to_all.10.refs_0_ = f32[32,1,512]{2,1,0:T(1,128)S(1)} all-to-all(f32[32,1,512]{2,1,0:T(1,128)S(1)} %shard_map.116), channel_id=1, replica_groups=mesh['pts'=8,'top'=4] {'pts','top'}, dimensions={0} | all-to-all | bytes 131072 | tf_op jit(solution)/shard_map/all_to_all | solution.py:907
  83.9 1.4 %shard_map.117 = f32[8,1024]{1,0:T(8,128)} custom-call(f32[32,1,512]{2,1,0:T(1,128)S(1)} %all_to_all.10.refs_0_, s32[1,1024]{1,0:T(1,128)S(1)} %copy-done.9), custom_call_target="tpu_custom_call" | custom-call | flops 268435456 | bytes 1048576 | tf_op jit(solution)/shard_map/pallas_call | solution.py:160
  (29 shorter events, 0.3 us)
Async XLA Ops:
  3.9 22.5 %all-to-all-start = ((f32[32,16,256]{2,1,0:T(8,128)}), f32[32,16,256]{2,1,0:T(8,128)S(1)}, u32[]{:S(2)}, u32[]{:S(2)}) async-start(f32[32,16,256]{2,1,0:T(8,128)} %bitcast.15), calls=%async_computation | async-start | bytes 1048576 | tf_op jit(solution)/shard_map/all_to_all | solution.py:828
  11.3 8.7 %copy-start.1 = (f32[184832]{0:T(1024)S(1)}, f32[184832]{0:T(1024)}, u32[]{:S(2)}) copy-start(f32[184832]{0:T(1024)} %param.16) | copy-start | bytes 2217988
  11.3 8.7 %copy-start.2 = (f32[184832]{0:T(1024)S(1)}, f32[184832]{0:T(1024)}, u32[]{:S(2)}) copy-start(f32[184832]{0:T(1024)} %param.20) | copy-start | bytes 2217988
  11.3 8.7 %copy-start.3 = (f32[152,152]{1,0:T(8,128)S(1)}, f32[152,152]{1,0:T(8,128)}, u32[]{:S(2)}) copy-start(f32[152,152]{1,0:T(8,128)} %refs_2_.2) | copy-start | bytes 277252
  11.3 8.7 %copy-start.4 = (f32[152,152]{1,0:T(8,128)S(1)}, f32[152,152]{1,0:T(8,128)}, u32[]{:S(2)}) copy-start(f32[152,152]{1,0:T(8,128)} %refs_3_.1) | copy-start | bytes 277252
  11.3 8.7 %copy-start.5 = (f32[152,152]{1,0:T(8,128)S(1)}, f32[152,152]{1,0:T(8,128)}, u32[]{:S(2)}) copy-start(f32[152,152]{1,0:T(8,128)} %refs_4_.1) | copy-start | bytes 277252
  11.3 8.7 %copy-start.6 = (f32[152,128]{1,0:T(8,128)S(1)}, f32[152,128]{1,0:T(8,128)}, u32[]{:S(2)}) copy-start(f32[152,128]{1,0:T(8,128)} %constant.11.clone.refs_5_.refs_2_) | copy-start | bytes 233476
  24.9 1.5 %copy-start.7 = (bf16[34,152,152]{2,1,0:T(8,128)(2,1)}, bf16[34,152,152]{2,1,0:T(8,128)(2,1)S(1)}, u32[]{:S(2)}) copy-start(bf16[34,152,152]{2,1,0:T(8,128)(2,1)S(1)} %get-tuple-element.62.refs_8_) | copy-start | bytes 4713220
  37.7 9.4 %collective-permute-start.2 = (bf16[160,256]{1,0:T(8,128)(2,1)S(1)}, bf16[160,256]{1,0:T(8,128)(2,1)S(1)}, u32[]{:S(2)}, u32[]{:S(2)}) collective-permute-start(bf16[160,256]{1,0:T(8,128)(2,1)S(1)} %get-tuple-element.52.refs_1_.refs_0_), channel_id=1, source_target_pairs={{0,24},{4,28},{8,16},{12,20},{16,8},{20,12},{24,0},{28,4},{1,25},{... | collective-permute-start | bytes 245768 | tf_op jit(solution)/shard_map/ppermute | solution.py:783
  40.4 6.6 %collective-permute-start.1 = (bf16[160,256]{1,0:T(8,128)(2,1)S(1)}, bf16[160,256]{1,0:T(8,128)(2,1)S(1)}, u32[]{:S(2)}, u32[]{:S(2)}) collective-permute-start(bf16[160,256]{1,0:T(8,128)(2,1)S(1)} %get-tuple-element.52.refs_1_.refs_0_), channel_id=1, source_target_pairs={{0,16},{4,20},{8,24},{12,28},{16,0},{20,4},{24,8},{28,12},{1,17},{... | collective-permute-start | bytes 245768 | tf_op jit(solution)/shard_map/ppermute | solution.py:783
  41.0 6.1 %collective-permute-start = (bf16[160,256]{1,0:T(8,128)(2,1)S(1)}, bf16[160,256]{1,0:T(8,128)(2,1)S(1)}, u32[]{:S(2)}, u32[]{:S(2)}) collective-permute-start(bf16[160,256]{1,0:T(8,128)(2,1)S(1)} %get-tuple-element.52.refs_1_.refs_0_), channel_id=1, source_target_pairs={{0,8},{4,12},{8,0},{12,4},{16,24},{20,28},{24,16},{28,20},{1,9},{5... | collective-permute-start | bytes 245768 | tf_op jit(solution)/shard_map/ppermute | solution.py:783
  41.2 7.9 %copy-start = (bf16[4,7,48,1152]{3,2,1,0:T(8,128)(2,1)S(1)}, bf16[4,7,48,1152]{3,2,1,0:T(8,128)(2,1)}, u32[]{:S(2)}) copy-start(bf16[4,7,48,1152]{3,2,1,0:T(8,128)(2,1)} %get-tuple-element.56.refs_9_) | copy-start | bytes 9289732
  47.1 11.0 %copy-start.8 = (bf16[34,152,152]{2,1,0:T(8,128)(2,1)S(1)}, bf16[34,152,152]{2,1,0:T(8,128)(2,1)}, u32[]{:S(2)}) copy-start(bf16[34,152,152]{2,1,0:T(8,128)(2,1)} %copy-done.7) | copy-start | bytes 4713220
  47.1 1.3 %collective-permute-start.3 = (bf16[160,256]{1,0:T(8,128)(2,1)S(1)}, bf16[160,256]{1,0:T(8,128)(2,1)S(1)}, u32[]{:S(2)}, u32[]{:S(2)}) collective-permute-start(bf16[160,256]{1,0:T(8,128)(2,1)S(1)} %get-tuple-element.52.refs_1_.refs_0_), channel_id=1, source_target_pairs={{0,4},{4,0},{8,12},{12,8},{16,20},{20,16},{24,28},{28,24},{1,5},{5... | collective-permute-start | bytes 245768 | tf_op jit(solution)/shard_map/ppermute | solution.py:783
  47.2 1.4 %collective-permute-start.4 = (bf16[160,256]{1,0:T(8,128)(2,1)S(1)}, bf16[160,256]{1,0:T(8,128)(2,1)S(1)}, u32[]{:S(2)}, u32[]{:S(2)}) collective-permute-start(bf16[160,256]{1,0:T(8,128)(2,1)S(1)} %collective-permute-done.refs_3_.refs_2_), channel_id=1, source_target_pairs={{0,4},{4,0},{8,12},{12,8},{16,20},{20,16},{24,28},{28,24},{1,5},{5... | collective-permute-start | bytes 245768 | tf_op jit(solution)/shard_map/ppermute | solution.py:783
  47.7 1.3 %collective-permute-start.5 = (bf16[160,256]{1,0:T(8,128)(2,1)S(1)}, bf16[160,256]{1,0:T(8,128)(2,1)S(1)}, u32[]{:S(2)}, u32[]{:S(2)}) collective-permute-start(bf16[160,256]{1,0:T(8,128)(2,1)S(1)} %collective-permute-done.1.refs_5_.refs_4_), channel_id=1, source_target_pairs={{0,4},{4,0},{8,12},{12,8},{16,20},{20,16},{24,28},{28,24},{1,5},{5... | collective-permute-start | bytes 245768 | tf_op jit(solution)/shard_map/ppermute | solution.py:783
  47.7 1.4 %collective-permute-start.6 = (bf16[160,256]{1,0:T(8,128)(2,1)S(1)}, bf16[160,256]{1,0:T(8,128)(2,1)S(1)}, u32[]{:S(2)}, u32[]{:S(2)}) collective-permute-start(bf16[160,256]{1,0:T(8,128)(2,1)S(1)} %collective-permute-done.2.refs_7_.refs_6_), channel_id=1, source_target_pairs={{0,4},{4,0},{8,12},{12,8},{16,20},{20,16},{24,28},{28,24},{1,5},{5... | collective-permute-start | bytes 245768 | tf_op jit(solution)/shard_map/ppermute | solution.py:783
  54.5 9.8 %collective-permute-start.9 = (bf16[80,256]{1,0:T(8,128)(2,1)S(1)}, bf16[80,256]{1,0:T(8,128)(2,1)S(1)}, u32[]{:S(2)}, u32[]{:S(2)}) collective-permute-start(bf16[80,256]{1,0:T(8,128)(2,1)S(1)} %shard_map.114.refs_2_), channel_id=1, source_target_pairs={{0,24},{4,28},{8,16},{12,20},{16,8},{20,12},{24,0},{28,4},{1,25},{... | collective-permute-start | bytes 122888 | tf_op jit(solution)/shard_map/ppermute | solution.py:783
  57.2 7.1 %collective-permute-start.8 = (bf16[80,256]{1,0:T(8,128)(2,1)S(1)}, bf16[80,256]{1,0:T(8,128)(2,1)S(1)}, u32[]{:S(2)}, u32[]{:S(2)}) collective-permute-start(bf16[80,256]{1,0:T(8,128)(2,1)S(1)} %shard_map.114.refs_2_), channel_id=1, source_target_pairs={{0,16},{4,20},{8,24},{12,28},{16,0},{20,4},{24,8},{28,12},{1,17},{... | collective-permute-start | bytes 122888 | tf_op jit(solution)/shard_map/ppermute | solution.py:783
  57.8 6.5 %collective-permute-start.7 = (bf16[80,256]{1,0:T(8,128)(2,1)S(1)}, bf16[80,256]{1,0:T(8,128)(2,1)S(1)}, u32[]{:S(2)}, u32[]{:S(2)}) collective-permute-start(bf16[80,256]{1,0:T(8,128)(2,1)S(1)} %shard_map.114.refs_2_), channel_id=1, source_target_pairs={{0,8},{4,12},{8,0},{12,4},{16,24},{20,28},{24,16},{28,20},{1,9},{5... | collective-permute-start | bytes 122888 | tf_op jit(solution)/shard_map/ppermute | solution.py:783
  64.3 1.3 %collective-permute-start.10 = (bf16[80,256]{1,0:T(8,128)(2,1)S(1)}, bf16[80,256]{1,0:T(8,128)(2,1)S(1)}, u32[]{:S(2)}, u32[]{:S(2)}) collective-permute-start(bf16[80,256]{1,0:T(8,128)(2,1)S(1)} %shard_map.114.refs_2_), channel_id=1, source_target_pairs={{0,4},{4,0},{8,12},{12,8},{16,20},{20,16},{24,28},{28,24},{1,5},{5... | collective-permute-start | bytes 122888 | tf_op jit(solution)/shard_map/ppermute | solution.py:783
  64.4 1.4 %collective-permute-start.11 = (bf16[80,256]{1,0:T(8,128)(2,1)S(1)}, bf16[80,256]{1,0:T(8,128)(2,1)S(1)}, u32[]{:S(2)}, u32[]{:S(2)}) collective-permute-start(bf16[80,256]{1,0:T(8,128)(2,1)S(1)} %collective-permute-done.7.refs_4_), channel_id=1, source_target_pairs={{0,4},{4,0},{8,12},{12,8},{16,20},{20,16},{24,28},{28,24},{1,5},{5... | collective-permute-start | bytes 122888 | tf_op jit(solution)/shard_map/ppermute | solution.py:783
  64.9 1.2 %collective-permute-start.12 = (bf16[80,256]{1,0:T(8,128)(2,1)S(1)}, bf16[80,256]{1,0:T(8,128)(2,1)S(1)}, u32[]{:S(2)}, u32[]{:S(2)}) collective-permute-start(bf16[80,256]{1,0:T(8,128)(2,1)S(1)} %collective-permute-done.8.refs_6_), channel_id=1, source_target_pairs={{0,4},{4,0},{8,12},{12,8},{16,20},{20,16},{24,28},{28,24},{1,5},{5... | collective-permute-start | bytes 122888 | tf_op jit(solution)/shard_map/ppermute | solution.py:783
  65.0 1.3 %collective-permute-start.13 = (bf16[80,256]{1,0:T(8,128)(2,1)S(1)}, bf16[80,256]{1,0:T(8,128)(2,1)S(1)}, u32[]{:S(2)}, u32[]{:S(2)}) collective-permute-start(bf16[80,256]{1,0:T(8,128)(2,1)S(1)} %collective-permute-done.9.refs_8_), channel_id=1, source_target_pairs={{0,4},{4,0},{8,12},{12,8},{16,20},{20,16},{24,28},{28,24},{1,5},{5... | collective-permute-start | bytes 122888 | tf_op jit(solution)/shard_map/ppermute | solution.py:783
  66.3 17.6 %copy-start.9 = (s32[1,1024]{1,0:T(1,128)S(1)}, s32[1,1024]{1,0:T(1,128)}, u32[]{:S(2)}) copy-start(s32[1,1024]{1,0:T(1,128)} %get-tuple-element.72.refs_1_) | copy-start | bytes 12292

commit v7 on v6

--- a/solution.py
+++ b/solution.py
@@ -46,6 +46,7 @@
 FEATURES = 4
 PB = 256
 STRIP = 16
+UNROLL_FIND, UNROLL_APPLY, UNROLL_GATHER = 16, 8, 8
 GRANT = 28
 GRANT_FIRST = 60
 GRANT_EARLY = 52
@@ -345,14 +346,13 @@
 
     plane = split(column[...])
 
-    def stack(pieces, first):
+    def side_by_side(pieces):
         wide = []
         for piece in pieces:
             high, low = split(dot3(split(piece), plane)[:, 8 : 8 + FEATURES])
             wide += [piece, high.astype(f32), low.astype(f32)]
             wide.append(jnp.zeros((COEF, CPAD - COEF - 2 * FEATURES), f32))
-        wide = jnp.concatenate([w for w in wide if w.shape[1]], axis=1).astype(bf16)
-        w_both[first : first + COEF] = wide
+        return jnp.concatenate([w for w in wide if w.shape[1]], axis=1)
 
     def matrix(o):
         at = slice(o * COEF, (o + 1) * COEF)
@@ -365,7 +365,7 @@
         high, low = split(matrix(o))
         coarse[o], coarse[8 + o] = high, low
         pieces.append(dot3((high, low), first))
-    stack(pieces, 0)
+    upward = side_by_side(pieces)
     io.wait(1)
     square(l2l, rows)
     pieces = []
@@ -373,7 +373,7 @@
         value = matrix(o)
         coarse[16 + o], coarse[24 + o] = split(value)
         pieces.append(jnp.transpose(value) * scale)
-    stack(pieces, COEF)
+    w_both[...] = jnp.concatenate([upward, side_by_side(pieces)], axis=0).astype(bf16)
     high, low = split(dc2e[...])
     i = lax.broadcasted_iota(jnp.int32, (COEF, ROWS), 0)
     r = lax.broadcasted_iota(jnp.int32, (COEF, ROWS), 1)
@@ -516,7 +516,7 @@
     return place
 
 
-def points_kernel(n_top, box_cap, io, offsets, buf, surf):
+def points_kernel(n_top, box_cap, io, offsets, buf, surf, octants, outgoing):
     got, column, oper = io.ins
     out, field, place = io.outs
     sources, _, cap = got.shape
@@ -551,23 +551,43 @@
     table = jnp.transpose(table).astype(bf16)
     out_rows = out.shape[1]
 
-    def block(j, total):
-        to = pl.ds(pl.multiple_of(j * PB, PB), PB)
-        value = buf[:, to]
-        box, octant = look_up(value[3:4].astype(jnp.int32), table)
+    blocks_of = own // PB
+
+    def spot(j):
+        return pl.ds(pl.multiple_of(j * PB, PB), PB)
+
+    def find(j, carry):
+        to = spot(j)
+        box, octant = look_up(buf[3:4, to].astype(jnp.int32), table)
         place[:, to] = box.astype(jnp.int32)
-        both = octant_product(value[0:3], octant, surf, oper)
+        octants[:, to] = octant
+        return carry
+
+    lax.fori_loop(0, blocks_of, find, 0, unroll=UNROLL_FIND)
+
+    def apply(j, carry):
+        to = spot(j)
+        both = octant_product(buf[0:3, to], octants[:, to], surf, oper)
+        outgoing[:, to] = both[0:COEF]
         field[:, to] = both[COEF : 2 * COEF]
-        high, low = split(both[0:COEF])
+        return carry
+
+    lax.fori_loop(0, blocks_of, apply, 0, unroll=UNROLL_APPLY)
+
+    def gather(j, total):
+        to = spot(j)
+        high, low = split(outgoing[:, to])
         rows = []
-        at = lax.broadcasted_iota(jnp.int32, (box_cap, PB), 0).astype(f32)
+        at = lax.broadcasted_iota(jnp.int32, (box_cap, PB), 0)
+        here = place[:, to] == at
         for k in range(out_rows // box_cap):
-            rows.append(jnp.where(box == at, value[5 + k : 6 + k], 0.0))
+            rows.append(jnp.where(here, buf[5 + k : 6 + k, to], 0.0))
         a_high, a_low = split(jnp.concatenate(rows, axis=0))
         both = dot(jnp.concatenate([high, low], axis=0), a_high, NT)
         return total + both[0:COEF] + both[COEF : 2 * COEF] + dot(high, a_low, NT)
 
-    total = lax.fori_loop(0, own // PB, block, jnp.zeros((COEF, out_rows), f32), unroll=2)
+    total = jnp.zeros((COEF, out_rows), f32)
+    total = lax.fori_loop(0, blocks_of, gather, total, unroll=UNROLL_GATHER)
     digits = jnp.concatenate([first >> 3, first & 7], axis=0).astype(f32)
     digits = jnp.broadcast_to(digits, (2, out_rows))
     blank = jnp.zeros((out.shape[0] - COEF - 2, out_rows), f32)
@@ -578,7 +598,7 @@
 def box_ids(parts, dens):
     ids = []
     for part in parts:
-        digits = part[COEF : COEF + 8, 0:1].astype(f32).astype(jnp.int32)
+        digits = part[COEF - 8 : COEF + 8, :].astype(f32)[8:16, 0:1].astype(jnp.int32)
         first = digits[0:1] * 8 + digits[1:2]
         at = lax.broadcasted_iota(jnp.int32, (1, part.shape[1] // dens), 1)
         ids.append(first + at)
@@ -678,7 +698,7 @@
     rows = jnp.concatenate(level, axis=0)
     rows = dot3(split(rows), (opers[32], opers[33]), NT)
     level = [rows[k : k + 1] for k in range(dens)]
-    for _ in range(LEVEL):
+    for _ in range(LEVEL - 1):
         count = level[0].shape[0]
         rows = split(jnp.concatenate(level, axis=0))
         children = [dot3_rows(rows, (opers[16 + o], opers[24 + o]), NT) for o in range(8)]
@@ -686,16 +706,12 @@
             jnp.concatenate([c[k * count : (k + 1) * count] for c in children], axis=0)
             for k in range(dens)
         ]
-    at = lax.broadcasted_iota(jnp.int32, (1, BOXES4), 1)
-    number = jnp.zeros_like(at)
-    for b in range(LEVEL):
-        digit = ((at >> (2 * LEVEL + b)) & 1) * 4 + ((at >> (LEVEL + b)) & 1) * 2 + ((at >> b) & 1)
-        number = number + (digit << (3 * (LEVEL - 1 - b)))
-    row = lax.broadcasted_iota(jnp.int32, (BOXES4, BOXES4), 0)
-    move = jnp.where(row == number, 1.0, 0.0).astype(bf16)
+    count = level[0].shape[0]
+    rows = split(jnp.concatenate(level, axis=0))
+    children = [dot3((opers[16 + o], opers[24 + o]), rows, NT) for o in range(8)]
     for k in range(dens):
-        high, low = split(level[k])
-        out[k] = dot(high, move, TURNED) + dot(low, move, TURNED)
+        pieces = [c[:, k * count : (k + 1) * count] for c in children]
+        out[k] = jnp.concatenate(pieces, axis=1)
 
 
 def evaluate_kernel(slabs, step, window, io, stack, found):
@@ -725,26 +741,25 @@
             pieces = [value[:, k * PLANE : (k + 1) * PLANE] for k in range(dens)]
         width = slabs * PLANE
         for k in range(dens):
-            at = m ^ group
-            if width % LANE == 0:
-                base = lattice[k, :, pl.ds(pl.multiple_of(at * width, width), width)]
-            else:
-                pair = lattice[k, :, pl.ds(pl.multiple_of(at // 2 * LANE, LANE), LANE)]
-                base = jnp.where(at % 2 == 0, pair[:, :width], pair[:, width:])
-            high, low = split(pieces[k] + base)
+            high, low = split(pieces[k])
             rows = pl.ds(k * CPAD, COEF)
             stack[rows, m * width : (m + 1) * width] = high.astype(f32)
             rows = pl.ds((dens + k) * CPAD, COEF)
             stack[rows, m * width : (m + 1) * width] = low.astype(f32)
     box = offsets[sources] + lax.broadcasted_iota(jnp.int32, (1, window), 1)
     want = morton_place(box) ^ (group * (slabs * PLANE))
-    want = jnp.where(box < BOXES4, want, -1)
-    pick = want == lax.broadcasted_iota(jnp.int32, (BOXES4, window), 0)
+    turned = BOXES4 + ((box & 7) << 6) + (box & 56) + (box >> 6)
+    at = lax.broadcasted_iota(jnp.int32, (2 * BOXES4, window), 0)
+    pick = ((at == want) | (at == turned)) & (box < BOXES4)
     pick = jnp.where(pick, 1.0, 0.0).astype(bf16)
+    for k in range(dens):
+        high, low = split(lattice[k])
+        stack[pl.ds(k * CPAD, COEF), BOXES4:] = high.astype(f32)
+        stack[pl.ds((dens + k) * CPAD, COEF), BOXES4:] = low.astype(f32)
     half = dens * CPAD
-    local = jnp.concatenate(
-        [dot(stack[h * half : (h + 1) * half].astype(bf16), pick) for h in range(2)], axis=1
-    ).astype(bf16)
+    local = dot(stack[...].astype(bf16), pick)
+    high, low = split(local[0:half] + local[half:])
+    local = jnp.concatenate([high, low], axis=1)
     found[:, place.shape[1] :] = jnp.zeros((8, found.shape[1] - place.shape[1]), f32)
     io.wait(*range(len(io.ins)))
 
@@ -763,7 +778,7 @@
         found[:, at] = jnp.concatenate(rows, axis=0)
         return carry
 
-    lax.fori_loop(0, place.shape[1] // PB, block, 0, unroll=2)
+    lax.fori_loop(0, place.shape[1] // PB, block, 0, unroll=8)
 
     wide = up(cap, LANE) + LANE
 
@@ -784,9 +799,9 @@
 
 
 def gather_by(value, distances, beside):
-    got = {m: shift_by("pts", value, m) if m else value for m in distances if m % 2 == 0}
+    got = {m: shift_by("pts", value, m) if m else value for m in distances if m < 2 or m % 2 == 0}
     got, beside = lax.optimization_barrier((got, beside))
-    got.update({m + 1: shift_by("pts", got[m], 1) for m in list(got) if m + 1 in distances})
+    got.update({m + 1: shift_by("pts", got[m], 1) for m in list(got) if m % 2 == 0 and m})
     return [got[m] for m in distances], beside
 
 
@@ -835,7 +850,7 @@
         [m2m.reshape(flat), l2l.reshape(flat), uc2e, dc2e, lattice, column],
         [shape(2 * coef, 8 * CPAD), shape(34, coef, coef)] + [shape(2, coef, ROWS)] * 2,
         1 << 30,
-        late=(0, 1),
+        here=range(6),
         stays=range(4),
         scratch=[pltpu.VMEM((2, 8 * coef, LANE), f32)],
     )
@@ -859,6 +874,8 @@
         scratch=[
             pltpu.VMEM((8, up(own + up(cap, LANE) + LANE, PB)), f32),
             pltpu.VMEM((3 + FEATURES, coef, PB), f32),
+            pltpu.VMEM((1, own), f32),
+            pltpu.VMEM((coef, own), f32),
         ],
     )
     later, flat_ops = lax.optimization_barrier((partial, m2l_ops))
@@ -900,7 +917,7 @@
         4 << 30,
         here=range(len(gathered), len(gathered) + 5),
         scratch=[
-            pltpu.VMEM((2 * dens * CPAD, BOXES4), f32),
+            pltpu.VMEM((2 * dens * CPAD, 2 * BOXES4), f32),
             pltpu.VMEM((8, own + up(cap, LANE) + LANE), f32),
         ],
     )

time: 85.9 us -> 82 us (0.955)
  Pallas kernels: 51.9 us -> 48 us
    pallas_call x7, Pallas kernels: 37.5 us -> 33.6 us  [run(): call(body, tuple(outs) + tuple(numbers), grant, flops, in_specs=[SMEM] *...]
  transfers between devices with their start and end apart: 15 -> 15, of which waited for: 8 -> 7; matrix products, arithmetic and copies ran while one was open for 0% -> 0% of each run, Pallas kernels for 30% -> 29%
where the time goes in v7:
time: 82 us; the launch traced here: 81.5 us
  Pallas kernels  48 us (59%)
  starting transfers between devices  16.6 us (20%)
  blocking collectives  12.4 us (15%)
  waiting for transfers between devices  2.52 us (3%)
  local copies, waits for them, and re-layouts  1.54 us (2%)
    pallas_call x7, Pallas kernels, run(): call(body, tuple(outs) + tuple(numbers), grant, flops, in_specs=[SMEM] *...  33.6 us
    pallas_call x2, Pallas kernels, relayout(): call(functools.partial(relayout_kernel, nrows, step0, steps), tuple((jax....  14.4 us
    all_to_all x1, blocking collectives, per_device(): lax.all_to_all(reply, ('pts', 'top'), split_axis=0, concat_axis=0, tiled=...  12.4 us
    ppermute x14, starting transfers between devices, shift_by(): return lax.ppermute(value, axis, [(i, i ^ distance) for i in range(size)])  9.26 us
    all_to_all x1, starting transfers between devices, per_device(): lax.all_to_all(outgoing, ('pts', 'top'), split_axis=0, concat_axis=0, til...  7.3 us
    ppermute x14, waiting for transfers between devices, shift_by(): return lax.ppermute(value, axis, [(i, i ^ distance) for i in range(size)])  2 us
  transfers between devices with their start and end apart: 15, of which 7 were waited for; matrix products, arithmetic and copies ran while one was open for 0% of the time, Pallas kernels for 29%

profile of v7, /device:TPU:0, one launch (start us, length us, event | category | flops | bytes accessed | tf_op | source)
XLA Modules:
  0.0 81.5 jit_solution(13016466171862810097)
XLA Ops:
  0.0 3.9 %shard_map.109 = (f32[8,4,16,256]{3,2,1,0:T(8,128)}, s32[1,1024]{1,0:T(1,128)}) custom-call(f32[3,1024]{1,0:T(4,128)} %refs_0_.1, f32[8,1024]{1,0:T(8,128)} %refs_1_.1, s32[1,1024]{1,0:T(1,128)} %bitcast.16, s32[8,128]{1,0:T(8,128)} %bitcast.17), custom_call_target="tpu_custom_call" | custom-call | flops 134217728 | bytes 1048576 | tf_op jit(solution)/shard_map/pallas_call | solution.py:161
  3.9 7.3 %all-to-all-start = ((f32[32,16,256]{2,1,0:T(8,128)}), f32[32,16,256]{2,1,0:T(8,128)S(1)}, u32[]{:S(2)}, u32[]{:S(2)}) async-start(f32[32,16,256]{2,1,0:T(8,128)} %bitcast.15), calls=%async_computation | async-start | bytes 1048576 | tf_op jit(solution)/shard_map/all_to_all | solution.py:843
  11.3 8.6 %shard_map.110 = (bf16[4,7,48,1152]{3,2,1,0:T(8,128)(2,1)}, bf16[3,4,48,1152]{3,2,1,0:T(8,128)(2,1)S(1)}, bf16[3,3,48,640]{3,2,1,0:T(8,128)(2,1)S(1)}) custom-call(s32[2]{0:T(128)S(1)} %pad_add_fusion.me_ref.refs_0_, bf16[57038,128]{1,0:T(8,128)(2,1)} %bitcast.11, bf16[57038,128]{1,0:T(8,128)(2,1)} %bitcast.12), custom_call_target="tpu_custom_call" | custom-call | flops 1048576 | bytes 6291456 | tf_op jit(solution)/shard_map/pallas_call | solution.py:298
  20.0 3.5 %shard_map.111 = (bf16[304,1280]{1,0:T(8,128)(2,1)S(1)}, bf16[34,152,152]{2,1,0:T(8,128)(2,1)S(1)}, bf16[2,152,80]{2,1,0:T(8,128)(2,1)S(1)}, bf16[2,152,80]{2,1,0:T(8,128)(2,1)S(1)}) custom-call(f32[1444,128]{1,0:T(8,128)S(1)} %bitcast.9, f32[1444,128]{1,0:T(8,128)S(1)} %bitcast.10, f32[152,152]{1,0:T(8,128)S(1)} %copy-done.3, f32[152,152]{1,0:T(8,128)S(1)} %copy-done.4, ...), custom_call_target="tpu_custom_call" | custom-call | flops 1073741824 | bytes 1048576 | tf_op jit(solution)/shard_map/pallas_call | solution.py:161
  23.6 1.5 %copy-done.7 = bf16[34,152,152]{2,1,0:T(8,128)(2,1)} copy-done((bf16[34,152,152]{2,1,0:T(8,128)(2,1)}, bf16[34,152,152]{2,1,0:T(8,128)(2,1)S(1)}, u32[]{:S(2)}) %copy-start.7) | copy-done | bytes 1571096
  25.1 0.5 all-to-all-done.refs_1_
  25.6 10.0 %shard_map.112 = (bf16[160,256]{1,0:T(8,128)(2,1)S(1)}, f32[152,4096]{1,0:T(8,128)S(1)}, s32[1,4096]{1,0:T(1,128)S(1)}, s32[33]{0:T(128)S(1)}) custom-call(s32[2]{0:T(128)S(1)} %pad_add_fusion.me_ref.refs_0_, f32[32,16,256]{2,1,0:T(8,128)S(1)} %all-to-all-done.refs_1_, f32[152,128]{1,0:T(8,128)S(1)} %copy-done.6, bf16[304,1280]{1,0:T(8,128)(2,1)S(1)} %get-tuple-element.46.refs_3_), custom_call_target="tpu_custom_call" | custom-call | flops 8589934592 | bytes 1048576 | tf_op jit(solution)/shard_map/pallas_call | solution.py:161
  35.5 2.3 %collective-permute-start.3 = (bf16[160,256]{1,0:T(8,128)(2,1)S(1)}, bf16[160,256]{1,0:T(8,128)(2,1)S(1)}, u32[]{:S(2)}, u32[]{:S(2)}) collective-permute-start(bf16[160,256]{1,0:T(8,128)(2,1)S(1)} %get-tuple-element.54.refs_1_.refs_0_), channel_id=1, source_target_pairs={{0,24},{4,28},{8,16},{12,20},{16,8},{20,12},{24,0},{28,4},{1,25},{... | collective-permute-start | bytes 245768 | tf_op jit(solution)/shard_map/ppermute | solution.py:798
  37.8 0.7 collective-permute-start.2
  38.5 0.5 collective-permute-start.1
  39.1 0.3 collective-permute-start
  39.4 5.8 %shard_map.113 = (bf16[4,7,32,1152]{3,2,1,0:T(8,128)(2,1)S(1)}, bf16[3,4,32,1152]{3,2,1,0:T(8,128)(2,1)S(1)}, bf16[3,3,32,640]{3,2,1,0:T(8,128)(2,1)S(1)}) custom-call(s32[2]{0:T(128)S(1)} %pad_add_fusion.me_ref.refs_0_, bf16[57038,128]{1,0:T(8,128)(2,1)} %bitcast.13, bf16[57038,128]{1,0:T(8,128)(2,1)} %bitcast.14), custom_call_target="tpu_custom_call" | custom-call | flops 1048576 | bytes 4194304 | tf_op jit(solution)/shard_map/pallas_call | solution.py:298
  45.3 0.2 collective-permute-start.4
  45.5 0.3 collective-permute-start.5
  45.9 0.2 collective-permute-start.6
  46.0 0.6 collective-permute-done.4.refs_4_.refs_3_
  46.6 0.2 collective-permute-done.5.refs_6_.refs_5_
  46.8 0.3 collective-permute-done.6.refs_8_.refs_7_
  47.1 5.6 %shard_map.114.refs_2_ = bf16[80,256]{1,0:T(8,128)(2,1)S(1)} custom-call(s32[2]{0:T(128)S(1)} %pad_add_fusion.me_ref.refs_0_, bf16[160,256]{1,0:T(8,128)(2,1)S(1)} %get-tuple-element.54.refs_1_.refs_0_, bf16[160,256]{1,0:T(8,128)(2,1)S(1)} %collective-permute-done.refs_2_.refs_1_, bf16[160,256]{1,0:T(8,128)(2,1)S(1)} %collective-permute-done.1.refs_3_.refs_2_, ...), custom_call_target="tpu_custom_call" | custom-call | flops 8589934592 | bytes 1048576 | tf_op jit(solution)/shard_map/pallas_call | solution.py:161
  52.7 2.1 %collective-permute-start.10 = (bf16[80,256]{1,0:T(8,128)(2,1)S(1)}, bf16[80,256]{1,0:T(8,128)(2,1)S(1)}, u32[]{:S(2)}, u32[]{:S(2)}) collective-permute-start(bf16[80,256]{1,0:T(8,128)(2,1)S(1)} %shard_map.114.refs_2_), channel_id=1, source_target_pairs={{0,24},{4,28},{8,16},{12,20},{16,8},{20,12},{24,0},{28,4},{1,25},{... | collective-permute-start | bytes 122888 | tf_op jit(solution)/shard_map/ppermute | solution.py:798
  54.8 0.9 %collective-permute-start.9 = (bf16[80,256]{1,0:T(8,128)(2,1)S(1)}, bf16[80,256]{1,0:T(8,128)(2,1)S(1)}, u32[]{:S(2)}, u32[]{:S(2)}) collective-permute-start(bf16[80,256]{1,0:T(8,128)(2,1)S(1)} %shard_map.114.refs_2_), channel_id=1, source_target_pairs={{0,16},{4,20},{8,24},{12,28},{16,0},{20,4},{24,8},{28,12},{1,17},{... | collective-permute-start | bytes 122888 | tf_op jit(solution)/shard_map/ppermute | solution.py:798
  55.7 0.5 collective-permute-start.8
  56.3 5.7 %shard_map.115.refs_12_ = f32[2,152,512]{2,1,0:T(8,128)S(1)} custom-call(bf16[160,256]{1,0:T(8,128)(2,1)S(1)} %get-tuple-element.54.refs_1_.refs_0_, bf16[160,256]{1,0:T(8,128)(2,1)S(1)} %collective-permute-done.refs_2_.refs_1_, bf16[160,256]{1,0:T(8,128)(2,1)S(1)} %collective-permute-done.1.refs_3_.refs_2_, ...), custom_call_target="tpu_custom_call" | custom-call | flops 4294967296 | bytes 1048576 | tf_op jit(solution)/shard_map/pallas_call | solution.py:161
  62.0 0.6 collective-permute-start.11
  62.6 0.1 collective-permute-start.12
  62.7 0.4 collective-permute-start.13
  63.1 0.4 collective-permute-done.11.refs_5_
  63.5 0.3 collective-permute-done.12.refs_7_
  63.8 0.2 collective-permute-done.13.refs_9_
  64.0 3.6 %shard_map.116 = f32[32,1,512]{2,1,0:T(1,128)S(1)} custom-call(s32[2]{0:T(128)S(1)} %pad_add_fusion.me_ref.refs_0_, s32[33]{0:T(128)S(1)} %get-tuple-element.47.refs_1_, bf16[80,256]{1,0:T(8,128)(2,1)S(1)} %shard_map.114.refs_2_, bf16[80,256]{1,0:T(8,128)(2,1)S(1)} %collective-permute-done.7.refs_3_, bf16[80,256]{1,0:T(8,128)(2,1)S(1)} %collective-permute-done.8.refs_4_, ...), custom_call_target="tpu_custom_call" | custom-call | flops 4294967296 | bytes 1048576 | tf_op jit(solution)/shard_map/pallas_call | solution.py:161
  67.6 12.4 %all_to_all.10.refs_0_ = f32[32,1,512]{2,1,0:T(1,128)S(1)} all-to-all(f32[32,1,512]{2,1,0:T(1,128)S(1)} %shard_map.116), channel_id=1, replica_groups=mesh['pts'=8,'top'=4] {'pts','top'}, dimensions={0} | all-to-all | bytes 131072 | tf_op jit(solution)/shard_map/all_to_all | solution.py:924
  80.0 1.4 %shard_map.117 = f32[8,1024]{1,0:T(8,128)} custom-call(f32[32,1,512]{2,1,0:T(1,128)S(1)} %all_to_all.10.refs_0_, s32[1,1024]{1,0:T(1,128)S(1)} %copy-done.9), custom_call_target="tpu_custom_call" | custom-call | flops 268435456 | bytes 1048576 | tf_op jit(solution)/shard_map/pallas_call | solution.py:161
  (29 shorter events, 0.1 us)
Async XLA Ops:
  3.9 21.7 %all-to-all-start = ((f32[32,16,256]{2,1,0:T(8,128)}), f32[32,16,256]{2,1,0:T(8,128)S(1)}, u32[]{:S(2)}, u32[]{:S(2)}) async-start(f32[32,16,256]{2,1,0:T(8,128)} %bitcast.15), calls=%async_computation | async-start | bytes 1048576 | tf_op jit(solution)/shard_map/all_to_all | solution.py:843
  11.3 8.7 %copy-start.1 = (f32[184832]{0:T(1024)S(1)}, f32[184832]{0:T(1024)}, u32[]{:S(2)}) copy-start(f32[184832]{0:T(1024)} %param.16) | copy-start | bytes 2217988
  11.3 8.7 %copy-start.2 = (f32[184832]{0:T(1024)S(1)}, f32[184832]{0:T(1024)}, u32[]{:S(2)}) copy-start(f32[184832]{0:T(1024)} %param.20) | copy-start | bytes 2217988
  11.3 8.7 %copy-start.3 = (f32[152,152]{1,0:T(8,128)S(1)}, f32[152,152]{1,0:T(8,128)}, u32[]{:S(2)}) copy-start(f32[152,152]{1,0:T(8,128)} %refs_2_.2) | copy-start | bytes 277252
  11.3 8.7 %copy-start.4 = (f32[152,152]{1,0:T(8,128)S(1)}, f32[152,152]{1,0:T(8,128)}, u32[]{:S(2)}) copy-start(f32[152,152]{1,0:T(8,128)} %refs_3_.1) | copy-start | bytes 277252
  11.3 8.7 %copy-start.5 = (f32[152,152]{1,0:T(8,128)S(1)}, f32[152,152]{1,0:T(8,128)}, u32[]{:S(2)}) copy-start(f32[152,152]{1,0:T(8,128)} %refs_4_.1) | copy-start | bytes 277252
  11.3 8.7 %copy-start.6 = (f32[152,128]{1,0:T(8,128)S(1)}, f32[152,128]{1,0:T(8,128)}, u32[]{:S(2)}) copy-start(f32[152,128]{1,0:T(8,128)} %constant.11.clone.refs_5_.refs_2_) | copy-start | bytes 233476
  23.5 1.5 %copy-start.7 = (bf16[34,152,152]{2,1,0:T(8,128)(2,1)}, bf16[34,152,152]{2,1,0:T(8,128)(2,1)S(1)}, u32[]{:S(2)}) copy-start(bf16[34,152,152]{2,1,0:T(8,128)(2,1)S(1)} %get-tuple-element.65.refs_8_) | copy-start | bytes 4713220
  35.5 9.7 %collective-permute-start.3 = (bf16[160,256]{1,0:T(8,128)(2,1)S(1)}, bf16[160,256]{1,0:T(8,128)(2,1)S(1)}, u32[]{:S(2)}, u32[]{:S(2)}) collective-permute-start(bf16[160,256]{1,0:T(8,128)(2,1)S(1)} %get-tuple-element.54.refs_1_.refs_0_), channel_id=1, source_target_pairs={{0,24},{4,28},{8,16},{12,20},{16,8},{20,12},{24,0},{28,4},{1,25},{... | collective-permute-start | bytes 245768 | tf_op jit(solution)/shard_map/ppermute | solution.py:798
  37.8 7.4 %collective-permute-start.2 = (bf16[160,256]{1,0:T(8,128)(2,1)S(1)}, bf16[160,256]{1,0:T(8,128)(2,1)S(1)}, u32[]{:S(2)}, u32[]{:S(2)}) collective-permute-start(bf16[160,256]{1,0:T(8,128)(2,1)S(1)} %get-tuple-element.54.refs_1_.refs_0_), channel_id=1, source_target_pairs={{0,16},{4,20},{8,24},{12,28},{16,0},{20,4},{24,8},{28,12},{1,17},{... | collective-permute-start | bytes 245768 | tf_op jit(solution)/shard_map/ppermute | solution.py:798
  38.5 6.7 %collective-permute-start.1 = (bf16[160,256]{1,0:T(8,128)(2,1)S(1)}, bf16[160,256]{1,0:T(8,128)(2,1)S(1)}, u32[]{:S(2)}, u32[]{:S(2)}) collective-permute-start(bf16[160,256]{1,0:T(8,128)(2,1)S(1)} %get-tuple-element.54.refs_1_.refs_0_), channel_id=1, source_target_pairs={{0,8},{4,12},{8,0},{12,4},{16,24},{20,28},{24,16},{28,20},{1,9},{5... | collective-permute-start | bytes 245768 | tf_op jit(solution)/shard_map/ppermute | solution.py:798
  39.1 6.2 %collective-permute-start = (bf16[160,256]{1,0:T(8,128)(2,1)S(1)}, bf16[160,256]{1,0:T(8,128)(2,1)S(1)}, u32[]{:S(2)}, u32[]{:S(2)}) collective-permute-start(bf16[160,256]{1,0:T(8,128)(2,1)S(1)} %get-tuple-element.54.refs_1_.refs_0_), channel_id=1, source_target_pairs={{0,4},{4,0},{8,12},{12,8},{16,20},{20,16},{24,28},{28,24},{1,5},{5... | collective-permute-start | bytes 245768 | tf_op jit(solution)/shard_map/ppermute | solution.py:798
  39.4 7.7 %copy-start = (bf16[4,7,48,1152]{3,2,1,0:T(8,128)(2,1)S(1)}, bf16[4,7,48,1152]{3,2,1,0:T(8,128)(2,1)}, u32[]{:S(2)}) copy-start(bf16[4,7,48,1152]{3,2,1,0:T(8,128)(2,1)} %get-tuple-element.59.refs_9_) | copy-start | bytes 9289732
  45.3 11.0 %copy-start.8 = (bf16[34,152,152]{2,1,0:T(8,128)(2,1)S(1)}, bf16[34,152,152]{2,1,0:T(8,128)(2,1)}, u32[]{:S(2)}) copy-start(bf16[34,152,152]{2,1,0:T(8,128)(2,1)} %copy-done.7) | copy-start | bytes 4713220
  45.3 1.3 %collective-permute-start.4 = (bf16[160,256]{1,0:T(8,128)(2,1)S(1)}, bf16[160,256]{1,0:T(8,128)(2,1)S(1)}, u32[]{:S(2)}, u32[]{:S(2)}) collective-permute-start(bf16[160,256]{1,0:T(8,128)(2,1)S(1)} %collective-permute-done.1.refs_3_.refs_2_), channel_id=1, source_target_pairs={{0,4},{4,0},{8,12},{12,8},{16,20},{20,16},{24,28},{28,24},{1,5},{5... | collective-permute-start | bytes 245768 | tf_op jit(solution)/shard_map/ppermute | solution.py:798
  45.5 1.3 %collective-permute-start.5 = (bf16[160,256]{1,0:T(8,128)(2,1)S(1)}, bf16[160,256]{1,0:T(8,128)(2,1)S(1)}, u32[]{:S(2)}, u32[]{:S(2)}) collective-permute-start(bf16[160,256]{1,0:T(8,128)(2,1)S(1)} %collective-permute-done.2.refs_5_.refs_4_), channel_id=1, source_target_pairs={{0,4},{4,0},{8,12},{12,8},{16,20},{20,16},{24,28},{28,24},{1,5},{5... | collective-permute-start | bytes 245768 | tf_op jit(solution)/shard_map/ppermute | solution.py:798
  45.9 1.3 %collective-permute-start.6 = (bf16[160,256]{1,0:T(8,128)(2,1)S(1)}, bf16[160,256]{1,0:T(8,128)(2,1)S(1)}, u32[]{:S(2)}, u32[]{:S(2)}) collective-permute-start(bf16[160,256]{1,0:T(8,128)(2,1)S(1)} %collective-permute-done.3.refs_7_.refs_6_), channel_id=1, source_target_pairs={{0,4},{4,0},{8,12},{12,8},{16,20},{20,16},{24,28},{28,24},{1,5},{5... | collective-permute-start | bytes 245768 | tf_op jit(solution)/shard_map/ppermute | solution.py:798
  52.7 9.3 %collective-permute-start.10 = (bf16[80,256]{1,0:T(8,128)(2,1)S(1)}, bf16[80,256]{1,0:T(8,128)(2,1)S(1)}, u32[]{:S(2)}, u32[]{:S(2)}) collective-permute-start(bf16[80,256]{1,0:T(8,128)(2,1)S(1)} %shard_map.114.refs_2_), channel_id=1, source_target_pairs={{0,24},{4,28},{8,16},{12,20},{16,8},{20,12},{24,0},{28,4},{1,25},{... | collective-permute-start | bytes 122888 | tf_op jit(solution)/shard_map/ppermute | solution.py:798
  54.8 7.2 %collective-permute-start.9 = (bf16[80,256]{1,0:T(8,128)(2,1)S(1)}, bf16[80,256]{1,0:T(8,128)(2,1)S(1)}, u32[]{:S(2)}, u32[]{:S(2)}) collective-permute-start(bf16[80,256]{1,0:T(8,128)(2,1)S(1)} %shard_map.114.refs_2_), channel_id=1, source_target_pairs={{0,16},{4,20},{8,24},{12,28},{16,0},{20,4},{24,8},{28,12},{1,17},{... | collective-permute-start | bytes 122888 | tf_op jit(solution)/shard_map/ppermute | solution.py:798
  55.7 6.3 %collective-permute-start.8 = (bf16[80,256]{1,0:T(8,128)(2,1)S(1)}, bf16[80,256]{1,0:T(8,128)(2,1)S(1)}, u32[]{:S(2)}, u32[]{:S(2)}) collective-permute-start(bf16[80,256]{1,0:T(8,128)(2,1)S(1)} %shard_map.114.refs_2_), channel_id=1, source_target_pairs={{0,8},{4,12},{8,0},{12,4},{16,24},{20,28},{24,16},{28,20},{1,9},{5... | collective-permute-start | bytes 122888 | tf_op jit(solution)/shard_map/ppermute | solution.py:798
  56.3 5.7 %collective-permute-start.7 = (bf16[80,256]{1,0:T(8,128)(2,1)S(1)}, bf16[80,256]{1,0:T(8,128)(2,1)S(1)}, u32[]{:S(2)}, u32[]{:S(2)}) collective-permute-start(bf16[80,256]{1,0:T(8,128)(2,1)S(1)} %shard_map.114.refs_2_), channel_id=1, source_target_pairs={{0,4},{4,0},{8,12},{12,8},{16,20},{20,16},{24,28},{28,24},{1,5},{5... | collective-permute-start | bytes 122888 | tf_op jit(solution)/shard_map/ppermute | solution.py:798
  62.0 1.4 %collective-permute-start.11 = (bf16[80,256]{1,0:T(8,128)(2,1)S(1)}, bf16[80,256]{1,0:T(8,128)(2,1)S(1)}, u32[]{:S(2)}, u32[]{:S(2)}) collective-permute-start(bf16[80,256]{1,0:T(8,128)(2,1)S(1)} %collective-permute-done.8.refs_4_), channel_id=1, source_target_pairs={{0,4},{4,0},{8,12},{12,8},{16,20},{20,16},{24,28},{28,24},{1,5},{5... | collective-permute-start | bytes 122888 | tf_op jit(solution)/shard_map/ppermute | solution.py:798
  62.6 1.2 %collective-permute-start.12 = (bf16[80,256]{1,0:T(8,128)(2,1)S(1)}, bf16[80,256]{1,0:T(8,128)(2,1)S(1)}, u32[]{:S(2)}, u32[]{:S(2)}) collective-permute-start(bf16[80,256]{1,0:T(8,128)(2,1)S(1)} %collective-permute-done.9.refs_6_), channel_id=1, source_target_pairs={{0,4},{4,0},{8,12},{12,8},{16,20},{20,16},{24,28},{28,24},{1,5},{5... | collective-permute-start | bytes 122888 | tf_op jit(solution)/shard_map/ppermute | solution.py:798
  62.7 1.3 %collective-permute-start.13 = (bf16[80,256]{1,0:T(8,128)(2,1)S(1)}, bf16[80,256]{1,0:T(8,128)(2,1)S(1)}, u32[]{:S(2)}, u32[]{:S(2)}) collective-permute-start(bf16[80,256]{1,0:T(8,128)(2,1)S(1)} %collective-permute-done.10.refs_8_), channel_id=1, source_target_pairs={{0,4},{4,0},{8,12},{12,8},{16,20},{20,16},{24,28},{28,24},{1,5},{5... | collective-permute-start | bytes 122888 | tf_op jit(solution)/shard_map/ppermute | solution.py:798
  64.0 16.1 %copy-start.9 = (s32[1,1024]{1,0:T(1,128)S(1)}, s32[1,1024]{1,0:T(1,128)}, u32[]{:S(2)}) copy-start(s32[1,1024]{1,0:T(1,128)} %get-tuple-element.76.refs_1_) | copy-start | bytes 12292

commit v8 on v7

--- a/solution.py
+++ b/solution.py
@@ -592,7 +592,6 @@
     digits = jnp.broadcast_to(digits, (2, out_rows))
     blank = jnp.zeros((out.shape[0] - COEF - 2, out_rows), f32)
     out[...] = jnp.concatenate([total, digits, blank], axis=0).astype(bf16)
-    io.send(0)
 
 
 def box_ids(parts, dens):
@@ -867,9 +866,8 @@
             shape(1, own, dtype=jnp.int32),
         ],
         8 << 30,
-        late=(0,),
-        here=(2,),
-        stays=(1, 2),
+        here=range(3),
+        stays=range(3),
         numbers=[shape(sources + 1, dtype=jnp.int32)],
         scratch=[
             pltpu.VMEM((8, up(own + up(cap, LANE) + LANE, PB)), f32),
@@ -889,7 +887,8 @@
         [*parts, *first, *rest],
         [shape(ROWS, slabs * columns)],
         8 << 30,
-        here=range(n_pts, n_pts + 6),
+        here=range(n_pts + 6),
+        stays=(0,),
         scratch=[
             pltpu.VMEM(((7 + slabs - 1) * columns, WFULL), bf16),
             pltpu.VMEM(((7 + slabs - 1) * columns, WIN), bf16),
@@ -902,7 +901,7 @@
         [*parts, opers],
         [shape(dens, coef, BOXES4, dtype=f32)],
         4 << 30,
-        here=(n_pts,),
+        here=range(n_pts + 1),
         stays=(0,),
     )
     step = n_pts // SIDE * slabs
@@ -915,7 +914,8 @@
         [*gathered, *halves, lattice4, place, field],
         [shape(sources, 1, dens * cap, dtype=f32)],
         4 << 30,
-        here=range(len(gathered), len(gathered) + 5),
+        here=range(len(gathered) + 5),
+        stays=(0,),
         scratch=[
             pltpu.VMEM((2 * dens * CPAD, 2 * BOXES4), f32),
             pltpu.VMEM((8, own + up(cap, LANE) + LANE), f32),
@@ -928,7 +928,7 @@
         [returned, entries],
         [shape(DENS, points, dtype=f32)],
         1 << 28,
-        here=(1,),
+        here=range(2),
     )
     return out
 

time: 82 us -> 78.8 us (0.961)
  Pallas kernels: 48 us -> 44.8 us
    pallas_call x7, Pallas kernels: 33.6 us -> 30.2 us  [run(): call(body, tuple(outs) + tuple(numbers), grant, flops, in_specs=[SMEM] *...]
where the time goes in v8:
time: 78.8 us; the launch traced here: 78.4 us
  Pallas kernels  44.8 us (57%)
  starting transfers between devices  16.6 us (21%)
  blocking collectives  12.4 us (16%)
  waiting for transfers between devices  2.52 us (3%)
  local copies, waits for them, and re-layouts  1.54 us (2%)
    pallas_call x7, Pallas kernels, run(): call(body, tuple(outs) + tuple(numbers), grant, flops, in_specs=[SMEM] *...  30.2 us
    pallas_call x2, Pallas kernels, relayout(): call(functools.partial(relayout_kernel, nrows, step0, steps), tuple((jax....  14.6 us
    all_to_all x1, blocking collectives, per_device(): lax.all_to_all(reply, ('pts', 'top'), split_axis=0, concat_axis=0, tiled=...  12.4 us
    ppermute x14, starting transfers between devices, shift_by(): return lax.ppermute(value, axis, [(i, i ^ distance) for i in range(size)])  9.27 us
    all_to_all x1, starting transfers between devices, per_device(): lax.all_to_all(outgoing, ('pts', 'top'), split_axis=0, concat_axis=0, til...  7.3 us
    ppermute x14, waiting for transfers between devices, shift_by(): return lax.ppermute(value, axis, [(i, i ^ distance) for i in range(size)])  2 us
  transfers between devices with their start and end apart: 15, of which 7 were waited for; matrix products, arithmetic and copies ran while one was open for 0% of the time, Pallas kernels for 29%

profile of v8, /device:TPU:0, one launch (start us, length us, event | category | flops | bytes accessed | tf_op | source)
XLA Modules:
  0.0 78.4 jit_solution(13465615124960387208)
XLA Ops:
  0.0 3.9 %shard_map.109 = (f32[8,4,16,256]{3,2,1,0:T(8,128)}, s32[1,1024]{1,0:T(1,128)}) custom-call(f32[3,1024]{1,0:T(4,128)} %refs_0_.1, f32[8,1024]{1,0:T(8,128)} %refs_1_.1, s32[1,1024]{1,0:T(1,128)} %bitcast.16, s32[8,128]{1,0:T(8,128)} %bitcast.17), custom_call_target="tpu_custom_call" | custom-call | flops 134217728 | bytes 1048576 | tf_op jit(solution)/shard_map/pallas_call | solution.py:161
  3.9 7.3 %all-to-all-start = ((f32[32,16,256]{2,1,0:T(8,128)}), f32[32,16,256]{2,1,0:T(8,128)S(1)}, u32[]{:S(2)}, u32[]{:S(2)}) async-start(f32[32,16,256]{2,1,0:T(8,128)} %bitcast.15), calls=%async_computation | async-start | bytes 1048576 | tf_op jit(solution)/shard_map/all_to_all | solution.py:842
  11.3 8.6 %shard_map.110 = (bf16[4,7,48,1152]{3,2,1,0:T(8,128)(2,1)}, bf16[3,4,48,1152]{3,2,1,0:T(8,128)(2,1)S(1)}, bf16[3,3,48,640]{3,2,1,0:T(8,128)(2,1)S(1)}) custom-call(s32[2]{0:T(128)S(1)} %pad_add_fusion.me_ref.refs_0_, bf16[57038,128]{1,0:T(8,128)(2,1)} %bitcast.11, bf16[57038,128]{1,0:T(8,128)(2,1)} %bitcast.12), custom_call_target="tpu_custom_call" | custom-call | flops 1048576 | bytes 6291456 | tf_op jit(solution)/shard_map/pallas_call | solution.py:298
  20.0 3.5 %shard_map.111 = (bf16[304,1280]{1,0:T(8,128)(2,1)S(1)}, bf16[34,152,152]{2,1,0:T(8,128)(2,1)S(1)}, bf16[2,152,80]{2,1,0:T(8,128)(2,1)S(1)}, bf16[2,152,80]{2,1,0:T(8,128)(2,1)S(1)}) custom-call(f32[1444,128]{1,0:T(8,128)S(1)} %bitcast.9, f32[1444,128]{1,0:T(8,128)S(1)} %bitcast.10, f32[152,152]{1,0:T(8,128)S(1)} %copy-done.3, f32[152,152]{1,0:T(8,128)S(1)} %copy-done.4, ...), custom_call_target="tpu_custom_call" | custom-call | flops 1073741824 | bytes 1048576 | tf_op jit(solution)/shard_map/pallas_call | solution.py:161
  23.6 1.5 %copy-done.7 = bf16[34,152,152]{2,1,0:T(8,128)(2,1)} copy-done((bf16[34,152,152]{2,1,0:T(8,128)(2,1)}, bf16[34,152,152]{2,1,0:T(8,128)(2,1)S(1)}, u32[]{:S(2)}) %copy-start.7) | copy-done | bytes 1571096
  25.1 0.5 all-to-all-done.refs_1_
  25.6 9.1 %shard_map.112 = (bf16[160,256]{1,0:T(8,128)(2,1)S(1)}, f32[152,4096]{1,0:T(8,128)S(1)}, s32[1,4096]{1,0:T(1,128)S(1)}, s32[33]{0:T(128)S(1)}) custom-call(s32[2]{0:T(128)S(1)} %pad_add_fusion.me_ref.refs_0_, f32[32,16,256]{2,1,0:T(8,128)S(1)} %all-to-all-done.refs_1_, f32[152,128]{1,0:T(8,128)S(1)} %copy-done.6, bf16[304,1280]{1,0:T(8,128)(2,1)S(1)} %get-tuple-element.46.refs_3_), custom_call_target="tpu_custom_call" | custom-call | flops 8589934592 | bytes 1048576 | tf_op jit(solution)/shard_map/pallas_call | solution.py:161
  34.7 2.3 %collective-permute-start.3 = (bf16[160,256]{1,0:T(8,128)(2,1)S(1)}, bf16[160,256]{1,0:T(8,128)(2,1)S(1)}, u32[]{:S(2)}, u32[]{:S(2)}) collective-permute-start(bf16[160,256]{1,0:T(8,128)(2,1)S(1)} %get-tuple-element.54.refs_1_.refs_0_), channel_id=1, source_target_pairs={{0,24},{4,28},{8,16},{12,20},{16,8},{20,12},{24,0},{28,4},{1,25},{... | collective-permute-start | bytes 245768 | tf_op jit(solution)/shard_map/ppermute | solution.py:797
  36.9 0.7 collective-permute-start.2
  37.7 0.6 collective-permute-start.1
  38.2 0.3 collective-permute-start
  38.6 6.0 %shard_map.113 = (bf16[4,7,32,1152]{3,2,1,0:T(8,128)(2,1)S(1)}, bf16[3,4,32,1152]{3,2,1,0:T(8,128)(2,1)S(1)}, bf16[3,3,32,640]{3,2,1,0:T(8,128)(2,1)S(1)}) custom-call(s32[2]{0:T(128)S(1)} %pad_add_fusion.me_ref.refs_0_, bf16[57038,128]{1,0:T(8,128)(2,1)} %bitcast.13, bf16[57038,128]{1,0:T(8,128)(2,1)} %bitcast.14), custom_call_target="tpu_custom_call" | custom-call | flops 1048576 | bytes 4194304 | tf_op jit(solution)/shard_map/pallas_call | solution.py:298
  44.6 0.2 collective-permute-start.4
  44.8 0.3 collective-permute-start.5
  45.2 0.2 collective-permute-start.6
  45.3 0.6 collective-permute-done.4.refs_4_.refs_3_
  45.9 0.2 collective-permute-done.5.refs_6_.refs_5_
  46.1 0.3 collective-permute-done.6.refs_8_.refs_7_
  46.5 4.5 %shard_map.114.refs_2_ = bf16[80,256]{1,0:T(8,128)(2,1)S(1)} custom-call(s32[2]{0:T(128)S(1)} %pad_add_fusion.me_ref.refs_0_, bf16[160,256]{1,0:T(8,128)(2,1)S(1)} %get-tuple-element.54.refs_1_.refs_0_, bf16[160,256]{1,0:T(8,128)(2,1)S(1)} %collective-permute-done.refs_2_.refs_1_, bf16[160,256]{1,0:T(8,128)(2,1)S(1)} %collective-permute-done.1.refs_3_.refs_2_, ...), custom_call_target="tpu_custom_call" | custom-call | flops 8589934592 | bytes 1048576 | tf_op jit(solution)/shard_map/pallas_call | solution.py:161
  51.0 2.1 %collective-permute-start.10 = (bf16[80,256]{1,0:T(8,128)(2,1)S(1)}, bf16[80,256]{1,0:T(8,128)(2,1)S(1)}, u32[]{:S(2)}, u32[]{:S(2)}) collective-permute-start(bf16[80,256]{1,0:T(8,128)(2,1)S(1)} %shard_map.114.refs_2_), channel_id=1, source_target_pairs={{0,24},{4,28},{8,16},{12,20},{16,8},{20,12},{24,0},{28,4},{1,25},{... | collective-permute-start | bytes 122888 | tf_op jit(solution)/shard_map/ppermute | solution.py:797
  53.0 0.9 %collective-permute-start.9 = (bf16[80,256]{1,0:T(8,128)(2,1)S(1)}, bf16[80,256]{1,0:T(8,128)(2,1)S(1)}, u32[]{:S(2)}, u32[]{:S(2)}) collective-permute-start(bf16[80,256]{1,0:T(8,128)(2,1)S(1)} %shard_map.114.refs_2_), channel_id=1, source_target_pairs={{0,16},{4,20},{8,24},{12,28},{16,0},{20,4},{24,8},{28,12},{1,17},{... | collective-permute-start | bytes 122888 | tf_op jit(solution)/shard_map/ppermute | solution.py:797
  54.0 0.6 collective-permute-start.8
  54.5 4.8 %shard_map.115.refs_12_ = f32[2,152,512]{2,1,0:T(8,128)S(1)} custom-call(bf16[160,256]{1,0:T(8,128)(2,1)S(1)} %get-tuple-element.54.refs_1_.refs_0_, bf16[160,256]{1,0:T(8,128)(2,1)S(1)} %collective-permute-done.refs_2_.refs_1_, bf16[160,256]{1,0:T(8,128)(2,1)S(1)} %collective-permute-done.1.refs_3_.refs_2_, ...), custom_call_target="tpu_custom_call" | custom-call | flops 4294967296 | bytes 1048576 | tf_op jit(solution)/shard_map/pallas_call | solution.py:161
  59.4 0.6 collective-permute-start.11
  60.0 0.1 collective-permute-start.12
  60.1 0.4 collective-permute-start.13
  60.5 0.4 collective-permute-done.11.refs_5_
  60.9 0.3 collective-permute-done.12.refs_7_
  61.2 0.2 collective-permute-done.13.refs_9_
  61.4 3.1 %shard_map.116 = f32[32,1,512]{2,1,0:T(1,128)S(1)} custom-call(s32[2]{0:T(128)S(1)} %pad_add_fusion.me_ref.refs_0_, s32[33]{0:T(128)S(1)} %get-tuple-element.47.refs_1_, bf16[80,256]{1,0:T(8,128)(2,1)S(1)} %shard_map.114.refs_2_, bf16[80,256]{1,0:T(8,128)(2,1)S(1)} %collective-permute-done.7.refs_3_, bf16[80,256]{1,0:T(8,128)(2,1)S(1)} %collective-permute-done.8.refs_4_, ...), custom_call_target="tpu_custom_call" | custom-call | flops 4294967296 | bytes 1048576 | tf_op jit(solution)/shard_map/pallas_call | solution.py:161
  64.5 12.4 %all_to_all.10.refs_0_ = f32[32,1,512]{2,1,0:T(1,128)S(1)} all-to-all(f32[32,1,512]{2,1,0:T(1,128)S(1)} %shard_map.116), channel_id=1, replica_groups=mesh['pts'=8,'top'=4] {'pts','top'}, dimensions={0} | all-to-all | bytes 131072 | tf_op jit(solution)/shard_map/all_to_all | solution.py:924
  76.9 1.3 %shard_map.117 = f32[8,1024]{1,0:T(8,128)} custom-call(f32[32,1,512]{2,1,0:T(1,128)S(1)} %all_to_all.10.refs_0_, s32[1,1024]{1,0:T(1,128)S(1)} %copy-done.9), custom_call_target="tpu_custom_call" | custom-call | flops 268435456 | bytes 1048576 | tf_op jit(solution)/shard_map/pallas_call | solution.py:161
  (29 shorter events, 0.1 us)
Async XLA Ops:
  3.9 21.7 %all-to-all-start = ((f32[32,16,256]{2,1,0:T(8,128)}), f32[32,16,256]{2,1,0:T(8,128)S(1)}, u32[]{:S(2)}, u32[]{:S(2)}) async-start(f32[32,16,256]{2,1,0:T(8,128)} %bitcast.15), calls=%async_computation | async-start | bytes 1048576 | tf_op jit(solution)/shard_map/all_to_all | solution.py:842
  11.3 8.7 %copy-start.1 = (f32[184832]{0:T(1024)S(1)}, f32[184832]{0:T(1024)}, u32[]{:S(2)}) copy-start(f32[184832]{0:T(1024)} %param.16) | copy-start | bytes 2217988
  11.3 8.7 %copy-start.2 = (f32[184832]{0:T(1024)S(1)}, f32[184832]{0:T(1024)}, u32[]{:S(2)}) copy-start(f32[184832]{0:T(1024)} %param.20) | copy-start | bytes 2217988
  11.3 8.7 %copy-start.3 = (f32[152,152]{1,0:T(8,128)S(1)}, f32[152,152]{1,0:T(8,128)}, u32[]{:S(2)}) copy-start(f32[152,152]{1,0:T(8,128)} %refs_2_.2) | copy-start | bytes 277252
  11.3 8.7 %copy-start.4 = (f32[152,152]{1,0:T(8,128)S(1)}, f32[152,152]{1,0:T(8,128)}, u32[]{:S(2)}) copy-start(f32[152,152]{1,0:T(8,128)} %refs_3_.1) | copy-start | bytes 277252
  11.3 8.7 %copy-start.5 = (f32[152,152]{1,0:T(8,128)S(1)}, f32[152,152]{1,0:T(8,128)}, u32[]{:S(2)}) copy-start(f32[152,152]{1,0:T(8,128)} %refs_4_.1) | copy-start | bytes 277252
  11.3 8.7 %copy-start.6 = (f32[152,128]{1,0:T(8,128)S(1)}, f32[152,128]{1,0:T(8,128)}, u32[]{:S(2)}) copy-start(f32[152,128]{1,0:T(8,128)} %constant.11.clone.refs_5_.refs_2_) | copy-start | bytes 233476
  23.5 1.5 %copy-start.7 = (bf16[34,152,152]{2,1,0:T(8,128)(2,1)}, bf16[34,152,152]{2,1,0:T(8,128)(2,1)S(1)}, u32[]{:S(2)}) copy-start(bf16[34,152,152]{2,1,0:T(8,128)(2,1)S(1)} %get-tuple-element.65.refs_8_) | copy-start | bytes 4713220
  34.7 9.9 %collective-permute-start.3 = (bf16[160,256]{1,0:T(8,128)(2,1)S(1)}, bf16[160,256]{1,0:T(8,128)(2,1)S(1)}, u32[]{:S(2)}, u32[]{:S(2)}) collective-permute-start(bf16[160,256]{1,0:T(8,128)(2,1)S(1)} %get-tuple-element.54.refs_1_.refs_0_), channel_id=1, source_target_pairs={{0,24},{4,28},{8,16},{12,20},{16,8},{20,12},{24,0},{28,4},{1,25},{... | collective-permute-start | bytes 245768 | tf_op jit(solution)/shard_map/ppermute | solution.py:797
  36.9 7.6 %collective-permute-start.2 = (bf16[160,256]{1,0:T(8,128)(2,1)S(1)}, bf16[160,256]{1,0:T(8,128)(2,1)S(1)}, u32[]{:S(2)}, u32[]{:S(2)}) collective-permute-start(bf16[160,256]{1,0:T(8,128)(2,1)S(1)} %get-tuple-element.54.refs_1_.refs_0_), channel_id=1, source_target_pairs={{0,16},{4,20},{8,24},{12,28},{16,0},{20,4},{24,8},{28,12},{1,17},{... | collective-permute-start | bytes 245768 | tf_op jit(solution)/shard_map/ppermute | solution.py:797
  37.7 6.9 %collective-permute-start.1 = (bf16[160,256]{1,0:T(8,128)(2,1)S(1)}, bf16[160,256]{1,0:T(8,128)(2,1)S(1)}, u32[]{:S(2)}, u32[]{:S(2)}) collective-permute-start(bf16[160,256]{1,0:T(8,128)(2,1)S(1)} %get-tuple-element.54.refs_1_.refs_0_), channel_id=1, source_target_pairs={{0,8},{4,12},{8,0},{12,4},{16,24},{20,28},{24,16},{28,20},{1,9},{5... | collective-permute-start | bytes 245768 | tf_op jit(solution)/shard_map/ppermute | solution.py:797
  38.2 6.3 %collective-permute-start = (bf16[160,256]{1,0:T(8,128)(2,1)S(1)}, bf16[160,256]{1,0:T(8,128)(2,1)S(1)}, u32[]{:S(2)}, u32[]{:S(2)}) collective-permute-start(bf16[160,256]{1,0:T(8,128)(2,1)S(1)} %get-tuple-element.54.refs_1_.refs_0_), channel_id=1, source_target_pairs={{0,4},{4,0},{8,12},{12,8},{16,20},{20,16},{24,28},{28,24},{1,5},{5... | collective-permute-start | bytes 245768 | tf_op jit(solution)/shard_map/ppermute | solution.py:797
  38.6 7.9 %copy-start = (bf16[4,7,48,1152]{3,2,1,0:T(8,128)(2,1)S(1)}, bf16[4,7,48,1152]{3,2,1,0:T(8,128)(2,1)}, u32[]{:S(2)}) copy-start(bf16[4,7,48,1152]{3,2,1,0:T(8,128)(2,1)} %get-tuple-element.59.refs_9_) | copy-start | bytes 9289732
  44.6 9.9 %copy-start.8 = (bf16[34,152,152]{2,1,0:T(8,128)(2,1)S(1)}, bf16[34,152,152]{2,1,0:T(8,128)(2,1)}, u32[]{:S(2)}) copy-start(bf16[34,152,152]{2,1,0:T(8,128)(2,1)} %copy-done.7) | copy-start | bytes 4713220
  44.6 1.3 %collective-permute-start.4 = (bf16[160,256]{1,0:T(8,128)(2,1)S(1)}, bf16[160,256]{1,0:T(8,128)(2,1)S(1)}, u32[]{:S(2)}, u32[]{:S(2)}) collective-permute-start(bf16[160,256]{1,0:T(8,128)(2,1)S(1)} %collective-permute-done.1.refs_3_.refs_2_), channel_id=1, source_target_pairs={{0,4},{4,0},{8,12},{12,8},{16,20},{20,16},{24,28},{28,24},{1,5},{5... | collective-permute-start | bytes 245768 | tf_op jit(solution)/shard_map/ppermute | solution.py:797
  44.8 1.3 %collective-permute-start.5 = (bf16[160,256]{1,0:T(8,128)(2,1)S(1)}, bf16[160,256]{1,0:T(8,128)(2,1)S(1)}, u32[]{:S(2)}, u32[]{:S(2)}) collective-permute-start(bf16[160,256]{1,0:T(8,128)(2,1)S(1)} %collective-permute-done.2.refs_5_.refs_4_), channel_id=1, source_target_pairs={{0,4},{4,0},{8,12},{12,8},{16,20},{20,16},{24,28},{28,24},{1,5},{5... | collective-permute-start | bytes 245768 | tf_op jit(solution)/shard_map/ppermute | solution.py:797
  45.2 1.3 %collective-permute-start.6 = (bf16[160,256]{1,0:T(8,128)(2,1)S(1)}, bf16[160,256]{1,0:T(8,128)(2,1)S(1)}, u32[]{:S(2)}, u32[]{:S(2)}) collective-permute-start(bf16[160,256]{1,0:T(8,128)(2,1)S(1)} %collective-permute-done.3.refs_7_.refs_6_), channel_id=1, source_target_pairs={{0,4},{4,0},{8,12},{12,8},{16,20},{20,16},{24,28},{28,24},{1,5},{5... | collective-permute-start | bytes 245768 | tf_op jit(solution)/shard_map/ppermute | solution.py:797
  51.0 8.4 %collective-permute-start.10 = (bf16[80,256]{1,0:T(8,128)(2,1)S(1)}, bf16[80,256]{1,0:T(8,128)(2,1)S(1)}, u32[]{:S(2)}, u32[]{:S(2)}) collective-permute-start(bf16[80,256]{1,0:T(8,128)(2,1)S(1)} %shard_map.114.refs_2_), channel_id=1, source_target_pairs={{0,24},{4,28},{8,16},{12,20},{16,8},{20,12},{24,0},{28,4},{1,25},{... | collective-permute-start | bytes 122888 | tf_op jit(solution)/shard_map/ppermute | solution.py:797
  53.0 6.3 %collective-permute-start.9 = (bf16[80,256]{1,0:T(8,128)(2,1)S(1)}, bf16[80,256]{1,0:T(8,128)(2,1)S(1)}, u32[]{:S(2)}, u32[]{:S(2)}) collective-permute-start(bf16[80,256]{1,0:T(8,128)(2,1)S(1)} %shard_map.114.refs_2_), channel_id=1, source_target_pairs={{0,16},{4,20},{8,24},{12,28},{16,0},{20,4},{24,8},{28,12},{1,17},{... | collective-permute-start | bytes 122888 | tf_op jit(solution)/shard_map/ppermute | solution.py:797
  54.0 5.4 %collective-permute-start.8 = (bf16[80,256]{1,0:T(8,128)(2,1)S(1)}, bf16[80,256]{1,0:T(8,128)(2,1)S(1)}, u32[]{:S(2)}, u32[]{:S(2)}) collective-permute-start(bf16[80,256]{1,0:T(8,128)(2,1)S(1)} %shard_map.114.refs_2_), channel_id=1, source_target_pairs={{0,8},{4,12},{8,0},{12,4},{16,24},{20,28},{24,16},{28,20},{1,9},{5... | collective-permute-start | bytes 122888 | tf_op jit(solution)/shard_map/ppermute | solution.py:797
  54.5 4.9 %collective-permute-start.7 = (bf16[80,256]{1,0:T(8,128)(2,1)S(1)}, bf16[80,256]{1,0:T(8,128)(2,1)S(1)}, u32[]{:S(2)}, u32[]{:S(2)}) collective-permute-start(bf16[80,256]{1,0:T(8,128)(2,1)S(1)} %shard_map.114.refs_2_), channel_id=1, source_target_pairs={{0,4},{4,0},{8,12},{12,8},{16,20},{20,16},{24,28},{28,24},{1,5},{5... | collective-permute-start | bytes 122888 | tf_op jit(solution)/shard_map/ppermute | solution.py:797
  59.4 1.4 %collective-permute-start.11 = (bf16[80,256]{1,0:T(8,128)(2,1)S(1)}, bf16[80,256]{1,0:T(8,128)(2,1)S(1)}, u32[]{:S(2)}, u32[]{:S(2)}) collective-permute-start(bf16[80,256]{1,0:T(8,128)(2,1)S(1)} %collective-permute-done.8.refs_4_), channel_id=1, source_target_pairs={{0,4},{4,0},{8,12},{12,8},{16,20},{20,16},{24,28},{28,24},{1,5},{5... | collective-permute-start | bytes 122888 | tf_op jit(solution)/shard_map/ppermute | solution.py:797
  60.0 1.2 %collective-permute-start.12 = (bf16[80,256]{1,0:T(8,128)(2,1)S(1)}, bf16[80,256]{1,0:T(8,128)(2,1)S(1)}, u32[]{:S(2)}, u32[]{:S(2)}) collective-permute-start(bf16[80,256]{1,0:T(8,128)(2,1)S(1)} %collective-permute-done.9.refs_6_), channel_id=1, source_target_pairs={{0,4},{4,0},{8,12},{12,8},{16,20},{20,16},{24,28},{28,24},{1,5},{5... | collective-permute-start | bytes 122888 | tf_op jit(solution)/shard_map/ppermute | solution.py:797
  60.1 1.3 %collective-permute-start.13 = (bf16[80,256]{1,0:T(8,128)(2,1)S(1)}, bf16[80,256]{1,0:T(8,128)(2,1)S(1)}, u32[]{:S(2)}, u32[]{:S(2)}) collective-permute-start(bf16[80,256]{1,0:T(8,128)(2,1)S(1)} %collective-permute-done.10.refs_8_), channel_id=1, source_target_pairs={{0,4},{4,0},{8,12},{12,8},{16,20},{20,16},{24,28},{28,24},{1,5},{5... | collective-permute-start | bytes 122888 | tf_op jit(solution)/shard_map/ppermute | solution.py:797
  61.4 15.5 %copy-start.9 = (s32[1,1024]{1,0:T(1,128)S(1)}, s32[1,1024]{1,0:T(1,128)}, u32[]{:S(2)}) copy-start(s32[1,1024]{1,0:T(1,128)} %get-tuple-element.76.refs_1_) | copy-start | bytes 12292

commit v9 on v8

--- a/solution.py
+++ b/solution.py
@@ -181,7 +181,7 @@
 ROWS = 16 * STEPS
 CHUNK = up(HG + 15, 16)
 TAIL = 32
-EARLY = 3
+EARLY = 2
 STRIDE = 17
 PIECES = ((4, 7, WFULL), (3, 4, WFULL), (3, 3, WIN))
 
@@ -423,9 +423,8 @@
     block = max(cap, LANE)
     per = DENS // n_top
     leaves = leaf[...].astype(f32)
-    if leaves.shape[1] < cap:
-        blank = jnp.zeros((leaves.shape[0], cap - leaves.shape[1]), f32)
-        leaves = jnp.concatenate([leaves, blank], axis=1)
+    leaves = [leaves[r : r + 1] for r in range(leaves.shape[0])]
+    lanes = leaf.shape[1]
     for o in range(owners * cap // block):
         there = entry == o * block + lax.broadcasted_iota(jnp.int32, (block, points), 0)
         there = jnp.where(there, 1.0, 0.0).astype(bf16)
@@ -434,13 +433,15 @@
         where = got[width : width + 1] * 64.0 + got[width + 1 : width + 2]
         valid = got[width + 2 : width + 3]
         for q in range(n_top):
-            rows = [value[0:3], where, valid, value[3 + per * q : 3 + per * (q + 1)]]
-            rows.append(jnp.zeros((8 - 5 - per, block), f32))
-            packed = jnp.concatenate([r for r in rows if r.shape[0]], axis=0)
+            rows = [value[r : r + 1] for r in range(3)] + [where, valid]
+            rows += [value[3 + per * q + k : 4 + per * q + k] for k in range(per)]
             for i in range(block // cap):
                 at = o * (block // cap) + i
-                out[at, q, 0:8] = packed[:, i * cap : (i + 1) * cap]
-                out[at, q, 8:] = leaves
+                for r, value_row in enumerate(rows):
+                    out[at, q, :, r * cap : (r + 1) * cap] = value_row[:, i * cap : (i + 1) * cap]
+                for r, value_row in enumerate(leaves):
+                    base = len(rows) * cap + r * lanes
+                    out[at, q, :, base : base + lanes] = value_row
 
 
 def restore_kernel(n_top, io):
@@ -517,11 +518,15 @@
 
 
 def points_kernel(n_top, box_cap, io, offsets, buf, surf, octants, outgoing):
-    got, column, oper = io.ins
+    got, column, oper = io.ins[:3]
     out, field, place = io.outs
-    sources, _, cap = got.shape
+    sources = got.shape[0]
+    own = field.shape[1]
+    dens = out.shape[1] // box_cap
+    points = own // n_top
+    cap = 2 * points * n_top // sources
+    leaf_at = (5 + dens) * cap
     lanes = min(cap, LANE)
-    own = field.shape[1]
     wide = up(cap, LANE)
     me = io.scalars[0][0]
     buf[...] = jnp.zeros_like(buf)
@@ -529,7 +534,11 @@
     io.wait(0)
 
     def put(i, offset):
-        values = [got[i * STRIP + s, 0:8] for s in range(STRIP)]
+        values = []
+        for s in range(STRIP):
+            pieces = [got[i * STRIP + s, :, r * cap : (r + 1) * cap] for r in range(5 + dens)]
+            pieces.append(jnp.zeros((3 - dens, cap), f32))
+            values.append(jnp.concatenate(pieces, axis=0))
         counts = [jnp.sum(v[4:5]).astype(jnp.int32) for v in values]
         for s, (value, count) in enumerate(zip(values, counts)):
             offsets[i * STRIP + s] = offset
@@ -542,10 +551,13 @@
         return offset
 
     lax.fori_loop(0, sources // STRIP, put, jnp.int32(0))
-    leaf = got[pl.ds(me * n_top, n_top), 8:, 0:lanes].reshape(own // lanes, lanes)
-    leaf = leaf.astype(jnp.int32)
-    first = got[me * n_top, 8:9, 0:1].astype(jnp.int32) >> 3
-    offsets[sources] = jnp.sum(got[me * n_top, 8:9, 0:1]).astype(jnp.int32) >> 3
+    leaf = []
+    for t in range(n_top):
+        for r in range(points // lanes):
+            leaf.append(got[me * n_top + t, :, leaf_at + r * lanes : leaf_at + (r + 1) * lanes])
+    leaf = jnp.concatenate(leaf, axis=0).astype(jnp.int32)
+    first = leaf[0:1, 0:1] >> 3
+    offsets[sources] = jnp.sum(first.astype(f32)).astype(jnp.int32)
     io.wait(2)
     table = jnp.concatenate([(leaf >> 3) - first, leaf & 7], axis=1).astype(f32)
     table = jnp.transpose(table).astype(bf16)
@@ -819,7 +831,7 @@
     coef = uc2e.shape[0]
     sources = n_pts * n_top
     lanes = min(cap, LANE)
-    rows = 8 + points // lanes
+    width = (5 + dens) * cap + points
 
     def shape(*dims, dtype=bf16):
         return jax.ShapeDtypeStruct(dims, dtype)
@@ -833,12 +845,12 @@
             morton_slot.reshape(1, points),
             slot_leaf.reshape(points // lanes, lanes),
         ],
-        [shape(n_pts, n_top, rows, cap, dtype=f32), shape(1, points, dtype=jnp.int32)],
+        [shape(n_pts, n_top, 1, width, dtype=f32), shape(1, points, dtype=jnp.int32)],
         1 << 27,
         stays=(1,),
         grant=GRANT_FIRST,
     )
-    outgoing = outgoing.reshape(sources, rows, cap)
+    outgoing = outgoing.reshape(sources, 1, width)
     incoming = lax.all_to_all(outgoing, ("pts", "top"), split_axis=0, concat_axis=0, tiled=True)
 
     flat = (-1, LANE)

time: 78.8 us -> 78.3 us (level)
  blocking collectives: 12.4 us -> 13.2 us
  transfers between devices with their start and end apart: 15 -> 15, of which waited for: 7 -> 6; matrix products, arithmetic and copies ran while one was open for 0% -> 0% of each run, Pallas kernels for 29% -> 29%
where the time goes in v9:
time: 78.3 us; the launch traced here: 77.9 us
  Pallas kernels  44.3 us (57%)
  starting transfers between devices  16.6 us (21%)
  blocking collectives  13.2 us (17%)
  waiting for transfers between devices  1.82 us (2%)
  local copies, waits for them, and re-layouts  1.55 us (2%)
    pallas_call x7, Pallas kernels, run(): call(body, tuple(outs) + tuple(numbers), grant, flops, in_specs=[SMEM] *...  30.2 us
    pallas_call x2, Pallas kernels, relayout(): call(functools.partial(relayout_kernel, nrows, step0, steps), tuple((jax....  14.1 us
    all_to_all x1, blocking collectives, per_device(): lax.all_to_all(reply, ('pts', 'top'), split_axis=0, concat_axis=0, tiled=...  13.2 us
    ppermute x14, starting transfers between devices, shift_by(): return lax.ppermute(value, axis, [(i, i ^ distance) for i in range(size)])  9.27 us
    all_to_all x1, starting transfers between devices, per_device(): lax.all_to_all(outgoing, ('pts', 'top'), split_axis=0, concat_axis=0, til...  7.3 us
    ppermute x14, waiting for transfers between devices, shift_by(): return lax.ppermute(value, axis, [(i, i ^ distance) for i in range(size)])  1.81 us
  transfers between devices with their start and end apart: 15, of which 6 were waited for; matrix products, arithmetic and copies ran while one was open for 0% of the time, Pallas kernels for 29%

profile of v9, /device:TPU:0, one launch (start us, length us, event | category | flops | bytes accessed | tf_op | source)
XLA Modules:
  0.0 77.9 jit_solution(1565047161724814971)
XLA Ops:
  0.0 3.8 %shard_map.109 = (f32[8,4,1,2816]{3,2,1,0:T(1,128)}, s32[1,1024]{1,0:T(1,128)}) custom-call(f32[3,1024]{1,0:T(4,128)} %refs_0_.1, f32[8,1024]{1,0:T(8,128)} %refs_1_.1, s32[1,1024]{1,0:T(1,128)} %bitcast.16, s32[8,128]{1,0:T(8,128)} %bitcast.17), custom_call_target="tpu_custom_call" | custom-call | flops 134217728 | bytes 1048576 | tf_op jit(solution)/shard_map/pallas_call | solution.py:161
  3.8 7.3 %all-to-all-start = ((f32[32,1,2816]{2,1,0:T(1,128)}), f32[32,1,2816]{2,1,0:T(1,128)S(1)}, u32[]{:S(2)}, u32[]{:S(2)}) async-start(f32[32,1,2816]{2,1,0:T(1,128)} %bitcast.15), calls=%async_computation | async-start | bytes 720896 | tf_op jit(solution)/shard_map/all_to_all | solution.py:854
  11.1 0.1 pad_add_fusion.me_ref.refs_0_
  11.2 0.0 copy-start.6
  11.2 6.9 %shard_map.110 = (bf16[4,7,32,1152]{3,2,1,0:T(8,128)(2,1)}, bf16[3,4,32,1152]{3,2,1,0:T(8,128)(2,1)S(1)}, bf16[3,3,32,640]{3,2,1,0:T(8,128)(2,1)S(1)}) custom-call(s32[2]{0:T(128)S(1)} %pad_add_fusion.me_ref.refs_0_, bf16[57038,128]{1,0:T(8,128)(2,1)} %bitcast.11, bf16[57038,128]{1,0:T(8,128)(2,1)} %bitcast.12), custom_call_target="tpu_custom_call" | custom-call | flops 1048576 | bytes 4194304 | tf_op jit(solution)/shard_map/pallas_call | solution.py:298
  18.2 3.5 %shard_map.111 = (bf16[304,1280]{1,0:T(8,128)(2,1)S(1)}, bf16[34,152,152]{2,1,0:T(8,128)(2,1)S(1)}, bf16[2,152,80]{2,1,0:T(8,128)(2,1)S(1)}, bf16[2,152,80]{2,1,0:T(8,128)(2,1)S(1)}) custom-call(f32[1444,128]{1,0:T(8,128)S(1)} %bitcast.9, f32[1444,128]{1,0:T(8,128)S(1)} %bitcast.10, f32[152,152]{1,0:T(8,128)S(1)} %copy-done.3, f32[152,152]{1,0:T(8,128)S(1)} %copy-done.4, ...), custom_call_target="tpu_custom_call" | custom-call | flops 1073741824 | bytes 1048576 | tf_op jit(solution)/shard_map/pallas_call | solution.py:161
  21.7 1.5 %copy-done.7 = bf16[34,152,152]{2,1,0:T(8,128)(2,1)} copy-done((bf16[34,152,152]{2,1,0:T(8,128)(2,1)}, bf16[34,152,152]{2,1,0:T(8,128)(2,1)S(1)}, u32[]{:S(2)}) %copy-start.7) | copy-done | bytes 1571096
  23.3 9.2 %shard_map.112 = (bf16[160,256]{1,0:T(8,128)(2,1)S(1)}, f32[152,4096]{1,0:T(8,128)S(1)}, s32[1,4096]{1,0:T(1,128)S(1)}, s32[33]{0:T(128)S(1)}) custom-call(s32[2]{0:T(128)S(1)} %pad_add_fusion.me_ref.refs_0_, f32[32,1,2816]{2,1,0:T(1,128)S(1)} %all-to-all-done.refs_1_, f32[152,128]{1,0:T(8,128)S(1)} %copy-done.6, bf16[304,1280]{1,0:T(8,128)(2,1)S(1)} %get-tuple-element.46.refs_3_), custom_call_target="tpu_custom_call" | custom-call | flops 8589934592 | bytes 1048576 | tf_op jit(solution)/shard_map/pallas_call | solution.py:161
  32.4 2.7 %collective-permute-start.3 = (bf16[160,256]{1,0:T(8,128)(2,1)S(1)}, bf16[160,256]{1,0:T(8,128)(2,1)S(1)}, u32[]{:S(2)}, u32[]{:S(2)}) collective-permute-start(bf16[160,256]{1,0:T(8,128)(2,1)S(1)} %get-tuple-element.54.refs_1_.refs_0_), channel_id=1, source_target_pairs={{0,24},{4,28},{8,16},{12,20},{16,8},{20,12},{24,0},{28,4},{1,25},{... | collective-permute-start | bytes 245768 | tf_op jit(solution)/shard_map/ppermute | solution.py:809
  35.1 0.6 collective-permute-start.2
  35.7 0.3 collective-permute-start.1
  36.0 7.2 %shard_map.113 = (bf16[4,7,48,1152]{3,2,1,0:T(8,128)(2,1)S(1)}, bf16[3,4,48,1152]{3,2,1,0:T(8,128)(2,1)S(1)}, bf16[3,3,48,640]{3,2,1,0:T(8,128)(2,1)S(1)}) custom-call(s32[2]{0:T(128)S(1)} %pad_add_fusion.me_ref.refs_0_, bf16[57038,128]{1,0:T(8,128)(2,1)} %bitcast.13, bf16[57038,128]{1,0:T(8,128)(2,1)} %bitcast.14), custom_call_target="tpu_custom_call" | custom-call | flops 1048576 | bytes 6291456 | tf_op jit(solution)/shard_map/pallas_call | solution.py:298
  43.3 0.6 collective-permute-start.4
  43.8 0.1 collective-permute-start.5
  43.9 0.4 collective-permute-start.6
  44.4 0.4 collective-permute-done.4.refs_4_.refs_3_
  44.8 0.4 collective-permute-done.5.refs_6_.refs_5_
  45.1 0.2 collective-permute-done.6.refs_8_.refs_7_
  45.3 4.5 %shard_map.114.refs_2_ = bf16[80,256]{1,0:T(8,128)(2,1)S(1)} custom-call(s32[2]{0:T(128)S(1)} %pad_add_fusion.me_ref.refs_0_, bf16[160,256]{1,0:T(8,128)(2,1)S(1)} %get-tuple-element.54.refs_1_.refs_0_, bf16[160,256]{1,0:T(8,128)(2,1)S(1)} %collective-permute-done.refs_2_.refs_1_, bf16[160,256]{1,0:T(8,128)(2,1)S(1)} %collective-permute-done.1.refs_3_.refs_2_, ...), custom_call_target="tpu_custom_call" | custom-call | flops 8589934592 | bytes 1048576 | tf_op jit(solution)/shard_map/pallas_call | solution.py:161
  49.7 2.7 %collective-permute-start.10 = (bf16[80,256]{1,0:T(8,128)(2,1)S(1)}, bf16[80,256]{1,0:T(8,128)(2,1)S(1)}, u32[]{:S(2)}, u32[]{:S(2)}) collective-permute-start(bf16[80,256]{1,0:T(8,128)(2,1)S(1)} %shard_map.114.refs_2_), channel_id=1, source_target_pairs={{0,24},{4,28},{8,16},{12,20},{16,8},{20,12},{24,0},{28,4},{1,25},{... | collective-permute-start | bytes 122888 | tf_op jit(solution)/shard_map/ppermute | solution.py:809
  52.5 0.6 collective-permute-start.9
  53.0 0.3 collective-permute-start.8
  53.3 4.8 %shard_map.115.refs_12_ = f32[2,152,512]{2,1,0:T(8,128)S(1)} custom-call(bf16[160,256]{1,0:T(8,128)(2,1)S(1)} %get-tuple-element.54.refs_1_.refs_0_, bf16[160,256]{1,0:T(8,128)(2,1)S(1)} %collective-permute-done.refs_2_.refs_1_, bf16[160,256]{1,0:T(8,128)(2,1)S(1)} %collective-permute-done.1.refs_3_.refs_2_, ...), custom_call_target="tpu_custom_call" | custom-call | flops 4294967296 | bytes 1048576 | tf_op jit(solution)/shard_map/pallas_call | solution.py:161
  58.2 0.6 collective-permute-start.11
  58.8 0.1 collective-permute-start.12
  58.9 0.4 collective-permute-start.13
  59.3 0.4 collective-permute-done.11.refs_5_
  59.6 0.3 collective-permute-done.12.refs_7_
  60.0 0.2 collective-permute-done.13.refs_9_
  60.2 3.1 %shard_map.116 = f32[32,1,512]{2,1,0:T(1,128)S(1)} custom-call(s32[2]{0:T(128)S(1)} %pad_add_fusion.me_ref.refs_0_, s32[33]{0:T(128)S(1)} %get-tuple-element.47.refs_1_, bf16[80,256]{1,0:T(8,128)(2,1)S(1)} %shard_map.114.refs_2_, bf16[80,256]{1,0:T(8,128)(2,1)S(1)} %collective-permute-done.7.refs_3_, bf16[80,256]{1,0:T(8,128)(2,1)S(1)} %collective-permute-done.8.refs_4_, ...), custom_call_target="tpu_custom_call" | custom-call | flops 4294967296 | bytes 1048576 | tf_op jit(solution)/shard_map/pallas_call | solution.py:161
  63.2 13.2 %all_to_all.10.refs_0_ = f32[32,1,512]{2,1,0:T(1,128)S(1)} all-to-all(f32[32,1,512]{2,1,0:T(1,128)S(1)} %shard_map.116), channel_id=1, replica_groups=mesh['pts'=8,'top'=4] {'pts','top'}, dimensions={0} | all-to-all | bytes 131072 | tf_op jit(solution)/shard_map/all_to_all | solution.py:936
  76.4 1.3 %shard_map.117 = f32[8,1024]{1,0:T(8,128)} custom-call(f32[32,1,512]{2,1,0:T(1,128)S(1)} %all_to_all.10.refs_0_, s32[1,1024]{1,0:T(1,128)S(1)} %copy-done.9), custom_call_target="tpu_custom_call" | custom-call | flops 268435456 | bytes 1048576 | tf_op jit(solution)/shard_map/pallas_call | solution.py:161
  (29 shorter events, 0.1 us)
Async XLA Ops:
  3.8 19.4 %all-to-all-start = ((f32[32,1,2816]{2,1,0:T(1,128)}), f32[32,1,2816]{2,1,0:T(1,128)S(1)}, u32[]{:S(2)}, u32[]{:S(2)}) async-start(f32[32,1,2816]{2,1,0:T(1,128)} %bitcast.15), calls=%async_computation | async-start | bytes 720896 | tf_op jit(solution)/shard_map/all_to_all | solution.py:854
  11.2 6.9 %copy-start.1 = (f32[184832]{0:T(1024)S(1)}, f32[184832]{0:T(1024)}, u32[]{:S(2)}) copy-start(f32[184832]{0:T(1024)} %param.16) | copy-start | bytes 2217988
  11.2 7.0 %copy-start.2 = (f32[184832]{0:T(1024)S(1)}, f32[184832]{0:T(1024)}, u32[]{:S(2)}) copy-start(f32[184832]{0:T(1024)} %param.20) | copy-start | bytes 2217988
  11.2 7.0 %copy-start.3 = (f32[152,152]{1,0:T(8,128)S(1)}, f32[152,152]{1,0:T(8,128)}, u32[]{:S(2)}) copy-start(f32[152,152]{1,0:T(8,128)} %refs_2_.2) | copy-start | bytes 277252
  11.2 7.0 %copy-start.4 = (f32[152,152]{1,0:T(8,128)S(1)}, f32[152,152]{1,0:T(8,128)}, u32[]{:S(2)}) copy-start(f32[152,152]{1,0:T(8,128)} %refs_3_.1) | copy-start | bytes 277252
  11.2 7.0 %copy-start.5 = (f32[152,152]{1,0:T(8,128)S(1)}, f32[152,152]{1,0:T(8,128)}, u32[]{:S(2)}) copy-start(f32[152,152]{1,0:T(8,128)} %refs_4_.1) | copy-start | bytes 277252
  11.2 7.0 %copy-start.6 = (f32[152,128]{1,0:T(8,128)S(1)}, f32[152,128]{1,0:T(8,128)}, u32[]{:S(2)}) copy-start(f32[152,128]{1,0:T(8,128)} %constant.11.clone.refs_5_.refs_2_) | copy-start | bytes 233476
  21.7 1.5 %copy-start.7 = (bf16[34,152,152]{2,1,0:T(8,128)(2,1)}, bf16[34,152,152]{2,1,0:T(8,128)(2,1)S(1)}, u32[]{:S(2)}) copy-start(bf16[34,152,152]{2,1,0:T(8,128)(2,1)S(1)} %get-tuple-element.65.refs_8_) | copy-start | bytes 4713220
  32.4 10.8 %collective-permute-start.3 = (bf16[160,256]{1,0:T(8,128)(2,1)S(1)}, bf16[160,256]{1,0:T(8,128)(2,1)S(1)}, u32[]{:S(2)}, u32[]{:S(2)}) collective-permute-start(bf16[160,256]{1,0:T(8,128)(2,1)S(1)} %get-tuple-element.54.refs_1_.refs_0_), channel_id=1, source_target_pairs={{0,24},{4,28},{8,16},{12,20},{16,8},{20,12},{24,0},{28,4},{1,25},{... | collective-permute-start | bytes 245768 | tf_op jit(solution)/shard_map/ppermute | solution.py:809
  35.1 8.1 %collective-permute-start.2 = (bf16[160,256]{1,0:T(8,128)(2,1)S(1)}, bf16[160,256]{1,0:T(8,128)(2,1)S(1)}, u32[]{:S(2)}, u32[]{:S(2)}) collective-permute-start(bf16[160,256]{1,0:T(8,128)(2,1)S(1)} %get-tuple-element.54.refs_1_.refs_0_), channel_id=1, source_target_pairs={{0,16},{4,20},{8,24},{12,28},{16,0},{20,4},{24,8},{28,12},{1,17},{... | collective-permute-start | bytes 245768 | tf_op jit(solution)/shard_map/ppermute | solution.py:809
  35.7 7.6 %collective-permute-start.1 = (bf16[160,256]{1,0:T(8,128)(2,1)S(1)}, bf16[160,256]{1,0:T(8,128)(2,1)S(1)}, u32[]{:S(2)}, u32[]{:S(2)}) collective-permute-start(bf16[160,256]{1,0:T(8,128)(2,1)S(1)} %get-tuple-element.54.refs_1_.refs_0_), channel_id=1, source_target_pairs={{0,8},{4,12},{8,0},{12,4},{16,24},{20,28},{24,16},{28,20},{1,9},{5... | collective-permute-start | bytes 245768 | tf_op jit(solution)/shard_map/ppermute | solution.py:809
  36.0 7.3 %collective-permute-start = (bf16[160,256]{1,0:T(8,128)(2,1)S(1)}, bf16[160,256]{1,0:T(8,128)(2,1)S(1)}, u32[]{:S(2)}, u32[]{:S(2)}) collective-permute-start(bf16[160,256]{1,0:T(8,128)(2,1)S(1)} %get-tuple-element.54.refs_1_.refs_0_), channel_id=1, source_target_pairs={{0,4},{4,0},{8,12},{12,8},{16,20},{20,16},{24,28},{28,24},{1,5},{5... | collective-permute-start | bytes 245768 | tf_op jit(solution)/shard_map/ppermute | solution.py:809
  36.0 9.3 %copy-start = (bf16[4,7,32,1152]{3,2,1,0:T(8,128)(2,1)S(1)}, bf16[4,7,32,1152]{3,2,1,0:T(8,128)(2,1)}, u32[]{:S(2)}) copy-start(bf16[4,7,32,1152]{3,2,1,0:T(8,128)(2,1)} %get-tuple-element.59.refs_9_) | copy-start | bytes 6193156
  43.3 10.0 %copy-start.8 = (bf16[34,152,152]{2,1,0:T(8,128)(2,1)S(1)}, bf16[34,152,152]{2,1,0:T(8,128)(2,1)}, u32[]{:S(2)}) copy-start(bf16[34,152,152]{2,1,0:T(8,128)(2,1)} %copy-done.7) | copy-start | bytes 4713220
  43.3 1.5 %collective-permute-start.4 = (bf16[160,256]{1,0:T(8,128)(2,1)S(1)}, bf16[160,256]{1,0:T(8,128)(2,1)S(1)}, u32[]{:S(2)}, u32[]{:S(2)}) collective-permute-start(bf16[160,256]{1,0:T(8,128)(2,1)S(1)} %collective-permute-done.1.refs_3_.refs_2_), channel_id=1, source_target_pairs={{0,4},{4,0},{8,12},{12,8},{16,20},{20,16},{24,28},{28,24},{1,5},{5... | collective-permute-start | bytes 245768 | tf_op jit(solution)/shard_map/ppermute | solution.py:809
  43.8 1.3 %collective-permute-start.5 = (bf16[160,256]{1,0:T(8,128)(2,1)S(1)}, bf16[160,256]{1,0:T(8,128)(2,1)S(1)}, u32[]{:S(2)}, u32[]{:S(2)}) collective-permute-start(bf16[160,256]{1,0:T(8,128)(2,1)S(1)} %collective-permute-done.2.refs_5_.refs_4_), channel_id=1, source_target_pairs={{0,4},{4,0},{8,12},{12,8},{16,20},{20,16},{24,28},{28,24},{1,5},{5... | collective-permute-start | bytes 245768 | tf_op jit(solution)/shard_map/ppermute | solution.py:809
  43.9 1.4 %collective-permute-start.6 = (bf16[160,256]{1,0:T(8,128)(2,1)S(1)}, bf16[160,256]{1,0:T(8,128)(2,1)S(1)}, u32[]{:S(2)}, u32[]{:S(2)}) collective-permute-start(bf16[160,256]{1,0:T(8,128)(2,1)S(1)} %collective-permute-done.3.refs_7_.refs_6_), channel_id=1, source_target_pairs={{0,4},{4,0},{8,12},{12,8},{16,20},{20,16},{24,28},{28,24},{1,5},{5... | collective-permute-start | bytes 245768 | tf_op jit(solution)/shard_map/ppermute | solution.py:809
  49.7 8.4 %collective-permute-start.10 = (bf16[80,256]{1,0:T(8,128)(2,1)S(1)}, bf16[80,256]{1,0:T(8,128)(2,1)S(1)}, u32[]{:S(2)}, u32[]{:S(2)}) collective-permute-start(bf16[80,256]{1,0:T(8,128)(2,1)S(1)} %shard_map.114.refs_2_), channel_id=1, source_target_pairs={{0,24},{4,28},{8,16},{12,20},{16,8},{20,12},{24,0},{28,4},{1,25},{... | collective-permute-start | bytes 122888 | tf_op jit(solution)/shard_map/ppermute | solution.py:809
  52.5 5.7 %collective-permute-start.9 = (bf16[80,256]{1,0:T(8,128)(2,1)S(1)}, bf16[80,256]{1,0:T(8,128)(2,1)S(1)}, u32[]{:S(2)}, u32[]{:S(2)}) collective-permute-start(bf16[80,256]{1,0:T(8,128)(2,1)S(1)} %shard_map.114.refs_2_), channel_id=1, source_target_pairs={{0,16},{4,20},{8,24},{12,28},{16,0},{20,4},{24,8},{28,12},{1,17},{... | collective-permute-start | bytes 122888 | tf_op jit(solution)/shard_map/ppermute | solution.py:809
  53.0 5.2 %collective-permute-start.8 = (bf16[80,256]{1,0:T(8,128)(2,1)S(1)}, bf16[80,256]{1,0:T(8,128)(2,1)S(1)}, u32[]{:S(2)}, u32[]{:S(2)}) collective-permute-start(bf16[80,256]{1,0:T(8,128)(2,1)S(1)} %shard_map.114.refs_2_), channel_id=1, source_target_pairs={{0,8},{4,12},{8,0},{12,4},{16,24},{20,28},{24,16},{28,20},{1,9},{5... | collective-permute-start | bytes 122888 | tf_op jit(solution)/shard_map/ppermute | solution.py:809
  53.3 4.9 %collective-permute-start.7 = (bf16[80,256]{1,0:T(8,128)(2,1)S(1)}, bf16[80,256]{1,0:T(8,128)(2,1)S(1)}, u32[]{:S(2)}, u32[]{:S(2)}) collective-permute-start(bf16[80,256]{1,0:T(8,128)(2,1)S(1)} %shard_map.114.refs_2_), channel_id=1, source_target_pairs={{0,4},{4,0},{8,12},{12,8},{16,20},{20,16},{24,28},{28,24},{1,5},{5... | collective-permute-start | bytes 122888 | tf_op jit(solution)/shard_map/ppermute | solution.py:809
  58.2 1.4 %collective-permute-start.11 = (bf16[80,256]{1,0:T(8,128)(2,1)S(1)}, bf16[80,256]{1,0:T(8,128)(2,1)S(1)}, u32[]{:S(2)}, u32[]{:S(2)}) collective-permute-start(bf16[80,256]{1,0:T(8,128)(2,1)S(1)} %collective-permute-done.8.refs_4_), channel_id=1, source_target_pairs={{0,4},{4,0},{8,12},{12,8},{16,20},{20,16},{24,28},{28,24},{1,5},{5... | collective-permute-start | bytes 122888 | tf_op jit(solution)/shard_map/ppermute | solution.py:809
  58.8 1.2 %collective-permute-start.12 = (bf16[80,256]{1,0:T(8,128)(2,1)S(1)}, bf16[80,256]{1,0:T(8,128)(2,1)S(1)}, u32[]{:S(2)}, u32[]{:S(2)}) collective-permute-start(bf16[80,256]{1,0:T(8,128)(2,1)S(1)} %collective-permute-done.9.refs_6_), channel_id=1, source_target_pairs={{0,4},{4,0},{8,12},{12,8},{16,20},{20,16},{24,28},{28,24},{1,5},{5... | collective-permute-start | bytes 122888 | tf_op jit(solution)/shard_map/ppermute | solution.py:809
  58.9 1.3 %collective-permute-start.13 = (bf16[80,256]{1,0:T(8,128)(2,1)S(1)}, bf16[80,256]{1,0:T(8,128)(2,1)S(1)}, u32[]{:S(2)}, u32[]{:S(2)}) collective-permute-start(bf16[80,256]{1,0:T(8,128)(2,1)S(1)} %collective-permute-done.10.refs_8_), channel_id=1, source_target_pairs={{0,4},{4,0},{8,12},{12,8},{16,20},{20,16},{24,28},{28,24},{1,5},{5... | collective-permute-start | bytes 122888 | tf_op jit(solution)/shard_map/ppermute | solution.py:809
  60.2 16.2 %copy-start.9 = (s32[1,1024]{1,0:T(1,128)S(1)}, s32[1,1024]{1,0:T(1,128)}, u32[]{:S(2)}) copy-start(s32[1,1024]{1,0:T(1,128)} %get-tuple-element.76.refs_1_) | copy-start | bytes 12292

commit v10 on v9

--- a/solution.py
+++ b/solution.py
@@ -46,7 +46,7 @@
 FEATURES = 4
 PB = 256
 STRIP = 16
-UNROLL_FIND, UNROLL_APPLY, UNROLL_GATHER = 16, 8, 8
+UNROLL_FIND, UNROLL_APPLY, UNROLL_GATHER = 16, 16, 16
 GRANT = 28
 GRANT_FIRST = 60
 GRANT_EARLY = 52

time: 78.3 us -> 76.9 us (0.982)
  Pallas kernels: 44.3 us -> 42.9 us
    pallas_call x7, Pallas kernels: 30.2 us -> 28.9 us  [run(): call(body, tuple(outs) + tuple(numbers), grant, flops, in_specs=[SMEM] *...]
where the time goes in v10:
time: 76.9 us; the launch traced here: 76.5 us
  Pallas kernels  42.9 us (56%)
  starting transfers between devices  16.6 us (22%)
  blocking collectives  13.2 us (17%)
  waiting for transfers between devices  1.82 us (2%)
  local copies, waits for them, and re-layouts  1.55 us (2%)
    pallas_call x7, Pallas kernels, run(): call(body, tuple(outs) + tuple(numbers), grant, flops, in_specs=[SMEM] *...  28.9 us
    pallas_call x2, Pallas kernels, relayout(): call(functools.partial(relayout_kernel, nrows, step0, steps), tuple((jax....  14.1 us
    all_to_all x1, blocking collectives, per_device(): lax.all_to_all(reply, ('pts', 'top'), split_axis=0, concat_axis=0, tiled=...  13.2 us
    ppermute x14, starting transfers between devices, shift_by(): return lax.ppermute(value, axis, [(i, i ^ distance) for i in range(size)])  9.27 us
    all_to_all x1, starting transfers between devices, per_device(): lax.all_to_all(outgoing, ('pts', 'top'), split_axis=0, concat_axis=0, til...  7.3 us
    ppermute x14, waiting for transfers between devices, shift_by(): return lax.ppermute(value, axis, [(i, i ^ distance) for i in range(size)])  1.81 us
    unnamed x20, local copies, waits for them, and re-layouts  1.55 us
  transfers between devices with their start and end apart: 15, of which 6 were waited for; matrix products, arithmetic and copies ran while one was open for 0% of the time, Pallas kernels for 29%

profile of v10, /device:TPU:0, one launch (start us, length us, event | category | flops | bytes accessed | tf_op | source)
XLA Modules:
  0.0 76.5 jit_solution(4876071677180435989)
XLA Ops:
  0.0 3.8 %shard_map.109 = (f32[8,4,1,2816]{3,2,1,0:T(1,128)}, s32[1,1024]{1,0:T(1,128)}) custom-call(f32[3,1024]{1,0:T(4,128)} %refs_0_.1, f32[8,1024]{1,0:T(8,128)} %refs_1_.1, s32[1,1024]{1,0:T(1,128)} %bitcast.16, s32[8,128]{1,0:T(8,128)} %bitcast.17), custom_call_target="tpu_custom_call" | custom-call | flops 134217728 | bytes 1048576 | tf_op jit(solution)/shard_map/pallas_call | solution.py:161
  3.8 7.3 %all-to-all-start = ((f32[32,1,2816]{2,1,0:T(1,128)}), f32[32,1,2816]{2,1,0:T(1,128)S(1)}, u32[]{:S(2)}, u32[]{:S(2)}) async-start(f32[32,1,2816]{2,1,0:T(1,128)} %bitcast.15), calls=%async_computation | async-start | bytes 720896 | tf_op jit(solution)/shard_map/all_to_all | solution.py:854
  11.1 0.1 pad_add_fusion.me_ref.refs_0_
  11.2 0.0 copy-start.6
  11.2 6.9 %shard_map.110 = (bf16[4,7,32,1152]{3,2,1,0:T(8,128)(2,1)}, bf16[3,4,32,1152]{3,2,1,0:T(8,128)(2,1)S(1)}, bf16[3,3,32,640]{3,2,1,0:T(8,128)(2,1)S(1)}) custom-call(s32[2]{0:T(128)S(1)} %pad_add_fusion.me_ref.refs_0_, bf16[57038,128]{1,0:T(8,128)(2,1)} %bitcast.11, bf16[57038,128]{1,0:T(8,128)(2,1)} %bitcast.12), custom_call_target="tpu_custom_call" | custom-call | flops 1048576 | bytes 4194304 | tf_op jit(solution)/shard_map/pallas_call | solution.py:298
  18.2 3.5 %shard_map.111 = (bf16[304,1280]{1,0:T(8,128)(2,1)S(1)}, bf16[34,152,152]{2,1,0:T(8,128)(2,1)S(1)}, bf16[2,152,80]{2,1,0:T(8,128)(2,1)S(1)}, bf16[2,152,80]{2,1,0:T(8,128)(2,1)S(1)}) custom-call(f32[1444,128]{1,0:T(8,128)S(1)} %bitcast.9, f32[1444,128]{1,0:T(8,128)S(1)} %bitcast.10, f32[152,152]{1,0:T(8,128)S(1)} %copy-done.3, f32[152,152]{1,0:T(8,128)S(1)} %copy-done.4, ...), custom_call_target="tpu_custom_call" | custom-call | flops 1073741824 | bytes 1048576 | tf_op jit(solution)/shard_map/pallas_call | solution.py:161
  21.7 1.5 %copy-done.7 = bf16[34,152,152]{2,1,0:T(8,128)(2,1)} copy-done((bf16[34,152,152]{2,1,0:T(8,128)(2,1)}, bf16[34,152,152]{2,1,0:T(8,128)(2,1)S(1)}, u32[]{:S(2)}) %copy-start.7) | copy-done | bytes 1571096
  23.3 7.9 %shard_map.112 = (bf16[160,256]{1,0:T(8,128)(2,1)S(1)}, f32[152,4096]{1,0:T(8,128)S(1)}, s32[1,4096]{1,0:T(1,128)S(1)}, s32[33]{0:T(128)S(1)}) custom-call(s32[2]{0:T(128)S(1)} %pad_add_fusion.me_ref.refs_0_, f32[32,1,2816]{2,1,0:T(1,128)S(1)} %all-to-all-done.refs_1_, f32[152,128]{1,0:T(8,128)S(1)} %copy-done.6, bf16[304,1280]{1,0:T(8,128)(2,1)S(1)} %get-tuple-element.46.refs_3_), custom_call_target="tpu_custom_call" | custom-call | flops 8589934592 | bytes 1048576 | tf_op jit(solution)/shard_map/pallas_call | solution.py:161
  31.1 2.7 %collective-permute-start.3 = (bf16[160,256]{1,0:T(8,128)(2,1)S(1)}, bf16[160,256]{1,0:T(8,128)(2,1)S(1)}, u32[]{:S(2)}, u32[]{:S(2)}) collective-permute-start(bf16[160,256]{1,0:T(8,128)(2,1)S(1)} %get-tuple-element.54.refs_1_.refs_0_), channel_id=1, source_target_pairs={{0,24},{4,28},{8,16},{12,20},{16,8},{20,12},{24,0},{28,4},{1,25},{... | collective-permute-start | bytes 245768 | tf_op jit(solution)/shard_map/ppermute | solution.py:809
  33.9 0.6 collective-permute-start.2
  34.4 0.3 collective-permute-start.1
  34.7 7.2 %shard_map.113 = (bf16[4,7,48,1152]{3,2,1,0:T(8,128)(2,1)S(1)}, bf16[3,4,48,1152]{3,2,1,0:T(8,128)(2,1)S(1)}, bf16[3,3,48,640]{3,2,1,0:T(8,128)(2,1)S(1)}) custom-call(s32[2]{0:T(128)S(1)} %pad_add_fusion.me_ref.refs_0_, bf16[57038,128]{1,0:T(8,128)(2,1)} %bitcast.13, bf16[57038,128]{1,0:T(8,128)(2,1)} %bitcast.14), custom_call_target="tpu_custom_call" | custom-call | flops 1048576 | bytes 6291456 | tf_op jit(solution)/shard_map/pallas_call | solution.py:298
  41.9 0.6 collective-permute-start.4
  42.5 0.1 collective-permute-start.5
  42.6 0.4 collective-permute-start.6
  43.0 0.4 collective-permute-done.4.refs_4_.refs_3_
  43.4 0.4 collective-permute-done.5.refs_6_.refs_5_
  43.8 0.2 collective-permute-done.6.refs_8_.refs_7_
  43.9 4.5 %shard_map.114.refs_2_ = bf16[80,256]{1,0:T(8,128)(2,1)S(1)} custom-call(s32[2]{0:T(128)S(1)} %pad_add_fusion.me_ref.refs_0_, bf16[160,256]{1,0:T(8,128)(2,1)S(1)} %get-tuple-element.54.refs_1_.refs_0_, bf16[160,256]{1,0:T(8,128)(2,1)S(1)} %collective-permute-done.refs_2_.refs_1_, bf16[160,256]{1,0:T(8,128)(2,1)S(1)} %collective-permute-done.1.refs_3_.refs_2_, ...), custom_call_target="tpu_custom_call" | custom-call | flops 8589934592 | bytes 1048576 | tf_op jit(solution)/shard_map/pallas_call | solution.py:161
  48.4 2.7 %collective-permute-start.10 = (bf16[80,256]{1,0:T(8,128)(2,1)S(1)}, bf16[80,256]{1,0:T(8,128)(2,1)S(1)}, u32[]{:S(2)}, u32[]{:S(2)}) collective-permute-start(bf16[80,256]{1,0:T(8,128)(2,1)S(1)} %shard_map.114.refs_2_), channel_id=1, source_target_pairs={{0,24},{4,28},{8,16},{12,20},{16,8},{20,12},{24,0},{28,4},{1,25},{... | collective-permute-start | bytes 122888 | tf_op jit(solution)/shard_map/ppermute | solution.py:809
  51.1 0.6 collective-permute-start.9
  51.7 0.3 collective-permute-start.8
  52.0 4.8 %shard_map.115.refs_12_ = f32[2,152,512]{2,1,0:T(8,128)S(1)} custom-call(bf16[160,256]{1,0:T(8,128)(2,1)S(1)} %get-tuple-element.54.refs_1_.refs_0_, bf16[160,256]{1,0:T(8,128)(2,1)S(1)} %collective-permute-done.refs_2_.refs_1_, bf16[160,256]{1,0:T(8,128)(2,1)S(1)} %collective-permute-done.1.refs_3_.refs_2_, ...), custom_call_target="tpu_custom_call" | custom-call | flops 4294967296 | bytes 1048576 | tf_op jit(solution)/shard_map/pallas_call | solution.py:161
  56.8 0.6 collective-permute-start.11
  57.4 0.1 collective-permute-start.12
  57.5 0.4 collective-permute-start.13
  57.9 0.4 collective-permute-done.11.refs_5_
  58.3 0.3 collective-permute-done.12.refs_7_
  58.6 0.2 collective-permute-done.13.refs_9_
  58.8 3.1 %shard_map.116 = f32[32,1,512]{2,1,0:T(1,128)S(1)} custom-call(s32[2]{0:T(128)S(1)} %pad_add_fusion.me_ref.refs_0_, s32[33]{0:T(128)S(1)} %get-tuple-element.47.refs_1_, bf16[80,256]{1,0:T(8,128)(2,1)S(1)} %shard_map.114.refs_2_, bf16[80,256]{1,0:T(8,128)(2,1)S(1)} %collective-permute-done.7.refs_3_, bf16[80,256]{1,0:T(8,128)(2,1)S(1)} %collective-permute-done.8.refs_4_, ...), custom_call_target="tpu_custom_call" | custom-call | flops 4294967296 | bytes 1048576 | tf_op jit(solution)/shard_map/pallas_call | solution.py:161
  61.9 13.2 %all_to_all.10.refs_0_ = f32[32,1,512]{2,1,0:T(1,128)S(1)} all-to-all(f32[32,1,512]{2,1,0:T(1,128)S(1)} %shard_map.116), channel_id=1, replica_groups=mesh['pts'=8,'top'=4] {'pts','top'}, dimensions={0} | all-to-all | bytes 131072 | tf_op jit(solution)/shard_map/all_to_all | solution.py:936
  75.0 1.3 %shard_map.117 = f32[8,1024]{1,0:T(8,128)} custom-call(f32[32,1,512]{2,1,0:T(1,128)S(1)} %all_to_all.10.refs_0_, s32[1,1024]{1,0:T(1,128)S(1)} %copy-done.9), custom_call_target="tpu_custom_call" | custom-call | flops 268435456 | bytes 1048576 | tf_op jit(solution)/shard_map/pallas_call | solution.py:161
  (29 shorter events, 0.1 us)
Async XLA Ops:
  3.8 19.4 %all-to-all-start = ((f32[32,1,2816]{2,1,0:T(1,128)}), f32[32,1,2816]{2,1,0:T(1,128)S(1)}, u32[]{:S(2)}, u32[]{:S(2)}) async-start(f32[32,1,2816]{2,1,0:T(1,128)} %bitcast.15), calls=%async_computation | async-start | bytes 720896 | tf_op jit(solution)/shard_map/all_to_all | solution.py:854
  11.2 6.9 %copy-start.1 = (f32[184832]{0:T(1024)S(1)}, f32[184832]{0:T(1024)}, u32[]{:S(2)}) copy-start(f32[184832]{0:T(1024)} %param.16) | copy-start | bytes 2217988
  11.2 7.0 %copy-start.2 = (f32[184832]{0:T(1024)S(1)}, f32[184832]{0:T(1024)}, u32[]{:S(2)}) copy-start(f32[184832]{0:T(1024)} %param.20) | copy-start | bytes 2217988
  11.2 7.0 %copy-start.3 = (f32[152,152]{1,0:T(8,128)S(1)}, f32[152,152]{1,0:T(8,128)}, u32[]{:S(2)}) copy-start(f32[152,152]{1,0:T(8,128)} %refs_2_.2) | copy-start | bytes 277252
  11.2 7.0 %copy-start.4 = (f32[152,152]{1,0:T(8,128)S(1)}, f32[152,152]{1,0:T(8,128)}, u32[]{:S(2)}) copy-start(f32[152,152]{1,0:T(8,128)} %refs_3_.1) | copy-start | bytes 277252
  11.2 7.0 %copy-start.5 = (f32[152,152]{1,0:T(8,128)S(1)}, f32[152,152]{1,0:T(8,128)}, u32[]{:S(2)}) copy-start(f32[152,152]{1,0:T(8,128)} %refs_4_.1) | copy-start | bytes 277252
  11.2 7.0 %copy-start.6 = (f32[152,128]{1,0:T(8,128)S(1)}, f32[152,128]{1,0:T(8,128)}, u32[]{:S(2)}) copy-start(f32[152,128]{1,0:T(8,128)} %constant.11.clone.refs_5_.refs_2_) | copy-start | bytes 233476
  21.7 1.5 %copy-start.7 = (bf16[34,152,152]{2,1,0:T(8,128)(2,1)}, bf16[34,152,152]{2,1,0:T(8,128)(2,1)S(1)}, u32[]{:S(2)}) copy-start(bf16[34,152,152]{2,1,0:T(8,128)(2,1)S(1)} %get-tuple-element.65.refs_8_) | copy-start | bytes 4713220
  31.1 10.7 %collective-permute-start.3 = (bf16[160,256]{1,0:T(8,128)(2,1)S(1)}, bf16[160,256]{1,0:T(8,128)(2,1)S(1)}, u32[]{:S(2)}, u32[]{:S(2)}) collective-permute-start(bf16[160,256]{1,0:T(8,128)(2,1)S(1)} %get-tuple-element.54.refs_1_.refs_0_), channel_id=1, source_target_pairs={{0,24},{4,28},{8,16},{12,20},{16,8},{20,12},{24,0},{28,4},{1,25},{... | collective-permute-start | bytes 245768 | tf_op jit(solution)/shard_map/ppermute | solution.py:809
  33.9 8.0 %collective-permute-start.2 = (bf16[160,256]{1,0:T(8,128)(2,1)S(1)}, bf16[160,256]{1,0:T(8,128)(2,1)S(1)}, u32[]{:S(2)}, u32[]{:S(2)}) collective-permute-start(bf16[160,256]{1,0:T(8,128)(2,1)S(1)} %get-tuple-element.54.refs_1_.refs_0_), channel_id=1, source_target_pairs={{0,16},{4,20},{8,24},{12,28},{16,0},{20,4},{24,8},{28,12},{1,17},{... | collective-permute-start | bytes 245768 | tf_op jit(solution)/shard_map/ppermute | solution.py:809
  34.4 7.5 %collective-permute-start.1 = (bf16[160,256]{1,0:T(8,128)(2,1)S(1)}, bf16[160,256]{1,0:T(8,128)(2,1)S(1)}, u32[]{:S(2)}, u32[]{:S(2)}) collective-permute-start(bf16[160,256]{1,0:T(8,128)(2,1)S(1)} %get-tuple-element.54.refs_1_.refs_0_), channel_id=1, source_target_pairs={{0,8},{4,12},{8,0},{12,4},{16,24},{20,28},{24,16},{28,20},{1,9},{5... | collective-permute-start | bytes 245768 | tf_op jit(solution)/shard_map/ppermute | solution.py:809
  34.7 7.2 %collective-permute-start = (bf16[160,256]{1,0:T(8,128)(2,1)S(1)}, bf16[160,256]{1,0:T(8,128)(2,1)S(1)}, u32[]{:S(2)}, u32[]{:S(2)}) collective-permute-start(bf16[160,256]{1,0:T(8,128)(2,1)S(1)} %get-tuple-element.54.refs_1_.refs_0_), channel_id=1, source_target_pairs={{0,4},{4,0},{8,12},{12,8},{16,20},{20,16},{24,28},{28,24},{1,5},{5... | collective-permute-start | bytes 245768 | tf_op jit(solution)/shard_map/ppermute | solution.py:809
  34.7 9.2 %copy-start = (bf16[4,7,32,1152]{3,2,1,0:T(8,128)(2,1)S(1)}, bf16[4,7,32,1152]{3,2,1,0:T(8,128)(2,1)}, u32[]{:S(2)}) copy-start(bf16[4,7,32,1152]{3,2,1,0:T(8,128)(2,1)} %get-tuple-element.59.refs_9_) | copy-start | bytes 6193156
  41.9 10.0 %copy-start.8 = (bf16[34,152,152]{2,1,0:T(8,128)(2,1)S(1)}, bf16[34,152,152]{2,1,0:T(8,128)(2,1)}, u32[]{:S(2)}) copy-start(bf16[34,152,152]{2,1,0:T(8,128)(2,1)} %copy-done.7) | copy-start | bytes 4713220
  41.9 1.5 %collective-permute-start.4 = (bf16[160,256]{1,0:T(8,128)(2,1)S(1)}, bf16[160,256]{1,0:T(8,128)(2,1)S(1)}, u32[]{:S(2)}, u32[]{:S(2)}) collective-permute-start(bf16[160,256]{1,0:T(8,128)(2,1)S(1)} %collective-permute-done.1.refs_3_.refs_2_), channel_id=1, source_target_pairs={{0,4},{4,0},{8,12},{12,8},{16,20},{20,16},{24,28},{28,24},{1,5},{5... | collective-permute-start | bytes 245768 | tf_op jit(solution)/shard_map/ppermute | solution.py:809
  42.5 1.3 %collective-permute-start.5 = (bf16[160,256]{1,0:T(8,128)(2,1)S(1)}, bf16[160,256]{1,0:T(8,128)(2,1)S(1)}, u32[]{:S(2)}, u32[]{:S(2)}) collective-permute-start(bf16[160,256]{1,0:T(8,128)(2,1)S(1)} %collective-permute-done.2.refs_5_.refs_4_), channel_id=1, source_target_pairs={{0,4},{4,0},{8,12},{12,8},{16,20},{20,16},{24,28},{28,24},{1,5},{5... | collective-permute-start | bytes 245768 | tf_op jit(solution)/shard_map/ppermute | solution.py:809
  42.6 1.4 %collective-permute-start.6 = (bf16[160,256]{1,0:T(8,128)(2,1)S(1)}, bf16[160,256]{1,0:T(8,128)(2,1)S(1)}, u32[]{:S(2)}, u32[]{:S(2)}) collective-permute-start(bf16[160,256]{1,0:T(8,128)(2,1)S(1)} %collective-permute-done.3.refs_7_.refs_6_), channel_id=1, source_target_pairs={{0,4},{4,0},{8,12},{12,8},{16,20},{20,16},{24,28},{28,24},{1,5},{5... | collective-permute-start | bytes 245768 | tf_op jit(solution)/shard_map/ppermute | solution.py:809
  48.4 8.4 %collective-permute-start.10 = (bf16[80,256]{1,0:T(8,128)(2,1)S(1)}, bf16[80,256]{1,0:T(8,128)(2,1)S(1)}, u32[]{:S(2)}, u32[]{:S(2)}) collective-permute-start(bf16[80,256]{1,0:T(8,128)(2,1)S(1)} %shard_map.114.refs_2_), channel_id=1, source_target_pairs={{0,24},{4,28},{8,16},{12,20},{16,8},{20,12},{24,0},{28,4},{1,25},{... | collective-permute-start | bytes 122888 | tf_op jit(solution)/shard_map/ppermute | solution.py:809
  51.1 5.7 %collective-permute-start.9 = (bf16[80,256]{1,0:T(8,128)(2,1)S(1)}, bf16[80,256]{1,0:T(8,128)(2,1)S(1)}, u32[]{:S(2)}, u32[]{:S(2)}) collective-permute-start(bf16[80,256]{1,0:T(8,128)(2,1)S(1)} %shard_map.114.refs_2_), channel_id=1, source_target_pairs={{0,16},{4,20},{8,24},{12,28},{16,0},{20,4},{24,8},{28,12},{1,17},{... | collective-permute-start | bytes 122888 | tf_op jit(solution)/shard_map/ppermute | solution.py:809
  51.7 5.1 %collective-permute-start.8 = (bf16[80,256]{1,0:T(8,128)(2,1)S(1)}, bf16[80,256]{1,0:T(8,128)(2,1)S(1)}, u32[]{:S(2)}, u32[]{:S(2)}) collective-permute-start(bf16[80,256]{1,0:T(8,128)(2,1)S(1)} %shard_map.114.refs_2_), channel_id=1, source_target_pairs={{0,8},{4,12},{8,0},{12,4},{16,24},{20,28},{24,16},{28,20},{1,9},{5... | collective-permute-start | bytes 122888 | tf_op jit(solution)/shard_map/ppermute | solution.py:809
  52.0 4.9 %collective-permute-start.7 = (bf16[80,256]{1,0:T(8,128)(2,1)S(1)}, bf16[80,256]{1,0:T(8,128)(2,1)S(1)}, u32[]{:S(2)}, u32[]{:S(2)}) collective-permute-start(bf16[80,256]{1,0:T(8,128)(2,1)S(1)} %shard_map.114.refs_2_), channel_id=1, source_target_pairs={{0,4},{4,0},{8,12},{12,8},{16,20},{20,16},{24,28},{28,24},{1,5},{5... | collective-permute-start | bytes 122888 | tf_op jit(solution)/shard_map/ppermute | solution.py:809
  56.8 1.4 %collective-permute-start.11 = (bf16[80,256]{1,0:T(8,128)(2,1)S(1)}, bf16[80,256]{1,0:T(8,128)(2,1)S(1)}, u32[]{:S(2)}, u32[]{:S(2)}) collective-permute-start(bf16[80,256]{1,0:T(8,128)(2,1)S(1)} %collective-permute-done.8.refs_4_), channel_id=1, source_target_pairs={{0,4},{4,0},{8,12},{12,8},{16,20},{20,16},{24,28},{28,24},{1,5},{5... | collective-permute-start | bytes 122888 | tf_op jit(solution)/shard_map/ppermute | solution.py:809
  57.4 1.2 %collective-permute-start.12 = (bf16[80,256]{1,0:T(8,128)(2,1)S(1)}, bf16[80,256]{1,0:T(8,128)(2,1)S(1)}, u32[]{:S(2)}, u32[]{:S(2)}) collective-permute-start(bf16[80,256]{1,0:T(8,128)(2,1)S(1)} %collective-permute-done.9.refs_6_), channel_id=1, source_target_pairs={{0,4},{4,0},{8,12},{12,8},{16,20},{20,16},{24,28},{28,24},{1,5},{5... | collective-permute-start | bytes 122888 | tf_op jit(solution)/shard_map/ppermute | solution.py:809
  57.5 1.3 %collective-permute-start.13 = (bf16[80,256]{1,0:T(8,128)(2,1)S(1)}, bf16[80,256]{1,0:T(8,128)(2,1)S(1)}, u32[]{:S(2)}, u32[]{:S(2)}) collective-permute-start(bf16[80,256]{1,0:T(8,128)(2,1)S(1)} %collective-permute-done.10.refs_8_), channel_id=1, source_target_pairs={{0,4},{4,0},{8,12},{12,8},{16,20},{20,16},{24,28},{28,24},{1,5},{5... | collective-permute-start | bytes 122888 | tf_op jit(solution)/shard_map/ppermute | solution.py:809
  58.8 16.2 %copy-start.9 = (s32[1,1024]{1,0:T(1,128)S(1)}, s32[1,1024]{1,0:T(1,128)}, u32[]{:S(2)}) copy-start(s32[1,1024]{1,0:T(1,128)} %get-tuple-element.76.refs_1_) | copy-start | bytes 12292

commit v11 on v10

--- a/solution.py
+++ b/solution.py
@@ -45,7 +45,7 @@
 OFFSETS = (2 * REACH + 1) ** 3 - 27
 FEATURES = 4
 PB = 256
-STRIP = 16
+STRIP = 32
 UNROLL_FIND, UNROLL_APPLY, UNROLL_GATHER = 16, 16, 16
 GRANT = 28
 GRANT_FIRST = 60
@@ -136,7 +136,8 @@
                 self.going[i] = copy
 
 
-def run(kernel, scalars, ins, outs, flops, scratch=(), late=(), here=(), stays=(), numbers=(), grant=GRANT):
+def run(kernel, scalars, ins, outs, flops, scratch=(), late=(), here=(), stays=(), numbers=(), grant=GRANT,
+        by_kernel=()):
     n_s, n_i, n_o, n_n = len(scalars), len(ins), len(outs), len(numbers)
     moved_in = [i for i in range(n_i) if i not in here]
     moved_out = [i for i in range(n_o) if i not in stays]
@@ -154,8 +155,9 @@
         io.wait(*[i for i in moved_in if i not in late])
         kernel(io, *counts, *refs)
         io.wait(*moved_in)
-        io.send(*moved_out)
-        for i in moved_out:
+        mine = [i for i in moved_out if i not in by_kernel]
+        io.send(*mine)
+        for i in mine:
             io.going[i].wait()
 
     return call(
@@ -384,7 +386,7 @@
         d_lo[h] = dot(low, here).astype(bf16)
 
 
-def route_kernel(own, cap, n_top, io):
+def route_kernel(own, cap, n_top, io, sem):
     pos, dens, slot, leaf = io.ins
     out, entries = io.outs
     points = pos.shape[1]
@@ -409,6 +411,7 @@
     entry = owner * cap + rank.astype(jnp.int32)
     entries[...] = entry
     inside_hi = inside // 64
+    io.wait(0, 1, 3)
     value = jnp.concatenate([pos[...], dens[...]], axis=0)
     width = value.shape[0]
     high, low = split(value)
@@ -425,6 +428,7 @@
     leaves = leaf[...].astype(f32)
     leaves = [leaves[r : r + 1] for r in range(leaves.shape[0])]
     lanes = leaf.shape[1]
+    going = []
     for o in range(owners * cap // block):
         there = entry == o * block + lax.broadcasted_iota(jnp.int32, (block, points), 0)
         there = jnp.where(there, 1.0, 0.0).astype(bf16)
@@ -442,6 +446,11 @@
                 for r, value_row in enumerate(leaves):
                     base = len(rows) * cap + r * lanes
                     out[at, q, :, base : base + lanes] = value_row
+        here = pl.ds(o * (block // cap), block // cap)
+        going.append(pltpu.make_async_copy(out.at[here], io.targets[0].at[here], sem.at[o]))
+        going[-1].start()
+    for copy in going:
+        copy.wait()
 
 
 def restore_kernel(n_top, io):
@@ -847,7 +856,10 @@
         ],
         [shape(n_pts, n_top, 1, width, dtype=f32), shape(1, points, dtype=jnp.int32)],
         1 << 27,
+        late=(0, 1, 3),
         stays=(1,),
+        by_kernel=(0,),
+        scratch=[pltpu.SemaphoreType.DMA((2 * points // max(cap, LANE),))],
         grant=GRANT_FIRST,
     )
     outgoing = outgoing.reshape(sources, 1, width)

time: 76.9 us -> 76.2 us (level)
  transfers between devices with their start and end apart: 15 -> 15, of which waited for: 6 -> 6; matrix products, arithmetic and copies ran while one was open for 0% -> 0% of each run, Pallas kernels for 29% -> 30%
where the time goes in v11:
time: 76.2 us; the launch traced here: 75.9 us
  Pallas kernels  42.3 us (56%)
  starting transfers between devices  16.6 us (22%)
  blocking collectives  13.2 us (17%)
  waiting for transfers between devices  1.82 us (2%)
  local copies, waits for them, and re-layouts  1.55 us (2%)
    pallas_call x7, Pallas kernels, run(): call(body, tuple(outs) + tuple(numbers), grant, flops, in_specs=[SMEM] *...  28.3 us
    pallas_call x2, Pallas kernels, relayout(): call(functools.partial(relayout_kernel, nrows, step0, steps), tuple((jax....  14.1 us
    all_to_all x1, blocking collectives, per_device(): lax.all_to_all(reply, ('pts', 'top'), split_axis=0, concat_axis=0, tiled=...  13.2 us
    ppermute x14, starting transfers between devices, shift_by(): return lax.ppermute(value, axis, [(i, i ^ distance) for i in range(size)])  9.27 us
    all_to_all x1, starting transfers between devices, per_device(): lax.all_to_all(outgoing, ('pts', 'top'), split_axis=0, concat_axis=0, til...  7.3 us
    ppermute x14, waiting for transfers between devices, shift_by(): return lax.ppermute(value, axis, [(i, i ^ distance) for i in range(size)])  1.81 us
    unnamed x20, local copies, waits for them, and re-layouts  1.55 us
  transfers between devices with their start and end apart: 15, of which 6 were waited for; matrix products, arithmetic and copies ran while one was open for 0% of the time, Pallas kernels for 30%

profile of v11, /device:TPU:0, one launch (start us, length us, event | category | flops | bytes accessed | tf_op | source)
XLA Modules:
  0.0 75.9 jit_solution(13228672606673138695)
XLA Ops:
  0.0 3.7 %shard_map.109 = (f32[8,4,1,2816]{3,2,1,0:T(1,128)}, s32[1,1024]{1,0:T(1,128)}) custom-call(f32[3,1024]{1,0:T(4,128)} %refs_0_.1, f32[8,1024]{1,0:T(8,128)} %refs_1_.1, s32[1,1024]{1,0:T(1,128)} %bitcast.16, s32[8,128]{1,0:T(8,128)} %bitcast.17), custom_call_target="tpu_custom_call" | custom-call | flops 134217728 | bytes 1048576 | tf_op jit(solution)/shard_map/pallas_call | solution.py:163
  3.7 7.3 %all-to-all-start = ((f32[32,1,2816]{2,1,0:T(1,128)}), f32[32,1,2816]{2,1,0:T(1,128)S(1)}, u32[]{:S(2)}, u32[]{:S(2)}) async-start(f32[32,1,2816]{2,1,0:T(1,128)} %bitcast.15), calls=%async_computation | async-start | bytes 720896 | tf_op jit(solution)/shard_map/all_to_all | solution.py:866
  11.1 0.1 pad_add_fusion.me_ref.refs_0_
  11.2 0.0 copy-start.6
  11.2 6.9 %shard_map.110 = (bf16[4,7,32,1152]{3,2,1,0:T(8,128)(2,1)}, bf16[3,4,32,1152]{3,2,1,0:T(8,128)(2,1)S(1)}, bf16[3,3,32,640]{3,2,1,0:T(8,128)(2,1)S(1)}) custom-call(s32[2]{0:T(128)S(1)} %pad_add_fusion.me_ref.refs_0_, bf16[57038,128]{1,0:T(8,128)(2,1)} %bitcast.11, bf16[57038,128]{1,0:T(8,128)(2,1)} %bitcast.12), custom_call_target="tpu_custom_call" | custom-call | flops 1048576 | bytes 4194304 | tf_op jit(solution)/shard_map/pallas_call | solution.py:300
  18.1 3.5 %shard_map.111 = (bf16[304,1280]{1,0:T(8,128)(2,1)S(1)}, bf16[34,152,152]{2,1,0:T(8,128)(2,1)S(1)}, bf16[2,152,80]{2,1,0:T(8,128)(2,1)S(1)}, bf16[2,152,80]{2,1,0:T(8,128)(2,1)S(1)}) custom-call(f32[1444,128]{1,0:T(8,128)S(1)} %bitcast.9, f32[1444,128]{1,0:T(8,128)S(1)} %bitcast.10, f32[152,152]{1,0:T(8,128)S(1)} %copy-done.3, f32[152,152]{1,0:T(8,128)S(1)} %copy-done.4, ...), custom_call_target="tpu_custom_call" | custom-call | flops 1073741824 | bytes 1048576 | tf_op jit(solution)/shard_map/pallas_call | solution.py:163
  21.7 1.5 %copy-done.7 = bf16[34,152,152]{2,1,0:T(8,128)(2,1)} copy-done((bf16[34,152,152]{2,1,0:T(8,128)(2,1)}, bf16[34,152,152]{2,1,0:T(8,128)(2,1)S(1)}, u32[]{:S(2)}) %copy-start.7) | copy-done | bytes 1571096
  23.2 7.4 %shard_map.112 = (bf16[160,256]{1,0:T(8,128)(2,1)S(1)}, f32[152,4096]{1,0:T(8,128)S(1)}, s32[1,4096]{1,0:T(1,128)S(1)}, s32[33]{0:T(128)S(1)}) custom-call(s32[2]{0:T(128)S(1)} %pad_add_fusion.me_ref.refs_0_, f32[32,1,2816]{2,1,0:T(1,128)S(1)} %all-to-all-done.refs_1_, f32[152,128]{1,0:T(8,128)S(1)} %copy-done.6, bf16[304,1280]{1,0:T(8,128)(2,1)S(1)} %get-tuple-element.46.refs_3_), custom_call_target="tpu_custom_call" | custom-call | flops 8589934592 | bytes 1048576 | tf_op jit(solution)/shard_map/pallas_call | solution.py:163
  30.6 2.7 %collective-permute-start.3 = (bf16[160,256]{1,0:T(8,128)(2,1)S(1)}, bf16[160,256]{1,0:T(8,128)(2,1)S(1)}, u32[]{:S(2)}, u32[]{:S(2)}) collective-permute-start(bf16[160,256]{1,0:T(8,128)(2,1)S(1)} %get-tuple-element.54.refs_1_.refs_0_), channel_id=1, source_target_pairs={{0,24},{4,28},{8,16},{12,20},{16,8},{20,12},{24,0},{28,4},{1,25},{... | collective-permute-start | bytes 245768 | tf_op jit(solution)/shard_map/ppermute | solution.py:818
  33.4 0.6 collective-permute-start.2
  33.9 0.3 collective-permute-start.1
  34.2 7.2 %shard_map.113 = (bf16[4,7,48,1152]{3,2,1,0:T(8,128)(2,1)S(1)}, bf16[3,4,48,1152]{3,2,1,0:T(8,128)(2,1)S(1)}, bf16[3,3,48,640]{3,2,1,0:T(8,128)(2,1)S(1)}) custom-call(s32[2]{0:T(128)S(1)} %pad_add_fusion.me_ref.refs_0_, bf16[57038,128]{1,0:T(8,128)(2,1)} %bitcast.13, bf16[57038,128]{1,0:T(8,128)(2,1)} %bitcast.14), custom_call_target="tpu_custom_call" | custom-call | flops 1048576 | bytes 6291456 | tf_op jit(solution)/shard_map/pallas_call | solution.py:300
  41.4 0.6 collective-permute-start.4
  42.0 0.1 collective-permute-start.5
  42.1 0.4 collective-permute-start.6
  42.5 0.4 collective-permute-done.4.refs_4_.refs_3_
  42.9 0.4 collective-permute-done.5.refs_6_.refs_5_
  43.3 0.2 collective-permute-done.6.refs_8_.refs_7_
  43.4 4.5 %shard_map.114.refs_2_ = bf16[80,256]{1,0:T(8,128)(2,1)S(1)} custom-call(s32[2]{0:T(128)S(1)} %pad_add_fusion.me_ref.refs_0_, bf16[160,256]{1,0:T(8,128)(2,1)S(1)} %get-tuple-element.54.refs_1_.refs_0_, bf16[160,256]{1,0:T(8,128)(2,1)S(1)} %collective-permute-done.refs_2_.refs_1_, bf16[160,256]{1,0:T(8,128)(2,1)S(1)} %collective-permute-done.1.refs_3_.refs_2_, ...), custom_call_target="tpu_custom_call" | custom-call | flops 8589934592 | bytes 1048576 | tf_op jit(solution)/shard_map/pallas_call | solution.py:163
  47.9 2.7 %collective-permute-start.10 = (bf16[80,256]{1,0:T(8,128)(2,1)S(1)}, bf16[80,256]{1,0:T(8,128)(2,1)S(1)}, u32[]{:S(2)}, u32[]{:S(2)}) collective-permute-start(bf16[80,256]{1,0:T(8,128)(2,1)S(1)} %shard_map.114.refs_2_), channel_id=1, source_target_pairs={{0,24},{4,28},{8,16},{12,20},{16,8},{20,12},{24,0},{28,4},{1,25},{... | collective-permute-start | bytes 122888 | tf_op jit(solution)/shard_map/ppermute | solution.py:818
  50.6 0.6 collective-permute-start.9
  51.2 0.3 collective-permute-start.8
  51.4 4.8 %shard_map.115.refs_12_ = f32[2,152,512]{2,1,0:T(8,128)S(1)} custom-call(bf16[160,256]{1,0:T(8,128)(2,1)S(1)} %get-tuple-element.54.refs_1_.refs_0_, bf16[160,256]{1,0:T(8,128)(2,1)S(1)} %collective-permute-done.refs_2_.refs_1_, bf16[160,256]{1,0:T(8,128)(2,1)S(1)} %collective-permute-done.1.refs_3_.refs_2_, ...), custom_call_target="tpu_custom_call" | custom-call | flops 4294967296 | bytes 1048576 | tf_op jit(solution)/shard_map/pallas_call | solution.py:163
  56.3 0.6 collective-permute-start.11
  56.9 0.1 collective-permute-start.12
  57.0 0.4 collective-permute-start.13
  57.4 0.4 collective-permute-done.11.refs_5_
  57.8 0.3 collective-permute-done.12.refs_7_
  58.1 0.2 collective-permute-done.13.refs_9_
  58.3 3.0 %shard_map.116 = f32[32,1,512]{2,1,0:T(1,128)S(1)} custom-call(s32[2]{0:T(128)S(1)} %pad_add_fusion.me_ref.refs_0_, s32[33]{0:T(128)S(1)} %get-tuple-element.47.refs_1_, bf16[80,256]{1,0:T(8,128)(2,1)S(1)} %shard_map.114.refs_2_, bf16[80,256]{1,0:T(8,128)(2,1)S(1)} %collective-permute-done.7.refs_3_, bf16[80,256]{1,0:T(8,128)(2,1)S(1)} %collective-permute-done.8.refs_4_, ...), custom_call_target="tpu_custom_call" | custom-call | flops 4294967296 | bytes 1048576 | tf_op jit(solution)/shard_map/pallas_call | solution.py:163
  61.3 13.2 %all_to_all.10.refs_0_ = f32[32,1,512]{2,1,0:T(1,128)S(1)} all-to-all(f32[32,1,512]{2,1,0:T(1,128)S(1)} %shard_map.116), channel_id=1, replica_groups=mesh['pts'=8,'top'=4] {'pts','top'}, dimensions={0} | all-to-all | bytes 131072 | tf_op jit(solution)/shard_map/all_to_all | solution.py:948
  74.4 1.3 %shard_map.117 = f32[8,1024]{1,0:T(8,128)} custom-call(f32[32,1,512]{2,1,0:T(1,128)S(1)} %all_to_all.10.refs_0_, s32[1,1024]{1,0:T(1,128)S(1)} %copy-done.9), custom_call_target="tpu_custom_call" | custom-call | flops 268435456 | bytes 1048576 | tf_op jit(solution)/shard_map/pallas_call | solution.py:163
  (29 shorter events, 0.1 us)
Async XLA Ops:
  3.7 19.4 %all-to-all-start = ((f32[32,1,2816]{2,1,0:T(1,128)}), f32[32,1,2816]{2,1,0:T(1,128)S(1)}, u32[]{:S(2)}, u32[]{:S(2)}) async-start(f32[32,1,2816]{2,1,0:T(1,128)} %bitcast.15), calls=%async_computation | async-start | bytes 720896 | tf_op jit(solution)/shard_map/all_to_all | solution.py:866
  11.1 6.9 %copy-start.1 = (f32[184832]{0:T(1024)S(1)}, f32[184832]{0:T(1024)}, u32[]{:S(2)}) copy-start(f32[184832]{0:T(1024)} %param.16) | copy-start | bytes 2217988
  11.1 7.0 %copy-start.2 = (f32[184832]{0:T(1024)S(1)}, f32[184832]{0:T(1024)}, u32[]{:S(2)}) copy-start(f32[184832]{0:T(1024)} %param.20) | copy-start | bytes 2217988
  11.1 7.0 %copy-start.3 = (f32[152,152]{1,0:T(8,128)S(1)}, f32[152,152]{1,0:T(8,128)}, u32[]{:S(2)}) copy-start(f32[152,152]{1,0:T(8,128)} %refs_2_.2) | copy-start | bytes 277252
  11.1 7.0 %copy-start.4 = (f32[152,152]{1,0:T(8,128)S(1)}, f32[152,152]{1,0:T(8,128)}, u32[]{:S(2)}) copy-start(f32[152,152]{1,0:T(8,128)} %refs_3_.1) | copy-start | bytes 277252
  11.1 7.0 %copy-start.5 = (f32[152,152]{1,0:T(8,128)S(1)}, f32[152,152]{1,0:T(8,128)}, u32[]{:S(2)}) copy-start(f32[152,152]{1,0:T(8,128)} %refs_4_.1) | copy-start | bytes 277252
  11.2 7.0 %copy-start.6 = (f32[152,128]{1,0:T(8,128)S(1)}, f32[152,128]{1,0:T(8,128)}, u32[]{:S(2)}) copy-start(f32[152,128]{1,0:T(8,128)} %constant.11.clone.refs_5_.refs_2_) | copy-start | bytes 233476
  21.7 1.5 %copy-start.7 = (bf16[34,152,152]{2,1,0:T(8,128)(2,1)}, bf16[34,152,152]{2,1,0:T(8,128)(2,1)S(1)}, u32[]{:S(2)}) copy-start(bf16[34,152,152]{2,1,0:T(8,128)(2,1)S(1)} %get-tuple-element.65.refs_8_) | copy-start | bytes 4713220
  30.6 10.7 %collective-permute-start.3 = (bf16[160,256]{1,0:T(8,128)(2,1)S(1)}, bf16[160,256]{1,0:T(8,128)(2,1)S(1)}, u32[]{:S(2)}, u32[]{:S(2)}) collective-permute-start(bf16[160,256]{1,0:T(8,128)(2,1)S(1)} %get-tuple-element.54.refs_1_.refs_0_), channel_id=1, source_target_pairs={{0,24},{4,28},{8,16},{12,20},{16,8},{20,12},{24,0},{28,4},{1,25},{... | collective-permute-start | bytes 245768 | tf_op jit(solution)/shard_map/ppermute | solution.py:818
  33.4 8.0 %collective-permute-start.2 = (bf16[160,256]{1,0:T(8,128)(2,1)S(1)}, bf16[160,256]{1,0:T(8,128)(2,1)S(1)}, u32[]{:S(2)}, u32[]{:S(2)}) collective-permute-start(bf16[160,256]{1,0:T(8,128)(2,1)S(1)} %get-tuple-element.54.refs_1_.refs_0_), channel_id=1, source_target_pairs={{0,16},{4,20},{8,24},{12,28},{16,0},{20,4},{24,8},{28,12},{1,17},{... | collective-permute-start | bytes 245768 | tf_op jit(solution)/shard_map/ppermute | solution.py:818
  33.9 7.5 %collective-permute-start.1 = (bf16[160,256]{1,0:T(8,128)(2,1)S(1)}, bf16[160,256]{1,0:T(8,128)(2,1)S(1)}, u32[]{:S(2)}, u32[]{:S(2)}) collective-permute-start(bf16[160,256]{1,0:T(8,128)(2,1)S(1)} %get-tuple-element.54.refs_1_.refs_0_), channel_id=1, source_target_pairs={{0,8},{4,12},{8,0},{12,4},{16,24},{20,28},{24,16},{28,20},{1,9},{5... | collective-permute-start | bytes 245768 | tf_op jit(solution)/shard_map/ppermute | solution.py:818
  34.2 7.2 %collective-permute-start = (bf16[160,256]{1,0:T(8,128)(2,1)S(1)}, bf16[160,256]{1,0:T(8,128)(2,1)S(1)}, u32[]{:S(2)}, u32[]{:S(2)}) collective-permute-start(bf16[160,256]{1,0:T(8,128)(2,1)S(1)} %get-tuple-element.54.refs_1_.refs_0_), channel_id=1, source_target_pairs={{0,4},{4,0},{8,12},{12,8},{16,20},{20,16},{24,28},{28,24},{1,5},{5... | collective-permute-start | bytes 245768 | tf_op jit(solution)/shard_map/ppermute | solution.py:818
  34.2 9.2 %copy-start = (bf16[4,7,32,1152]{3,2,1,0:T(8,128)(2,1)S(1)}, bf16[4,7,32,1152]{3,2,1,0:T(8,128)(2,1)}, u32[]{:S(2)}) copy-start(bf16[4,7,32,1152]{3,2,1,0:T(8,128)(2,1)} %get-tuple-element.59.refs_9_) | copy-start | bytes 6193156
  41.4 10.0 %copy-start.8 = (bf16[34,152,152]{2,1,0:T(8,128)(2,1)S(1)}, bf16[34,152,152]{2,1,0:T(8,128)(2,1)}, u32[]{:S(2)}) copy-start(bf16[34,152,152]{2,1,0:T(8,128)(2,1)} %copy-done.7) | copy-start | bytes 4713220
  41.4 1.5 %collective-permute-start.4 = (bf16[160,256]{1,0:T(8,128)(2,1)S(1)}, bf16[160,256]{1,0:T(8,128)(2,1)S(1)}, u32[]{:S(2)}, u32[]{:S(2)}) collective-permute-start(bf16[160,256]{1,0:T(8,128)(2,1)S(1)} %collective-permute-done.1.refs_3_.refs_2_), channel_id=1, source_target_pairs={{0,4},{4,0},{8,12},{12,8},{16,20},{20,16},{24,28},{28,24},{1,5},{5... | collective-permute-start | bytes 245768 | tf_op jit(solution)/shard_map/ppermute | solution.py:818
  42.0 1.3 %collective-permute-start.5 = (bf16[160,256]{1,0:T(8,128)(2,1)S(1)}, bf16[160,256]{1,0:T(8,128)(2,1)S(1)}, u32[]{:S(2)}, u32[]{:S(2)}) collective-permute-start(bf16[160,256]{1,0:T(8,128)(2,1)S(1)} %collective-permute-done.2.refs_5_.refs_4_), channel_id=1, source_target_pairs={{0,4},{4,0},{8,12},{12,8},{16,20},{20,16},{24,28},{28,24},{1,5},{5... | collective-permute-start | bytes 245768 | tf_op jit(solution)/shard_map/ppermute | solution.py:818
  42.1 1.4 %collective-permute-start.6 = (bf16[160,256]{1,0:T(8,128)(2,1)S(1)}, bf16[160,256]{1,0:T(8,128)(2,1)S(1)}, u32[]{:S(2)}, u32[]{:S(2)}) collective-permute-start(bf16[160,256]{1,0:T(8,128)(2,1)S(1)} %collective-permute-done.3.refs_7_.refs_6_), channel_id=1, source_target_pairs={{0,4},{4,0},{8,12},{12,8},{16,20},{20,16},{24,28},{28,24},{1,5},{5... | collective-permute-start | bytes 245768 | tf_op jit(solution)/shard_map/ppermute | solution.py:818
  47.9 8.4 %collective-permute-start.10 = (bf16[80,256]{1,0:T(8,128)(2,1)S(1)}, bf16[80,256]{1,0:T(8,128)(2,1)S(1)}, u32[]{:S(2)}, u32[]{:S(2)}) collective-permute-start(bf16[80,256]{1,0:T(8,128)(2,1)S(1)} %shard_map.114.refs_2_), channel_id=1, source_target_pairs={{0,24},{4,28},{8,16},{12,20},{16,8},{20,12},{24,0},{28,4},{1,25},{... | collective-permute-start | bytes 122888 | tf_op jit(solution)/shard_map/ppermute | solution.py:818
  50.6 5.7 %collective-permute-start.9 = (bf16[80,256]{1,0:T(8,128)(2,1)S(1)}, bf16[80,256]{1,0:T(8,128)(2,1)S(1)}, u32[]{:S(2)}, u32[]{:S(2)}) collective-permute-start(bf16[80,256]{1,0:T(8,128)(2,1)S(1)} %shard_map.114.refs_2_), channel_id=1, source_target_pairs={{0,16},{4,20},{8,24},{12,28},{16,0},{20,4},{24,8},{28,12},{1,17},{... | collective-permute-start | bytes 122888 | tf_op jit(solution)/shard_map/ppermute | solution.py:818
  51.2 5.1 %collective-permute-start.8 = (bf16[80,256]{1,0:T(8,128)(2,1)S(1)}, bf16[80,256]{1,0:T(8,128)(2,1)S(1)}, u32[]{:S(2)}, u32[]{:S(2)}) collective-permute-start(bf16[80,256]{1,0:T(8,128)(2,1)S(1)} %shard_map.114.refs_2_), channel_id=1, source_target_pairs={{0,8},{4,12},{8,0},{12,4},{16,24},{20,28},{24,16},{28,20},{1,9},{5... | collective-permute-start | bytes 122888 | tf_op jit(solution)/shard_map/ppermute | solution.py:818
  51.4 4.9 %collective-permute-start.7 = (bf16[80,256]{1,0:T(8,128)(2,1)S(1)}, bf16[80,256]{1,0:T(8,128)(2,1)S(1)}, u32[]{:S(2)}, u32[]{:S(2)}) collective-permute-start(bf16[80,256]{1,0:T(8,128)(2,1)S(1)} %shard_map.114.refs_2_), channel_id=1, source_target_pairs={{0,4},{4,0},{8,12},{12,8},{16,20},{20,16},{24,28},{28,24},{1,5},{5... | collective-permute-start | bytes 122888 | tf_op jit(solution)/shard_map/ppermute | solution.py:818
  56.3 1.4 %collective-permute-start.11 = (bf16[80,256]{1,0:T(8,128)(2,1)S(1)}, bf16[80,256]{1,0:T(8,128)(2,1)S(1)}, u32[]{:S(2)}, u32[]{:S(2)}) collective-permute-start(bf16[80,256]{1,0:T(8,128)(2,1)S(1)} %collective-permute-done.8.refs_4_), channel_id=1, source_target_pairs={{0,4},{4,0},{8,12},{12,8},{16,20},{20,16},{24,28},{28,24},{1,5},{5... | collective-permute-start | bytes 122888 | tf_op jit(solution)/shard_map/ppermute | solution.py:818
  56.9 1.2 %collective-permute-start.12 = (bf16[80,256]{1,0:T(8,128)(2,1)S(1)}, bf16[80,256]{1,0:T(8,128)(2,1)S(1)}, u32[]{:S(2)}, u32[]{:S(2)}) collective-permute-start(bf16[80,256]{1,0:T(8,128)(2,1)S(1)} %collective-permute-done.9.refs_6_), channel_id=1, source_target_pairs={{0,4},{4,0},{8,12},{12,8},{16,20},{20,16},{24,28},{28,24},{1,5},{5... | collective-permute-start | bytes 122888 | tf_op jit(solution)/shard_map/ppermute | solution.py:818
  57.0 1.3 %collective-permute-start.13 = (bf16[80,256]{1,0:T(8,128)(2,1)S(1)}, bf16[80,256]{1,0:T(8,128)(2,1)S(1)}, u32[]{:S(2)}, u32[]{:S(2)}) collective-permute-start(bf16[80,256]{1,0:T(8,128)(2,1)S(1)} %collective-permute-done.10.refs_8_), channel_id=1, source_target_pairs={{0,4},{4,0},{8,12},{12,8},{16,20},{20,16},{24,28},{28,24},{1,5},{5... | collective-permute-start | bytes 122888 | tf_op jit(solution)/shard_map/ppermute | solution.py:818
  58.3 16.2 %copy-start.9 = (s32[1,1024]{1,0:T(1,128)S(1)}, s32[1,1024]{1,0:T(1,128)}, u32[]{:S(2)}) copy-start(s32[1,1024]{1,0:T(1,128)} %get-tuple-element.76.refs_1_) | copy-start | bytes 12292
